TPU v7x, 128 devices: a whole 4x4x4 slice. The times are simulated.
128 devices in a mesh: ctx: 64 (over z, y_hi, x, core), wsh: 2 (over y_lo).
Axes of the slice: x: 4, y: 4 (y_hi: 2, y_lo: 2; y = y_hi * 2 + y_lo), z: 4, core: 2. Of those that a mesh axis runs over, the one named last changes fastest.
Arguments:
- tokens: bfloat16 [8192, 2048], P('ctx'), may hold values from -6 to 6
- cotangent: bfloat16 [8192, 2048], P('ctx'), may hold values from -6 to 6
- seq_lengths: int32 [4], replicated, may hold values from 1 to 4096, 8192 in all
- block_order: int32 [128], replicated, may hold values from 0 to 127, as said below
- routes: int32 [8192, 8], P('ctx'), may hold values from 0 to 127, all different within a row; in each aligned block of 128 rows (0 to 127, 128 to 255, ...) at most 12 rows name the same one
- w_query: float32 [2048, 4096], P('ctx', 'wsh'), may hold values from -0.125 to 0.125
- key_weight: float32 [2048, 512], P('ctx', 'wsh'), may hold values from -0.125 to 0.125
- value_weight: float32 [2048, 512], P('ctx', 'wsh'), may hold values from -0.125 to 0.125
- w_out: float32 [4096, 2048], P('wsh', 'ctx'), may hold values from -0.75 to 0.75
- gain_attn: float32 [2048], P('ctx'), may hold values from 0.5 to 1.5
- gain_query: float32 [128], replicated, may hold values from 0.5 to 1.5
- gain_key: float32 [128], replicated, may hold values from 0.5 to 1.5
- gain_ffn: float32 [2048], P('ctx'), may hold values from 0.5 to 1.5
- w_router: float32 [2048, 128], P('ctx'), may hold values from -0.0625 to 0.0625
- w_gate: float32 [128, 2048, 768], P('ctx', None, 'wsh'), may hold values from -0.125 to 0.125
- w_up: float32 [128, 2048, 768], P('ctx', None, 'wsh'), may hold values from -0.125 to 0.125
- w_down: float32 [128, 768, 2048], P('ctx', 'wsh'), may hold values from -0.875 to 0.875
Outputs:
- out_stream: float32 [8192, 2048], P('ctx')
- grad_tokens: float32 [8192, 2048], P('ctx')
- grad_query: float32 [2048, 4096], P('ctx', 'wsh')
- grad_key: float32 [2048, 512], P('ctx', 'wsh')
- grad_value: float32 [2048, 512], P('ctx', 'wsh')
- grad_out: float32 [4096, 2048], P('wsh', 'ctx')
- grad_gain_attn: float32 [2048], P('ctx')
- grad_gain_query: float32 [128], replicated
- grad_gain_key: float32 [128], replicated
- grad_gain_ffn: float32 [2048], P('ctx')
- grad_router: float32 [2048, 128], P('ctx')
- grad_gate: float32 [128, 2048, 768], P('ctx', None, 'wsh')
- grad_up: float32 [128, 2048, 768], P('ctx', None, 'wsh')
- grad_down: float32 [128, 768, 2048], P('ctx', 'wsh')
Inputs may be any that keep to these rules, and one draw needn't show every extreme that they name: `seq_lengths`: the lengths of the 4 sequences sum to 8192; the longest is exactly 4096. `block_order`: A permutation of the 128 natural blocks. The blocks of one device, entries c * 2 to c * 2 + 1, lie one in each aligned run of 64 consecutive natural blocks. `routes`: each row names 8 different experts; within the rows of one device no expert is named more than 12 times.
All inputs are finite; a program needn't handle non-finite values.
Results may differ from a plain program's by a relative error of at most 0.03.
Values may be sent and summed in bfloat16 or wider, within the bound.
A program may use at most 384 MiB of HBM per device.

v0:
```python
import math

import jax
import jax.numpy as jnp
from jax import lax
from jax.sharding import PartitionSpec as P

HEAD_WIDTH = 128
TOPK = 8
BLK = 64
MAX_SEQ_TOKENS = 4096


EPSILON = 1e-06
ROPE_BASE = 1000000.0
MASKED = -1e30


def to_low(value_rows):
    return value_rows.astype(jnp.bfloat16)


def rounded(value_rows):
    return lax.optimization_barrier(value_rows.astype(jnp.bfloat16)).astype(jnp.float32)


def matmul(left, right):
    return jnp.dot(left, right, preferred_element_type=jnp.float32)


def times_transposed(left, right):
    return lax.dot_general(
        left, right, (((1,), (1,)), ((), ())), preferred_element_type=jnp.float32
    )


def transposed_times(left, right):
    return lax.dot_general(
        left, right, (((0,), (0,)), ((), ())), preferred_element_type=jnp.float32
    )


def norm_rows(value_rows, gain_vec):
    inverse_rms = lax.rsqrt(jnp.mean(value_rows * value_rows, axis=-1, keepdims=True) + EPSILON)
    return (value_rows * inverse_rms * gain_vec, inverse_rms)


def norm_back(value_rows, inverse_rms, gain_vec, gradient):
    weighted = gradient * gain_vec
    mean_term = jnp.mean(weighted * value_rows, axis=-1, keepdims=True)
    d_values = (
        inverse_rms * weighted - value_rows * (inverse_rms * inverse_rms * inverse_rms) * mean_term
    )
    return (d_values, gradient * value_rows * inverse_rms)


def rope_tables(positions):
    half_dim = HEAD_WIDTH // 2
    frequency = jnp.power(ROPE_BASE, -2.0 * jnp.arange(half_dim, dtype=jnp.float32) / HEAD_WIDTH)
    angles = positions.astype(jnp.float32)[:, None] * frequency[None, :]
    angles = jnp.concatenate([angles, angles], axis=-1)
    return (jnp.cos(angles)[:, None, :], jnp.sin(angles)[:, None, :])


def rotate(value_rows, cosine, sine_tab):
    half_dim = value_rows.shape[-1] // 2
    turned = jnp.concatenate([-value_rows[..., half_dim:], value_rows[..., :half_dim]], axis=-1)
    return value_rows * cosine + turned * sine_tab


def rotate_back(gradient, cosine, sine_tab):
    half_dim = gradient.shape[-1] // 2
    shifted = gradient * sine_tab
    return gradient * cosine + jnp.concatenate(
        [shifted[..., half_dim:], -shifted[..., :half_dim]], axis=-1
    )


def seq_starts(positions, seq_lengths):
    offsets = jnp.cumsum(seq_lengths) - seq_lengths
    inside = offsets[None, :] <= positions[:, None]
    return jnp.max(jnp.where(inside, offsets[None, :], 0), axis=1)


def local(
    tokens,
    cotangent,
    seq_lengths,
    block_order,
    routes,
    w_query,
    key_weight,
    value_weight,
    w_out,
    gain_attn,
    gain_query,
    gain_key,
    gain_ffn,
    w_router,
    w_gate,
    w_up,
    w_down,
):
    row_count = tokens.shape[0]
    model_width = tokens.shape[1]
    ctx_count = lax.axis_size("ctx")
    total_rows = row_count * ctx_count
    per_device = row_count // BLK
    block_count = total_rows // BLK
    q_heads = w_query.shape[1] // HEAD_WIDTH
    kv_heads = key_weight.shape[1] // HEAD_WIDTH
    query_per_key_head = q_heads // kv_heads
    channels = kv_heads * HEAD_WIDTH
    experts = w_router.shape[1]
    capacity = max(2, 3 * row_count * TOPK // (2 * experts))
    pair_count = row_count * TOPK
    score_scale = 1.0 / math.sqrt(HEAD_WIDTH)
    margin = MAX_SEQ_TOKENS - BLK
    wsh_here = lax.axis_index("wsh")
    device_here = lax.axis_index("ctx")
    my_blocks = lax.dynamic_slice_in_dim(block_order, device_here * per_device, per_device, 0)
    query_pos = (my_blocks[:, None] * BLK + jnp.arange(BLK, dtype=jnp.int32)[None, :]).reshape(
        row_count
    )
    query_start = seq_starts(query_pos, seq_lengths)
    cosine, sine_tab = rope_tables(query_pos - query_start)
    wq, key_matrix, value_matrix, wo, wr, g_attn, g_ffn = (
        lax.all_gather(to_low(w_query), "ctx", axis=0, tiled=True),
        lax.all_gather(to_low(key_weight), "ctx", axis=0, tiled=True),
        lax.all_gather(to_low(value_weight), "ctx", axis=0, tiled=True),
        lax.all_gather(to_low(w_out), "ctx", axis=1, tiled=True),
        lax.all_gather(to_low(w_router), "ctx", axis=0, tiled=True),
        lax.all_gather(to_low(gain_attn), "ctx", axis=0, tiled=True),
        lax.all_gather(to_low(gain_ffn), "ctx", axis=0, tiled=True),
    )
    g_query = rounded(gain_query)
    g_key = rounded(gain_key)
    stream = tokens.astype(jnp.float32)
    normed_one, inverse_one = norm_rows(stream, g_attn.astype(jnp.float32))
    hidden_after_attn = to_low(normed_one)
    q_pre = matmul(hidden_after_attn, wq).reshape(row_count, q_heads, HEAD_WIDTH)
    key_before_norm = matmul(hidden_after_attn, key_matrix).reshape(row_count, kv_heads, HEAD_WIDTH)
    values_own = to_low(matmul(hidden_after_attn, value_matrix))
    q_normed, q_inverse = norm_rows(q_pre, g_query)
    k_normed, k_inverse = norm_rows(key_before_norm, g_key)
    query_matrix = to_low(rotate(q_normed, cosine, sine_tab))
    keys_own = to_low(rotate(k_normed, cosine, sine_tab)).reshape(row_count, channels)
    keys_all, values_all = (
        lax.all_gather(keys_own, "ctx", axis=0, tiled=True),
        lax.all_gather(values_own, "ctx", axis=0, tiled=True),
    )
    inverse_order = (
        jnp.zeros((block_count,), jnp.int32)
        .at[block_order]
        .set(jnp.arange(block_count, dtype=jnp.int32))
    )

    def natural_pad(source):
        ordered = jnp.take(
            source.reshape(block_count, BLK, channels), inverse_order, axis=0
        ).reshape(total_rows, channels)
        return jnp.concatenate([jnp.zeros((margin, channels), ordered.dtype), ordered], axis=0)

    def windows(source):

        def one_window(block_id):
            return lax.dynamic_slice_in_dim(source, block_id * BLK, MAX_SEQ_TOKENS, 0)

        return jax.vmap(one_window)(my_blocks).reshape(
            per_device, MAX_SEQ_TOKENS, kv_heads, HEAD_WIDTH
        )

    key_win = windows(natural_pad(keys_all))
    value_win = windows(natural_pad(values_all))
    key_pos = (
        my_blocks[:, None] * BLK
        + BLK
        - MAX_SEQ_TOKENS
        + jnp.arange(MAX_SEQ_TOKENS, dtype=jnp.int32)[None, :]
    )
    qpos_blocks = query_pos.reshape(per_device, BLK)
    qstart_blocks = query_start.reshape(per_device, BLK)
    allowed = (key_pos[:, None, :] <= qpos_blocks[:, :, None]) & (
        key_pos[:, None, :] >= qstart_blocks[:, :, None]
    )
    q_blocks = query_matrix.reshape(per_device, BLK, kv_heads, query_per_key_head, HEAD_WIDTH)

    def scores_of():
        scored = (
            jnp.einsum("nqkgd,nskd->nkgqs", q_blocks, key_win, preferred_element_type=jnp.float32)
            * score_scale
        )
        return jnp.where(allowed[:, None, None, :, :], scored, MASKED)

    scores = scores_of()
    highest = jnp.max(scores, axis=-1, keepdims=True)
    exps = jnp.exp(scores - highest)
    row_totals = jnp.sum(exps, axis=-1, keepdims=True)
    probs = exps / row_totals
    log_totals = highest + jnp.log(row_totals)
    mixed = jnp.einsum(
        "nkgqs,nskd->nqkgd", to_low(probs), value_win, preferred_element_type=jnp.float32
    )
    attn_heads = to_low(mixed.reshape(row_count, q_heads * HEAD_WIDTH))
    attn_total = lax.psum(matmul(attn_heads, wo).astype(jnp.bfloat16), "wsh").astype(jnp.float32)
    residual = stream + attn_total
    normed_two, inverse_two = norm_rows(residual, g_ffn.astype(jnp.float32))
    hidden_two = to_low(normed_two)
    logits = matmul(hidden_two, wr)
    route_mask = (routes[:, :, None] == jnp.arange(experts, dtype=jnp.int32)[None, None, :]).astype(
        jnp.float32
    )
    chosen = jnp.sum(logits[:, None, :] * route_mask, axis=-1)
    chosen_top = jnp.max(chosen, axis=-1, keepdims=True)
    gate_exps = jnp.exp(chosen - chosen_top)
    gates = gate_exps / jnp.sum(gate_exps, axis=-1, keepdims=True)
    flat_routes = routes.reshape(pair_count)
    expert_hits = (flat_routes[:, None] == jnp.arange(experts, dtype=jnp.int32)[None, :]).astype(
        jnp.int32
    )
    slot_rank = jnp.sum((jnp.cumsum(expert_hits, axis=0) - expert_hits) * expert_hits, axis=1)
    slot_index = flat_routes * capacity + slot_rank
    pair_of_slot = (
        jnp.full((experts * capacity,), pair_count, jnp.int32)
        .at[slot_index]
        .set(jnp.arange(pair_count, dtype=jnp.int32))
    )

    def send_rows(rows):
        landed = lax.all_to_all(rows, "ctx", split_axis=0, concat_axis=1, tiled=True)
        return landed

    def return_rows(parts):
        return lax.all_to_all(
            parts.astype(jnp.bfloat16), "ctx", split_axis=1, concat_axis=0, tiled=True
        ).astype(parts.dtype)

    def pick_pairs(back):
        share = back.shape[1]
        local_slot = flat_routes * share + slot_rank % share
        owned = slot_rank // share == wsh_here % (capacity // share)
        taken = jnp.take(back.reshape(experts * share, model_width), local_slot, axis=0)
        return jnp.where(owned[:, None], taken, 0.0)

    hidden_ext = jnp.concatenate([hidden_two, jnp.zeros((1, model_width), jnp.bfloat16)], axis=0)
    outgoing = jnp.take(hidden_ext, pair_of_slot // TOPK, axis=0).reshape(
        experts, capacity, model_width
    )
    arrived = send_rows(outgoing)
    gate_w = to_low(w_gate)
    up_w = to_low(w_up)
    down_w = to_low(w_down)
    gate_pre = jnp.einsum("ecd,edf->ecf", arrived, gate_w, preferred_element_type=jnp.float32)
    up_pre = jnp.einsum("ecd,edf->ecf", arrived, up_w, preferred_element_type=jnp.float32)
    sigma = jax.nn.sigmoid(gate_pre)
    activated = to_low(gate_pre * sigma * up_pre)
    expert_part = jnp.einsum("ecf,efd->ecd", activated, down_w, preferred_element_type=jnp.float32)
    returned = return_rows(expert_part)
    per_pair = pick_pairs(returned).reshape(row_count, TOPK, model_width)
    moe_total = lax.psum(
        jnp.sum(gates[:, :, None] * per_pair, axis=1).astype(jnp.bfloat16), "wsh"
    ).astype(jnp.float32)
    out_stream = residual + moe_total
    wq, key_matrix, value_matrix, wo, wr, g_attn, g_ffn = (
        lax.all_gather(to_low(w_query), "ctx", axis=0, tiled=True),
        lax.all_gather(to_low(key_weight), "ctx", axis=0, tiled=True),
        lax.all_gather(to_low(value_weight), "ctx", axis=0, tiled=True),
        lax.all_gather(to_low(w_out), "ctx", axis=1, tiled=True),
        lax.all_gather(to_low(w_router), "ctx", axis=0, tiled=True),
        lax.all_gather(to_low(gain_attn), "ctx", axis=0, tiled=True),
        lax.all_gather(to_low(gain_ffn), "ctx", axis=0, tiled=True),
    )
    d_out = cotangent.astype(jnp.float32)
    d_gates_part = jnp.sum(per_pair * d_out[:, None, :], axis=-1)
    d_pairs = to_low(gates[:, :, None] * d_out[:, None, :]).reshape(pair_count, model_width)
    d_pairs_ext = jnp.concatenate([d_pairs, jnp.zeros((1, model_width), jnp.bfloat16)], axis=0)
    d_outgoing = jnp.take(d_pairs_ext, pair_of_slot, axis=0).reshape(experts, capacity, model_width)
    d_arrived = send_rows(d_outgoing)
    d_act = jnp.einsum("ecd,efd->ecf", d_arrived, down_w, preferred_element_type=jnp.float32)
    grad_down = jnp.einsum("ecf,ecd->efd", activated, d_arrived, preferred_element_type=jnp.float32)
    d_gate_pre = to_low(d_act * up_pre * sigma * (1.0 + gate_pre * (1.0 - sigma)))
    d_up_pre = to_low(d_act * gate_pre * sigma)
    grad_gate = jnp.einsum("ecd,ecf->edf", arrived, d_gate_pre, preferred_element_type=jnp.float32)
    grad_up = jnp.einsum("ecd,ecf->edf", arrived, d_up_pre, preferred_element_type=jnp.float32)
    d_rows = jnp.einsum(
        "ecf,edf->ecd", d_gate_pre, gate_w, preferred_element_type=jnp.float32
    ) + jnp.einsum("ecf,edf->ecd", d_up_pre, up_w, preferred_element_type=jnp.float32)
    d_returned = return_rows(d_rows)
    d_hidden_part = jnp.sum(pick_pairs(d_returned).reshape(row_count, TOPK, model_width), axis=1)
    d_hidden_moe, d_gates = (
        lax.psum(d_hidden_part.astype(jnp.bfloat16), "wsh").astype(jnp.float32),
        lax.psum(d_gates_part.astype(jnp.bfloat16), "wsh").astype(jnp.float32),
    )
    d_chosen = gates * (d_gates - jnp.sum(gates * d_gates, axis=-1, keepdims=True))
    d_logits = to_low(jnp.sum(d_chosen[:, :, None] * route_mask, axis=1))
    grad_router = transposed_times(hidden_two, d_logits)
    d_hidden_two = d_hidden_moe + times_transposed(d_logits, wr)
    d_res_norm, ffn_gain_terms = norm_back(
        residual, inverse_two, g_ffn.astype(jnp.float32), d_hidden_two
    )
    d_residual = d_out + d_res_norm
    d_attn = to_low(d_residual)
    grad_out = transposed_times(attn_heads, d_attn)
    d_heads = to_low(times_transposed(d_attn, wo)).reshape(
        per_device, BLK, kv_heads, query_per_key_head, HEAD_WIDTH
    )
    scores_again = scores_of()
    probs_back = jnp.exp(scores_again - log_totals)
    d_probs = jnp.einsum(
        "nqkgd,nskd->nkgqs", d_heads, value_win, preferred_element_type=jnp.float32
    )
    d_rowsum = jnp.sum(probs_back * d_probs, axis=-1, keepdims=True)
    d_scores = to_low(probs_back * (d_probs - d_rowsum))
    d_queries = (
        jnp.einsum("nkgqs,nskd->nqkgd", d_scores, key_win, preferred_element_type=jnp.float32)
        * score_scale
    )
    d_key_win = (
        jnp.einsum("nkgqs,nqkgd->nskd", d_scores, q_blocks, preferred_element_type=jnp.float32)
        * score_scale
    ).reshape(per_device, MAX_SEQ_TOKENS, channels)
    d_value_win = jnp.einsum(
        "nkgqs,nqkgd->nskd", to_low(probs_back), d_heads, preferred_element_type=jnp.float32
    ).reshape(per_device, MAX_SEQ_TOKENS, channels)

    def place(block_index, carried):
        key_acc, value_acc = carried
        begin_at = my_blocks[block_index] * BLK
        key_now = (
            lax.dynamic_slice_in_dim(key_acc, begin_at, MAX_SEQ_TOKENS, 0) + d_key_win[block_index]
        )
        value_now = (
            lax.dynamic_slice_in_dim(value_acc, begin_at, MAX_SEQ_TOKENS, 0)
            + d_value_win[block_index]
        )
        return (
            lax.dynamic_update_slice_in_dim(key_acc, key_now, begin_at, 0),
            lax.dynamic_update_slice_in_dim(value_acc, value_now, begin_at, 0),
        )

    empty_acc = jnp.zeros((margin + total_rows, channels), jnp.float32)
    key_acc, value_acc = lax.fori_loop(0, per_device, place, (empty_acc, empty_acc))
    key_dealt = jnp.take(
        key_acc[margin:].reshape(block_count, BLK, channels), block_order, axis=0
    ).reshape(total_rows, channels)
    value_dealt = jnp.take(
        value_acc[margin:].reshape(block_count, BLK, channels), block_order, axis=0
    ).reshape(total_rows, channels)
    d_keys_own, d_values_own = (
        lax.psum_scatter(key_dealt, "ctx", scatter_dimension=0, tiled=True),
        lax.psum_scatter(value_dealt, "ctx", scatter_dimension=0, tiled=True),
    )
    d_k_norm = rotate_back(d_keys_own.reshape(row_count, kv_heads, HEAD_WIDTH), cosine, sine_tab)
    d_k_pre, key_gain_terms = norm_back(key_before_norm, k_inverse, g_key, d_k_norm)
    d_k_pre = to_low(d_k_pre.reshape(row_count, channels))
    d_q_norm = rotate_back(d_queries.reshape(row_count, q_heads, HEAD_WIDTH), cosine, sine_tab)
    d_q_pre, query_gain_terms = norm_back(q_pre, q_inverse, g_query, d_q_norm)
    d_q_pre = to_low(d_q_pre.reshape(row_count, q_heads * HEAD_WIDTH))
    d_values = to_low(d_values_own)
    grad_query = transposed_times(hidden_after_attn, d_q_pre)
    grad_key = transposed_times(hidden_after_attn, d_k_pre)
    grad_value = transposed_times(hidden_after_attn, d_values)
    d_hidden_one_part = (
        times_transposed(d_q_pre, wq)
        + times_transposed(d_k_pre, key_matrix)
        + times_transposed(d_values, value_matrix)
    )
    d_hidden_one = lax.psum(d_hidden_one_part.astype(jnp.bfloat16), "wsh").astype(jnp.float32)
    d_stream_norm, attn_gain_terms = norm_back(
        stream, inverse_one, g_attn.astype(jnp.float32), d_hidden_one
    )
    grad_tokens = d_residual + d_stream_norm
    grad_query, grad_key, grad_value, grad_out, grad_router, grad_gain_attn, grad_gain_ffn = (
        lax.psum_scatter(grad_query, "ctx", scatter_dimension=0, tiled=True),
        lax.psum_scatter(grad_key, "ctx", scatter_dimension=0, tiled=True),
        lax.psum_scatter(grad_value, "ctx", scatter_dimension=0, tiled=True),
        lax.psum_scatter(grad_out, "ctx", scatter_dimension=1, tiled=True),
        lax.psum_scatter(grad_router, "ctx", scatter_dimension=0, tiled=True),
        lax.psum_scatter(jnp.sum(attn_gain_terms, axis=0), "ctx", scatter_dimension=0, tiled=True),
        lax.psum_scatter(jnp.sum(ffn_gain_terms, axis=0), "ctx", scatter_dimension=0, tiled=True),
    )
    grad_gain_query, grad_gain_key = lax.psum(
        (jnp.sum(query_gain_terms, axis=(0, 1)), jnp.sum(key_gain_terms, axis=(0, 1))),
        ("ctx", "wsh"),
    )
    return (
        out_stream,
        grad_tokens,
        grad_query,
        grad_key,
        grad_value,
        grad_out,
        grad_gain_attn,
        grad_gain_query,
        grad_gain_key,
        grad_gain_ffn,
        grad_router,
        grad_gate,
        grad_up,
        grad_down,
    )


def solution(mesh):
    in_specs = (
        P("ctx", None),
        P("ctx", None),
        P(),
        P(),
        P("ctx", None),
        P("ctx", "wsh"),
        P("ctx", "wsh"),
        P("ctx", "wsh"),
        P("wsh", "ctx"),
        P("ctx"),
        P(),
        P(),
        P("ctx"),
        P("ctx", None),
        P("ctx", None, "wsh"),
        P("ctx", None, "wsh"),
        P("ctx", "wsh", None),
    )
    out_specs = (
        P("ctx", None),
        P("ctx", None),
        P("ctx", "wsh"),
        P("ctx", "wsh"),
        P("ctx", "wsh"),
        P("wsh", "ctx"),
        P("ctx"),
        P(),
        P(),
        P("ctx"),
        P("ctx", None),
        P("ctx", None, "wsh"),
        P("ctx", None, "wsh"),
        P("ctx", "wsh", None),
    )
    return jax.shard_map(local, mesh=mesh, in_specs=in_specs, out_specs=out_specs, check_vma=False)
```

profile of v0, /device:TPU:0, one launch (start us, length us, event | category | flops | bytes accessed | tf_op | source)
XLA Modules:
  0.0 4064.6 jit_solution(7300203926888853863)
XLA Ops:
  14.0 173.2 %all-reduce.11 = (bf16[2048]{0:T(1024)(128)(2,1)S(1)}, bf16[2048]{0:T(1024)(128)(2,1)S(1)}) all-reduce(bf16[2048]{0:T(1024)(128)(2,1)S(1)} %dynamic-update-slice.4, bf16[2048]{0:T(1024)(128)(2,1)S(1)} %dynamic-update-slice.5), channel_id=1, replica_groups=mesh['ctx'=64,'wsh'=2] {'ctx'}, use_global_device_ids=true, to_apply=%add.5 | all-reduce | flops 4096 | bytes 16384
  205.7 58.3 %all-gather.13.cloned.1.call-done = bf16[8192,256]{1,0:T(8,128)(2,1)} async-done(((bf16[128,256]{1,0:T(8,128)(2,1)}), bf16[8192,256]{1,0:T(8,128)(2,1)}) %all-gather.13.cloned.1.call-update) | async-done | bytes 4194320 | tf_op jit(solution)/shard_map/all_gather | solution.py:149
  268.9 67.5 %all-gather.9.cloned.1.call-done = bf16[8192,256]{1,0:T(8,128)(2,1)} async-done(((bf16[128,256]{1,0:T(8,128)(2,1)}), bf16[8192,256]{1,0:T(8,128)(2,1)}) %all-gather.9.cloned.1.call-update) | async-done | bytes 4194320 | tf_op jit(solution)/shard_map/all_gather | solution.py:150
  346.9 10.6 concatenate.56
  373.6 7.1 concatenate.52
  397.0 21.6 all-gather.15.cloned.1.call-done
  433.3 17.3 fusion.12
  450.6 15.4 fusion.5
  466.7 16.5 fusion.50
  483.8 18.1 all-gather.17.cloned.1.call-done
  513.4 28.5 all-reduce.17.cloned.1.call-done
  552.1 10.6 gather.30
  562.6 7.5 broadcast_select_fusion.1
  570.1 107.9 %all_to_all.54 = bf16[128,12,2048]{2,1,0:T(8,128)(2,1)S(1)} all-to-all(bf16[128,12,2048]{2,1,0:T(8,128)(2,1)} %broadcast_select_fusion.1), channel_id=1, replica_groups=mesh['ctx'=64,'wsh'=2] {'ctx'}, dimensions={0} | all-to-all | bytes 12582912 | tf_op jit(solution)/shard_map/all_to_all | solution.py:230
  678.1 15.2 copy.306
  693.3 16.2 copy.288
  709.4 9.6 fusion.37
  719.0 8.2 multiply_convert_fusion.2
  730.9 18.8 copy.257
  756.1 157.7 %all_gather.42 = bf16[2048,128]{1,0:T(8,128)(2,1)S(1)} all-gather(bf16[32,128]{1,0:T(8,128)(2,1)S(1)} %convert_element_type.238), channel_id=1, replica_groups=mesh['ctx'=64,'wsh'=2] {'ctx'}, dimensions={0}, use_global_device_ids=true | all-gather | bytes 532480 | tf_op jit(solution)/shard_map/all_gather | solution.py:132
  915.6 10.2 convert_bitcast_fusion.1
  925.8 22.7 copy.258
  948.6 15.5 reshape.621
  964.1 13.6 gather_fusion.4
  992.7 15.4 gather_fusion.1
  1008.1 10.6 gather.32
  1018.7 7.5 broadcast_select_fusion
  1026.1 102.8 %all_to_all.55 = bf16[128,12,2048]{2,1,0:T(8,128)(2,1)S(1)} all-to-all(bf16[128,12,2048]{2,1,0:T(8,128)(2,1)} %broadcast_select_fusion), channel_id=1, replica_groups=mesh['ctx'=64,'wsh'=2] {'ctx'}, dimensions={0} | all-to-all | bytes 12582912 | tf_op jit(solution)/shard_map/all_to_all | solution.py:230
  1129.0 13.1 copy.308
  1142.1 11.8 multiply_convert_fusion
  1160.4 8.5 add_convert_fusion
  1168.9 18.8 copy.262
  1196.0 77.1 %all-to-all-done.3 = bf16[2,768,2048]{2,0,1:T(2,128)(2,1)} async-done(((bf16[2,768,2048]{2,0,1:T(2,128)(2,1)}), bf16[2,768,2048]{2,0,1:T(2,128)(2,1)}, u32[]{:S(2)}, u32[]{:S(2)}) %all-to-all-start.3) | async-done | bytes 6291488 | tf_op jit(solution)/shard_map/all_to_all | solution.py:234
  1273.1 10.2 convert_bitcast_fusion
  1283.3 22.8 copy.263
  1306.1 15.5 reshape.622
  1321.6 13.5 gather_fusion.5
  1335.2 13.1 bitcast_reduce_fusion
  1349.0 34.0 all-reduce.19.cloned.1.call-done
  1390.9 28.5 fusion.2
  1419.4 33.5 fusion.6
  1452.9 19.4 fusion.7
  1472.4 20.1 bitcast_multiply_fusion.3
  1502.1 64.2 %while.17 = (s32[]{:T(128)}, f32[12224,256]{1,0:T(8,128)}, f32[12224,256]{1,0:T(8,128)}, s32[2]{0:T(128)S(1)}, f32[2,4096,256]{1,2,0:T(8,128)}, /*index=5*/f32[2...) while((s32[]{:T(128)}, f32[12224,256]{1,0:T(8,128)}, f32[12224,256]{1,0:T(8,128)}, ...), condition=%wide.region_29.32_spmd, body=%wide.region_28.31_spmd.sunk | while | flops 2097158 | bytes 58720428 | solution.py:342
  1523.9 10.2 fusion.160
  1555.9 10.3 fusion.160
  1566.3 8.4 slice.44
  1580.1 7.9 gather_fusion.6
  1588.0 7.9 gather_fusion.7
  1595.9 11.2 broadcast_select_fusion.2
  1611.1 9.7 fusion.45
  1636.3 318.3 %reduce-scatter.8.cloned.1.call-done = f32[128,256]{1,0:T(8,128)} async-done(((f32[8192,256]{1,0:T(8,128)}), f32[128,256]{1,0:T(8,128)}) %reduce-scatter.8.cloned.1.call-update) | async-done | bytes 131088 | tf_op jit(solution)/shard_map/reduce_scatter | solution.py:350
  1960.5 336.9 %reduce-scatter.10.cloned.1.call-done = f32[128,256]{1,0:T(8,128)} async-done(((f32[8192,256]{1,0:T(8,128)}), f32[128,256]{1,0:T(8,128)}) %reduce-scatter.10.cloned.1.call-update) | async-done | bytes 131088 | tf_op jit(solution)/shard_map/reduce_scatter | solution.py:351
  2305.8 8.1 fusion.74
  2314.2 8.2 fusion.112
  2323.8 10.2 fusion.18
  2334.0 9.0 fusion.125
  2343.0 9.0 fusion.126
  2352.0 63.6 %all-reduce.9 = (f32[128]{0:T(128)}, f32[128]{0:T(128)}) all-reduce(f32[128]{0:T(128)S(1)} %bitcast_reduce_fusion.1, f32[128]{0:T(128)S(1)} %bitcast_reduce_fusion.2), channel_id=1, replica_groups=mesh['ctx'=64,'wsh'=2] {'ctx','wsh'}, use_global_device_ids=true, to_apply=%region_43.47 | all-reduce | flops 256 | bytes 2048 | tf_op jit(solution)/shard_map/psum | solution.py:382
  2417.1 324.7 %all-reduce.10 = (f32[2048]{0:T(1024)S(1)}, f32[2048]{0:T(1024)S(1)}) all-reduce(f32[2048]{0:T(1024)S(1)} %get-tuple-element.231, f32[2048]{0:T(1024)S(1)} %copy-done.70), channel_id=8, replica_groups=mesh['ctx'=64,'wsh'=2] {'ctx'}, use_global_device_ids=true, to_apply=%region_40.44.clone | all-reduce | flops 4096 | bytes 32768
  2746.0 264.9 %reduce-scatter.14.cloned.1.call-done = f32[32,256]{1,0:T(8,128)} async-done(((f32[2048,256]{1,0:T(8,128)}), f32[32,256]{1,0:T(8,128)}) %reduce-scatter.14.cloned.1.call-update) | async-done | bytes 32784 | tf_op jit(solution)/shard_map/reduce_scatter | solution.py:375
  3010.9 332.1 %reduce-scatter.16.cloned.1.call-done = f32[32,256]{1,0:T(8,128)} async-done(((f32[2048,256]{1,0:T(8,128)}), f32[32,256]{1,0:T(8,128)}) %reduce-scatter.16.cloned.1.call-update) | async-done | bytes 32784 | tf_op jit(solution)/shard_map/reduce_scatter | solution.py:376
  3343.0 357.4 %reduce-scatter.18.cloned.1.call-done = f32[2048,32]{0,1:T(8,128)} async-done(((f32[2048,2048]{0,1:T(8,128)}), f32[2048,32]{0,1:T(8,128)}) %reduce-scatter.18.cloned.1.call-update) | async-done | bytes 262160 | tf_op jit(solution)/shard_map/reduce_scatter | solution.py:377
  3700.4 357.4 %reduce-scatter.12.cloned.1.call-done = f32[32,2048]{1,0:T(8,128)} async-done(((f32[2048,2048]{1,0:T(8,128)}), f32[32,2048]{1,0:T(8,128)}) %reduce-scatter.12.cloned.1.call-update) | async-done | bytes 262160 | tf_op jit(solution)/shard_map/reduce_scatter | solution.py:374
  (435 shorter events, 270.2 us)
Async XLA Ops:
  7.2 194.7 %copy-start.88 = (s32[128]{0:T(128)S(1)}, s32[128]{0:T(128)}, u32[]{:S(2)}) copy-start(s32[128]{0:T(128)} %param.28) | copy-start | bytes 1540
  7.2 193.1 %copy-start.56 = (f32[32,2048]{1,0:T(8,128)S(1)}, f32[32,2048]{1,0:T(8,128)}, u32[]{:S(2)}) copy-start(f32[32,2048]{1,0:T(8,128)} %param.30) | copy-start | bytes 786436
  7.2 193.9 %copy-start.57 = (f32[2048,32]{0,1:T(8,128)S(1)}, f32[2048,32]{0,1:T(8,128)}, u32[]{:S(2)}) copy-start(f32[2048,32]{0,1:T(8,128)} %param.33) | copy-start | bytes 786436
  7.2 195.8 %copy-start.72 = (s32[128,8]{0,1:T(8,128)S(1)}, s32[128,8]{0,1:T(8,128)}, u32[]{:S(2)}) copy-start(s32[128,8]{0,1:T(8,128)} %param.29) | copy-start | bytes 12292
  7.2 196.2 %copy-start.92 = (f32[128]{0:T(128)S(1)}, f32[128]{0:T(128)}, u32[]{:S(2)}) copy-start(f32[128]{0:T(128)} %param.35) | copy-start | bytes 1540
  7.2 185.5 %all-gather.11.cloned.1.call-start = ((), (), s32[]{:S(2)}) async-start(), calls=%async_computation.13 | async-start | bytes 1064960 | tf_op jit(solution)/shard_map/all_gather | solution.py:129
  8.7 189.1 %all-gather.7.cloned.1.call-start = ((), (), s32[]{:S(2)}) async-start(), calls=%async_computation.11 | async-start | bytes 1064960 | tf_op jit(solution)/shard_map/all_gather | solution.py:130
  10.2 253.7 %all-gather.13.cloned.1.call-start = ((), (), s32[]{:S(2)}) async-start(), calls=%async_computation.14 | async-start | bytes 4259840 | tf_op jit(solution)/shard_map/all_gather | solution.py:149
  187.3 231.4 %copy-start.45 = (f32[2048]{0:T(1024)}, f32[2048]{0:T(1024)S(1)}, u32[]{:S(2)}) copy-start(f32[2048]{0:T(1024)S(1)} %convert_element_type.214) | copy-start | bytes 24580
  189.2 14.1 copy-start.81
  192.7 225.9 %copy-start.68 = (f32[128]{0:T(128)}, f32[128]{0:T(128)S(1)}, u32[]{:S(2)}) copy-start(f32[128]{0:T(128)S(1)} %get-tuple-element.315) | copy-start | bytes 1540
  192.7 76.2 %copy-start.79 = (f32[256]{0:T(256)}, f32[256]{0:T(256)S(1)}, u32[]{:S(2)}) copy-start(f32[256]{0:T(256)S(1)} %broadcast_bitcast_fusion.1) | copy-start | bytes 3076
  197.8 138.6 %all-gather.9.cloned.1.call-start = ((), (), s32[]{:S(2)}) async-start(), calls=%async_computation.12 | async-start | bytes 4259840 | tf_op jit(solution)/shard_map/all_gather | solution.py:150
  200.3 218.4 %all-gather.15.cloned.1.call-start = ((), (), s32[]{:S(2)}) async-start(), calls=%async_computation.15 | async-start | bytes 8519680 | tf_op jit(solution)/shard_map/all_gather | solution.py:128
  201.0 300.8 %all-gather.17.cloned.1.call-start = ((), (), s32[]{:S(2)}) async-start(), calls=%async_computation.16 | async-start | bytes 8519680 | tf_op jit(solution)/shard_map/all_gather | solution.py:131
  201.8 340.1 %all-reduce.17.cloned.1.call-start = ((), (), s32[]{:S(2)}) async-start(), calls=%async_computation.17 | async-start | bytes 1048576 | tf_op jit(solution)/shard_map/psum | solution.py:205
  203.3 65.6 %copy-start.66 = (s32[1024]{0:T(1024)}, s32[1024]{0:T(1024)S(1)}, u32[]{:S(2)}) copy-start(s32[1024]{0:T(1024)S(1)} %eq.57) | copy-start | bytes 12292
  203.4 227.6 %copy-start.74 = (f32[128]{0:T(128)}, f32[128]{0:T(128)S(1)}, u32[]{:S(2)}) copy-start(f32[128]{0:T(128)S(1)} %convert_element_type.225) | copy-start | bytes 1540
  204.5 261.6 %copy-start.4 = (pred[2,64,4096]{2,1,0:T(8,128)(4,1)}, pred[2,64,4096]{2,1,0:T(8,128)(4,1)S(1)}, u32[]{:S(2)}) copy-start(pred[2,64,4096]{2,1,0:T(8,128)(4,1)S(1)} %compare_and_fusion) | copy-start | bytes 1572868
  204.6 339.2 %copy-start.58 = (f32[2048]{0:T(1024)}, f32[2048]{0:T(1024)S(1)}, u32[]{:S(2)}) copy-start(f32[2048]{0:T(1024)S(1)} %convert_element_type.236) | copy-start | bytes 24580
  390.0 28.7 copy-start.1
  433.3 17.3 copy-start.22
  450.6 15.4 copy-start.62
  483.7 60.0 %copy-start.18 = (bf16[128,2048]{1,0:T(8,128)(2,1)}, bf16[128,2048]{1,0:T(8,128)(2,1)S(1)}, u32[]{:S(2)}) copy-start(bf16[128,2048]{1,0:T(8,128)(2,1)S(1)} %convert_element_type.231) | copy-start | bytes 1572868
  545.0 368.8 %copy-start.14 = (bf16[128,2048]{1,0:T(8,128)(2,1)}, bf16[128,2048]{1,0:T(8,128)(2,1)S(1)}, u32[]{:S(2)}) copy-start(bf16[128,2048]{1,0:T(8,128)(2,1)S(1)} %multiply_convert_fusion.3) | copy-start | bytes 1572868
  709.4 17.8 slice-start.2
  749.7 165.2 %copy-start.29 = (s32[128,8]{1,0:T(8,128)S(1)}, s32[128,8]{1,0:T(8,128)}, u32[]{:S(2)}) copy-start(s32[128,8]{1,0:T(8,128)} %copy-done.28) | copy-start | bytes 12292
  749.7 165.9 %all-to-all-start.1 = ((bf16[2,768,2048]{2,0,1:T(2,128)(2,1)}), bf16[2,768,2048]{2,0,1:T(2,128)(2,1)}, u32[]{:S(2)}, u32[]{:S(2)}) async-start(bf16[2,768,2048]{2,0,1:T(2,128)(2,1)} %copy.257), calls=%async_computation.1 | async-start | bytes 12582912 | tf_op jit(solution)/shard_map/all_to_all | solution.py:234
  1129.0 25.0 slice-start
  1187.7 85.5 %all-to-all-start.3 = ((bf16[2,768,2048]{2,0,1:T(2,128)(2,1)}), bf16[2,768,2048]{2,0,1:T(2,128)(2,1)}, u32[]{:S(2)}, u32[]{:S(2)}) async-start(bf16[2,768,2048]{2,0,1:T(2,128)(2,1)} %copy.262), calls=%async_computation.3 | async-start | bytes 12582912 | tf_op jit(solution)/shard_map/all_to_all | solution.py:234
  1194.8 188.2 %all-reduce.19.cloned.1.call-start = ((), (), s32[]{:S(2)}) async-start(), calls=%async_computation.18 | async-start | bytes 1048576 | tf_op jit(solution)/shard_map/psum | solution.py:291
  1335.2 47.8 %copy-start.2 = (bf16[128,2048]{1,0:T(8,128)(2,1)S(1)}, bf16[128,2048]{1,0:T(8,128)(2,1)}, u32[]{:S(2)}) copy-start(bf16[128,2048]{1,0:T(8,128)(2,1)} %param.25) | copy-start | bytes 1572868
  1335.2 47.7 %copy-start.12 = (bf16[128,2048]{1,0:T(8,128)(2,1)S(1)}, bf16[128,2048]{1,0:T(8,128)(2,1)}, u32[]{:S(2)}) copy-start(bf16[128,2048]{1,0:T(8,128)(2,1)} %all-reduce.17.cloned.1.call-done) | copy-start | bytes 1572868
  1335.2 47.7 %copy-start.21 = (bf16[2048,128]{1,0:T(8,128)(2,1)S(1)}, bf16[2048,128]{1,0:T(8,128)(2,1)}, u32[]{:S(2)}) copy-start(bf16[2048,128]{1,0:T(8,128)(2,1)} %copy-done.20) | copy-start | bytes 1572868
  1335.2 47.7 %copy-start.59 = (f32[2048]{0:T(1024)S(1)}, f32[2048]{0:T(1024)}, u32[]{:S(2)}) copy-start(f32[2048]{0:T(1024)} %copy-done.58) | copy-start | bytes 24580
  1335.2 47.7 %copy-start.77 = (f32[128]{0:T(128)S(1)}, f32[128]{0:T(128)}, u32[]{:S(2)}) copy-start(f32[128]{0:T(128)} %copy-done.76) | copy-start | bytes 1540
  1335.2 50.0 %copy-start.25 = (bf16[128,2048]{1,0:T(8,128)(2,1)S(1)}, bf16[128,2048]{1,0:T(8,128)(2,1)}, u32[]{:S(2)}) copy-start(bf16[128,2048]{1,0:T(8,128)(2,1)} %param.26) | copy-start | bytes 1572868
  1335.2 50.0 %copy-start.84 = (f32[128]{0:T(128)S(1)}, f32[128]{0:T(128)}, u32[]{:S(2)}) copy-start(f32[128]{0:T(128)} %get-tuple-element.318) | copy-start | bytes 1540
  1348.4 606.2 %reduce-scatter.8.cloned.1.call-start = ((), (), s32[]{:S(2)}) async-start(), calls=%async_computation.19 | async-start | bytes 8519680 | tf_op jit(solution)/shard_map/reduce_scatter | solution.py:350
  1348.9 41.8 %copy-start.54 = (bf16[128,128]{1,0:T(8,128)(2,1)}, bf16[128,128]{1,0:T(8,128)(2,1)S(1)}, u32[]{:S(2)}) copy-start(bf16[128,128]{1,0:T(8,128)(2,1)S(1)} %select_reduce_fusion) | copy-start | bytes 98308
  1452.9 19.5 copy-start.23
  1607.2 690.2 %reduce-scatter.10.cloned.1.call-start = ((), (), s32[]{:S(2)}) async-start(), calls=%async_computation.20 | async-start | bytes 8519680 | tf_op jit(solution)/shard_map/reduce_scatter | solution.py:351
  1607.8 807.9 %all-reduce.21.cloned.1.call-start = ((), (), s32[]{:S(2)}) async-start(), calls=%async_computation.26 | async-start | bytes 2097152 | tf_op jit(solution)/shard_map/psum | solution.py:260
  1629.9 325.7 %copy-start.48 = (f32[128,128]{1,0:T(8,128)S(1)}, f32[128,128]{1,0:T(8,128)}, u32[]{:S(2)}) copy-start(f32[128,128]{1,0:T(8,128)} %copy-done.47) | copy-start | bytes 196612
  1629.9 326.0 %copy-start.27 = (f32[128,2,128]{2,1,0:T(2,128)S(1)}, f32[128,2,128]{2,1,0:T(2,128)}, u32[]{:S(2)}) copy-start(f32[128,2,128]{2,1,0:T(2,128)} %copy-done.26) | copy-start | bytes 393220
  1629.9 326.0 %copy-start.52 = (f32[128,128]{1,0:T(8,128)S(1)}, f32[128,128]{1,0:T(8,128)}, u32[]{:S(2)}) copy-start(f32[128,128]{1,0:T(8,128)} %copy-done.51) | copy-start | bytes 196612
  1629.9 326.0 %copy-start.82 = (f32[128]{0:T(128)S(1)}, f32[128]{0:T(128)}, u32[]{:S(2)}) copy-start(f32[128]{0:T(128)} %copy-done.81) | copy-start | bytes 1540
  1629.9 326.9 %copy-start.36 = (f32[128,256]{1,0:T(8,128)S(1)}, f32[128,256]{1,0:T(8,128)}, u32[]{:S(2)}) copy-start(f32[128,256]{1,0:T(8,128)} %copy-done.35) | copy-start | bytes 393220
  1629.9 326.9 %copy-start.38 = (f32[128,2,128]{2,1,0:T(2,128)S(1)}, f32[128,2,128]{2,1,0:T(2,128)}, u32[]{:S(2)}) copy-start(f32[128,2,128]{2,1,0:T(2,128)} %copy-done.37) | copy-start | bytes 393220
  1629.9 326.9 %copy-start.40 = (f32[128,2,128]{2,1,0:T(2,128)S(1)}, f32[128,2,128]{2,1,0:T(2,128)}, u32[]{:S(2)}) copy-start(f32[128,2,128]{2,1,0:T(2,128)} %copy-done.39) | copy-start | bytes 393220
  1629.9 326.9 %copy-start.80 = (f32[256]{0:T(256)S(1)}, f32[256]{0:T(256)}, u32[]{:S(2)}) copy-start(f32[256]{0:T(256)} %copy-done.79) | copy-start | bytes 3076
  1636.3 664.1 %copy-start.15 = (bf16[128,2048]{1,0:T(8,128)(2,1)S(1)}, bf16[128,2048]{1,0:T(8,128)(2,1)}, u32[]{:S(2)}) copy-start(bf16[128,2048]{1,0:T(8,128)(2,1)} %copy-done.14) | copy-start | bytes 1572868
  1636.3 664.1 %copy-start.55 = (bf16[128,128]{1,0:T(8,128)(2,1)S(1)}, bf16[128,128]{1,0:T(8,128)(2,1)}, u32[]{:S(2)}) copy-start(bf16[128,128]{1,0:T(8,128)(2,1)} %copy-done.54) | copy-start | bytes 98308
  1955.7 346.2 %copy-start.3 = (bf16[128,2048]{1,0:T(8,128)(2,1)S(1)}, bf16[128,2048]{1,0:T(8,128)(2,1)}, u32[]{:S(2)}) copy-start(bf16[128,2048]{1,0:T(8,128)(2,1)} %param.25) | copy-start | bytes 1572868
  1955.7 346.2 %copy-start.46 = (f32[2048]{0:T(1024)S(1)}, f32[2048]{0:T(1024)}, u32[]{:S(2)}) copy-start(f32[2048]{0:T(1024)} %copy-done.45) | copy-start | bytes 24580
  1955.7 346.2 %copy-start.69 = (f32[128]{0:T(128)S(1)}, f32[128]{0:T(128)}, u32[]{:S(2)}) copy-start(f32[128]{0:T(128)} %copy-done.68) | copy-start | bytes 1540
  2300.4 445.6 %reduce-scatter.20.cloned.1.call-start = ((), (), s32[]{:S(2)}) async-start(), calls=%async_computation.25 | async-start | bytes 1064960 | tf_op jit(solution)/shard_map/reduce_scatter | solution.py:378
  2301.8 709.1 %reduce-scatter.14.cloned.1.call-start = ((), (), s32[]{:S(2)}) async-start(), calls=%async_computation.22 | async-start | bytes 2129920 | tf_op jit(solution)/shard_map/reduce_scatter | solution.py:375
  2303.7 1039.3 %reduce-scatter.16.cloned.1.call-start = ((), (), s32[]{:S(2)}) async-start(), calls=%async_computation.23 | async-start | bytes 2129920 | tf_op jit(solution)/shard_map/reduce_scatter | solution.py:376
  2305.7 1394.7 %reduce-scatter.18.cloned.1.call-start = ((), (), s32[]{:S(2)}) async-start(), calls=%async_computation.24 | async-start | bytes 17039360 | tf_op jit(solution)/shard_map/reduce_scatter | solution.py:377
  2314.0 1743.8 %reduce-scatter.12.cloned.1.call-start = ((), (), s32[]{:S(2)}) async-start(), calls=%async_computation.21 | async-start | bytes 17039360 | tf_op jit(solution)/shard_map/reduce_scatter | solution.py:374
  2343.0 74.1 %copy-start.70 = (f32[2048]{0:T(1024)S(1)}, f32[2048]{0:T(1024)}, u32[]{:S(2)}) copy-start(f32[2048]{0:T(1024)} %get-tuple-element.229) | copy-start | bytes 24580
  2343.0 400.0 %copy-start.13 = (bf16[128,2048]{1,0:T(8,128)(2,1)S(1)}, bf16[128,2048]{1,0:T(8,128)(2,1)}, u32[]{:S(2)}) copy-start(bf16[128,2048]{1,0:T(8,128)(2,1)} %all-reduce.17.cloned.1.call-done) | copy-start | bytes 1572868
  2343.0 400.0 %copy-start.83 = (f32[128]{0:T(128)S(1)}, f32[128]{0:T(128)}, u32[]{:S(2)}) copy-start(f32[128]{0:T(128)} %get-tuple-element.314) | copy-start | bytes 1540
  (51 other events, 304.1 us)
Sparse Core Ops, SparseCore 0:
  11.8 68.4 all-gather.10
  84.0 62.5 all-gather.6
  197.9 65.9 all-gather.12
  267.5 68.8 all-gather.8
  340.1 78.5 all-gather.14
  422.4 79.4 all-gather.16
  509.0 32.8 all-reduce.16
  1348.5 34.3 all-reduce.18
  1607.3 347.2 reduce-scatter.7
  1956.8 340.5 reduce-scatter.9
  2300.5 40.8 all-reduce.20
  2344.3 334.0 reduce-scatter.19
  2681.3 329.5 reduce-scatter.13
  3013.8 329.1 reduce-scatter.15
  3345.8 354.5 reduce-scatter.17
  3703.3 354.5 reduce-scatter.11
where the time goes:
time: 4070 us; the launch traced here: 4060 us
  waiting for transfers between devices  2270 us (56%)
  blocking collectives  937 us (23%)
  local copies, waits for them, and re-layouts  402 us (10%)
  matrix products  245 us (6%)
  other arithmetic  175 us (4%)
    unnamed x2, blocking collectives  498 us
    reduce_scatter x1, waiting for transfers between devices, local(): lax.psum_scatter(grad_out, 'ctx', scatter_dimension=1, tiled=True)  357 us
    reduce_scatter x1, waiting for transfers between devices, local(): lax.psum_scatter(grad_query, 'ctx', scatter_dimension=0, tiled=True)  357 us
    reduce_scatter x1, waiting for transfers between devices, local(): lax.psum_scatter(value_dealt, 'ctx', scatter_dimension=0, tiled=True)  337 us
    reduce_scatter x1, waiting for transfers between devices, local(): lax.psum_scatter(grad_value, 'ctx', scatter_dimension=0, tiled=True)  332 us
    reduce_scatter x1, waiting for transfers between devices, local(): lax.psum_scatter(key_dealt, 'ctx', scatter_dimension=0, tiled=True)  318 us
    reduce_scatter x1, waiting for transfers between devices, local(): lax.psum_scatter(grad_key, 'ctx', scatter_dimension=0, tiled=True)  265 us
    all_to_all x2, blocking collectives, send_rows(): lax.all_to_all(rows, 'ctx', split_axis=0, concat_axis=1, tiled=True)  211 us
  transfers between devices with their start and end apart: 18, of which 13 were waited for; matrix products, arithmetic and copies ran while one was open for 6% of the time, Pallas kernels for 0%

commit v1 on v0

v1 whole, which is shorter than its diff:
```python
import functools
import math

import jax
import jax.numpy as jnp
from jax import lax
from jax.experimental import pallas as pl
from jax.experimental.pallas import tpu as pltpu
from jax.sharding import PartitionSpec as P

HEAD_WIDTH = 128
TOPK = 8
BLK = 64
MAX_SEQ_TOKENS = 4096
CAP = 12
CHUNK = 512

EPSILON = 1e-06
ROPE_BASE = 1000000.0
MASKED = -1e30
MESH = pl.DeviceIdType.MESH
BF = jnp.bfloat16
F32 = jnp.float32


def to_low(value_rows):
    return value_rows.astype(jnp.bfloat16)


def rounded(value_rows):
    return lax.optimization_barrier(value_rows.astype(jnp.bfloat16)).astype(jnp.float32)


def matmul(left, right):
    return jnp.dot(left, right, preferred_element_type=jnp.float32)


def times_transposed(left, right):
    return lax.dot_general(
        left, right, (((1,), (1,)), ((), ())), preferred_element_type=jnp.float32
    )


def transposed_times(left, right):
    return lax.dot_general(
        left, right, (((0,), (0,)), ((), ())), preferred_element_type=jnp.float32
    )


def norm_back(value_rows, inverse_rms, gain_vec, gradient):
    weighted = gradient * gain_vec
    mean_term = jnp.mean(weighted * value_rows, axis=-1, keepdims=True)
    d_values = (
        inverse_rms * weighted - value_rows * (inverse_rms * inverse_rms * inverse_rms) * mean_term
    )
    return (d_values, gradient * value_rows * inverse_rms)


def inverse_root(value_rows):
    return lax.rsqrt(jnp.mean(value_rows * value_rows, axis=-1, keepdims=True) + EPSILON)


def rope_tables(positions):
    half_dim = HEAD_WIDTH // 2
    frequency = jnp.power(ROPE_BASE, -2.0 * jnp.arange(half_dim, dtype=jnp.float32) / HEAD_WIDTH)
    angles = positions.astype(jnp.float32)[:, None] * frequency[None, :]
    cosine, sine_tab = jnp.cos(angles), jnp.sin(angles)
    return (
        jnp.concatenate([cosine, cosine], axis=-1),
        jnp.concatenate([sine_tab, sine_tab], axis=-1),
    )


def rotate(value_rows, cosine, sine_tab):
    half_dim = value_rows.shape[-1] // 2
    turned = jnp.concatenate([-value_rows[..., half_dim:], value_rows[..., :half_dim]], axis=-1)
    return value_rows * cosine + turned * sine_tab


def rotate_back(gradient, cosine, sine_tab):
    half_dim = gradient.shape[-1] // 2
    shifted = gradient * sine_tab
    return gradient * cosine + jnp.concatenate(
        [shifted[..., half_dim:], -shifted[..., :half_dim]], axis=-1
    )


def seq_starts(positions, seq_lengths):
    offsets = jnp.cumsum(seq_lengths) - seq_lengths
    inside = offsets[None, :] <= positions[:, None]
    return jnp.max(jnp.where(inside, offsets[None, :], 0), axis=1)


def coords(c):
    return (
        lax.div(c, 16),
        lax.rem(lax.div(c, 8), 2),
        lax.rem(lax.div(c, 2), 4),
        lax.rem(c, 2),
    )


def index_of(z, y, x, k):
    return ((z * 2 + y) * 4 + x) * 2 + k


def shifted(me, dz, dy, dx, dk):
    z, y, x, k = coords(me)
    return index_of(lax.rem(z + dz, 4), lax.rem(y + dy, 2), lax.rem(x + dx, 4), lax.rem(k + dk, 2))


def remote(src, dst, send, recv, ctx, wsh):
    return pltpu.make_async_remote_copy(
        src_ref=src,
        dst_ref=dst,
        send_sem=send,
        recv_sem=recv,
        device_id=(ctx, wsh),
        device_id_type=MESH,
    )


def greet(targets):
    barrier = pltpu.get_barrier_semaphore()
    for ctx, wsh in targets:
        pl.semaphore_signal(barrier, inc=1, device_id=(ctx, wsh), device_id_type=MESH)
    return barrier, len(targets)


def greet_many(count, target, wsh):
    barrier = pltpu.get_barrier_semaphore()

    def one(step, carried):
        pl.semaphore_signal(barrier, inc=1, device_id=(target(step), wsh), device_id_type=MESH)
        return carried

    lax.fori_loop(1, count, one, 0)
    return barrier, count - 1


ANY = pl.BlockSpec(memory_space=pl.ANY)
VMEM = pl.BlockSpec(memory_space=pltpu.VMEM)
DMA = pltpu.SemaphoreType.DMA


def call_params(collective_id, limit=None):
    return pltpu.CompilerParams(
        collective_id=collective_id, has_side_effects=True, vmem_limit_bytes=limit
    )


def row_gather_start(src, out, me, wsh, send, recv):
    place = lax.rem(me, 8)
    copies = []
    for at, (dx, dk) in enumerate(((1, 0), (3, 0), (2, 0), (0, 1))):
        copy = remote(
            src, out.at[place], send.at[at], recv.at[at], shifted(me, 0, 0, dx, dk), wsh
        )
        copy.start()
        copies.append(copy)
    return copies


def row_gather_finish(out, me, wsh, copies, send, recv):
    partner = shifted(me, 0, 0, 0, 1)
    forwards = []
    for at, dx in enumerate((1, 3, 2)):
        copies[at].wait_recv()
        from_place = lax.rem(shifted(me, 0, 0, 4 - dx, 0), 8)
        forward = remote(
            out.at[from_place],
            out.at[from_place],
            send.at[4 + at],
            recv.at[4 + at],
            partner,
            wsh,
        )
        forward.start()
        forwards.append(forward)
    for copy in copies:
        copy.wait_send()
    copies[3].wait_recv()
    for forward in forwards:
        forward.wait()


def gather_first(weights, tokens, small, routes, cotangent):
    def body(w_in, t_in, s_in, r_in, c_in, w_out, t_out, s_out, r_out, c_out, wide, row_s, row_r, pair, local):
        me, wsh = lax.axis_index("ctx"), lax.axis_index("wsh")
        core = lax.rem(me, 2)
        place = lax.rem(me, 8)

        def target(step):
            return shifted(
                me, lax.div(step, 16), lax.rem(lax.div(step, 8), 2), lax.rem(lax.div(step, 2), 4), lax.rem(step, 2)
            )

        barrier, amount = greet_many(64, target, wsh)
        locals_ = [
            pltpu.make_async_copy(t_in, t_out.at[place], local.at[0]),
            pltpu.make_async_copy(w_in.at[place], w_out.at[me], local.at[1]),
            pltpu.make_async_copy(s_in, s_out.at[me], local.at[2]),
            pltpu.make_async_copy(r_in, r_out.at[core], local.at[3]),
            pltpu.make_async_copy(c_in, c_out.at[core], local.at[4]),
        ]
        for copy in locals_:
            copy.start()
        pl.semaphore_wait(barrier, amount)
        row_copies = row_gather_start(t_in, t_out, me, wsh, row_s, row_r)

        def send(step, carried):
            turned = lax.rem(step * 13, 64)
            ctx = target(turned)
            remote(s_in, s_out.at[me], wide.at[0], wide.at[1], ctx, wsh).start()
            remote(w_in.at[lax.rem(ctx, 8)], w_out.at[me], wide.at[2], wide.at[3], ctx, wsh).start()
            return carried

        lax.fori_loop(1, 64, send, 0)
        partner = shifted(me, 0, 0, 0, 1)
        pair_copies = [
            remote(r_in, r_out.at[core], pair.at[0], pair.at[1], partner, wsh),
            remote(c_in, c_out.at[core], pair.at[2], pair.at[3], partner, wsh),
        ]
        for copy in pair_copies:
            copy.start()
        row_gather_finish(t_out, me, wsh, row_copies, row_s, row_r)
        for copy in pair_copies:
            copy.wait()
        for copy in locals_:
            copy.wait()
        for at, out in ((0, s_out), (2, w_out)):
            rest = out.at[pl.ds(0, 63)]
            done = remote(rest, rest, wide.at[at], wide.at[at + 1], partner, wsh)
            done.wait_send()
            done.wait_recv()

    sds = jax.ShapeDtypeStruct
    return pl.pallas_call(
        body,
        out_shape=(
            sds((64,) + weights.shape[1:], weights.dtype),
            sds((8,) + tokens.shape, tokens.dtype),
            sds((64,) + small.shape, small.dtype),
            sds((2,) + routes.shape, routes.dtype),
            sds((2,) + cotangent.shape, cotangent.dtype),
        ),
        in_specs=[ANY] * 5,
        out_specs=[ANY] * 5,
        scratch_shapes=[DMA((4,)), DMA((7,)), DMA((7,)), DMA((4,)), DMA((5,))],
        compiler_params=call_params(0),
        name="gather_first",
    )(weights, tokens, small, routes, cotangent)


def gather_row(block, collective_id):
    def body(src, out, row_s, row_r, local):
        me, wsh = lax.axis_index("ctx"), lax.axis_index("wsh")
        barrier, amount = greet([(shifted(me, 0, 0, dx, dk), wsh) for dx, dk in ((1, 0), (3, 0), (2, 0), (0, 1))])
        mine = pltpu.make_async_copy(src, out.at[lax.rem(me, 8)], local)
        mine.start()
        pl.semaphore_wait(barrier, amount)
        copies = row_gather_start(src, out, me, wsh, row_s, row_r)
        row_gather_finish(out, me, wsh, copies, row_s, row_r)
        mine.wait()

    return pl.pallas_call(
        body,
        out_shape=jax.ShapeDtypeStruct((8,) + block.shape, block.dtype),
        in_specs=[ANY],
        out_specs=ANY,
        scratch_shapes=[DMA((7,)), DMA((7,)), DMA],
        compiler_params=call_params(collective_id),
        name="gather_row",
    )(block)


COLUMN_STEPS = ((1, 0), (3, 0), (0, 1), (2, 0), (1, 1), (3, 1), (2, 1))


def gather_keys(rows, collective_id):
    count = rows.shape[0]
    half = count // 2

    def body(src, out, send, recv, local):
        me, wsh = lax.axis_index("ctx"), lax.axis_index("wsh")
        core = lax.rem(me, 2)
        group = lax.div(me, 8)
        partner = shifted(me, 0, 0, 0, 1)
        peers = [shifted(me, dz, dy, 0, 0) for dz, dy in COLUMN_STEPS]
        barrier, amount = greet([(peer, wsh) for peer in peers + [partner]])
        mine = pltpu.make_async_copy(src, out.at[group], local)
        mine.start()
        pl.semaphore_wait(barrier, amount)
        my_half = pl.ds(pl.multiple_of(core * half, half), half)
        copies = []
        for at, peer in enumerate(peers):
            copy = remote(src.at[my_half], out.at[group, my_half], send.at[at], recv.at[at], peer, wsh)
            copy.start()
            copies.append(copy)
        forwards = []
        for at, (dz, dy) in enumerate(COLUMN_STEPS):
            copies[at].wait_recv()
            origin = lax.div(shifted(me, 4 - dz, 2 - dy, 0, 0), 8)
            part = out.at[origin, my_half]
            forward = remote(part, part, send.at[7 + at], recv.at[7 + at], partner, wsh)
            forward.start()
            forwards.append(forward)
        for copy in copies:
            copy.wait_send()
        for forward in forwards:
            forward.wait()
        mine.wait()

    return pl.pallas_call(
        body,
        out_shape=jax.ShapeDtypeStruct((8,) + rows.shape, rows.dtype),
        in_specs=[ANY],
        out_specs=ANY,
        scratch_shapes=[DMA((14,)), DMA((14,)), DMA],
        compiler_params=call_params(collective_id),
        name="gather_keys",
    )(rows)


def reduce_row(parts, collective_id, both):
    _, rows, width = parts.shape
    block = (rows, width)

    def body(src, out, arrived, summed, landed, swapped, total, send, recv, local):
        me, wsh = lax.axis_index("ctx"), lax.axis_index("wsh")
        other = 1 - wsh
        core = lax.rem(me, 2)
        _, _, x, _ = coords(me)
        partner = shifted(me, 0, 0, 0, 1)
        peers = [shifted(me, 0, 0, dx, 0) for dx in (1, 2, 3)]
        barrier, amount = greet([(peer, wsh) for peer in peers + [partner]] + [(me, other)])
        pl.semaphore_wait(barrier, amount)
        first = []
        for at, dx in enumerate((2, 1, 3, 0)):
            chip = lax.rem(x + dx, 4)
            copy = remote(
                src.at[chip * 2 + 1 - core], arrived.at[at], send.at[at], recv.at[at], partner, wsh
            )
            copy.start()
            first.append(copy)
        second = []
        for at, dx in enumerate((2, 1, 3)):
            chip = lax.rem(x + dx, 4)
            first[at].wait_recv()
            summed[at] = (src[chip * 2 + core].astype(F32) + arrived[at].astype(F32)).astype(BF)
            copy = remote(
                summed.at[at],
                landed.at[at],
                send.at[4 + at],
                recv.at[4 + at],
                shifted(me, 0, 0, dx, 0),
                wsh,
            )
            copy.start()
            second.append(copy)
        first[3].wait_recv()
        total[...] = src[x * 2 + core].astype(F32) + arrived[3].astype(F32)
        for at in (1, 2, 0):
            second[at].wait_recv()
        swapped[0] = (
            total[...] + landed[0].astype(F32) + landed[1].astype(F32) + landed[2].astype(F32)
        ).astype(BF)
        swap = remote(swapped.at[0], swapped.at[1], send.at[7], recv.at[7], me, other)
        swap.start()
        swap.wait()
        total[...] = swapped[0].astype(F32) + swapped[1].astype(F32)
        if both:
            keep = pltpu.make_async_copy(total, out.at[core], local)
            keep.start()
            give = remote(total, out.at[core], send.at[8], recv.at[8], partner, wsh)
            give.start()
            give.wait()
            keep.wait()
        else:
            out[...] = total[...]
        for copy in first + second:
            copy.wait_send()

    return pl.pallas_call(
        body,
        out_shape=jax.ShapeDtypeStruct((2,) + block if both else block, F32),
        in_specs=[VMEM],
        out_specs=VMEM,
        scratch_shapes=[
            pltpu.VMEM((4,) + block, BF),
            pltpu.VMEM((3,) + block, BF),
            pltpu.VMEM((3,) + block, BF),
            pltpu.VMEM((2,) + block, BF),
            pltpu.VMEM(block, F32),
            DMA((9,)),
            DMA((9,)),
            DMA,
        ],
        compiler_params=call_params(collective_id, 40 * 1024 * 1024),
        name="reduce_row",
    )(parts)


def reduce_chip(parts, extra, collective_id):
    _, rows, width = parts.shape
    extra_block = None if extra is None else extra.shape[1:]

    def body(*refs):
        if extra is None:
            src, out, arrived, swapped, total, send, recv = refs
        else:
            src, src2, out, out2, arrived, swapped, total, arrived2, swapped2, send, recv = refs
        me, wsh = lax.axis_index("ctx"), lax.axis_index("wsh")
        other = 1 - wsh
        core = lax.rem(me, 2)
        partner = shifted(me, 0, 0, 0, 1)
        barrier, amount = greet([(partner, wsh), (me, other)])
        pl.semaphore_wait(barrier, amount)
        give = remote(src.at[1 - core], arrived, send.at[0], recv.at[0], partner, wsh)
        give.start()
        if extra is not None:
            give2 = remote(src2.at[1 - core], arrived2, send.at[2], recv.at[2], partner, wsh)
            give2.start()
        give.wait()
        swapped[0] = (src[core].astype(F32) + arrived[...].astype(F32)).astype(BF)
        swap = remote(swapped.at[0], swapped.at[1], send.at[1], recv.at[1], me, other)
        swap.start()
        if extra is not None:
            give2.wait()
            swapped2[0] = src2[core] + arrived2[...]
            swap2 = remote(swapped2.at[0], swapped2.at[1], send.at[3], recv.at[3], me, other)
            swap2.start()
            swap2.wait()
            out2[...] = swapped2[0] + swapped2[1]
        swap.wait()
        out[...] = swapped[0].astype(F32) + swapped[1].astype(F32)

    sds = jax.ShapeDtypeStruct
    block = (rows, width)
    shapes = [sds(block, F32)]
    scratch = [pltpu.VMEM(block, BF), pltpu.VMEM((2,) + block, BF), pltpu.VMEM(block, F32)]
    operands = [parts]
    if extra is not None:
        shapes.append(sds(extra_block, F32))
        scratch += [pltpu.VMEM(extra_block, F32), pltpu.VMEM((2,) + extra_block, F32)]
        operands.append(extra)
    scratch += [DMA((4,)), DMA((4,))]
    return pl.pallas_call(
        body,
        out_shape=shapes,
        in_specs=[VMEM] * len(operands),
        out_specs=[VMEM] * len(operands),
        scratch_shapes=scratch,
        compiler_params=call_params(collective_id, 40 * 1024 * 1024),
        name="reduce_chip",
    )(*operands)


def reduce_keys(parts, collective_id):
    _, groups, _, rows, width = parts.shape

    def body(src, out, arrived, summed, landed, send, recv, fsend, frecv):
        me, wsh = lax.axis_index("ctx"), lax.axis_index("wsh")
        core = lax.rem(me, 2)
        z, y, x, _ = coords(me)
        pair = lax.div(x, 2) * 2
        side = lax.rem(x, 2)
        partner = shifted(me, 0, 0, 0, 1)

        def target(step):
            dz, dy, db = lax.div(step, 4), lax.rem(lax.div(step, 2), 2), lax.rem(step, 2)
            return (
                lax.rem(z + dz, 4) * 2 + lax.rem(y + dy, 2),
                lax.rem(side + db, 2),
            )

        barrier = pltpu.get_barrier_semaphore()
        pl.semaphore_signal(barrier, inc=1, device_id=(partner, wsh), device_id_type=MESH)
        for step in range(1, 16):
            group, b = target(step)
            pl.semaphore_signal(
                barrier, inc=1, device_id=((group * 4 + pair + b) * 2 + core, wsh), device_id_type=MESH
            )
        pl.semaphore_wait(barrier, 16)
        order = (1, 4, 2, 8, 12, 3, 5, 6, 9, 13, 10, 14, 7, 11, 15, 0)
        first = []
        for at, step in enumerate(order):
            group, b = target(step)
            copy = remote(
                src.at[1 - core, group, b], arrived.at[step], fsend.at[at], frecv.at[at], partner, wsh
            )
            copy.start()
            first.append(copy)
        second = []
        for at, step in enumerate(order):
            group, b = target(step)
            first[at].wait_recv()
            value = src[core, group, b].astype(F32) + arrived[step].astype(F32)
            if step == 0:
                out[...] = value
            else:
                summed[step] = value.astype(BF)
                copy = remote(
                    summed.at[step],
                    landed.at[step],
                    send.at[at],
                    recv.at[at],
                    (group * 4 + pair + b) * 2 + core,
                    wsh,
                )
                copy.start()
                second.append((step, copy))
        for step, copy in second:
            copy.wait_recv()
            out[...] += landed[step].astype(F32)
        for copy in first:
            copy.wait_send()
        for _, copy in second:
            copy.wait_send()

    block = (rows, width)
    return pl.pallas_call(
        body,
        out_shape=jax.ShapeDtypeStruct(block, F32),
        in_specs=[VMEM],
        out_specs=VMEM,
        scratch_shapes=[
            pltpu.VMEM((16,) + block, BF),
            pltpu.VMEM((16,) + block, BF),
            pltpu.VMEM((16,) + block, BF),
            DMA((16,)),
            DMA((16,)),
            DMA((16,)),
            DMA((16,)),
        ],
        compiler_params=call_params(collective_id, 40 * 1024 * 1024),
        name="reduce_keys",
    )(parts)


def exchange_same_core(arrays, collective_id):
    amount = len(arrays)

    def body(*refs):
        ins, outs = refs[:amount], refs[amount : 2 * amount]
        send, recv, local = refs[2 * amount :]
        me, wsh = lax.axis_index("ctx"), lax.axis_index("wsh")
        chip = lax.div(me, 2)

        def target(step):
            return shifted(me, lax.div(step, 8), lax.rem(lax.div(step, 4), 2), lax.rem(step, 4), 0)

        barrier, count = greet_many(32, target, wsh)
        locals_ = []
        for at in range(amount):
            copy = pltpu.make_async_copy(ins[at].at[chip], outs[at].at[chip], local.at[at])
            copy.start()
            locals_.append(copy)
        pl.semaphore_wait(barrier, count)

        def one(step, carried):
            ctx = target(lax.rem(step * 13, 32))
            for at in range(amount):
                remote(
                    ins[at].at[lax.div(ctx, 2)], outs[at].at[chip], send.at[at], recv.at[at], ctx, wsh
                ).start()
            return carried

        lax.fori_loop(1, 32, one, 0)
        for copy in locals_:
            copy.wait()
        for at in range(amount):
            rest = outs[at].at[pl.ds(0, 31)]
            done = remote(rest, rest, send.at[at], recv.at[at], me, wsh)
            done.wait_send()
            done.wait_recv()

    return pl.pallas_call(
        body,
        out_shape=[jax.ShapeDtypeStruct(a.shape, a.dtype) for a in arrays],
        in_specs=[ANY] * amount,
        out_specs=[ANY] * amount,
        scratch_shapes=[DMA((amount,)), DMA((amount,)), DMA((amount,))],
        compiler_params=call_params(collective_id),
        name="exchange_same_core",
    )(*arrays)


def same_core_groups():
    return [[2 * i + core for i in range(32)] for core in range(2)]


def natural_order(inverse, kv_ref, keys, values, transposed):
    def one(block, carried):
        rows = kv_ref[pl.ds(pl.multiple_of(inverse[block] * BLK, BLK), BLK), :]
        at = pl.ds(pl.multiple_of(block * BLK, BLK), BLK)
        keys[at, :] = rows[:, :HEAD_WIDTH]
        values[at, :] = rows[:, HEAD_WIDTH:]
        return carried

    lax.fori_loop(0, kv_ref.shape[0] // BLK, one, 0)
    source, turned = transposed

    def turn(chunk, carried):
        at = pl.ds(pl.multiple_of(chunk * CHUNK, CHUNK), CHUNK)
        turned[:, at] = source[at, :].T
        return carried

    lax.fori_loop(0, kv_ref.shape[0] // CHUNK, turn, 0)


def stacked(ref, first, second):
    rows = [ref[pl.ds(pl.multiple_of(at * BLK, BLK), BLK), :] for at in (first, second)]
    return jnp.concatenate(
        [rows[0][:, :HEAD_WIDTH], rows[0][:, HEAD_WIDTH:], rows[1][:, :HEAD_WIDTH], rows[1][:, HEAD_WIDTH:]],
        axis=0,
    )


def unstacked(ref, first, second, value):
    for at, begin in ((first, 0), (second, 2 * BLK)):
        ref[pl.ds(pl.multiple_of(at * BLK, BLK), BLK), :] = jnp.concatenate(
            [value[begin : begin + BLK], value[begin + BLK : begin + 2 * BLK]], axis=1
        )


def forward_kernel(order, low, high, inverse, q_ref, kv_ref, pos_ref, start_ref, out_ref, lse_ref, keys, values, values_t, acc):
    step = pl.program_id(0)

    @pl.when(step == 0)
    def _():
        natural_order(inverse, kv_ref, keys, values, (values, values_t))

    first, second = order[2 * step], order[2 * step + 1]
    q_t = stacked(q_ref, first, second).astype(F32).T.astype(BF)
    q_pos, q_start = pos_ref[0], start_ref[0]
    scale = 1.0 / math.sqrt(HEAD_WIDTH)
    width = 4 * BLK
    acc[...] = jnp.zeros_like(acc)

    def chunk(index, carried):
        highest, total = carried
        at = pl.multiple_of(index * CHUNK, CHUNK)
        scores = matmul(keys[pl.ds(at, CHUNK), :], q_t) * scale
        k_pos = at + lax.broadcasted_iota(jnp.int32, (CHUNK, width), 0)
        scores = jnp.where((k_pos <= q_pos) & (k_pos >= q_start), scores, MASKED)
        top = jnp.maximum(highest, jnp.max(scores, axis=0, keepdims=True))
        probs = jnp.exp(scores - top)
        fade = jnp.exp(highest - top)
        acc[...] = acc[...] * fade + matmul(values_t[:, pl.ds(at, CHUNK)], probs.astype(BF))
        return top, total * fade + jnp.sum(probs, axis=0, keepdims=True)

    highest, total = lax.fori_loop(
        low[step],
        high[step],
        chunk,
        (jnp.full((1, width), MASKED, F32), jnp.zeros((1, width), F32)),
    )
    lse_ref[0] = highest + jnp.log(total)
    unstacked(out_ref, first, second, (acc[...] / total).T.astype(BF))


def attend(order, low, high, inverse, queries, kv, positions, starts):
    rows = queries.shape[0]
    steps = rows // (2 * BLK)
    everything = pl.BlockSpec(queries.shape, lambda i, *_: (0, 0))
    strip = pl.BlockSpec((1, 1, 4 * BLK), lambda i, *_: (i, 0, 0))
    sds = jax.ShapeDtypeStruct
    return pl.pallas_call(
        forward_kernel,
        out_shape=(sds(queries.shape, BF), sds((steps, 1, 4 * BLK), F32)),
        grid_spec=pltpu.PrefetchScalarGridSpec(
            num_scalar_prefetch=4,
            grid=(steps,),
            in_specs=[everything, pl.BlockSpec(kv.shape, lambda i, *_: (0, 0)), strip, strip],
            out_specs=[everything, strip],
            scratch_shapes=[
                pltpu.VMEM((kv.shape[0], HEAD_WIDTH), BF),
                pltpu.VMEM((kv.shape[0], HEAD_WIDTH), BF),
                pltpu.VMEM((HEAD_WIDTH, kv.shape[0]), BF),
                pltpu.VMEM((HEAD_WIDTH, 4 * BLK), F32),
            ],
        ),
        compiler_params=pltpu.CompilerParams(vmem_limit_bytes=50 * 1024 * 1024),
        name="attend",
    )(order, low, high, inverse, queries, kv, positions, starts)


def backward_kernel(order, low, high, inverse, q_ref, do_ref, kv_ref, pos_ref, start_ref, lse_ref, dot_ref, dq_ref, dkv_ref, keys, values, keys_t, d_keys, d_values, acc):
    step = pl.program_id(0)

    @pl.when(step == 0)
    def _():
        natural_order(inverse, kv_ref, keys, values, (keys, keys_t))
        d_keys[...] = jnp.zeros_like(d_keys)
        d_values[...] = jnp.zeros_like(d_values)

    first, second = order[2 * step], order[2 * step + 1]
    q = stacked(q_ref, first, second)
    d_out = stacked(do_ref, first, second)
    q_t = q.astype(F32).T.astype(BF)
    d_out_t = d_out.astype(F32).T.astype(BF)
    q_pos, q_start = pos_ref[0], start_ref[0]
    lse, dots = lse_ref[0], dot_ref[0]
    scale = 1.0 / math.sqrt(HEAD_WIDTH)
    width = 4 * BLK
    acc[...] = jnp.zeros_like(acc)

    def chunk(index, carried):
        at = pl.multiple_of(index * CHUNK, CHUNK)
        here = pl.ds(at, CHUNK)
        scores = matmul(keys[here, :], q_t) * scale
        k_pos = at + lax.broadcasted_iota(jnp.int32, (CHUNK, width), 0)
        scores = jnp.where((k_pos <= q_pos) & (k_pos >= q_start), scores, MASKED)
        probs = jnp.exp(scores - lse)
        d_probs = matmul(values[here, :], d_out_t)
        d_scores = (probs * (d_probs - dots)).astype(BF)
        d_values[here, :] += matmul(probs.astype(BF), d_out)
        d_keys[here, :] += matmul(d_scores, q)
        acc[...] += matmul(keys_t[:, here], d_scores)
        return carried

    lax.fori_loop(low[step], high[step], chunk, 0)
    unstacked(dq_ref, first, second, (acc[...] * scale).T)

    @pl.when(step == pl.num_programs(0) - 1)
    def _():
        def one(block, carried):
            dealt = inverse[block]
            group, inside = dealt // 16, dealt % 16
            half, rest = inside // 8, inside % 8
            at = pl.ds(pl.multiple_of(block * BLK, BLK), BLK)
            to = pl.ds(pl.multiple_of(rest * BLK, BLK), BLK)
            dkv_ref[half, group, 0, to, :] = (d_keys[at, :] * scale).astype(BF)
            dkv_ref[half, group, 1, to, :] = d_values[at, :].astype(BF)
            return carried

        lax.fori_loop(0, kv_ref.shape[0] // BLK, one, 0)


def attend_back(order, low, high, inverse, queries, d_heads, kv, positions, starts, lse, dots):
    rows = queries.shape[0]
    total = kv.shape[0]
    steps = rows // (2 * BLK)
    everything = pl.BlockSpec(queries.shape, lambda i, *_: (0, 0))
    strip = pl.BlockSpec((1, 1, 4 * BLK), lambda i, *_: (i, 0, 0))
    sds = jax.ShapeDtypeStruct
    dkv_shape = (2, total // rows, 2, rows // 2, HEAD_WIDTH)
    return pl.pallas_call(
        backward_kernel,
        out_shape=(sds(queries.shape, F32), sds(dkv_shape, BF)),
        grid_spec=pltpu.PrefetchScalarGridSpec(
            num_scalar_prefetch=4,
            grid=(steps,),
            in_specs=[everything, everything, pl.BlockSpec(kv.shape, lambda i, *_: (0, 0)), strip, strip, strip, strip],
            out_specs=[everything, pl.BlockSpec(dkv_shape, lambda i, *_: (0, 0, 0, 0, 0))],
            scratch_shapes=[
                pltpu.VMEM((total, HEAD_WIDTH), BF),
                pltpu.VMEM((total, HEAD_WIDTH), BF),
                pltpu.VMEM((HEAD_WIDTH, total), BF),
                pltpu.VMEM((total, HEAD_WIDTH), F32),
                pltpu.VMEM((total, HEAD_WIDTH), F32),
                pltpu.VMEM((HEAD_WIDTH, 4 * BLK), F32),
            ],
        ),
        compiler_params=pltpu.CompilerParams(vmem_limit_bytes=55 * 1024 * 1024),
        name="attend_back",
    )(order, low, high, inverse, queries, d_heads, kv, positions, starts, lse, dots)


def lanes_to(row, lanes=128):
    return jnp.pad(row, ((0, 0),) * (row.ndim - 1) + ((0, lanes - row.shape[-1]),))


def local(
    tokens,
    cotangent,
    seq_lengths,
    block_order,
    routes,
    w_query,
    key_weight,
    value_weight,
    w_out,
    gain_attn,
    gain_query,
    gain_key,
    gain_ffn,
    w_router,
    w_gate,
    w_up,
    w_down,
):
    rows = tokens.shape[0]
    width = tokens.shape[1]
    experts = w_router.shape[1]
    block_count = block_order.shape[0]
    wsh = lax.axis_index("wsh")
    me = lax.axis_index("ctx")
    core = lax.rem(me, 2)
    place = lax.rem(me, 8)
    group = lax.div(me, 8)
    row_tokens = 8 * rows
    row_blocks = row_tokens // BLK

    def of_mine(weight):
        return to_low(lax.dynamic_index_in_dim(weight, wsh, 0, keepdims=False))

    def of_other(weight):
        return to_low(lax.dynamic_index_in_dim(weight, 1 - wsh, 0, keepdims=False))

    def swap(value):
        return lax.ppermute(value, "wsh", [(0, 1), (1, 0)])

    gate_w = (of_mine(w_gate), swap(of_other(w_gate)))
    up_w = (of_mine(w_up), swap(of_other(w_up)))
    down_w = (of_mine(w_down), swap(of_other(w_down)))

    depth = w_query.shape[0]
    q_part = to_low(w_query).reshape(depth, 8, 256).transpose(1, 0, 2)
    k_part = jnp.repeat(to_low(key_weight).reshape(depth, 2, 128).transpose(1, 0, 2), 4, axis=0)
    v_part = jnp.repeat(to_low(value_weight).reshape(depth, 2, 128).transpose(1, 0, 2), 4, axis=0)
    w_pack = jnp.concatenate([q_part, k_part, v_part], axis=2)
    small = jnp.concatenate(
        [lanes_to(gain_attn[None, :]), lanes_to(gain_ffn[None, :]), jnp.zeros((6, 128), F32)], axis=0
    )
    w_all, row_rows, small_all, chip_routes, chip_cot = gather_first(
        w_pack, tokens, small, routes.T, cotangent
    )
    w_qkv = w_all.reshape(width, 512)
    g_attn = to_low(small_all[:, 0, :depth].reshape(width)).astype(F32)
    g_ffn = to_low(small_all[:, 1, :depth].reshape(width)).astype(F32)
    g_query = rounded(gain_query)
    g_key = rounded(gain_key)

    o_part = to_low(w_out).T.reshape(depth, 8, 256).transpose(1, 0, 2)
    r_part = jnp.broadcast_to(to_low(w_router)[None], (8, depth, experts))
    late_pack = jnp.tile(jnp.concatenate([o_part, r_part], axis=2), (8, 1, 1))
    late_all = lax.all_to_all(late_pack, "ctx", split_axis=0, concat_axis=0, tiled=True).reshape(width, 384)
    wo_t = late_all[:, :256]
    wr = late_all[:, 256:]

    route_rows = chip_routes.transpose(0, 2, 1)
    hits = jnp.any(
        route_rows[:, :, :, None] == jnp.arange(experts, dtype=jnp.int32)[None, None, None, :], axis=2
    )
    before = jnp.tril(jnp.ones((rows, rows), BF), -1)
    ranks = jnp.einsum("ts,hse->hte", before, hits.astype(BF), preferred_element_type=F32).astype(jnp.int32)
    ranks = jnp.where(hits, ranks + jnp.array([0, CAP], jnp.int32)[:, None, None], -1)
    hits = hits.reshape(2 * rows, experts)
    quarter = core * 2 + wsh
    my_ranks = lax.dynamic_index_in_dim(
        ranks.reshape(2 * rows, experts).T.reshape(experts // 4, 4, 2 * rows), quarter, 1, keepdims=False
    )
    chips = experts // 4
    slots = 2 * CAP
    pick = my_ranks[:, None, :] == jnp.arange(slots, dtype=jnp.int32)[None, :, None]
    pick_low = pick.astype(BF).reshape(chips * slots, 2 * rows)
    cot_rows = matmul(pick_low, chip_cot.reshape(2 * rows, width)).astype(BF)
    cot_there = lax.all_to_all(
        cot_rows.reshape(chips, slots, width),
        "ctx",
        split_axis=0,
        concat_axis=0,
        tiled=True,
        axis_index_groups=same_core_groups(),
    ).reshape(chips * slots, width)

    my_blocks = lax.dynamic_slice_in_dim(block_order, group * row_blocks, row_blocks, 0)
    positions = (my_blocks[:, None] * BLK + jnp.arange(BLK, dtype=jnp.int32)[None, :]).reshape(row_tokens)
    starts = seq_starts(positions, seq_lengths)
    cosine, sine_tab = rope_tables(positions - starts)
    inverse_order = (
        jnp.zeros((block_count,), jnp.int32)
        .at[block_order]
        .set(jnp.arange(block_count, dtype=jnp.int32))
    )
    smaller = jnp.sum((my_blocks[None, :] < my_blocks[:, None]).astype(jnp.int32), axis=1)
    order = jnp.sum(
        jnp.where(
            smaller[None, :] == jnp.arange(row_blocks, dtype=jnp.int32)[:, None],
            jnp.arange(row_blocks, dtype=jnp.int32)[None, :],
            0,
        ),
        axis=1,
    )
    first_start = starts.reshape(row_blocks, BLK)[:, 0]
    low = jnp.min(jnp.take(first_start, order).reshape(-1, 2), axis=1) // CHUNK
    high = jnp.max(jnp.take(my_blocks, order).reshape(-1, 2), axis=1) * BLK // CHUNK + 1

    def strips(per_token):
        by_block = jnp.take(per_token.reshape(row_blocks, BLK), order, axis=0).reshape(-1, 2, 1, BLK)
        return jnp.broadcast_to(by_block, (row_blocks // 2, 2, 2, BLK)).reshape(-1, 1, 4 * BLK)

    q_pos, q_start = strips(positions), strips(starts)

    stream = row_rows.reshape(row_tokens, width).astype(F32)
    inverse_one = inverse_root(stream)
    hidden_one = to_low(stream * inverse_one * g_attn)
    qkv = matmul(hidden_one, w_qkv)
    q_pre = qkv[:, :256].reshape(row_tokens, 2, HEAD_WIDTH)
    k_pre = qkv[:, 256:384]
    q_inverse = inverse_root(q_pre)
    k_inverse = inverse_root(k_pre)
    queries = to_low(rotate(q_pre * q_inverse * g_query, cosine[:, None], sine_tab[:, None]))
    queries = queries.reshape(row_tokens, 256)
    keys = to_low(rotate(k_pre * k_inverse * g_key, cosine, sine_tab))
    kv = jnp.concatenate([keys, to_low(qkv[:, 384:])], axis=1)
    kv_all = gather_keys(kv, 1).reshape(block_count * BLK, 256)
    heads, lse = attend(order, low, high, inverse_order, queries, kv_all, q_pos, q_start)

    attn_parts = to_low(times_transposed(heads, wo_t)).reshape(8, rows, width)
    attn_total = reduce_row(attn_parts, 2, True).reshape(2 * rows, width)
    chip_stream = lax.dynamic_slice_in_dim(stream, (place - core) * rows, 2 * rows, 0)
    chip_residual = chip_stream + attn_total
    chip_inverse_two = inverse_root(chip_residual)
    chip_hidden = to_low(chip_residual * chip_inverse_two * g_ffn)
    logits = matmul(chip_hidden, wr)
    masked_logits = jnp.where(hits, logits, MASKED)
    gate_exps = jnp.where(
        hits, jnp.exp(masked_logits - jnp.max(masked_logits, axis=-1, keepdims=True)), 0.0
    )
    gates = gate_exps / jnp.sum(gate_exps, axis=-1, keepdims=True)

    def my_rows(value):
        return lax.dynamic_slice_in_dim(value, core * rows, rows, 0)

    out_rows = matmul(pick_low, chip_hidden).astype(BF).reshape(chips, slots, width)
    my_gates = lax.dynamic_index_in_dim(
        gates.T.reshape(chips, 4, 2 * rows), quarter, 1, keepdims=False
    )
    slot_gates = jnp.sum(jnp.where(pick, my_gates[:, None, :], 0.0), axis=2)
    gate_tile = jnp.pad(slot_gates[:, None, :], ((0, 0), (0, 7), (0, 128 - slots)))
    arrived, gate_there = exchange_same_core([out_rows, gate_tile], 3)
    arrived = arrived.reshape(chips * slots, width)
    gate_col = gate_there[:, 0, :slots].reshape(chips * slots, 1)
    d_pairs = to_low(gate_col * cot_there.astype(F32))
    expert_out = 0.0
    d_rows = 0.0
    grads = []
    for gate_half, up_half, down_half in zip(gate_w, up_w, down_w):
        gate_pre = matmul(arrived, gate_half)
        up_pre = matmul(arrived, up_half)
        sigma = jax.nn.sigmoid(gate_pre)
        activated = to_low(gate_pre * sigma * up_pre)
        expert_out = expert_out + matmul(activated, down_half)
        d_act = times_transposed(d_pairs, down_half)
        grad_down = transposed_times(activated, d_pairs)
        d_gate_pre = to_low(d_act * up_pre * sigma * (1.0 + gate_pre * (1.0 - sigma)))
        d_up_pre = to_low(d_act * gate_pre * sigma)
        grad_gate = transposed_times(arrived, d_gate_pre)
        grad_up = transposed_times(arrived, d_up_pre)
        d_rows = (
            d_rows + times_transposed(d_gate_pre, gate_half) + times_transposed(d_up_pre, up_half)
        )
        grads.append((grad_gate, grad_up, grad_down))
    d_gate_slots = jnp.sum(expert_out * cot_there.astype(F32), axis=1).reshape(chips, 1, slots)
    d_gate_tile = jnp.pad(d_gate_slots, ((0, 0), (0, 7), (0, 128 - slots)))
    d_back, d_gate_back = exchange_same_core(
        [to_low(d_rows).reshape(chips, slots, width), d_gate_tile], 4
    )
    y_back = lax.all_to_all(
        to_low(gate_col * expert_out).reshape(chips, slots, width),
        "ctx",
        split_axis=0,
        concat_axis=0,
        tiled=True,
        axis_index_groups=same_core_groups(),
    )

    def paired(own, back):
        back = swap(to_low(back)).astype(F32)
        return jnp.where(wsh == 0, jnp.stack([own, back]), jnp.stack([back, own]))

    grad_gate, grad_up, grad_down = [paired(own, back) for own, back in zip(*grads)]

    def collect(back):
        return to_low(transposed_times(pick_low, back.reshape(chips * slots, width))).reshape(2, rows, width)

    d_gate_slots = d_gate_back[:, 0, :slots]
    d_gates_mine = jnp.sum(jnp.where(pick, d_gate_slots[:, :, None], 0.0), axis=1)
    d_gates_part = jnp.sum(
        jnp.where(
            jnp.arange(4, dtype=jnp.int32)[None, :, None] == quarter, d_gates_mine[:, None, :], 0.0
        ),
        axis=0,
        keepdims=True,
    ) if False else jnp.where(
        jnp.arange(4, dtype=jnp.int32)[None, :, None] == quarter, d_gates_mine[:, None, :], 0.0
    ).reshape(experts, 2 * rows)
    d_gates_part = d_gates_part.T.reshape(2, rows, experts)
    d_hidden_moe, d_gates = reduce_chip(collect(d_back), d_gates_part, 5)
    (moe_total,) = reduce_chip(collect(y_back), None, 6)
    residual = my_rows(chip_residual)
    out_stream = residual + moe_total

    own_gates = my_rows(gates)
    hidden_two = my_rows(chip_hidden)
    inverse_two = my_rows(chip_inverse_two)
    d_chosen = own_gates * (d_gates - jnp.sum(own_gates * d_gates, axis=-1, keepdims=True))
    d_logits = to_low(d_chosen)
    grad_router = transposed_times(hidden_two, d_logits)
    d_hidden_two = d_hidden_moe + times_transposed(d_logits, wr)
    d_res_norm, ffn_gain_terms = norm_back(residual, inverse_two, g_ffn, d_hidden_two)
    d_residual = cotangent.astype(F32) + d_res_norm
    gain_ffn_part = jnp.sum(ffn_gain_terms, axis=0)

    d_attn = gather_row(to_low(d_residual), 7).reshape(row_tokens, width)
    grad_out_t = transposed_times(d_attn, heads)
    d_heads = to_low(matmul(d_attn, wo_t))
    dots = jnp.sum(
        d_heads.astype(F32).reshape(row_tokens, 2, HEAD_WIDTH)
        * heads.astype(F32).reshape(row_tokens, 2, HEAD_WIDTH),
        axis=-1,
    )
    dot_strips = (
        jnp.take(dots.reshape(row_blocks, BLK, 2), order, axis=0)
        .transpose(0, 2, 1)
        .reshape(row_blocks // 2, 1, 4 * BLK)
    )
    early = jnp.concatenate(
        [
            to_low(grad_out_t[:, :128]).reshape(64, depth, 128),
            to_low(grad_out_t[:, 128:]).reshape(64, depth, 128),
            to_low(grad_router).reshape(64, depth, 128),
            jnp.pad(
                to_low(gain_ffn_part).reshape(64, 1, depth), ((0, 0), (0, 15), (0, 128 - depth))
            ),
        ],
        axis=1,
    )
    early = lax.all_to_all(early, "ctx", split_axis=0, concat_axis=0, tiled=True)
    d_queries, d_kv = attend_back(
        order, low, high, inverse_order, queries, d_heads, kv_all, q_pos, q_start, lse, dot_strips
    )
    d_side = reduce_keys(d_kv, 8)
    is_key = lax.rem(lax.div(me, 2), 2) == 0
    half_rows = row_tokens // 2

    def half_of(value):
        return lax.dynamic_slice_in_dim(value, core * half_rows, half_rows, 0)

    d_k_norm = rotate_back(d_side, half_of(cosine), half_of(sine_tab))
    d_k_pre, key_gain_terms = norm_back(half_of(k_pre), half_of(k_inverse), g_key, d_k_norm)
    key_gain_part = jnp.where(is_key, jnp.sum(key_gain_terms, axis=0), 0.0)
    d_side_pre = to_low(jnp.where(is_key, d_k_pre, d_side))
    d_q_norm = rotate_back(
        d_queries.reshape(row_tokens, 2, HEAD_WIDTH), cosine[:, None], sine_tab[:, None]
    )
    d_q_pre, query_gain_terms = norm_back(q_pre, q_inverse, g_query, d_q_norm)
    query_gain_part = jnp.sum(query_gain_terms, axis=(0, 1))
    d_q_pre = to_low(d_q_pre.reshape(row_tokens, 256))
    side_w = jnp.where(is_key, w_qkv[:, 256:384], w_qkv[:, 384:])
    d_side_full = jnp.where(
        (jnp.arange(row_tokens, dtype=jnp.int32) // half_rows == core)[:, None],
        jnp.concatenate([d_side_pre, d_side_pre], axis=0),
        jnp.zeros((), BF),
    )
    d_all = jnp.concatenate([d_q_pre, d_side_full], axis=1)
    d_hidden_parts = to_low(
        times_transposed(d_all, jnp.concatenate([w_qkv[:, :256], side_w], axis=1))
    ).reshape(8, rows, width)
    grad_in = to_low(transposed_times(hidden_one, d_all))
    tail = jnp.broadcast_to(
        jnp.pad(to_low(jnp.stack([query_gain_part, key_gain_part])), ((0, 14), (0, 0)))[None],
        (64, 16, 128),
    )
    late = jnp.concatenate(
        [grad_in[:, 128 * i : 128 * i + 128].reshape(64, depth, 128) for i in range(3)] + [tail], axis=1
    )
    late = lax.all_to_all(late, "ctx", split_axis=0, concat_axis=0, tiled=True)
    d_hidden_one = reduce_row(d_hidden_parts, 9, False)
    own_stream = tokens.astype(F32)
    d_stream_norm, _ = norm_back(own_stream, inverse_root(own_stream), g_attn, d_hidden_one)
    grad_tokens = d_residual + d_stream_norm

    def summed(value, terms):
        return jnp.sum(value.astype(F32).reshape((8,) + terms + value.shape[1:]), axis=0)

    early_q = summed(early[:, : 2 * depth], (8,)).reshape(8, 2, depth, 128)
    grad_out = early_q.transpose(0, 1, 3, 2).reshape(8 * 256, depth)
    grad_router = jnp.sum(early[:, 2 * depth : 3 * depth].astype(F32), axis=0)
    grad_gain_ffn = jnp.sum(early[:, 3 * depth, :depth].astype(F32), axis=0)
    late_q = summed(late[:, : 2 * depth], (8,)).reshape(8, 2, depth, 128)
    grad_query = late_q.transpose(2, 0, 1, 3).reshape(depth, 8 * 256)
    late_kv = jnp.sum(
        late[:, 2 * depth : 3 * depth].astype(F32).reshape(8, 2, 2, 2, depth, 128), axis=(0, 3)
    )
    grad_key = late_kv[:, 0].transpose(1, 0, 2).reshape(depth, 256)
    grad_value = late_kv[:, 1].transpose(1, 0, 2).reshape(depth, 256)
    gain_parts = jnp.sum(late[:, 3 * depth : 3 * depth + 2].astype(F32), axis=0)
    gain_attn_part = (
        jnp.sum(rounded(w_query) * grad_query, axis=1)
        + jnp.sum(rounded(key_weight) * grad_key, axis=1)
        + jnp.sum(rounded(value_weight) * grad_value, axis=1)
    ) / rounded(gain_attn)
    gain_parts = lax.psum(jnp.concatenate([gain_parts, lanes_to(gain_attn_part[None, :])], axis=0), "wsh")
    return (
        out_stream,
        grad_tokens,
        grad_query,
        grad_key,
        grad_value,
        grad_out,
        gain_parts[2, :depth],
        gain_parts[0],
        gain_parts[1],
        grad_gain_ffn,
        grad_router,
        grad_gate,
        grad_up,
        grad_down,
    )


def solution(mesh):
    in_specs = (
        P("ctx", None),
        P("ctx", None),
        P(),
        P(),
        P("ctx", None),
        P("ctx", "wsh"),
        P("ctx", "wsh"),
        P("ctx", "wsh"),
        P("wsh", "ctx"),
        P("ctx"),
        P(),
        P(),
        P("ctx"),
        P("ctx", None),
        P("ctx", None, "wsh"),
        P("ctx", None, "wsh"),
        P("ctx", "wsh", None),
    )
    out_specs = (
        P("ctx", None),
        P("ctx", None),
        P("ctx", "wsh"),
        P("ctx", "wsh"),
        P("ctx", "wsh"),
        P("wsh", "ctx"),
        P("ctx"),
        P(),
        P(),
        P("ctx"),
        P("ctx", None),
        P("ctx", None, "wsh"),
        P("ctx", None, "wsh"),
        P("ctx", "wsh", None),
    )
    return jax.shard_map(local, mesh=mesh, in_specs=in_specs, out_specs=out_specs, check_vma=False)
```

time: 4070 us -> 998 us (0.25)
  waiting for transfers between devices: 2270 us -> 139 us
  blocking collectives: 937 us -> 11.1 us
  Pallas kernels: 0 us -> 549 us
  local copies, waits for them, and re-layouts: 402 us -> 43.6 us
  matrix products: 245 us -> 116 us
  other arithmetic: 175 us -> 74.4 us
    reduce_scatter x7 -> x0, waiting for transfers between devices: 1970 us -> none  [the longest x1 357 us: local(): lax.psum_scatter(grad_out, 'ctx', scatter_dimension=1, tiled=True)]
    pallas_call x0 -> x12, Pallas kernels: none -> 549 us  [the longest x1 135 us: gather_first(): pl.pallas_call(body, out_shape=(sds((64,) + weights.shape[1:], weights.dt...]
    unnamed x2 -> x0, blocking collectives: 498 us -> none
    all_to_all x2 -> x0, blocking collectives: 211 us -> none  [send_rows(): lax.all_to_all(rows, 'ctx', split_axis=0, concat_axis=1, tiled=True)]
    dot_general x15 -> x1, matrix products: 188 us -> 0.21 us  [local(): jnp.einsum('ts,hse->hte', before, hits.astype(BF), preferred_element_type...]
    all_gather x6 -> x0, waiting for transfers between devices: 165 us -> none  [the longest x1 67.5 us: local(): lax.all_gather(values_own, 'ctx', axis=0, tiled=True)]
    all_gather x1 -> x0, blocking collectives: 158 us -> none  [local(): lax.all_gather(to_low(w_router), 'ctx', axis=0, tiled=True)]
    convert_element_type x7 -> x2, local copies, waits for them, and re-layouts: 114 us -> 0.14 us  [the longest x1 0.07 us: local(): g_attn = to_low(small_all[:, 0, :depth].reshape(width)).astype(F32)]
  transfers between devices with their start and end apart: 18 -> 11, of which waited for: 13 -> 5; matrix products, arithmetic and copies ran while one was open for 6% -> 16% of each run, Pallas kernels for 0% -> 32%
where the time goes in v1:
time: 998 us; the launch traced here: 986 us
  Pallas kernels  549 us (55%)
  waiting for transfers between devices  139 us (14%)
  matrix products  116 us (12%)
  other arithmetic  74.4 us (7%)
  starting transfers between devices  48.8 us (5%)
  local copies, waits for them, and re-layouts  43.6 us (4%)
  blocking collectives  11.1 us (1%)
    pallas_call x1, Pallas kernels, gather_first(): pl.pallas_call(body, out_shape=(sds((64,) + weights.shape[1:], weights.dt...  135 us
    pallas_call x2, Pallas kernels, reduce_row(): pl.pallas_call(body, out_shape=jax.ShapeDtypeStruct((2,) + block if both...  114 us
    ppermute x6, waiting for transfers between devices, swap(): return lax.ppermute(value, 'wsh', [(0, 1), (1, 0)])  106 us
    pallas_call x2, Pallas kernels, exchange_same_core(): pl.pallas_call(body, out_shape=[jax.ShapeDtypeStruct(a.shape, a.dtype) fo...  105 us
    dot_general x11, matrix products, matmul(): return jnp.dot(left, right, preferred_element_type=jnp.float32)  42.8 us
    pallas_call x1, Pallas kernels, reduce_keys(): pl.pallas_call(body, out_shape=jax.ShapeDtypeStruct(block, F32), in_specs...  41.6 us
    dot_general x9, matrix products, times_transposed(): lax.dot_general(left, right, (((1,), (1,)), ((), ())), preferred_element_...  36.7 us
    dot_general x11, matrix products, transposed_times(): lax.dot_general(left, right, (((0,), (0,)), ((), ())), preferred_element_...  36.7 us
  transfers between devices with their start and end apart: 11, of which 5 were waited for; matrix products, arithmetic and copies ran while one was open for 16% of the time, Pallas kernels for 32%

profile of v1, /device:TPU:0, one launch (start us, length us, event | category | flops | bytes accessed | tf_op | source)
XLA Modules:
  0.0 986.0 jit_solution(15008113754081957479)
XLA Ops:
  3.8 11.7 %all-to-all-start = ((bf16[64,32,384]{2,1,0:T(8,128)(2,1)}), bf16[64,32,384]{2,1,0:T(8,128)(2,1)}, u32[]{:S(2)}, u32[]{:S(2)}) async-start(bf16[64,32,384]{2,1,0:T(8,128)(2,1)} %bitcast.19), calls=%async_computation | async-start | bytes 3145728 | tf_op jit(solution)/shard_map/all_to_all | solution.py:839
  15.5 3.2 fusion.14
  19.4 3.2 fusion.15
  24.0 3.3 fusion.16
  30.2 134.5 %gather_first.1 = (bf16[64,32,512]{2,1,0:T(8,128)(2,1)}, bf16[8,128,2048]{2,1,0:T(8,128)(2,1)}, f32[64,8,128]{2,1,0:T(8,128)}, s32[2,8,128]{2,1,0:T(8,128)}, bf16[2,128,2048]{2,1,0:T(8,128)(2,1)}) custom-call(bf16[8,32,512]{2,1,0:T(8,128)(2,1)} %pad_maximum_fusion.8.w_in, bf16[128,2048]{1,0:T(8,128)(2,1)} %t_in.1, f32[8,128]{1,0:T(8,128)} %fusion.84.s_in, ...), custom_call_target="tpu_custom_call" | custom-call | tf_op jit(solution)/shard_map/gather_first/pallas_call | solution.py:238
  166.0 3.2 multiply_reduce_fusion
  184.2 2.7 multiply_multiply_fusion
  186.9 2.5 slice_negate_fusion.1
  193.5 31.4 %gather_keys.1 = bf16[8,1024,256]{2,1,0:T(8,128)(2,1)} custom-call(bf16[1024,256]{1,0:T(8,128)(2,1)} %pad_maximum_fusion.3.src), custom_call_target="tpu_custom_call" | custom-call | tf_op jit(solution)/shard_map/gather_keys/pallas_call | solution.py:314
  225.2 6.5 convert.57
  236.8 2.9 maximum_multiply_fusion
  241.8 26.3 %attend.1 = (bf16[1024,256]{1,0:T(8,128)(2,1)S(1)}, f32[8,1,256]{2,1,0:T(1,128)S(1)}) custom-call(s32[16]{0:T(128)S(1)} %select_reduce_fusion.3.order, s32[8]{0:T(128)S(1)} %get-tuple-element.123.low, s32[8]{0:T(128)S(1)} %get-tuple-element.124.high, s32[128]{0:T(128)S(1)} %scatter_custom_fusion.inverse, bf16[1024,256]{1,0:T(8,128)(2,1)S(1)} %fusion.30.q_ref, ...), custom_call_target="tpu_custom_call" | custom-call | tf_op jit(solution)/shard_map/attend/pallas_call | solution.py:669
  268.9 2.7 convolution_convert_fusion.2
  272.5 9.5 all-to-all-start.2
  282.0 2.5 convolution_convert_fusion.1
  284.5 72.3 %reduce_row.2 = f32[2,128,2048]{2,1,0:T(8,128)S(1)} custom-call(bf16[8,128,2048]{2,1,0:T(8,128)(2,1)S(1)} %bitcast.292), custom_call_target="tpu_custom_call" | custom-call | tf_op jit(solution)/shard_map/reduce_row/pallas_call | solution.py:384
  363.8 2.6 convolution_convert_fusion.3
  366.5 55.7 %exchange_same_core.2 = (bf16[32,24,2048]{2,1,0:T(8,128)(2,1)}, f32[32,8,128]{2,1,0:T(8,128)}) custom-call(bf16[32,24,2048]{2,1,0:T(8,128)(2,1)} %bitcast.306, f32[32,8,128]{2,1,0:T(8,128)} %pad.27.refs_1_), custom_call_target="tpu_custom_call" | custom-call | tf_op jit(solution)/shard_map/exchange_same_core/pallas_call | solution.py:578
  423.3 5.8 fusion.46
  429.1 4.7 fusion.42
  433.8 3.2 fusion.111
  437.0 4.7 multiply_convert_fusion.11
  441.7 2.6 fusion
  444.4 4.1 multiply_convert_fusion.9
  448.5 4.1 fusion.38
  452.7 6.4 fusion.44
  459.1 6.6 fusion.40
  465.7 3.7 convolution_bitcast_fusion.2
  469.4 6.2 fusion.2
  476.4 4.6 convolution_convert_fusion.4
  481.0 3.7 multiply_convert_fusion.8
  484.8 3.0 convolution_convert_fusion.6
  487.8 3.0 convolution_convert_fusion.5
  490.8 3.4 fusion.112
  494.3 5.1 add_convert_fusion
  499.4 49.0 %exchange_same_core.3 = (bf16[32,24,2048]{2,1,0:T(8,128)(2,1)}, f32[32,8,128]{2,1,0:T(8,128)}) custom-call(bf16[32,24,2048]{2,1,0:T(8,128)(2,1)} %bitcast.308, f32[32,8,128]{2,1,0:T(8,128)} %pad.28.refs_1_), custom_call_target="tpu_custom_call" | custom-call | tf_op jit(solution)/shard_map/exchange_same_core/pallas_call | solution.py:578
  548.3 2.9 fusion.9
  552.7 17.8 %reduce_chip.3 = (f32[128,2048]{1,0:T(8,128)S(1)}, f32[128,128]{1,0:T(8,128)S(1)}) custom-call(bf16[2,128,2048]{2,1,0:T(8,128)(2,1)S(1)} %bitcast.294, f32[2,128,128]{2,1,0:T(8,128)S(1)} %bitcast.296), custom_call_target="tpu_custom_call" | custom-call | tf_op jit(solution)/shard_map/reduce_chip/pallas_call | solution.py:448
  571.0 7.0 all-to-all-start.1
  580.6 5.7 convolution_bitcast_fusion.1
  586.2 2.5 multiply_reduce_fusion.2
  589.6 3.3 convolution_bitcast_fusion
  593.0 40.7 %collective-permute-done.3 = bf16[2048,384]{1,0:T(8,128)(2,1)} collective-permute-done((bf16[2048,384]{1,0:T(8,128)(2,1)}, bf16[2048,384]{1,0:T(8,128)(2,1)}, u32[]{:S(2)}, u32[]{:S(2)}) %collective-permute-start.3) | collective-permute-done | bytes 1572896 | tf_op jit(solution)/shard_map/ppermute | solution.py:813
  635.3 3.1 maximum_select_fusion
  638.4 37.4 %collective-permute-done.4 = bf16[2048,384]{1,0:T(8,128)(2,1)} collective-permute-done((bf16[2048,384]{1,0:T(8,128)(2,1)}, bf16[2048,384]{1,0:T(8,128)(2,1)}, u32[]{:S(2)}, u32[]{:S(2)}) %collective-permute-start.4) | collective-permute-done | bytes 1572896 | tf_op jit(solution)/shard_map/ppermute | solution.py:813
  677.4 2.9 maximum_select_fusion.1
  680.3 27.9 %collective-permute-done.5 = bf16[384,2048]{1,0:T(8,128)(2,1)S(1)} collective-permute-done((bf16[384,2048]{1,0:T(8,128)(2,1)}, bf16[384,2048]{1,0:T(8,128)(2,1)S(1)}, u32[]{:S(2)}, u32[]{:S(2)}) %collective-permute-start.5) | collective-permute-done | bytes 1572896 | tf_op jit(solution)/shard_map/ppermute | solution.py:813
  708.5 3.1 maximum_select_fusion.2
  711.7 3.1 fusion.8
  714.8 16.4 %reduce_chip.2 = f32[128,2048]{1,0:T(8,128)S(1)} custom-call(bf16[2,128,2048]{2,1,0:T(8,128)(2,1)S(1)} %bitcast.295), custom_call_target="tpu_custom_call" | custom-call | tf_op jit(solution)/shard_map/reduce_chip/pallas_call | solution.py:448
  733.1 28.7 %gather_row.1 = bf16[8,128,2048]{2,1,0:T(8,128)(2,1)} custom-call(bf16[128,2048]{1,0:T(8,128)(2,1)} %get-tuple-element.61.src), custom_call_target="tpu_custom_call" | custom-call | tf_op jit(solution)/shard_map/gather_row/pallas_call | solution.py:266
  761.8 4.5 convert_multiply_fusion.4
  769.8 33.4 %attend_back.1 = (f32[1024,256]{1,0:T(8,128)}, bf16[2,8,2,512,128]{4,3,2,1,0:T(8,128)(2,1)}) custom-call(s32[16]{0:T(128)} %copy-done.5, s32[8]{0:T(128)} %copy-done.6, s32[8]{0:T(128)} %copy-done.7, s32[128]{0:T(128)} %copy-done.8, bf16[1024,256]{1,0:T(8,128)(2,1)} %copy-done, bf16[1024,256]{1,0:T(8,128)(2,1)} %get-tuple-element.122.do_ref, ...), custom_call_target="tpu_custom_call" | custom-call | tf_op jit(solution)/shard_map/attend_back/pallas_call | solution.py:749
  805.4 41.6 %reduce_keys.1 = f32[512,128]{1,0:T(8,128)S(1)} custom-call(bf16[2,8,2,512,128]{4,3,2,1,0:T(8,128)(2,1)S(1)} %copy-done.1), custom_call_target="tpu_custom_call" | custom-call | tf_op jit(solution)/shard_map/reduce_keys/pallas_call | solution.py:522
  851.6 3.4 multiply_reduce_fusion.3
  859.8 2.4 convolution_convert_fusion
  862.2 42.1 %reduce_row.3 = f32[128,2048]{1,0:T(8,128)S(1)} custom-call(bf16[8,128,2048]{2,1,0:T(8,128)(2,1)S(1)} %bitcast.293), custom_call_target="tpu_custom_call" | custom-call | tf_op jit(solution)/shard_map/reduce_row/pallas_call | solution.py:384
  904.7 2.6 fusion.7
  909.0 9.9 %all-to-all-start.3 = ((bf16[64,112,128]{2,1,0:T(8,128)(2,1)}), bf16[64,112,128]{2,1,0:T(8,128)(2,1)S(1)}, u32[]{:S(2)}, u32[]{:S(2)}) async-start(bf16[64,112,128]{2,1,0:T(8,128)(2,1)} %pad_maximum_fusion), calls=%async_computation.3 | async-start | bytes 3670016 | tf_op jit(solution)/shard_map/all_to_all | solution.py:1071
  919.0 3.6 convolution_convert_fusion.7
  925.8 20.8 %all-to-all-done.3 = bf16[64,112,128]{2,1,0:T(8,128)(2,1)S(1)} async-done(((bf16[64,112,128]{2,1,0:T(8,128)(2,1)}), bf16[64,112,128]{2,1,0:T(8,128)(2,1)S(1)}, u32[]{:S(2)}, u32[]{:S(2)}) %all-to-all-start.3) | async-done | bytes 1835040 | tf_op jit(solution)/shard_map/all_to_all | solution.py:1071
  946.6 5.5 all-to-all-start.4
  954.8 11.1 %psum.7 = f32[3,128]{1,0:T(4,128)S(1)} all-reduce(f32[3,128]{1,0:T(4,128)S(1)} %select_maximum_fusion.1), channel_id=1, replica_groups=mesh['ctx'=64,'wsh'=2] {'wsh'}, use_global_device_ids=true, to_apply=%region_35.38 | all-reduce | flops 384 | bytes 3072 | tf_op jit(solution)/shard_map/psum | solution.py:1097
  966.9 12.8 %all-to-all-done.4 = bf16[64,112,128]{2,1,0:T(8,128)(2,1)} async-done(((bf16[64,112,128]{2,1,0:T(8,128)(2,1)}), bf16[64,112,128]{2,1,0:T(8,128)(2,1)}, u32[]{:S(2)}, u32[]{:S(2)}) %all-to-all-start.4) | async-done | bytes 1835040 | tf_op jit(solution)/shard_map/all_to_all | solution.py:1032
  (393 shorter events, 85.9 us)
Async XLA Ops:
  3.8 268.7 %all-to-all-start = ((bf16[64,32,384]{2,1,0:T(8,128)(2,1)}), bf16[64,32,384]{2,1,0:T(8,128)(2,1)}, u32[]{:S(2)}, u32[]{:S(2)}) async-start(bf16[64,32,384]{2,1,0:T(8,128)(2,1)} %bitcast.19), calls=%async_computation | async-start | bytes 3145728 | tf_op jit(solution)/shard_map/all_to_all | solution.py:839
  18.7 9.2 copy-start.62
  18.7 9.2 copy-start.63
  18.7 9.3 copy-start.57
  18.7 415.1 %collective-permute-start = (bf16[2048,384]{1,0:T(8,128)(2,1)}, bf16[2048,384]{1,0:T(8,128)(2,1)}, u32[]{:S(2)}, u32[]{:S(2)}) collective-permute-start(bf16[2048,384]{1,0:T(8,128)(2,1)} %fusion.14), channel_id=1, source_target_pairs={{0,1},{1,0},{2,3},{3,2},{4,5},{5,4},{6,7},{7,6},{8,9},{9,8},{10,11... | collective-permute-start | bytes 4718600 | tf_op jit(solution)/shard_map/ppermute | solution.py:813
  22.6 7.0 copy-start.76
  22.6 7.0 copy-start.77
  22.6 414.4 %collective-permute-start.1 = (bf16[2048,384]{1,0:T(8,128)(2,1)}, bf16[2048,384]{1,0:T(8,128)(2,1)}, u32[]{:S(2)}, u32[]{:S(2)}) collective-permute-start(bf16[2048,384]{1,0:T(8,128)(2,1)} %fusion.15), channel_id=1, source_target_pairs={{0,1},{1,0},{2,3},{3,2},{4,5},{5,4},{6,7},{7,6},{8,9},{9,8},{10,11... | collective-permute-start | bytes 4718600 | tf_op jit(solution)/shard_map/ppermute | solution.py:813
  27.2 442.2 %collective-permute-start.2 = (bf16[384,2048]{1,0:T(8,128)(2,1)}, bf16[384,2048]{1,0:T(8,128)(2,1)}, u32[]{:S(2)}, u32[]{:S(2)}) collective-permute-start(bf16[384,2048]{1,0:T(8,128)(2,1)} %fusion.16), channel_id=1, source_target_pairs={{0,1},{1,0},{2,3},{3,2},{4,5},{5,4},{6,7},{7,6},{8,9},{9,8},{10,11... | collective-permute-start | bytes 4718600 | tf_op jit(solution)/shard_map/ppermute | solution.py:813
  27.9 141.3 %copy-start.58 = (bf16[32,256]{1,0:T(8,128)(2,1)}, bf16[32,256]{1,0:T(8,128)(2,1)S(1)}, u32[]{:S(2)}) copy-start(bf16[32,256]{1,0:T(8,128)(2,1)S(1)} %convert_element_type.308) | copy-start | bytes 49156
  28.0 141.3 %copy-start.60 = (bf16[32,256]{1,0:T(8,128)(2,1)}, bf16[32,256]{1,0:T(8,128)(2,1)S(1)}, u32[]{:S(2)}) copy-start(bf16[32,256]{1,0:T(8,128)(2,1)S(1)} %convert_element_type.307) | copy-start | bytes 49156
  174.8 7.7 copy-start.82
  175.7 6.3 slice-start.4
  175.8 92.3 %copy-start.5 = (s32[16]{0:T(128)}, s32[16]{0:T(128)S(1)}, u32[]{:S(2)}) copy-start(s32[16]{0:T(128)S(1)} %select_reduce_fusion.3.order) | copy-start | bytes 196
  181.1 43.7 %copy-start.65 = (pred[16]{0:T(512)(128)(4,1)}, pred[16]{0:T(512)(128)(4,1)S(1)}, u32[]{:S(2)}) copy-start(pred[16]{0:T(512)(128)(4,1)S(1)} %get-tuple-element.68) | copy-start | bytes 52
  182.5 6.8 copy-start.15
  182.6 6.8 copy-start.71
  184.2 57.2 %copy-start.67 = (f32[256]{0:T(256)}, f32[256]{0:T(256)S(1)}, u32[]{:S(2)}) copy-start(f32[256]{0:T(256)S(1)} %broadcast_bitcast_fusion) | copy-start | bytes 3076
  184.2 5.2 copy-start.83
  184.2 5.2 copy-start.18
  191.8 33.1 %copy-start.31 = (f32[1024,64]{1,0:T(8,128)}, f32[1024,64]{1,0:T(8,128)S(1)}, u32[]{:S(2)}) copy-start(f32[1024,64]{1,0:T(8,128)S(1)} %get-tuple-element.106) | copy-start | bytes 786436
  192.6 44.3 %copy-start.27 = (f32[1024,128]{1,0:T(8,128)}, f32[1024,128]{1,0:T(8,128)S(1)}, u32[]{:S(2)}) copy-start(f32[1024,128]{1,0:T(8,128)S(1)} %get-tuple-element.95) | copy-start | bytes 1572868
  225.1 16.7 %copy-start.2 = (s32[8,1,256]{2,1,0:T(1,128)}, s32[8,1,256]{2,1,0:T(1,128)S(1)}, u32[]{:S(2)}) copy-start(s32[8,1,256]{2,1,0:T(1,128)S(1)} %reshape.577.pos_ref) | copy-start | bytes 24580
  225.2 16.6 %copy-start.3 = (s32[8,1,256]{2,1,0:T(1,128)}, s32[8,1,256]{2,1,0:T(1,128)S(1)}, u32[]{:S(2)}) copy-start(s32[8,1,256]{2,1,0:T(1,128)S(1)} %reshape.578.start_ref) | copy-start | bytes 24580
  225.2 6.7 copy-start.64
  234.9 6.9 copy-start.6
  234.9 6.9 copy-start.7
  235.9 5.9 copy-start.8
  236.8 4.6 copy-start.19
  241.4 26.8 %copy-start.23 = (f32[1024,2,128]{2,1,0:T(2,128)}, f32[1024,2,128]{2,1,0:T(2,128)S(1)}, u32[]{:S(2)}) copy-start(f32[1024,2,128]{2,1,0:T(2,128)S(1)} %mul.527) | copy-start | bytes 3145732
  241.8 29.8 %copy-start = (bf16[1024,256]{1,0:T(8,128)(2,1)}, bf16[1024,256]{1,0:T(8,128)(2,1)S(1)}, u32[]{:S(2)}) copy-start(bf16[1024,256]{1,0:T(8,128)(2,1)S(1)} %fusion.30.q_ref) | copy-start | bytes 1572868
  241.8 27.1 %copy-start.51 = (bf16[2,128,2048]{2,1,0:T(8,128)(2,1)S(1)}, bf16[2,128,2048]{2,1,0:T(8,128)(2,1)}, u32[]{:S(2)}) copy-start(bf16[2,128,2048]{2,1,0:T(8,128)(2,1)} %get-tuple-element.38) | copy-start | bytes 3145732
  272.5 169.2 %all-to-all-start.2 = ((bf16[32,24,2048]{2,1,0:T(8,128)(2,1)}), bf16[32,24,2048]{2,1,0:T(8,128)(2,1)}, u32[]{:S(2)}, u32[]{:S(2)}) async-start(bf16[32,24,2048]{2,1,0:T(8,128)(2,1)} %bitcast.305), calls=%async_computation.2 | async-start | bytes 6291456 | tf_op jit(solution)/shard_map/all_to_all | solution.py:860
  360.5 6.0 copy-start.25
  423.3 5.8 copy-start.78
  437.0 4.7 copy-start.86
  448.5 10.6 %copy-start.55 = (bf16[768,384]{1,0:T(8,128)(2,1)}, bf16[768,384]{1,0:T(8,128)(2,1)S(1)}, u32[]{:S(2)}) copy-start(bf16[768,384]{1,0:T(8,128)(2,1)S(1)} %get-tuple-element.76) | copy-start | bytes 1769476
  459.1 6.6 copy-start.79
  476.4 4.6 copy-start.11
  476.4 4.6 copy-start.87
  476.4 4.6 copy-start.88
  487.8 6.4 slice-start
  487.8 6.4 slice-start.2
  570.7 63.0 %collective-permute-start.3 = (bf16[2048,384]{1,0:T(8,128)(2,1)}, bf16[2048,384]{1,0:T(8,128)(2,1)}, u32[]{:S(2)}, u32[]{:S(2)}) collective-permute-start(bf16[2048,384]{1,0:T(8,128)(2,1)} %convolution_convert_fusion.6), channel_id=1, source_target_pairs={{0,1},{1,0},{2,3},{3,2},{4,5},{5,4},{6,7},{7,6},{8,9},{9,8},{10,11... | collective-permute-start | bytes 4718600 | tf_op jit(solution)/shard_map/ppermute | solution.py:813
  571.0 8.4 copy-start.26
  571.0 140.7 %all-to-all-start.1 = ((bf16[32,24,2048]{2,1,0:T(8,128)(2,1)}), bf16[32,24,2048]{2,1,0:T(8,128)(2,1)}, u32[]{:S(2)}, u32[]{:S(2)}) async-start(bf16[32,24,2048]{2,1,0:T(8,128)(2,1)} %bitcast.307), calls=%async_computation.1 | async-start | bytes 6291456 | tf_op jit(solution)/shard_map/all_to_all | solution.py:962
  578.0 97.7 %collective-permute-start.4 = (bf16[2048,384]{1,0:T(8,128)(2,1)}, bf16[2048,384]{1,0:T(8,128)(2,1)}, u32[]{:S(2)}, u32[]{:S(2)}) collective-permute-start(bf16[2048,384]{1,0:T(8,128)(2,1)} %convolution_convert_fusion.5), channel_id=1, source_target_pairs={{0,1},{1,0},{2,3},{3,2},{4,5},{5,4},{6,7},{7,6},{8,9},{9,8},{10,11... | collective-permute-start | bytes 4718600 | tf_op jit(solution)/shard_map/ppermute | solution.py:813
  580.5 5.7 copy-start.13
  588.8 119.3 %collective-permute-start.5 = (bf16[384,2048]{1,0:T(8,128)(2,1)}, bf16[384,2048]{1,0:T(8,128)(2,1)S(1)}, u32[]{:S(2)}, u32[]{:S(2)}) collective-permute-start(bf16[384,2048]{1,0:T(8,128)(2,1)} %convolution_convert_fusion.4), channel_id=1, source_target_pairs={{0,1},{1,0},{2,3},{3,2},{4,5},{5,4},{6,7},{7,6},{8,9},{9,8},{10,11... | collective-permute-start | bytes 4718600 | tf_op jit(solution)/shard_map/ppermute | solution.py:813
  592.9 42.3 %copy-start.40 = (f32[1,2048,384]{2,1,0:T(8,128)S(1)}, f32[1,2048,384]{2,1,0:T(8,128)}, u32[]{:S(2)}) copy-start(f32[1,2048,384]{2,1,0:T(8,128)} %convolution_bitcast_fusion.2) | copy-start | bytes 9437188
  638.4 39.0 %copy-start.41 = (f32[1,2048,384]{2,1,0:T(8,128)S(1)}, f32[1,2048,384]{2,1,0:T(8,128)}, u32[]{:S(2)}) copy-start(f32[1,2048,384]{2,1,0:T(8,128)} %convolution_bitcast_fusion.1) | copy-start | bytes 9437188
  711.7 19.5 %copy-start.14 = (f32[256,2048]{1,0:T(8,128)S(1)}, f32[256,2048]{1,0:T(8,128)}, u32[]{:S(2)}) copy-start(f32[256,2048]{1,0:T(8,128)} %copy-done.12) | copy-start | bytes 6291460
  711.7 19.5 %copy-start.39 = (f32[128,2048]{1,0:T(8,128)S(1)}, f32[128,2048]{1,0:T(8,128)}, u32[]{:S(2)}) copy-start(f32[128,2048]{1,0:T(8,128)} %get-tuple-element.120) | copy-start | bytes 3145732
  711.7 19.5 %copy-start.42 = (bf16[128,2048]{1,0:T(8,128)(2,1)S(1)}, bf16[128,2048]{1,0:T(8,128)(2,1)}, u32[]{:S(2)}) copy-start(bf16[128,2048]{1,0:T(8,128)(2,1)} %c_in.1) | copy-start | bytes 1572868
  805.4 41.6 %copy-start.30 = (f32[1024,64]{1,0:T(8,128)S(1)}, f32[1024,64]{1,0:T(8,128)}, u32[]{:S(2)}) copy-start(f32[1024,64]{1,0:T(8,128)} %copy-done.29) | copy-start | bytes 786436
  805.4 41.9 %copy-start.32 = (f32[1024,64]{1,0:T(8,128)S(1)}, f32[1024,64]{1,0:T(8,128)}, u32[]{:S(2)}) copy-start(f32[1024,64]{1,0:T(8,128)} %copy-done.31) | copy-start | bytes 786436
  805.4 41.9 %copy-start.46 = (f32[1024,128]{1,0:T(8,128)S(1)}, f32[1024,128]{1,0:T(8,128)}, u32[]{:S(2)}) copy-start(f32[1024,128]{1,0:T(8,128)} %get-tuple-element.81) | copy-start | bytes 1572868
  851.6 5.3 copy-start.43
  862.2 42.1 %copy-start.33 = (bf16[128,2048]{1,0:T(8,128)(2,1)S(1)}, bf16[128,2048]{1,0:T(8,128)(2,1)}, u32[]{:S(2)}) copy-start(bf16[128,2048]{1,0:T(8,128)(2,1)} %t_in.1) | copy-start | bytes 1572868
  862.2 42.4 %copy-start.10 = (bf16[8,128,2048]{2,1,0:T(8,128)(2,1)S(1)}, bf16[8,128,2048]{2,1,0:T(8,128)(2,1)}, u32[]{:S(2)}) copy-start(bf16[8,128,2048]{2,1,0:T(8,128)(2,1)} %get-tuple-element.31) | copy-start | bytes 12582916
  862.2 42.4 %copy-start.69 = (f32[1024]{0:T(1024)S(1)}, f32[1024]{0:T(1024)}, u32[]{:S(2)}) copy-start(f32[1024]{0:T(1024)} %get-tuple-element.108) | copy-start | bytes 12292
  909.0 37.6 %all-to-all-start.3 = ((bf16[64,112,128]{2,1,0:T(8,128)(2,1)}), bf16[64,112,128]{2,1,0:T(8,128)(2,1)S(1)}, u32[]{:S(2)}, u32[]{:S(2)}) async-start(bf16[64,112,128]{2,1,0:T(8,128)(2,1)} %pad_maximum_fusion), calls=%async_computation.3 | async-start | bytes 3670016 | tf_op jit(solution)/shard_map/all_to_all | solution.py:1071
  946.6 33.1 %all-to-all-start.4 = ((bf16[64,112,128]{2,1,0:T(8,128)(2,1)}), bf16[64,112,128]{2,1,0:T(8,128)(2,1)}, u32[]{:S(2)}, u32[]{:S(2)}) async-start(bf16[64,112,128]{2,1,0:T(8,128)(2,1)} %fusion.10), calls=%async_computation.4 | async-start | bytes 3670016 | tf_op jit(solution)/shard_map/all_to_all | solution.py:1032
  952.9 28.4 %copy-start.53 = (f32[32,2048]{1,0:T(8,128)}, f32[32,2048]{1,0:T(8,128)S(1)}, u32[]{:S(2)}) copy-start(f32[32,2048]{1,0:T(8,128)S(1)} %reshape.608) | copy-start | bytes 786436
  (41 other events, 103.2 us)

commit v2 on v1

--- a/solution.py
+++ b/solution.py
@@ -127,11 +127,11 @@
     return barrier, len(targets)
 
 
-def greet_many(count, target, wsh):
+def greet_many(count, target):
     barrier = pltpu.get_barrier_semaphore()
 
     def one(step, carried):
-        pl.semaphore_signal(barrier, inc=1, device_id=(target(step), wsh), device_id_type=MESH)
+        pl.semaphore_signal(barrier, inc=1, device_id=target(step), device_id_type=MESH)
         return carried
 
     lax.fori_loop(1, count, one, 0)
@@ -143,6 +143,10 @@
 DMA = pltpu.SemaphoreType.DMA
 
 
+def cost(microseconds):
+    return pl.CostEstimate(flops=0, bytes_accessed=int(microseconds * 3.6e6), transcendentals=0)
+
+
 def call_params(collective_id, limit=None):
     return pltpu.CompilerParams(
         collective_id=collective_id, has_side_effects=True, vmem_limit_bytes=limit
@@ -152,7 +156,7 @@
 def row_gather_start(src, out, me, wsh, send, recv):
     place = lax.rem(me, 8)
     copies = []
-    for at, (dx, dk) in enumerate(((1, 0), (3, 0), (2, 0), (0, 1))):
+    for at, (dx, dk) in enumerate(((1, 0), (3, 0), (0, 1))):
         copy = remote(
             src, out.at[place], send.at[at], recv.at[at], shifted(me, 0, 0, dx, dk), wsh
         )
@@ -163,23 +167,30 @@
 
 def row_gather_finish(out, me, wsh, copies, send, recv):
     partner = shifted(me, 0, 0, 0, 1)
+    half = out.shape[1] // 2
+    onward = []
     forwards = []
-    for at, dx in enumerate((1, 3, 2)):
+    for at, dx in enumerate((1, 3)):
         copies[at].wait_recv()
         from_place = lax.rem(shifted(me, 0, 0, 4 - dx, 0), 8)
-        forward = remote(
-            out.at[from_place],
-            out.at[from_place],
-            send.at[4 + at],
-            recv.at[4 + at],
-            partner,
-            wsh,
-        )
+        part = out.at[from_place, pl.ds(at * half, half)]
+        step = remote(part, part, send.at[3 + at], recv.at[3 + at], shifted(me, 0, 0, dx, 0), wsh)
+        step.start()
+        onward.append(step)
+        block = out.at[from_place]
+        forward = remote(block, block, send.at[5 + at], recv.at[5 + at], partner, wsh)
         forward.start()
         forwards.append(forward)
-    for copy in copies:
+    far = lax.rem(shifted(me, 0, 0, 2, 0), 8)
+    for at in (0, 1):
+        onward[at].wait_recv()
+        part = out.at[far, pl.ds(at * half, half)]
+        forward = remote(part, part, send.at[7 + at], recv.at[7 + at], partner, wsh)
+        forward.start()
+        forwards.append(forward)
+    copies[2].wait_recv()
+    for copy in copies + onward:
         copy.wait_send()
-    copies[3].wait_recv()
     for forward in forwards:
         forward.wait()
 
@@ -195,7 +206,7 @@
                 me, lax.div(step, 16), lax.rem(lax.div(step, 8), 2), lax.rem(lax.div(step, 2), 4), lax.rem(step, 2)
             )
 
-        barrier, amount = greet_many(64, target, wsh)
+        barrier, amount = greet_many(64, lambda step: (target(step), wsh))
         locals_ = [
             pltpu.make_async_copy(t_in, t_out.at[place], local.at[0]),
             pltpu.make_async_copy(w_in.at[place], w_out.at[me], local.at[1]),
@@ -246,16 +257,17 @@
         ),
         in_specs=[ANY] * 5,
         out_specs=[ANY] * 5,
-        scratch_shapes=[DMA((4,)), DMA((7,)), DMA((7,)), DMA((4,)), DMA((5,))],
+        scratch_shapes=[DMA((4,)), DMA((9,)), DMA((9,)), DMA((4,)), DMA((5,))],
         compiler_params=call_params(0),
         name="gather_first",
+        cost_estimate=cost(60),
     )(weights, tokens, small, routes, cotangent)
 
 
 def gather_row(block, collective_id):
     def body(src, out, row_s, row_r, local):
         me, wsh = lax.axis_index("ctx"), lax.axis_index("wsh")
-        barrier, amount = greet([(shifted(me, 0, 0, dx, dk), wsh) for dx, dk in ((1, 0), (3, 0), (2, 0), (0, 1))])
+        barrier, amount = greet([(shifted(me, 0, 0, dx, dk), wsh) for dx, dk in ((1, 0), (3, 0), (0, 1))])
         mine = pltpu.make_async_copy(src, out.at[lax.rem(me, 8)], local)
         mine.start()
         pl.semaphore_wait(barrier, amount)
@@ -268,9 +280,10 @@
         out_shape=jax.ShapeDtypeStruct((8,) + block.shape, block.dtype),
         in_specs=[ANY],
         out_specs=ANY,
-        scratch_shapes=[DMA((7,)), DMA((7,)), DMA],
+        scratch_shapes=[DMA((9,)), DMA((9,)), DMA],
         compiler_params=call_params(collective_id),
         name="gather_row",
+        cost_estimate=cost(26),
     )(block)
 
 
@@ -319,14 +332,24 @@
         scratch_shapes=[DMA((14,)), DMA((14,)), DMA],
         compiler_params=call_params(collective_id),
         name="gather_keys",
+        cost_estimate=cost(30),
     )(rows)
 
 
-def reduce_row(parts, collective_id, both):
+def reduce_row(parts, collective_id, both, extra=None):
     _, rows, width = parts.shape
     block = (rows, width)
-
-    def body(src, out, arrived, summed, landed, swapped, total, send, recv, local):
+    pieces = 2
+    columns = width // pieces
+    has_extra = extra is not None
+
+    def body(*refs):
+        refs = list(refs)
+        src = refs.pop(0)
+        src2 = refs.pop(0) if has_extra else None
+        out = refs.pop(0)
+        out2 = refs.pop(0) if has_extra else None
+        arrived, summed, landed, swapped, total, send, recv, local = refs[:8]
         me, wsh = lax.axis_index("ctx"), lax.axis_index("wsh")
         other = 1 - wsh
         core = lax.rem(me, 2)
@@ -335,70 +358,116 @@
         peers = [shifted(me, 0, 0, dx, 0) for dx in (1, 2, 3)]
         barrier, amount = greet([(peer, wsh) for peer in peers + [partner]] + [(me, other)])
         pl.semaphore_wait(barrier, amount)
+        spans = [pl.ds(piece * columns, columns) for piece in range(pieces)]
+        everything = pl.ds(0, rows)
         first = []
-        for at, dx in enumerate((2, 1, 3, 0)):
-            chip = lax.rem(x + dx, 4)
-            copy = remote(
-                src.at[chip * 2 + 1 - core], arrived.at[at], send.at[at], recv.at[at], partner, wsh
+        for piece, span in enumerate(spans):
+            for at, dx in enumerate((2, 1, 3, 0)):
+                chip = lax.rem(x + dx, 4)
+                copy = remote(
+                    src.at[chip * 2 + 1 - core, everything, span],
+                    arrived.at[at, everything, span],
+                    send.at[piece, at],
+                    recv.at[piece, at],
+                    partner,
+                    wsh,
+                )
+                copy.start()
+                first.append(copy)
+        if has_extra:
+            arrived2, swapped2 = refs[8:]
+            give2 = remote(src2.at[1 - core], arrived2, send.at[0, 8], recv.at[0, 8], partner, wsh)
+            give2.start()
+        second = []
+        for piece, span in enumerate(spans):
+            for at, dx in enumerate((2, 1, 3)):
+                chip = lax.rem(x + dx, 4)
+                first[piece * 4 + at].wait_recv()
+                summed[at, :, span] = (
+                    src[chip * 2 + core, :, span].astype(F32) + arrived[at, :, span].astype(F32)
+                ).astype(BF)
+                copy = remote(
+                    summed.at[at, everything, span],
+                    landed.at[at, everything, span],
+                    send.at[piece, 4 + at],
+                    recv.at[piece, 4 + at],
+                    shifted(me, 0, 0, dx, 0),
+                    wsh,
+                )
+                copy.start()
+                second.append(copy)
+            first[piece * 4 + 3].wait_recv()
+            total[:, span] = src[x * 2 + core, :, span].astype(F32) + arrived[3, :, span].astype(F32)
+        if has_extra:
+            give2.wait()
+            swapped2[0] = (src2[core].astype(F32) + arrived2[...].astype(F32)).astype(BF)
+            swap2 = remote(swapped2.at[0], swapped2.at[1], send.at[1, 8], recv.at[1, 8], me, other)
+            swap2.start()
+        swaps = []
+        for piece, span in enumerate(spans):
+            for at in (1, 2, 0):
+                second[piece * 3 + at].wait_recv()
+            swapped[0, :, span] = (
+                total[:, span]
+                + landed[0, :, span].astype(F32)
+                + landed[1, :, span].astype(F32)
+                + landed[2, :, span].astype(F32)
+            ).astype(BF)
+            swap = remote(
+                swapped.at[0, everything, span],
+                swapped.at[1, everything, span],
+                send.at[piece, 7],
+                recv.at[piece, 7],
+                me,
+                other,
             )
-            copy.start()
-            first.append(copy)
-        second = []
-        for at, dx in enumerate((2, 1, 3)):
-            chip = lax.rem(x + dx, 4)
-            first[at].wait_recv()
-            summed[at] = (src[chip * 2 + core].astype(F32) + arrived[at].astype(F32)).astype(BF)
-            copy = remote(
-                summed.at[at],
-                landed.at[at],
-                send.at[4 + at],
-                recv.at[4 + at],
-                shifted(me, 0, 0, dx, 0),
-                wsh,
-            )
-            copy.start()
-            second.append(copy)
-        first[3].wait_recv()
-        total[...] = src[x * 2 + core].astype(F32) + arrived[3].astype(F32)
-        for at in (1, 2, 0):
-            second[at].wait_recv()
-        swapped[0] = (
-            total[...] + landed[0].astype(F32) + landed[1].astype(F32) + landed[2].astype(F32)
-        ).astype(BF)
-        swap = remote(swapped.at[0], swapped.at[1], send.at[7], recv.at[7], me, other)
-        swap.start()
-        swap.wait()
-        total[...] = swapped[0].astype(F32) + swapped[1].astype(F32)
+            swap.start()
+            swaps.append(swap)
+        if has_extra:
+            swap2.wait()
+            out2[...] = swapped2[0].astype(F32) + swapped2[1].astype(F32)
+        for piece, span in enumerate(spans):
+            swaps[piece].wait()
+            if both:
+                total[:, span] = swapped[0, :, span].astype(F32) + swapped[1, :, span].astype(F32)
+            else:
+                out[:, span] = swapped[0, :, span].astype(F32) + swapped[1, :, span].astype(F32)
         if both:
             keep = pltpu.make_async_copy(total, out.at[core], local)
             keep.start()
-            give = remote(total, out.at[core], send.at[8], recv.at[8], partner, wsh)
+            give = remote(total, out.at[core], send.at[0, 9], recv.at[0, 9], partner, wsh)
             give.start()
             give.wait()
             keep.wait()
-        else:
-            out[...] = total[...]
         for copy in first + second:
             copy.wait_send()
 
+    shapes = [jax.ShapeDtypeStruct((2,) + block if both else block, F32)]
+    scratch = [
+        pltpu.VMEM((4,) + block, BF),
+        pltpu.VMEM((3,) + block, BF),
+        pltpu.VMEM((3,) + block, BF),
+        pltpu.VMEM((2,) + block, BF),
+        pltpu.VMEM(block, F32),
+        DMA((pieces, 10)),
+        DMA((pieces, 10)),
+        DMA,
+    ]
+    operands = [parts]
+    if has_extra:
+        shapes.append(jax.ShapeDtypeStruct(block, F32))
+        scratch += [pltpu.VMEM(block, BF), pltpu.VMEM((2,) + block, BF)]
+        operands.append(extra)
     return pl.pallas_call(
         body,
-        out_shape=jax.ShapeDtypeStruct((2,) + block if both else block, F32),
-        in_specs=[VMEM],
-        out_specs=VMEM,
-        scratch_shapes=[
-            pltpu.VMEM((4,) + block, BF),
-            pltpu.VMEM((3,) + block, BF),
-            pltpu.VMEM((3,) + block, BF),
-            pltpu.VMEM((2,) + block, BF),
-            pltpu.VMEM(block, F32),
-            DMA((9,)),
-            DMA((9,)),
-            DMA,
-        ],
+        out_shape=shapes,
+        in_specs=[VMEM] * len(operands),
+        out_specs=[VMEM] * len(operands),
+        scratch_shapes=scratch,
         compiler_params=call_params(collective_id, 40 * 1024 * 1024),
         name="reduce_row",
-    )(parts)
+        cost_estimate=cost(40),
+    )(*operands)
 
 
 def reduce_chip(parts, extra, collective_id):
@@ -453,69 +522,67 @@
         scratch_shapes=scratch,
         compiler_params=call_params(collective_id, 40 * 1024 * 1024),
         name="reduce_chip",
+        cost_estimate=cost(17),
     )(*operands)
 
 
 def reduce_keys(parts, collective_id):
     _, groups, _, rows, width = parts.shape
 
-    def body(src, out, arrived, summed, landed, send, recv, fsend, frecv):
+    def body(src, out, arrived, mid, beside, summed, landed, send, recv):
         me, wsh = lax.axis_index("ctx"), lax.axis_index("wsh")
         core = lax.rem(me, 2)
-        z, y, x, _ = coords(me)
-        pair = lax.div(x, 2) * 2
+        _, _, x, _ = coords(me)
         side = lax.rem(x, 2)
         partner = shifted(me, 0, 0, 0, 1)
-
-        def target(step):
-            dz, dy, db = lax.div(step, 4), lax.rem(lax.div(step, 2), 2), lax.rem(step, 2)
-            return (
-                lax.rem(z + dz, 4) * 2 + lax.rem(y + dy, 2),
-                lax.rem(side + db, 2),
-            )
-
-        barrier = pltpu.get_barrier_semaphore()
-        pl.semaphore_signal(barrier, inc=1, device_id=(partner, wsh), device_id_type=MESH)
-        for step in range(1, 16):
-            group, b = target(step)
-            pl.semaphore_signal(
-                barrier, inc=1, device_id=((group * 4 + pair + b) * 2 + core, wsh), device_id_type=MESH
-            )
-        pl.semaphore_wait(barrier, 16)
-        order = (1, 4, 2, 8, 12, 3, 5, 6, 9, 13, 10, 14, 7, 11, 15, 0)
+        neighbour = me + 2 - 4 * side
+        steps = COLUMN_STEPS + ((0, 0),)
+        peers = [shifted(me, dz, dy, 0, 0) for dz, dy in steps]
+        barrier, amount = greet([(peer, wsh) for peer in peers[:-1] + [partner, neighbour]])
+        pl.semaphore_wait(barrier, amount)
         first = []
-        for at, step in enumerate(order):
-            group, b = target(step)
-            copy = remote(
-                src.at[1 - core, group, b], arrived.at[step], fsend.at[at], frecv.at[at], partner, wsh
-            )
-            copy.start()
-            first.append(copy)
-        second = []
-        for at, step in enumerate(order):
-            group, b = target(step)
-            first[at].wait_recv()
-            value = src[core, group, b].astype(F32) + arrived[step].astype(F32)
-            if step == 0:
-                out[...] = value
-            else:
-                summed[step] = value.astype(BF)
+        for at, peer in enumerate(peers):
+            group = lax.div(peer, 8)
+            for turn, b in enumerate((1 - side, side)):
                 copy = remote(
-                    summed.at[step],
-                    landed.at[step],
-                    send.at[at],
-                    recv.at[at],
-                    (group * 4 + pair + b) * 2 + core,
+                    src.at[1 - core, group, b],
+                    arrived.at[turn, at],
+                    send.at[turn, at],
+                    recv.at[turn, at],
+                    partner,
                     wsh,
                 )
                 copy.start()
-                second.append((step, copy))
-        for step, copy in second:
+                first.append(copy)
+        across = []
+        for at, peer in enumerate(peers):
+            group = lax.div(peer, 8)
+            first[2 * at].wait_recv()
+            mid[at] = (src[core, group, 1 - side].astype(F32) + arrived[0, at].astype(F32)).astype(BF)
+            copy = remote(mid.at[at], beside.at[at], send.at[2, at], recv.at[2, at], neighbour, wsh)
+            copy.start()
+            across.append(copy)
+        last = []
+        for at, peer in enumerate(peers):
+            group = lax.div(peer, 8)
+            first[2 * at + 1].wait_recv()
+            across[at].wait_recv()
+            value = (
+                src[core, group, side].astype(F32)
+                + arrived[1, at].astype(F32)
+                + beside[at].astype(F32)
+            )
+            if at == groups - 1:
+                out[...] = value
+            else:
+                summed[at] = value.astype(BF)
+                copy = remote(summed.at[at], landed.at[at], send.at[3, at], recv.at[3, at], peer, wsh)
+                copy.start()
+                last.append(copy)
+        for at, copy in enumerate(last):
             copy.wait_recv()
-            out[...] += landed[step].astype(F32)
-        for copy in first:
-            copy.wait_send()
-        for _, copy in second:
+            out[...] += landed[at].astype(F32)
+        for copy in first + across + last:
             copy.wait_send()
 
     block = (rows, width)
@@ -525,20 +592,21 @@
         in_specs=[VMEM],
         out_specs=VMEM,
         scratch_shapes=[
-            pltpu.VMEM((16,) + block, BF),
-            pltpu.VMEM((16,) + block, BF),
-            pltpu.VMEM((16,) + block, BF),
-            DMA((16,)),
-            DMA((16,)),
-            DMA((16,)),
-            DMA((16,)),
+            pltpu.VMEM((2, groups) + block, BF),
+            pltpu.VMEM((groups,) + block, BF),
+            pltpu.VMEM((groups,) + block, BF),
+            pltpu.VMEM((groups,) + block, BF),
+            pltpu.VMEM((groups,) + block, BF),
+            DMA((4, groups)),
+            DMA((4, groups)),
         ],
         compiler_params=call_params(collective_id, 40 * 1024 * 1024),
         name="reduce_keys",
+        cost_estimate=cost(40),
     )(parts)
 
 
-def exchange_same_core(arrays, collective_id):
+def exchange(arrays, collective_id):
     amount = len(arrays)
 
     def body(*refs):
@@ -548,9 +616,10 @@
         chip = lax.div(me, 2)
 
         def target(step):
-            return shifted(me, lax.div(step, 8), lax.rem(lax.div(step, 4), 2), lax.rem(step, 4), 0)
-
-        barrier, count = greet_many(32, target, wsh)
+            dy = lax.rem(lax.div(step, 4), 2)
+            return shifted(me, lax.div(step, 8), dy, lax.rem(step, 4), 0), lax.rem(wsh + dy, 2)
+
+        barrier, count = greet_many(32, target)
         locals_ = []
         for at in range(amount):
             copy = pltpu.make_async_copy(ins[at].at[chip], outs[at].at[chip], local.at[at])
@@ -559,10 +628,10 @@
         pl.semaphore_wait(barrier, count)
 
         def one(step, carried):
-            ctx = target(lax.rem(step * 13, 32))
+            ctx, side = target(lax.rem(step * 13, 32))
             for at in range(amount):
                 remote(
-                    ins[at].at[lax.div(ctx, 2)], outs[at].at[chip], send.at[at], recv.at[at], ctx, wsh
+                    ins[at].at[lax.div(ctx, 2)], outs[at].at[chip], send.at[at], recv.at[at], ctx, side
                 ).start()
             return carried
 
@@ -582,12 +651,21 @@
         out_specs=[ANY] * amount,
         scratch_shapes=[DMA((amount,)), DMA((amount,)), DMA((amount,))],
         compiler_params=call_params(collective_id),
-        name="exchange_same_core",
+        name="exchange",
+        cost_estimate=cost(48),
     )(*arrays)
 
 
-def same_core_groups():
-    return [[2 * i + core for i in range(32)] for core in range(2)]
+def exchange_behind(value):
+    groups = []
+    for core in range(2):
+        for parity in range(2):
+            groups.append(
+                [(chip * 2 + core) * 2 + (parity + chip // 4) % 2 for chip in range(32)]
+            )
+    return lax.all_to_all(
+        value, ("ctx", "wsh"), split_axis=0, concat_axis=0, tiled=True, axis_index_groups=groups
+    )
 
 
 def natural_order(inverse, kv_ref, keys, values, transposed):
@@ -624,7 +702,22 @@
         )
 
 
-def forward_kernel(order, low, high, inverse, q_ref, kv_ref, pos_ref, start_ref, out_ref, lse_ref, keys, values, values_t, acc):
+def three_loops(step, low, inner_low, inner_high, high, chunk, state):
+    state = lax.fori_loop(low[step], inner_low[step], functools.partial(chunk, True), state)
+    state = lax.fori_loop(inner_low[step], inner_high[step], functools.partial(chunk, False), state)
+    return lax.fori_loop(inner_high[step], high[step], functools.partial(chunk, True), state)
+
+
+def kept(scores, at, q_pos, q_start):
+    k_pos = at + lax.broadcasted_iota(jnp.int32, scores.shape, 0)
+    return jnp.where((k_pos <= q_pos) & (k_pos >= q_start), scores, MASKED)
+
+
+SCORE_SCALE = 1.0 / math.sqrt(HEAD_WIDTH)
+TWO_SCALE = SCORE_SCALE / math.log(2.0)
+
+
+def forward_kernel(order, low, inner_low, inner_high, high, inverse, q_ref, kv_ref, pos_ref, start_ref, out_ref, lse_ref, keys, values, values_t, acc):
     step = pl.program_id(0)
 
     @pl.when(step == 0)
@@ -634,33 +727,35 @@
     first, second = order[2 * step], order[2 * step + 1]
     q_t = stacked(q_ref, first, second).astype(F32).T.astype(BF)
     q_pos, q_start = pos_ref[0], start_ref[0]
-    scale = 1.0 / math.sqrt(HEAD_WIDTH)
     width = 4 * BLK
     acc[...] = jnp.zeros_like(acc)
 
-    def chunk(index, carried):
+    def chunk(masked, index, carried):
         highest, total = carried
         at = pl.multiple_of(index * CHUNK, CHUNK)
-        scores = matmul(keys[pl.ds(at, CHUNK), :], q_t) * scale
-        k_pos = at + lax.broadcasted_iota(jnp.int32, (CHUNK, width), 0)
-        scores = jnp.where((k_pos <= q_pos) & (k_pos >= q_start), scores, MASKED)
+        scores = matmul(keys[pl.ds(at, CHUNK), :], q_t)
+        if masked:
+            scores = kept(scores, at, q_pos, q_start)
         top = jnp.maximum(highest, jnp.max(scores, axis=0, keepdims=True))
-        probs = jnp.exp(scores - top)
-        fade = jnp.exp(highest - top)
+        probs = jnp.exp2((scores - top) * TWO_SCALE)
+        fade = jnp.exp2((highest - top) * TWO_SCALE)
         acc[...] = acc[...] * fade + matmul(values_t[:, pl.ds(at, CHUNK)], probs.astype(BF))
         return top, total * fade + jnp.sum(probs, axis=0, keepdims=True)
 
-    highest, total = lax.fori_loop(
-        low[step],
-        high[step],
+    highest, total = three_loops(
+        step,
+        low,
+        inner_low,
+        inner_high,
+        high,
         chunk,
         (jnp.full((1, width), MASKED, F32), jnp.zeros((1, width), F32)),
     )
-    lse_ref[0] = highest + jnp.log(total)
+    lse_ref[0] = highest * TWO_SCALE + jnp.log2(total)
     unstacked(out_ref, first, second, (acc[...] / total).T.astype(BF))
 
 
-def attend(order, low, high, inverse, queries, kv, positions, starts):
+def attend(plan, queries, kv, positions, starts):
     rows = queries.shape[0]
     steps = rows // (2 * BLK)
     everything = pl.BlockSpec(queries.shape, lambda i, *_: (0, 0))
@@ -670,7 +765,7 @@
         forward_kernel,
         out_shape=(sds(queries.shape, BF), sds((steps, 1, 4 * BLK), F32)),
         grid_spec=pltpu.PrefetchScalarGridSpec(
-            num_scalar_prefetch=4,
+            num_scalar_prefetch=6,
             grid=(steps,),
             in_specs=[everything, pl.BlockSpec(kv.shape, lambda i, *_: (0, 0)), strip, strip],
             out_specs=[everything, strip],
@@ -683,10 +778,11 @@
         ),
         compiler_params=pltpu.CompilerParams(vmem_limit_bytes=50 * 1024 * 1024),
         name="attend",
-    )(order, low, high, inverse, queries, kv, positions, starts)
-
-
-def backward_kernel(order, low, high, inverse, q_ref, do_ref, kv_ref, pos_ref, start_ref, lse_ref, dot_ref, dq_ref, dkv_ref, keys, values, keys_t, d_keys, d_values, acc):
+        cost_estimate=cost(17),
+    )(*plan, queries, kv, positions, starts)
+
+
+def backward_kernel(order, low, inner_low, inner_high, high, inverse, q_ref, do_ref, kv_ref, pos_ref, start_ref, lse_ref, dot_ref, dq_ref, dkv_ref, keys, values, keys_t, d_keys, d_values, acc):
     step = pl.program_id(0)
 
     @pl.when(step == 0)
@@ -702,17 +798,15 @@
     d_out_t = d_out.astype(F32).T.astype(BF)
     q_pos, q_start = pos_ref[0], start_ref[0]
     lse, dots = lse_ref[0], dot_ref[0]
-    scale = 1.0 / math.sqrt(HEAD_WIDTH)
-    width = 4 * BLK
     acc[...] = jnp.zeros_like(acc)
 
-    def chunk(index, carried):
+    def chunk(masked, index, carried):
         at = pl.multiple_of(index * CHUNK, CHUNK)
         here = pl.ds(at, CHUNK)
-        scores = matmul(keys[here, :], q_t) * scale
-        k_pos = at + lax.broadcasted_iota(jnp.int32, (CHUNK, width), 0)
-        scores = jnp.where((k_pos <= q_pos) & (k_pos >= q_start), scores, MASKED)
-        probs = jnp.exp(scores - lse)
+        scores = matmul(keys[here, :], q_t)
+        if masked:
+            scores = kept(scores, at, q_pos, q_start)
+        probs = jnp.exp2(scores * TWO_SCALE - lse)
         d_probs = matmul(values[here, :], d_out_t)
         d_scores = (probs * (d_probs - dots)).astype(BF)
         d_values[here, :] += matmul(probs.astype(BF), d_out)
@@ -720,8 +814,8 @@
         acc[...] += matmul(keys_t[:, here], d_scores)
         return carried
 
-    lax.fori_loop(low[step], high[step], chunk, 0)
-    unstacked(dq_ref, first, second, (acc[...] * scale).T)
+    three_loops(step, low, inner_low, inner_high, high, chunk, 0)
+    unstacked(dq_ref, first, second, (acc[...] * SCORE_SCALE).T)
 
     @pl.when(step == pl.num_programs(0) - 1)
     def _():
@@ -731,14 +825,14 @@
             half, rest = inside // 8, inside % 8
             at = pl.ds(pl.multiple_of(block * BLK, BLK), BLK)
             to = pl.ds(pl.multiple_of(rest * BLK, BLK), BLK)
-            dkv_ref[half, group, 0, to, :] = (d_keys[at, :] * scale).astype(BF)
+            dkv_ref[half, group, 0, to, :] = (d_keys[at, :] * SCORE_SCALE).astype(BF)
             dkv_ref[half, group, 1, to, :] = d_values[at, :].astype(BF)
             return carried
 
         lax.fori_loop(0, kv_ref.shape[0] // BLK, one, 0)
 
 
-def attend_back(order, low, high, inverse, queries, d_heads, kv, positions, starts, lse, dots):
+def attend_back(plan, queries, d_heads, kv, positions, starts, lse, dots):
     rows = queries.shape[0]
     total = kv.shape[0]
     steps = rows // (2 * BLK)
@@ -750,7 +844,7 @@
         backward_kernel,
         out_shape=(sds(queries.shape, F32), sds(dkv_shape, BF)),
         grid_spec=pltpu.PrefetchScalarGridSpec(
-            num_scalar_prefetch=4,
+            num_scalar_prefetch=6,
             grid=(steps,),
             in_specs=[everything, everything, pl.BlockSpec(kv.shape, lambda i, *_: (0, 0)), strip, strip, strip, strip],
             out_specs=[everything, pl.BlockSpec(dkv_shape, lambda i, *_: (0, 0, 0, 0, 0))],
@@ -765,7 +859,12 @@
         ),
         compiler_params=pltpu.CompilerParams(vmem_limit_bytes=55 * 1024 * 1024),
         name="attend_back",
-    )(order, low, high, inverse, queries, d_heads, kv, positions, starts, lse, dots)
+        cost_estimate=cost(24),
+    )(*plan, queries, d_heads, kv, positions, starts, lse, dots)
+
+
+def after(value, earlier):
+    return lax.optimization_barrier((value, earlier))
 
 
 def lanes_to(row, lanes=128):
@@ -812,10 +911,6 @@
     def swap(value):
         return lax.ppermute(value, "wsh", [(0, 1), (1, 0)])
 
-    gate_w = (of_mine(w_gate), swap(of_other(w_gate)))
-    up_w = (of_mine(w_up), swap(of_other(w_up)))
-    down_w = (of_mine(w_down), swap(of_other(w_down)))
-
     depth = w_query.shape[0]
     q_part = to_low(w_query).reshape(depth, 8, 256).transpose(1, 0, 2)
     k_part = jnp.repeat(to_low(key_weight).reshape(depth, 2, 128).transpose(1, 0, 2), 4, axis=0)
@@ -827,6 +922,8 @@
     w_all, row_rows, small_all, chip_routes, chip_cot = gather_first(
         w_pack, tokens, small, routes.T, cotangent
     )
+    other_gate, small_all = after(of_other(w_gate), small_all)
+    gate_back = swap(other_gate)
     w_qkv = w_all.reshape(width, 512)
     g_attn = to_low(small_all[:, 0, :depth].reshape(width)).astype(F32)
     g_ffn = to_low(small_all[:, 1, :depth].reshape(width)).astype(F32)
@@ -836,9 +933,8 @@
     o_part = to_low(w_out).T.reshape(depth, 8, 256).transpose(1, 0, 2)
     r_part = jnp.broadcast_to(to_low(w_router)[None], (8, depth, experts))
     late_pack = jnp.tile(jnp.concatenate([o_part, r_part], axis=2), (8, 1, 1))
+    late_pack, small_all = after(late_pack, small_all)
     late_all = lax.all_to_all(late_pack, "ctx", split_axis=0, concat_axis=0, tiled=True).reshape(width, 384)
-    wo_t = late_all[:, :256]
-    wr = late_all[:, 256:]
 
     route_rows = chip_routes.transpose(0, 2, 1)
     hits = jnp.any(
@@ -848,24 +944,20 @@
     ranks = jnp.einsum("ts,hse->hte", before, hits.astype(BF), preferred_element_type=F32).astype(jnp.int32)
     ranks = jnp.where(hits, ranks + jnp.array([0, CAP], jnp.int32)[:, None, None], -1)
     hits = hits.reshape(2 * rows, experts)
-    quarter = core * 2 + wsh
-    my_ranks = lax.dynamic_index_in_dim(
-        ranks.reshape(2 * rows, experts).T.reshape(experts // 4, 4, 2 * rows), quarter, 1, keepdims=False
-    )
     chips = experts // 4
+    chip_ids = jnp.arange(chips, dtype=jnp.int32)
+    quarter = core * 2 + (wsh + chip_ids // 4 + lax.div(me, 8)) % 2
+
+    def my_quarter(value):
+        by_chip = value.reshape(2 * rows, experts).T.reshape(chips, 4, 2 * rows)
+        two = lax.dynamic_slice_in_dim(by_chip, core * 2, 2, 1)
+        return jnp.where((quarter % 2 == 0)[:, None], two[:, 0], two[:, 1])
+
+    my_ranks = my_quarter(ranks)
     slots = 2 * CAP
     pick = my_ranks[:, None, :] == jnp.arange(slots, dtype=jnp.int32)[None, :, None]
     pick_low = pick.astype(BF).reshape(chips * slots, 2 * rows)
     cot_rows = matmul(pick_low, chip_cot.reshape(2 * rows, width)).astype(BF)
-    cot_there = lax.all_to_all(
-        cot_rows.reshape(chips, slots, width),
-        "ctx",
-        split_axis=0,
-        concat_axis=0,
-        tiled=True,
-        axis_index_groups=same_core_groups(),
-    ).reshape(chips * slots, width)
-
     my_blocks = lax.dynamic_slice_in_dim(block_order, group * row_blocks, row_blocks, 0)
     positions = (my_blocks[:, None] * BLK + jnp.arange(BLK, dtype=jnp.int32)[None, :]).reshape(row_tokens)
     starts = seq_starts(positions, seq_lengths)
@@ -884,9 +976,14 @@
         ),
         axis=1,
     )
-    first_start = starts.reshape(row_blocks, BLK)[:, 0]
-    low = jnp.min(jnp.take(first_start, order).reshape(-1, 2), axis=1) // CHUNK
-    high = jnp.max(jnp.take(my_blocks, order).reshape(-1, 2), axis=1) * BLK // CHUNK + 1
+    block_starts = starts.reshape(row_blocks, BLK)
+    pair_blocks = jnp.take(my_blocks, order).reshape(-1, 2)
+    low = jnp.min(jnp.take(block_starts[:, 0], order).reshape(-1, 2), axis=1) // CHUNK
+    high = jnp.max(pair_blocks, axis=1) * BLK // CHUNK + 1
+    last_start = jnp.max(jnp.take(block_starts[:, BLK - 1], order).reshape(-1, 2), axis=1)
+    inner_low = jnp.clip((last_start + CHUNK - 1) // CHUNK, low, high)
+    inner_high = jnp.clip((jnp.min(pair_blocks, axis=1) * BLK + 1) // CHUNK, inner_low, high)
+    plan = (order, low, inner_low, inner_high, high, inverse_order)
 
     def strips(per_token):
         by_block = jnp.take(per_token.reshape(row_blocks, BLK), order, axis=0).reshape(-1, 2, 1, BLK)
@@ -906,11 +1003,19 @@
     queries = queries.reshape(row_tokens, 256)
     keys = to_low(rotate(k_pre * k_inverse * g_key, cosine, sine_tab))
     kv = jnp.concatenate([keys, to_low(qkv[:, 384:])], axis=1)
+    (gate_back, late_all), kv = after((gate_back, late_all), kv)
+    wo_t = late_all[:, :256]
+    wr = late_all[:, 256:]
     kv_all = gather_keys(kv, 1).reshape(block_count * BLK, 256)
-    heads, lse = attend(order, low, high, inverse_order, queries, kv_all, q_pos, q_start)
+    (cot_rows, other_up), kv_all = after((cot_rows, of_other(w_up)), kv_all)
+    up_back = swap(other_up)
+    cot_there = exchange_behind(cot_rows.reshape(chips, slots, width)).reshape(chips * slots, width)
+    heads, lse = attend(plan, queries, kv_all, q_pos, q_start)
 
     attn_parts = to_low(times_transposed(heads, wo_t)).reshape(8, rows, width)
-    attn_total = reduce_row(attn_parts, 2, True).reshape(2 * rows, width)
+    (up_back, cot_there, other_down), attn_parts = after((up_back, cot_there, of_other(w_down)), attn_parts)
+    down_back = swap(other_down)
+    attn_total = reduce_row(attn_parts, 2, True)[0].reshape(2 * rows, width)
     chip_stream = lax.dynamic_slice_in_dim(stream, (place - core) * rows, 2 * rows, 0)
     chip_residual = chip_stream + attn_total
     chip_inverse_two = inverse_root(chip_residual)
@@ -926,15 +1031,16 @@
         return lax.dynamic_slice_in_dim(value, core * rows, rows, 0)
 
     out_rows = matmul(pick_low, chip_hidden).astype(BF).reshape(chips, slots, width)
-    my_gates = lax.dynamic_index_in_dim(
-        gates.T.reshape(chips, 4, 2 * rows), quarter, 1, keepdims=False
-    )
+    my_gates = my_quarter(gates)
     slot_gates = jnp.sum(jnp.where(pick, my_gates[:, None, :], 0.0), axis=2)
     gate_tile = jnp.pad(slot_gates[:, None, :], ((0, 0), (0, 7), (0, 128 - slots)))
-    arrived, gate_there = exchange_same_core([out_rows, gate_tile], 3)
+    arrived, gate_there = exchange([out_rows, gate_tile], 3)
     arrived = arrived.reshape(chips * slots, width)
     gate_col = gate_there[:, 0, :slots].reshape(chips * slots, 1)
     d_pairs = to_low(gate_col * cot_there.astype(F32))
+    gate_w = (of_mine(w_gate), gate_back)
+    up_w = (of_mine(w_up), up_back)
+    down_w = (of_mine(w_down), down_back)
     expert_out = 0.0
     d_rows = 0.0
     grads = []
@@ -956,43 +1062,23 @@
         grads.append((grad_gate, grad_up, grad_down))
     d_gate_slots = jnp.sum(expert_out * cot_there.astype(F32), axis=1).reshape(chips, 1, slots)
     d_gate_tile = jnp.pad(d_gate_slots, ((0, 0), (0, 7), (0, 128 - slots)))
-    d_back, d_gate_back = exchange_same_core(
+    d_back, d_gate_back = exchange(
         [to_low(d_rows).reshape(chips, slots, width), d_gate_tile], 4
     )
-    y_back = lax.all_to_all(
-        to_low(gate_col * expert_out).reshape(chips, slots, width),
-        "ctx",
-        split_axis=0,
-        concat_axis=0,
-        tiled=True,
-        axis_index_groups=same_core_groups(),
-    )
-
-    def paired(own, back):
-        back = swap(to_low(back)).astype(F32)
-        return jnp.where(wsh == 0, jnp.stack([own, back]), jnp.stack([back, own]))
-
-    grad_gate, grad_up, grad_down = [paired(own, back) for own, back in zip(*grads)]
+    y_back = exchange_behind(to_low(gate_col * expert_out).reshape(chips, slots, width))
+    swapped_grads = [swap(to_low(back)) for back in grads[1]]
 
     def collect(back):
         return to_low(transposed_times(pick_low, back.reshape(chips * slots, width))).reshape(2, rows, width)
 
     d_gate_slots = d_gate_back[:, 0, :slots]
     d_gates_mine = jnp.sum(jnp.where(pick, d_gate_slots[:, :, None], 0.0), axis=1)
-    d_gates_part = jnp.sum(
-        jnp.where(
-            jnp.arange(4, dtype=jnp.int32)[None, :, None] == quarter, d_gates_mine[:, None, :], 0.0
-        ),
-        axis=0,
-        keepdims=True,
-    ) if False else jnp.where(
-        jnp.arange(4, dtype=jnp.int32)[None, :, None] == quarter, d_gates_mine[:, None, :], 0.0
+    d_gates_part = jnp.where(
+        jnp.arange(4, dtype=jnp.int32)[None, :, None] == quarter[:, None, None], d_gates_mine[:, None, :], 0.0
     ).reshape(experts, 2 * rows)
     d_gates_part = d_gates_part.T.reshape(2, rows, experts)
     d_hidden_moe, d_gates = reduce_chip(collect(d_back), d_gates_part, 5)
-    (moe_total,) = reduce_chip(collect(y_back), None, 6)
     residual = my_rows(chip_residual)
-    out_stream = residual + moe_total
 
     own_gates = my_rows(gates)
     hidden_two = my_rows(chip_hidden)
@@ -1030,9 +1116,9 @@
         axis=1,
     )
     early = lax.all_to_all(early, "ctx", split_axis=0, concat_axis=0, tiled=True)
-    d_queries, d_kv = attend_back(
-        order, low, high, inverse_order, queries, d_heads, kv_all, q_pos, q_start, lse, dot_strips
-    )
+    y_back, d_heads = after(y_back, d_heads)
+    d_queries, d_kv = attend_back(plan, queries, d_heads, kv_all, q_pos, q_start, lse, dot_strips)
+    (early, swapped_grads), d_kv = after((early, swapped_grads), d_kv)
     d_side = reduce_keys(d_kv, 8)
     is_key = lax.rem(lax.div(me, 2), 2) == 0
     half_rows = row_tokens // 2
@@ -1068,11 +1154,20 @@
     late = jnp.concatenate(
         [grad_in[:, 128 * i : 128 * i + 128].reshape(64, depth, 128) for i in range(3)] + [tail], axis=1
     )
+    late, d_hidden_parts = after(late, d_hidden_parts)
     late = lax.all_to_all(late, "ctx", split_axis=0, concat_axis=0, tiled=True)
-    d_hidden_one = reduce_row(d_hidden_parts, 9, False)
+    d_hidden_one, moe_total = reduce_row(d_hidden_parts, 9, False, collect(y_back))
+    out_stream = residual + moe_total
     own_stream = tokens.astype(F32)
     d_stream_norm, _ = norm_back(own_stream, inverse_root(own_stream), g_attn, d_hidden_one)
     grad_tokens = d_residual + d_stream_norm
+
+
+    def paired(own, back):
+        back = back.astype(F32)
+        return jnp.where(wsh == 0, jnp.stack([own, back]), jnp.stack([back, own]))
+
+    grad_gate, grad_up, grad_down = [paired(own, back) for own, back in zip(grads[0], swapped_grads)]
 
     def summed(value, terms):
         return jnp.sum(value.astype(F32).reshape((8,) + terms + value.shape[1:]), axis=0)

time: 998 us -> 827 us (0.83); the launches traced: 986 us -> 829 us
  Pallas kernels: 549 us -> 431 us
  waiting for transfers between devices: 139 us -> 69.3 us
  local copies, waits for them, and re-layouts: 43.6 us -> 56.2 us
  matrix products: 116 us -> 127 us
    pallas_call x1, Pallas kernels: 135 us -> 57 us  [gather_first(): pl.pallas_call(body, out_shape=(sds((64,) + weights.shape[1:], weights.dt...]
    ppermute x6, waiting for transfers between devices: 106 us -> 49.9 us  [swap(): return lax.ppermute(value, 'wsh', [(0, 1), (1, 0)])]
    pallas_call x4, Pallas kernels: 219 us -> 174 us  [the longest x2 99 us: exchange(): pl.pallas_call(body, out_shape=[jax.ShapeDtypeStruct(a.shape, a.dtype) fo...]
    pallas_call x1, Pallas kernels: 28.7 us -> 59.4 us  [gather_row(): pl.pallas_call(body, out_shape=jax.ShapeDtypeStruct((8,) + block.shape, b...]
    pallas_call x2 -> x1, Pallas kernels: 34.3 us -> 17.8 us  [reduce_chip(): pl.pallas_call(body, out_shape=shapes, in_specs=[VMEM] * len(operands), o...]
    all_to_all x1, waiting for transfers between devices: 20.8 us -> 6.94 us  [local(): late = lax.all_to_all(late, 'ctx', split_axis=0, concat_axis=0, tiled=True)]
    dot_general x9, matrix products: 36.7 us -> 49.3 us  [times_transposed(): lax.dot_general(left, right, (((1,), (1,)), ((), ())), preferred_element_...]
  transfers between devices with their start and end apart: 11 -> 11, of which waited for: 5 -> 6; matrix products, arithmetic and copies ran while one was open for 16% -> 19% of each run, Pallas kernels for 32% -> 14%
where the time goes in v2:
time: 827 us; the launch traced here: 829 us
  Pallas kernels  431 us (52%)
  matrix products  127 us (15%)
  other arithmetic  82.5 us (10%)
  waiting for transfers between devices  69.3 us (8%)
  local copies, waits for them, and re-layouts  56.2 us (7%)
  starting transfers between devices  55.6 us (7%)
    pallas_call x2, Pallas kernels, exchange(): pl.pallas_call(body, out_shape=[jax.ShapeDtypeStruct(a.shape, a.dtype) fo...  99 us
    pallas_call x2, Pallas kernels, reduce_row(): pl.pallas_call(body, out_shape=shapes, in_specs=[VMEM] * len(operands), o...  75.1 us
    pallas_call x1, Pallas kernels, gather_row(): pl.pallas_call(body, out_shape=jax.ShapeDtypeStruct((8,) + block.shape, b...  59.4 us
    pallas_call x1, Pallas kernels, gather_first(): pl.pallas_call(body, out_shape=(sds((64,) + weights.shape[1:], weights.dt...  57 us
    ppermute x6, waiting for transfers between devices, swap(): return lax.ppermute(value, 'wsh', [(0, 1), (1, 0)])  49.9 us
    dot_general x9, matrix products, times_transposed(): lax.dot_general(left, right, (((1,), (1,)), ((), ())), preferred_element_...  49.3 us
    dot_general x11, matrix products, matmul(): return jnp.dot(left, right, preferred_element_type=jnp.float32)  42 us
    dot_general x11, matrix products, transposed_times(): lax.dot_general(left, right, (((0,), (0,)), ((), ())), preferred_element_...  35.1 us
  transfers between devices with their start and end apart: 11, of which 6 were waited for; matrix products, arithmetic and copies ran while one was open for 19% of the time, Pallas kernels for 14%

profile of v2, /device:TPU:0, one launch (start us, length us, event | category | flops | bytes accessed | tf_op | source)
XLA Modules:
  0.0 828.9 jit_solution(18000938443565450662)
XLA Ops:
  6.1 5.0 fusion.10
  11.0 57.0 %gather_first.1 = (bf16[64,32,512]{2,1,0:T(8,128)(2,1)}, bf16[8,128,2048]{2,1,0:T(8,128)(2,1)}, f32[64,8,128]{2,1,0:T(8,128)}, s32[2,8,128]{2,1,0:T(8,128)}, bf16[2,128,2048]{2,1,0:T(8,128)(2,1)}) custom-call(bf16[8,32,512]{2,1,0:T(8,128)(2,1)} %pad_maximum_fusion.8.w_in, bf16[128,2048]{1,0:T(8,128)(2,1)} %t_in.1, f32[8,128]{1,0:T(8,128)} %fusion.82.s_in, ...), custom_call_target="tpu_custom_call" | custom-call | bytes 216000000 | tf_op jit(solution)/shard_map/gather_first/pallas_call | solution.py:249
  70.3 7.7 all-to-all-start
  78.3 3.2 multiply_reduce_fusion
  83.8 2.3 fusion.120
  105.4 2.6 multiply_cosine_fusion
  112.4 3.9 convolution_convert_fusion.3
  116.3 5.9 all-to-all-done
  122.2 31.6 %gather_keys.1 = bf16[8,1024,256]{2,1,0:T(8,128)(2,1)} custom-call(bf16[1024,256]{1,0:T(8,128)(2,1)} %pad_maximum_fusion.3.src), custom_call_target="tpu_custom_call" | custom-call | bytes 108000000 | tf_op jit(solution)/shard_map/gather_keys/pallas_call | solution.py:327
  153.8 16.6 %all-to-all-start.1 = ((bf16[32,24,2048]{2,1,0:T(8,128)(2,1)}), bf16[32,24,2048]{2,1,0:T(8,128)(2,1)}, u32[]{:S(2)}, u32[]{:S(2)}) async-start(bf16[32,24,2048]{2,1,0:T(8,128)(2,1)} %bitcast.289), calls=%async_computation.1 | async-start | bytes 6291456 | tf_op jit(solution)/shard_map/all_to_all | solution.py:666
  170.6 3.3 fusion.12
  173.9 2.4 multiply_multiply_fusion
  176.3 2.5 slice_negate_fusion.1
  183.8 6.5 convert.57
  193.0 2.9 maximum_multiply_fusion
  199.3 26.3 %attend.1 = (bf16[1024,256]{1,0:T(8,128)(2,1)S(1)}, f32[8,1,256]{2,1,0:T(1,128)S(1)}) custom-call(s32[16]{0:T(128)S(1)} %select_reduce_fusion.3.order, s32[8]{0:T(128)S(1)} %get-tuple-element.122.low, s32[8]{0:T(128)S(1)} %get-tuple-element.120.inner_low, s32[8]{0:T(128)S(1)} %get-tuple-element.119.inner_high, s32[8]{0:T(128)S(1)} %get-tuple-element.121.high, ...), custom_call_target="tpu_custom_call" | custom-call | bytes 61200000 | tf_op jit(solution)/shard_map/attend/pallas_call | solution.py:764
  225.7 4.5 convolution_convert_fusion.1
  232.4 39.2 %reduce_row.2 = f32[2,128,2048]{2,1,0:T(8,128)S(1)} custom-call(bf16[8,128,2048]{2,1,0:T(8,128)(2,1)S(1)} %bitcast.280), custom_call_target="tpu_custom_call" | custom-call | bytes 144000000 | tf_op jit(solution)/shard_map/reduce_row/pallas_call | solution.py:461
  274.0 2.7 convolution_convert_fusion.2
  279.7 55.1 %exchange.2 = (bf16[32,24,2048]{2,1,0:T(8,128)(2,1)}, f32[32,8,128]{2,1,0:T(8,128)}) custom-call(bf16[32,24,2048]{2,1,0:T(8,128)(2,1)} %bitcast.290, f32[32,8,128]{2,1,0:T(8,128)} %pad.27.refs_1_), custom_call_target="tpu_custom_call" | custom-call | bytes 172800000 | tf_op jit(solution)/shard_map/exchange/pallas_call | solution.py:647
  334.8 5.8 fusion.41
  340.6 4.7 fusion.45
  347.3 5.7 multiply_convert_fusion.12
  353.1 6.8 fusion.43
  359.9 6.4 fusion.39
  366.4 3.9 fusion.37
  370.2 3.2 fusion.121
  373.4 8.4 %collective-permute-done.2 = bf16[384,2048]{1,0:T(8,128)(2,1)S(1)} collective-permute-done((bf16[384,2048]{1,0:T(8,128)(2,1)}, bf16[384,2048]{1,0:T(8,128)(2,1)S(1)}, u32[]{:S(2)}, u32[]{:S(2)}) %collective-permute-start.2) | collective-permute-done | bytes 1572896 | tf_op jit(solution)/shard_map/ppermute | solution.py:912
  383.0 3.7 fusion.106
  386.7 4.4 multiply_convert_fusion.11
  391.2 6.4 fusion.122
  397.6 6.1 multiply_convert_fusion.2
  404.4 10.5 %add_convert_fusion = bf16[768,2048]{1,0:T(8,128)(2,1)} fusion(f32[768,2048]{1,0:T(8,128)} %fusion.122, f32[768,2048]{1,0:T(8,128)} %fusion.43, f32[768,2048]{1,0:T(8,128)} %fusion.39, bf16[768,384]{1,0:T(8,128)(2,1)S(1)} %copy-done.65, bf16[2048,384]{1,0:T(8,128)(2,1)} %collective-permute-done.1), kind=kOutput, calls=%fused_computation.17 | convolution fusion | flops 1214251008 | bytes 24182784 | tf_op jit(solution)/shard_map/dot_general | solution.py:39
  414.9 43.9 %exchange.3 = (bf16[32,24,2048]{2,1,0:T(8,128)(2,1)}, f32[32,8,128]{2,1,0:T(8,128)}) custom-call(bf16[32,24,2048]{2,1,0:T(8,128)(2,1)} %bitcast.292, f32[32,8,128]{2,1,0:T(8,128)} %pad.28.refs_1_), custom_call_target="tpu_custom_call" | custom-call | bytes 172800000 | tf_op jit(solution)/shard_map/exchange/pallas_call | solution.py:647
  458.8 2.9 fusion.7
  463.1 17.8 %reduce_chip.1 = (f32[128,2048]{1,0:T(8,128)S(1)}, f32[128,128]{1,0:T(8,128)S(1)}) custom-call(bf16[2,128,2048]{2,1,0:T(8,128)(2,1)S(1)} %bitcast.283, f32[2,128,128]{2,1,0:T(8,128)S(1)} %bitcast.284), custom_call_target="tpu_custom_call" | custom-call | bytes 61200000 | tf_op jit(solution)/shard_map/reduce_chip/pallas_call | solution.py:517
  481.2 2.8 multiply_reduce_fusion.4
  484.1 6.2 all-to-all-start.2
  490.3 2.9 fusion.111
  493.2 59.4 %gather_row.1 = bf16[8,128,2048]{2,1,0:T(8,128)(2,1)} custom-call(bf16[128,2048]{1,0:T(8,128)(2,1)} %get-tuple-element.113.src), custom_call_target="tpu_custom_call" | custom-call | bytes 93600000 | tf_op jit(solution)/shard_map/gather_row/pallas_call | solution.py:278
  552.6 5.0 convolution_convert_fusion.6
  557.7 3.0 convolution_convert_fusion.5
  562.7 4.6 convolution_convert_fusion.4
  570.9 10.9 %all-to-all-start.3 = ((bf16[64,112,128]{2,1,0:T(8,128)(2,1)}), bf16[64,112,128]{2,1,0:T(8,128)(2,1)S(1)}, u32[]{:S(2)}, u32[]{:S(2)}) async-start(bf16[64,112,128]{2,1,0:T(8,128)(2,1)} %fusion.9), calls=%async_computation.3 | async-start | bytes 3670016 | tf_op jit(solution)/shard_map/all_to_all | solution.py:1118
  581.8 5.3 convolution_bitcast_fusion
  587.1 3.5 convolution_bitcast_fusion.2
  590.6 3.5 convolution_bitcast_fusion.1
  594.1 3.6 convert_multiply_fusion.5
  604.1 31.8 %attend_back.1 = (f32[1024,256]{1,0:T(8,128)}, bf16[2,8,2,512,128]{4,3,2,1,0:T(8,128)(2,1)}) custom-call(s32[16]{0:T(128)} %copy-done.6, s32[8]{0:T(128)} %copy-done.10, s32[8]{0:T(128)} %copy-done.8, s32[8]{0:T(128)} %copy-done.7, s32[8]{0:T(128)} %copy-done.9, s32[128]{0:T(128)} %copy-done.11, bf16[1024,256]{1,0:T(8,128)(2,1)} %copy-done.1, ...), custom_call_target="tpu_custom_call" | custom-call | bytes 86400000 | tf_op jit(solution)/shard_map/attend_back/pallas_call | solution.py:843
  635.9 7.7 collective-permute-done.4
  643.6 33.7 %collective-permute-done.5 = bf16[384,2048]{1,0:T(8,128)(2,1)} collective-permute-done((bf16[384,2048]{1,0:T(8,128)(2,1)}, bf16[384,2048]{1,0:T(8,128)(2,1)}, u32[]{:S(2)}, u32[]{:S(2)}) %collective-permute-start.5) | collective-permute-done | bytes 1572896 | tf_op jit(solution)/shard_map/ppermute | solution.py:912
  677.4 6.5 all-to-all-done.3
  687.4 32.8 %reduce_keys.1 = f32[512,128]{1,0:T(8,128)S(1)} custom-call(bf16[2,8,2,512,128]{4,3,2,1,0:T(8,128)(2,1)S(1)} %copy-done.2), custom_call_target="tpu_custom_call" | custom-call | bytes 144000000 | tf_op jit(solution)/shard_map/reduce_keys/pallas_call | solution.py:589
  724.9 3.5 multiply_reduce_fusion.3
  733.4 2.6 fusion.6
  737.4 2.4 convolution_convert_fusion
  741.2 2.9 fusion.8
  744.2 35.9 %reduce_row.3 = (f32[128,2048]{1,0:T(8,128)S(1)}, f32[128,2048]{1,0:T(8,128)S(1)}) custom-call(bf16[8,128,2048]{2,1,0:T(8,128)(2,1)S(1)} %bitcast.281, bf16[2,128,2048]{2,1,0:T(8,128)(2,1)S(1)} %bitcast.282), custom_call_target="tpu_custom_call" | custom-call | bytes 144000000 | tf_op jit(solution)/shard_map/reduce_row/pallas_call | solution.py:461
  780.4 8.8 %all-to-all-start.4 = ((bf16[64,112,128]{2,1,0:T(8,128)(2,1)}), bf16[64,112,128]{2,1,0:T(8,128)(2,1)}, u32[]{:S(2)}, u32[]{:S(2)}) async-start(bf16[64,112,128]{2,1,0:T(8,128)(2,1)} %pad_maximum_fusion), calls=%async_computation.4 | async-start | bytes 3670016 | tf_op jit(solution)/shard_map/all_to_all | solution.py:1158
  796.2 3.2 maximum_select_fusion
  799.8 3.2 maximum_select_fusion.1
  803.5 3.1 maximum_select_fusion.2
  809.9 6.9 all-to-all-done.4
  822.6 4.9 psum.7
  (413 shorter events, 103.2 us)
Async XLA Ops:
  6.1 62.8 %copy-start.78 = (f32[32,128]{1,0:T(8,128)S(1)}, f32[32,128]{1,0:T(8,128)}, u32[]{:S(2)}) copy-start(f32[32,128]{1,0:T(8,128)} %param.35) | copy-start | bytes 49156
  6.1 62.8 %copy-start.68 = (f32[2048,32]{0,1:T(8,128)S(1)}, f32[2048,32]{0,1:T(8,128)}, u32[]{:S(2)}) copy-start(f32[2048,32]{0,1:T(8,128)} %param.30) | copy-start | bytes 786436
  68.1 54.2 %collective-permute-start = (bf16[2048,384]{1,0:T(8,128)(2,1)}, bf16[2048,384]{1,0:T(8,128)(2,1)}, u32[]{:S(2)}, u32[]{:S(2)}) collective-permute-start(bf16[2048,384]{1,0:T(8,128)(2,1)} %get-tuple-element.59), channel_id=1, source_target_pairs={{0,1},{1,0},{2,3},{3,2},{4,5},{5,4},{6,7},{7,6},{8,9},{9,8},{10,11... | collective-permute-start | bytes 4718600 | tf_op jit(solution)/shard_map/ppermute | solution.py:912
  68.9 9.1 %copy-start.69 = (f32[64,8,128]{2,1,0:T(8,128)S(1)}, f32[64,8,128]{2,1,0:T(8,128)}, u32[]{:S(2)}) copy-start(f32[64,8,128]{2,1,0:T(8,128)} %get-tuple-element.60) | copy-start | bytes 786436
  70.3 51.9 %all-to-all-start = ((bf16[64,32,384]{2,1,0:T(8,128)(2,1)}), bf16[64,32,384]{2,1,0:T(8,128)(2,1)}, u32[]{:S(2)}, u32[]{:S(2)}) async-start(bf16[64,32,384]{2,1,0:T(8,128)(2,1)} %bitcast.20), calls=%async_computation | async-start | bytes 3145728 | tf_op jit(solution)/shard_map/all_to_all | solution.py:937
  86.1 9.4 %copy-start.20 = (f32[1024,512]{1,0:T(8,128)}, f32[1024,512]{1,0:T(8,128)S(1)}, u32[]{:S(2)}) copy-start(f32[1024,512]{1,0:T(8,128)S(1)} %fusion.120) | copy-start | bytes 6291460
  86.1 6.8 copy-start.102
  86.1 7.9 copy-start.81
  87.7 8.8 %copy-start.82 = (pred[32]{0:T(512)(128)(4,1)}, pred[32]{0:T(512)(128)(4,1)S(1)}, u32[]{:S(2)}) copy-start(pred[32]{0:T(512)(128)(4,1)S(1)} %get-tuple-element.127) | copy-start | bytes 100
  89.8 109.4 %copy-start.6 = (s32[16]{0:T(128)}, s32[16]{0:T(128)S(1)}, u32[]{:S(2)}) copy-start(s32[16]{0:T(128)S(1)} %select_reduce_fusion.3.order) | copy-start | bytes 196
  95.5 5.7 slice-start
  101.7 72.1 %copy-start.17 = (f32[1024,2,128]{2,1,0:T(2,128)}, f32[1024,2,128]{2,1,0:T(2,128)S(1)}, u32[]{:S(2)}) copy-start(f32[1024,2,128]{2,1,0:T(2,128)S(1)} %reshape.676) | copy-start | bytes 3145732
  105.3 5.7 copy-start.76
  105.3 5.8 copy-start.77
  105.3 6.0 copy-start.75
  105.4 6.1 copy-start.90
  108.0 8.3 %copy-start.34 = (f32[1024,64]{1,0:T(8,128)}, f32[1024,64]{1,0:T(8,128)S(1)}, u32[]{:S(2)}) copy-start(f32[1024,64]{1,0:T(8,128)S(1)} %get-tuple-element.162) | copy-start | bytes 786436
  110.1 82.9 %copy-start.32 = (f32[1024,128]{1,0:T(8,128)}, f32[1024,128]{1,0:T(8,128)S(1)}, u32[]{:S(2)}) copy-start(f32[1024,128]{1,0:T(8,128)S(1)} %get-tuple-element.152) | copy-start | bytes 1572868
  110.1 85.8 %copy-start.30 = (f32[1024,128]{1,0:T(8,128)}, f32[1024,128]{1,0:T(8,128)S(1)}, u32[]{:S(2)}) copy-start(f32[1024,128]{1,0:T(8,128)S(1)} %get-tuple-element.150) | copy-start | bytes 1572868
  111.5 86.1 %copy-start.86 = (f32[256]{0:T(256)}, f32[256]{0:T(256)S(1)}, u32[]{:S(2)}) copy-start(f32[256]{0:T(256)S(1)} %broadcast_bitcast_fusion) | copy-start | bytes 3076
  111.5 87.7 %copy-start.7 = (s32[8]{0:T(128)}, s32[8]{0:T(128)S(1)}, u32[]{:S(2)}) copy-start(s32[8]{0:T(128)S(1)} %get-tuple-element.119.inner_high) | copy-start | bytes 100
  111.5 87.7 %copy-start.8 = (s32[8]{0:T(128)}, s32[8]{0:T(128)S(1)}, u32[]{:S(2)}) copy-start(s32[8]{0:T(128)S(1)} %get-tuple-element.120.inner_low) | copy-start | bytes 100
  111.6 87.7 %copy-start.9 = (s32[8]{0:T(128)}, s32[8]{0:T(128)S(1)}, u32[]{:S(2)}) copy-start(s32[8]{0:T(128)S(1)} %get-tuple-element.121.high) | copy-start | bytes 100
  111.6 87.7 %copy-start.10 = (s32[8]{0:T(128)}, s32[8]{0:T(128)S(1)}, u32[]{:S(2)}) copy-start(s32[8]{0:T(128)S(1)} %get-tuple-element.122.low) | copy-start | bytes 100
  153.8 16.6 %copy-start.74 = (s32[16,64]{1,0:T(8,128)S(1)}, s32[16,64]{1,0:T(8,128)}, u32[]{:S(2)}) copy-start(s32[16,64]{1,0:T(8,128)} %gather_fusion.4) | copy-start | bytes 12292
  153.8 16.6 %copy-start.80 = (pred[16]{0:T(512)(128)(4,1)S(1)}, pred[16]{0:T(512)(128)(4,1)}, u32[]{:S(2)}) copy-start(pred[16]{0:T(512)(128)(4,1)} %copy-done.79) | copy-start | bytes 52
  153.8 76.4 %all-to-all-start.1 = ((bf16[32,24,2048]{2,1,0:T(8,128)(2,1)}), bf16[32,24,2048]{2,1,0:T(8,128)(2,1)}, u32[]{:S(2)}, u32[]{:S(2)}) async-start(bf16[32,24,2048]{2,1,0:T(8,128)(2,1)} %bitcast.289), calls=%async_computation.1 | async-start | bytes 6291456 | tf_op jit(solution)/shard_map/all_to_all | solution.py:666
  176.3 6.7 copy-start.96
  178.8 51.4 %collective-permute-start.1 = (bf16[2048,384]{1,0:T(8,128)(2,1)}, bf16[2048,384]{1,0:T(8,128)(2,1)}, u32[]{:S(2)}, u32[]{:S(2)}) collective-permute-start(bf16[2048,384]{1,0:T(8,128)(2,1)} %get-tuple-element.64), channel_id=1, source_target_pairs={{0,1},{1,0},{2,3},{3,2},{4,5},{5,4},{6,7},{7,6},{8,9},{9,8},{10,11... | collective-permute-start | bytes 4718600 | tf_op jit(solution)/shard_map/ppermute | solution.py:912
  183.7 15.6 %copy-start.3 = (s32[8,1,256]{2,1,0:T(1,128)}, s32[8,1,256]{2,1,0:T(1,128)S(1)}, u32[]{:S(2)}) copy-start(s32[8,1,256]{2,1,0:T(1,128)S(1)} %reshape.677.pos_ref) | copy-start | bytes 24580
  183.8 15.5 %copy-start.4 = (s32[8,1,256]{2,1,0:T(1,128)}, s32[8,1,256]{2,1,0:T(1,128)S(1)}, u32[]{:S(2)}) copy-start(s32[8,1,256]{2,1,0:T(1,128)S(1)} %reshape.678.start_ref) | copy-start | bytes 24580
  192.9 6.3 copy-start.11
  198.3 27.4 %copy-start.1 = (bf16[1024,256]{1,0:T(8,128)(2,1)}, bf16[1024,256]{1,0:T(8,128)(2,1)S(1)}, u32[]{:S(2)}) copy-start(bf16[1024,256]{1,0:T(8,128)(2,1)S(1)} %fusion.29.q_ref) | copy-start | bytes 1572868
  334.8 5.8 copy-start.97
  345.4 36.5 %collective-permute-start.2 = (bf16[384,2048]{1,0:T(8,128)(2,1)}, bf16[384,2048]{1,0:T(8,128)(2,1)S(1)}, u32[]{:S(2)}, u32[]{:S(2)}) collective-permute-start(bf16[384,2048]{1,0:T(8,128)(2,1)} %fusion.12), channel_id=1, source_target_pairs={{0,1},{1,0},{2,3},{3,2},{4,5},{5,4},{6,7},{7,6},{8,9},{9,8},{10,11... | collective-permute-start | bytes 4718600 | tf_op jit(solution)/shard_map/ppermute | solution.py:912
  353.1 6.9 copy-start.63
  353.1 6.9 copy-start.61
  391.2 6.4 copy-start.59
  391.2 6.4 copy-start.47
  391.2 6.4 copy-start.54
  397.6 6.8 copy-start.65
  484.1 6.2 copy-start.15
  484.1 86.8 %all-to-all-start.2 = ((bf16[32,24,2048]{2,1,0:T(8,128)(2,1)}), bf16[32,24,2048]{2,1,0:T(8,128)(2,1)}, u32[]{:S(2)}, u32[]{:S(2)}) async-start(bf16[32,24,2048]{2,1,0:T(8,128)(2,1)} %bitcast.291), calls=%async_computation.2 | async-start | bytes 6291456 | tf_op jit(solution)/shard_map/all_to_all | solution.py:666
  493.2 59.4 %copy-start.60 = (bf16[768,384]{1,0:T(8,128)(2,1)S(1)}, bf16[768,384]{1,0:T(8,128)(2,1)}, u32[]{:S(2)}) copy-start(bf16[768,384]{1,0:T(8,128)(2,1)} %copy-done.59) | copy-start | bytes 1769476
  557.7 78.2 %collective-permute-start.3 = (bf16[2048,384]{1,0:T(8,128)(2,1)}, bf16[2048,384]{1,0:T(8,128)(2,1)}, u32[]{:S(2)}, u32[]{:S(2)}) collective-permute-start(bf16[2048,384]{1,0:T(8,128)(2,1)} %convolution_convert_fusion.6), channel_id=1, source_target_pairs={{0,1},{1,0},{2,3},{3,2},{4,5},{5,4},{6,7},{7,6},{8,9},{9,8},{10,11... | collective-permute-start | bytes 4718600 | tf_op jit(solution)/shard_map/ppermute | solution.py:912
  560.7 7.0 copy-start.28
  560.7 7.3 copy-start.42
  560.7 82.9 %collective-permute-start.4 = (bf16[2048,384]{1,0:T(8,128)(2,1)}, bf16[2048,384]{1,0:T(8,128)(2,1)}, u32[]{:S(2)}, u32[]{:S(2)}) collective-permute-start(bf16[2048,384]{1,0:T(8,128)(2,1)} %convolution_convert_fusion.5), channel_id=1, source_target_pairs={{0,1},{1,0},{2,3},{3,2},{4,5},{5,4},{6,7},{7,6},{8,9},{9,8},{10,11... | collective-permute-start | bytes 4718600 | tf_op jit(solution)/shard_map/ppermute | solution.py:912
  567.3 110.0 %collective-permute-start.5 = (bf16[384,2048]{1,0:T(8,128)(2,1)}, bf16[384,2048]{1,0:T(8,128)(2,1)}, u32[]{:S(2)}, u32[]{:S(2)}) collective-permute-start(bf16[384,2048]{1,0:T(8,128)(2,1)} %convolution_convert_fusion.4), channel_id=1, source_target_pairs={{0,1},{1,0},{2,3},{3,2},{4,5},{5,4},{6,7},{7,6},{8,9},{9,8},{10,11... | collective-permute-start | bytes 4718600 | tf_op jit(solution)/shard_map/ppermute | solution.py:912
  570.9 113.0 %all-to-all-start.3 = ((bf16[64,112,128]{2,1,0:T(8,128)(2,1)}), bf16[64,112,128]{2,1,0:T(8,128)(2,1)S(1)}, u32[]{:S(2)}, u32[]{:S(2)}) async-start(bf16[64,112,128]{2,1,0:T(8,128)(2,1)} %fusion.9), calls=%async_computation.3 | async-start | bytes 3670016 | tf_op jit(solution)/shard_map/all_to_all | solution.py:1118
  683.9 36.4 %copy-start.29 = (bf16[64,112,128]{2,1,0:T(8,128)(2,1)}, bf16[64,112,128]{2,1,0:T(8,128)(2,1)S(1)}, u32[]{:S(2)}) copy-start(bf16[64,112,128]{2,1,0:T(8,128)(2,1)S(1)} %all-to-all-done.3) | copy-start | bytes 5505028
  683.9 36.4 %copy-start.35 = (f32[1024,64]{1,0:T(8,128)S(1)}, f32[1024,64]{1,0:T(8,128)}, u32[]{:S(2)}) copy-start(f32[1024,64]{1,0:T(8,128)} %copy-done.34) | copy-start | bytes 786436
  687.4 33.2 %copy-start.38 = (f32[1024,64]{1,0:T(8,128)S(1)}, f32[1024,64]{1,0:T(8,128)}, u32[]{:S(2)}) copy-start(f32[1024,64]{1,0:T(8,128)} %copy-done.37) | copy-start | bytes 786436
  687.4 33.2 %copy-start.52 = (f32[1024,128]{1,0:T(8,128)S(1)}, f32[1024,128]{1,0:T(8,128)}, u32[]{:S(2)}) copy-start(f32[1024,128]{1,0:T(8,128)} %get-tuple-element.140) | copy-start | bytes 1572868
  687.4 33.2 %copy-start.85 = (f32[128]{0:T(128)S(1)}, f32[128]{0:T(128)}, u32[]{:S(2)}) copy-start(f32[128]{0:T(128)} %copy-done.84) | copy-start | bytes 1540
  724.9 6.3 copy-start.41
  744.2 35.9 %copy-start.39 = (bf16[128,2048]{1,0:T(8,128)(2,1)S(1)}, bf16[128,2048]{1,0:T(8,128)(2,1)}, u32[]{:S(2)}) copy-start(bf16[128,2048]{1,0:T(8,128)(2,1)} %t_in.1) | copy-start | bytes 1572868
  780.1 9.2 %slice-start.1 = ((bf16[64,112,128]{2,1,0:T(8,128)(2,1)}), bf16[64,64,128]{2,1,0:T(8,128)(2,1)S(1)}, s32[]{:S(2)}) async-start(bf16[64,112,128]{2,1,0:T(8,128)(2,1)} %copy-done.29), calls=%async_computation.6 | async-start | bytes 2097152 | tf_op jit(solution)/shard_map/slice | solution.py:1175
  780.4 36.4 %all-to-all-start.4 = ((bf16[64,112,128]{2,1,0:T(8,128)(2,1)}), bf16[64,112,128]{2,1,0:T(8,128)(2,1)}, u32[]{:S(2)}, u32[]{:S(2)}) async-start(bf16[64,112,128]{2,1,0:T(8,128)(2,1)} %pad_maximum_fusion), calls=%async_computation.4 | async-start | bytes 3670016 | tf_op jit(solution)/shard_map/all_to_all | solution.py:1158
  809.9 10.2 %copy-start.73 = (bf16[32,256]{1,0:T(8,128)(2,1)S(1)}, bf16[32,256]{1,0:T(8,128)(2,1)}, u32[]{:S(2)}) copy-start(bf16[32,256]{1,0:T(8,128)(2,1)} %copy-done.72) | copy-start | bytes 49156
  809.9 10.9 %copy-start.71 = (bf16[32,256]{1,0:T(8,128)(2,1)S(1)}, bf16[32,256]{1,0:T(8,128)(2,1)}, u32[]{:S(2)}) copy-start(bf16[32,256]{1,0:T(8,128)(2,1)} %copy-done.70) | copy-start | bytes 49156
  809.9 11.6 %copy-start.56 = (bf16[32,2048]{1,0:T(8,128)(2,1)S(1)}, bf16[32,2048]{1,0:T(8,128)(2,1)}, u32[]{:S(2)}) copy-start(bf16[32,2048]{1,0:T(8,128)(2,1)} %copy-done.55) | copy-start | bytes 393220
  809.9 11.8 %copy-start.94 = (bf16[32]{0:T(256)(128)(2,1)S(1)}, bf16[32]{0:T(256)(128)(2,1)}, u32[]{:S(2)}) copy-start(bf16[32]{0:T(256)(128)(2,1)} %convert_element_type.367) | copy-start | bytes 196
  818.7 9.9 %copy-start.58 = (f32[32,2048]{1,0:T(8,128)}, f32[32,2048]{1,0:T(8,128)S(1)}, u32[]{:S(2)}) copy-start(f32[32,2048]{1,0:T(8,128)S(1)} %reshape.705) | copy-start | bytes 786436
  (52 other events, 154.3 us)

commit v3 on v2

--- a/solution.py
+++ b/solution.py
@@ -13,7 +13,7 @@
 BLK = 64
 MAX_SEQ_TOKENS = 4096
 CAP = 12
-CHUNK = 512
+CHUNK = 1024
 
 EPSILON = 1e-06
 ROPE_BASE = 1000000.0
@@ -67,21 +67,7 @@
     cosine, sine_tab = jnp.cos(angles), jnp.sin(angles)
     return (
         jnp.concatenate([cosine, cosine], axis=-1),
-        jnp.concatenate([sine_tab, sine_tab], axis=-1),
-    )
-
-
-def rotate(value_rows, cosine, sine_tab):
-    half_dim = value_rows.shape[-1] // 2
-    turned = jnp.concatenate([-value_rows[..., half_dim:], value_rows[..., :half_dim]], axis=-1)
-    return value_rows * cosine + turned * sine_tab
-
-
-def rotate_back(gradient, cosine, sine_tab):
-    half_dim = gradient.shape[-1] // 2
-    shifted = gradient * sine_tab
-    return gradient * cosine + jnp.concatenate(
-        [shifted[..., half_dim:], -shifted[..., :half_dim]], axis=-1
+        jnp.concatenate([-sine_tab, sine_tab], axis=-1),
     )
 
 
@@ -144,12 +130,15 @@
 
 
 def cost(microseconds):
-    return pl.CostEstimate(flops=0, bytes_accessed=int(microseconds * 3.6e6), transcendentals=0)
-
-
-def call_params(collective_id, limit=None):
+    return pl.CostEstimate(flops=0, bytes_accessed=int(microseconds * 1.2e6), transcendentals=0)
+
+
+ROOM = 56 * 1024 * 1024
+
+
+def call_params(collective_id):
     return pltpu.CompilerParams(
-        collective_id=collective_id, has_side_effects=True, vmem_limit_bytes=limit
+        collective_id=collective_id, has_side_effects=True, vmem_limit_bytes=ROOM
     )
 
 
@@ -195,8 +184,40 @@
         forward.wait()
 
 
-def gather_first(weights, tokens, small, routes, cotangent):
-    def body(w_in, t_in, s_in, r_in, c_in, w_out, t_out, s_out, r_out, c_out, wide, row_s, row_r, pair, local):
+def cast_steps(wide, narrow, side):
+    sources, staging, lows, in_sems, out_sems = wide
+    steps = []
+    for src, dst in zip(sources, narrow):
+        at = 0 if src.shape[1] > src.shape[2] else 1
+        rows = staging[at].shape[1]
+        for chunk in range(src.shape[1] // rows):
+            steps.append((src, dst, at, pl.ds(chunk * rows, rows)))
+    loads, stores = [], []
+    for index, (src, dst, at, span) in enumerate(steps):
+        slot = index % 2
+        loads.append(pltpu.make_async_copy(src.at[side, span], staging[at].at[slot], in_sems.at[slot]))
+        stores.append(pltpu.make_async_copy(lows[at].at[slot], dst.at[span], out_sems.at[slot]))
+    loads[0].start()
+    loads[1].start()
+    for index, (_, _, at, _) in enumerate(steps):
+        slot = index % 2
+        loads[index].wait()
+        if index >= 2:
+            stores[index - 2].wait()
+        lows[at][slot] = staging[at][slot].astype(BF)
+        stores[index].start()
+        if index + 2 < len(steps):
+            loads[index + 2].start()
+    stores[-2].wait()
+    stores[-1].wait()
+
+
+def gather_first(weights, tokens, small, routes, cotangent, expert_weights):
+    def body(w_in, t_in, s_in, r_in, c_in, *refs):
+        sources, refs = refs[:3], refs[3:]
+        w_out, t_out, s_out, r_out, c_out = refs[:5]
+        lows, side_out, refs = refs[5:8], refs[8], refs[9:]
+        wide, row_s, row_r, pair, local, tall_f, flat_f, tall_b, flat_b, in_sems, out_sems = refs
         me, wsh = lax.axis_index("ctx"), lax.axis_index("wsh")
         core = lax.rem(me, 2)
         place = lax.rem(me, 8)
@@ -234,18 +255,27 @@
         ]
         for copy in pair_copies:
             copy.start()
+        cast_steps((sources, (tall_f, flat_f), (tall_b, flat_b), in_sems, out_sems), lows, 1 - wsh)
         row_gather_finish(t_out, me, wsh, row_copies, row_s, row_r)
         for copy in pair_copies:
             copy.wait()
-        for copy in locals_:
+        for copy in locals_[:1] + locals_[2:]:
             copy.wait()
         for at, out in ((0, s_out), (2, w_out)):
             rest = out.at[pl.ds(0, 63)]
             done = remote(rest, rest, wide.at[at], wide.at[at + 1], partner, wsh)
             done.wait_send()
             done.wait_recv()
+        locals_[1].wait()
+        lanes = side_out.shape[2]
+        share = w_out.at[pl.ds(0, 64), pl.ds(0, w_out.shape[1]), pl.ds(w_out.shape[2] - lanes, lanes)]
+        give = remote(share, side_out, pair.at[4], pair.at[5], partner, wsh)
+        give.start()
+        give.wait()
 
     sds = jax.ShapeDtypeStruct
+    tall = (expert_weights[0].shape[1] // 4, expert_weights[0].shape[2])
+    flat = (expert_weights[2].shape[1] // 4, expert_weights[2].shape[2])
     return pl.pallas_call(
         body,
         out_shape=(
@@ -254,14 +284,28 @@
             sds((64,) + small.shape, small.dtype),
             sds((2,) + routes.shape, routes.dtype),
             sds((2,) + cotangent.shape, cotangent.dtype),
-        ),
-        in_specs=[ANY] * 5,
-        out_specs=[ANY] * 5,
-        scratch_shapes=[DMA((4,)), DMA((9,)), DMA((9,)), DMA((4,)), DMA((5,))],
+        )
+        + tuple(sds(value.shape[1:], BF) for value in expert_weights)
+        + (sds((64, weights.shape[1], 128), weights.dtype),),
+        in_specs=[ANY] * 8,
+        out_specs=[ANY] * 9,
+        scratch_shapes=[
+            DMA((4,)),
+            DMA((9,)),
+            DMA((9,)),
+            DMA((6,)),
+            DMA((5,)),
+            pltpu.VMEM((2,) + tall, F32),
+            pltpu.VMEM((2,) + flat, F32),
+            pltpu.VMEM((2,) + tall, BF),
+            pltpu.VMEM((2,) + flat, BF),
+            DMA((2,)),
+            DMA((2,)),
+        ],
         compiler_params=call_params(0),
         name="gather_first",
         cost_estimate=cost(60),
-    )(weights, tokens, small, routes, cotangent)
+    )(weights, tokens, small, routes, cotangent, *expert_weights)
 
 
 def gather_row(block, collective_id):
@@ -339,7 +383,7 @@
 def reduce_row(parts, collective_id, both, extra=None):
     _, rows, width = parts.shape
     block = (rows, width)
-    pieces = 2
+    pieces = 4
     columns = width // pieces
     has_extra = extra is not None
 
@@ -464,7 +508,7 @@
         in_specs=[VMEM] * len(operands),
         out_specs=[VMEM] * len(operands),
         scratch_shapes=scratch,
-        compiler_params=call_params(collective_id, 40 * 1024 * 1024),
+        compiler_params=call_params(collective_id),
         name="reduce_row",
         cost_estimate=cost(40),
     )(*operands)
@@ -520,7 +564,7 @@
         in_specs=[VMEM] * len(operands),
         out_specs=[VMEM] * len(operands),
         scratch_shapes=scratch,
-        compiler_params=call_params(collective_id, 40 * 1024 * 1024),
+        compiler_params=call_params(collective_id),
         name="reduce_chip",
         cost_estimate=cost(17),
     )(*operands)
@@ -600,7 +644,7 @@
             DMA((4, groups)),
             DMA((4, groups)),
         ],
-        compiler_params=call_params(collective_id, 40 * 1024 * 1024),
+        compiler_params=call_params(collective_id),
         name="reduce_keys",
         cost_estimate=cost(40),
     )(parts)
@@ -676,7 +720,7 @@
         values[at, :] = rows[:, HEAD_WIDTH:]
         return carried
 
-    lax.fori_loop(0, kv_ref.shape[0] // BLK, one, 0)
+    lax.fori_loop(0, kv_ref.shape[0] // BLK, one, 0, unroll=8)
     source, turned = transposed
 
     def turn(chunk, carried):
@@ -684,7 +728,7 @@
         turned[:, at] = source[at, :].T
         return carried
 
-    lax.fori_loop(0, kv_ref.shape[0] // CHUNK, turn, 0)
+    lax.fori_loop(0, kv_ref.shape[0] // CHUNK, turn, 0, unroll=4)
 
 
 def stacked(ref, first, second):
@@ -730,28 +774,19 @@
     width = 4 * BLK
     acc[...] = jnp.zeros_like(acc)
 
-    def chunk(masked, index, carried):
-        highest, total = carried
+    def chunk(masked, index, total):
         at = pl.multiple_of(index * CHUNK, CHUNK)
         scores = matmul(keys[pl.ds(at, CHUNK), :], q_t)
         if masked:
             scores = kept(scores, at, q_pos, q_start)
-        top = jnp.maximum(highest, jnp.max(scores, axis=0, keepdims=True))
-        probs = jnp.exp2((scores - top) * TWO_SCALE)
-        fade = jnp.exp2((highest - top) * TWO_SCALE)
-        acc[...] = acc[...] * fade + matmul(values_t[:, pl.ds(at, CHUNK)], probs.astype(BF))
-        return top, total * fade + jnp.sum(probs, axis=0, keepdims=True)
-
-    highest, total = three_loops(
-        step,
-        low,
-        inner_low,
-        inner_high,
-        high,
-        chunk,
-        (jnp.full((1, width), MASKED, F32), jnp.zeros((1, width), F32)),
-    )
-    lse_ref[0] = highest * TWO_SCALE + jnp.log2(total)
+        probs = jnp.exp2(scores * TWO_SCALE)
+        acc[...] += matmul(values_t[:, pl.ds(at, CHUNK)], probs.astype(BF))
+        return total + jnp.sum(probs, axis=0, keepdims=True)
+
+    total = three_loops(
+        step, low, inner_low, inner_high, high, chunk, jnp.zeros((1, width), F32)
+    )
+    lse_ref[0] = jnp.log2(total)
     unstacked(out_ref, first, second, (acc[...] / total).T.astype(BF))
 
 
@@ -776,13 +811,13 @@
                 pltpu.VMEM((HEAD_WIDTH, 4 * BLK), F32),
             ],
         ),
-        compiler_params=pltpu.CompilerParams(vmem_limit_bytes=50 * 1024 * 1024),
+        compiler_params=pltpu.CompilerParams(vmem_limit_bytes=ROOM),
         name="attend",
         cost_estimate=cost(17),
     )(*plan, queries, kv, positions, starts)
 
 
-def backward_kernel(order, low, inner_low, inner_high, high, inverse, q_ref, do_ref, kv_ref, pos_ref, start_ref, lse_ref, dot_ref, dq_ref, dkv_ref, keys, values, keys_t, d_keys, d_values, acc):
+def backward_kernel(order, low, inner_low, inner_high, high, inverse, q_ref, heads_ref, da_ref, wo_ref, kv_ref, pos_ref, start_ref, lse_ref, dq_ref, dkv_ref, keys, values, keys_t, d_keys, d_values, acc):
     step = pl.program_id(0)
 
     @pl.when(step == 0)
@@ -793,11 +828,26 @@
 
     first, second = order[2 * step], order[2 * step + 1]
     q = stacked(q_ref, first, second)
-    d_out = stacked(do_ref, first, second)
+    d_rows = matmul(
+        jnp.concatenate(
+            [da_ref[pl.ds(pl.multiple_of(at * BLK, BLK), BLK), :] for at in (first, second)], axis=0
+        ),
+        wo_ref[...],
+    )
+    d_out = jnp.concatenate(
+        [
+            d_rows[begin : begin + BLK, head : head + HEAD_WIDTH]
+            for begin in (0, BLK)
+            for head in (0, HEAD_WIDTH)
+        ],
+        axis=0,
+    ).astype(BF)
     q_t = q.astype(F32).T.astype(BF)
-    d_out_t = d_out.astype(F32).T.astype(BF)
+    d_out_wide = d_out.astype(F32).T
+    d_out_t = d_out_wide.astype(BF)
     q_pos, q_start = pos_ref[0], start_ref[0]
-    lse, dots = lse_ref[0], dot_ref[0]
+    lse = lse_ref[0]
+    dots = jnp.sum(d_out_wide * stacked(heads_ref, first, second).astype(F32).T, axis=0, keepdims=True)
     acc[...] = jnp.zeros_like(acc)
 
     def chunk(masked, index, carried):
@@ -829,10 +879,10 @@
             dkv_ref[half, group, 1, to, :] = d_values[at, :].astype(BF)
             return carried
 
-        lax.fori_loop(0, kv_ref.shape[0] // BLK, one, 0)
-
-
-def attend_back(plan, queries, d_heads, kv, positions, starts, lse, dots):
+        lax.fori_loop(0, kv_ref.shape[0] // BLK, one, 0, unroll=4)
+
+
+def attend_back(plan, queries, heads, d_attn, wo_t, kv, positions, starts, lse):
     rows = queries.shape[0]
     total = kv.shape[0]
     steps = rows // (2 * BLK)
@@ -846,7 +896,16 @@
         grid_spec=pltpu.PrefetchScalarGridSpec(
             num_scalar_prefetch=6,
             grid=(steps,),
-            in_specs=[everything, everything, pl.BlockSpec(kv.shape, lambda i, *_: (0, 0)), strip, strip, strip, strip],
+            in_specs=[
+                everything,
+                everything,
+                pl.BlockSpec(d_attn.shape, lambda i, *_: (0, 0)),
+                pl.BlockSpec(wo_t.shape, lambda i, *_: (0, 0)),
+                pl.BlockSpec(kv.shape, lambda i, *_: (0, 0)),
+                strip,
+                strip,
+                strip,
+            ],
             out_specs=[everything, pl.BlockSpec(dkv_shape, lambda i, *_: (0, 0, 0, 0, 0))],
             scratch_shapes=[
                 pltpu.VMEM((total, HEAD_WIDTH), BF),
@@ -857,10 +916,363 @@
                 pltpu.VMEM((HEAD_WIDTH, 4 * BLK), F32),
             ],
         ),
-        compiler_params=pltpu.CompilerParams(vmem_limit_bytes=55 * 1024 * 1024),
+        compiler_params=pltpu.CompilerParams(vmem_limit_bytes=ROOM),
         name="attend_back",
         cost_estimate=cost(24),
-    )(*plan, queries, d_heads, kv, positions, starts, lse, dots)
+    )(*plan, queries, heads, d_attn, wo_t, kv, positions, starts, lse)
+
+
+def expert_kernel(side, x_ref, cot_ref, gate_ref, g_own, u_own, d_own, g_other, u_other, d_other, y_ref, dx_ref, dot_ref, a_ref, dg_ref, du_ref, dy_ref, gate_w, up_w, down_w, gate_f, up_f, down_f, sems):
+    half = g_other.shape[1]
+    own_copies, other_copies = [], []
+    for at, (own, other, whole, stage, columns) in enumerate(
+        (
+            (g_own, g_other, gate_w, gate_f, True),
+            (u_own, u_other, up_w, up_f, True),
+            (d_own, d_other, down_w, down_f, False),
+        )
+    ):
+        span = pl.ds(half, half)
+        target = whole.at[pl.ds(0, whole.shape[0]), span] if columns else whole.at[span]
+        own_copies.append(pltpu.make_async_copy(own.at[side[0]], stage, sems.at[at, 0]))
+        other_copies.append(pltpu.make_async_copy(other, target, sems.at[at, 1]))
+
+    @pl.when(pl.program_id(0) == 0)
+    def _():
+        for copy in own_copies + other_copies:
+            copy.start()
+        own_copies[0].wait()
+        gate_w[:, :half] = gate_f[...].astype(BF)
+        own_copies[1].wait()
+        up_w[:, :half] = up_f[...].astype(BF)
+        own_copies[2].wait()
+        down_w[:half, :] = down_f[...].astype(BF)
+        for copy in other_copies:
+            copy.wait()
+
+    x = x_ref[...]
+    gate_pre = matmul(x, gate_w[...])
+    up_pre = matmul(x, up_w[...])
+    sigma = 1.0 / (1.0 + jnp.exp(-gate_pre))
+    silu = gate_pre * sigma
+    activated = (silu * up_pre).astype(BF)
+    a_ref[...] = activated
+    gates = gate_ref[:, 0:1].astype(F32) + gate_ref[:, 64:65].astype(F32)
+    cot = cot_ref[...].astype(F32)
+    out = matmul(activated, down_w[...])
+    y_ref[...] = (out * gates).astype(BF)
+    dots = jnp.sum(out * cot, axis=1, keepdims=True)
+    high = dots.astype(BF).astype(F32)
+    lane = lax.broadcasted_iota(jnp.int32, dot_ref.shape, 1)
+    dot_ref[...] = jnp.where(lane < 64, high, dots - high).astype(BF)
+    d_pairs = (cot * gates).astype(BF)
+    dy_ref[...] = d_pairs
+    d_act = times_transposed(d_pairs, down_w[...])
+    d_gate = (d_act * up_pre * sigma * (1.0 + gate_pre * (1.0 - sigma))).astype(BF)
+    d_up = (d_act * silu).astype(BF)
+    dg_ref[...] = d_gate
+    du_ref[...] = d_up
+    dx_ref[...] = (times_transposed(d_gate, gate_w[...]) + times_transposed(d_up, up_w[...])).astype(BF)
+
+
+def run_expert(side, rows_in, cot, gates, own, other):
+    count, width = rows_in.shape
+    half = other[0].shape[1]
+    tile = 256
+    sds = jax.ShapeDtypeStruct
+
+    def by_rows(columns):
+        return pl.BlockSpec((tile, columns), lambda i, side: (i, 0))
+
+    return pl.pallas_call(
+        expert_kernel,
+        out_shape=(
+            sds((count, width), BF),
+            sds((count, width), BF),
+            sds((count, 128), BF),
+            sds((count, 2 * half), BF),
+            sds((count, 2 * half), BF),
+            sds((count, 2 * half), BF),
+            sds((count, width), BF),
+        ),
+        grid_spec=pltpu.PrefetchScalarGridSpec(
+            num_scalar_prefetch=1,
+            grid=(count // tile,),
+            in_specs=[by_rows(width), by_rows(width), by_rows(128)] + [ANY] * 6,
+            out_specs=[
+                by_rows(width),
+                by_rows(width),
+                by_rows(128),
+                by_rows(2 * half),
+                by_rows(2 * half),
+                by_rows(2 * half),
+                by_rows(width),
+            ],
+            scratch_shapes=[
+                pltpu.VMEM((width, 2 * half), BF),
+                pltpu.VMEM((width, 2 * half), BF),
+                pltpu.VMEM((2 * half, width), BF),
+                pltpu.VMEM((width, half), F32),
+                pltpu.VMEM((width, half), F32),
+                pltpu.VMEM((half, width), F32),
+                DMA((3, 2)),
+            ],
+        ),
+        compiler_params=pltpu.CompilerParams(vmem_limit_bytes=ROOM),
+        name="run_expert",
+        cost_estimate=cost(25),
+    )(side, rows_in, cot, gates, *own, *other)
+
+
+def expert_grads_kernel(side, x_ref, dy_ref, a_ref, dg_ref, du_ref, gate_ref, up_ref, down_ref, gate_out, up_out, down_out, a_t):
+    half = gate_ref.shape[-1]
+
+    @pl.when(pl.program_id(0) == 0)
+    def _():
+        a_t[...] = a_ref[...].T
+
+    x_t = x_ref[...].T
+    for grad_ref, own, other in ((dg_ref, gate_ref, gate_out), (du_ref, up_ref, up_out)):
+        value = matmul(x_t, grad_ref[...])
+        own[0] = value[:, :half]
+        other[...] = value[:, half:].astype(BF)
+    value = matmul(a_t[...], dy_ref[...])
+    down_ref[0] = value[:half]
+    down_out[...] = value[half:].astype(BF)
+
+
+def expert_grads(side, rows_in, d_pairs, activated, d_gate, d_up):
+    count, width = rows_in.shape
+    whole = activated.shape[1]
+    half = whole // 2
+    tile = 256
+    sds = jax.ShapeDtypeStruct
+    columns = pl.BlockSpec((count, tile), lambda i, side: (0, i))
+    full = pl.BlockSpec((count, whole), lambda i, side: (0, 0))
+    own_rows = pl.BlockSpec((1, tile, half), lambda i, side: (side[0], i, 0))
+    other_rows = pl.BlockSpec((tile, half), lambda i, side: (i, 0))
+    return pl.pallas_call(
+        expert_grads_kernel,
+        out_shape=(
+            sds((2, width, half), F32),
+            sds((2, width, half), F32),
+            sds((2, half, width), F32),
+            sds((width, half), BF),
+            sds((width, half), BF),
+            sds((half, width), BF),
+        ),
+        grid_spec=pltpu.PrefetchScalarGridSpec(
+            num_scalar_prefetch=1,
+            grid=(width // tile,),
+            in_specs=[columns, columns, full, full, full],
+            out_specs=[
+                own_rows,
+                own_rows,
+                pl.BlockSpec((1, half, tile), lambda i, side: (side[0], 0, i)),
+                other_rows,
+                other_rows,
+                pl.BlockSpec((half, tile), lambda i, side: (0, i)),
+            ],
+            scratch_shapes=[pltpu.VMEM((whole, count), BF)],
+        ),
+        compiler_params=pltpu.CompilerParams(vmem_limit_bytes=ROOM),
+        name="expert_grads",
+        cost_estimate=cost(12),
+    )(side, rows_in, d_pairs, activated, d_gate, d_up)
+
+
+def place_kernel(side, *refs):
+    for at in range(3):
+        refs[6 + at][0] = refs[at][...].astype(F32)
+
+
+def place_other(side, arrived, placed):
+    tile = 256
+    width, half = arrived[0].shape
+    rows_in = pl.BlockSpec((tile, half), lambda i, side: (i, 0))
+    rows_out = pl.BlockSpec((1, tile, half), lambda i, side: (1 - side[0], i, 0))
+    return pl.pallas_call(
+        place_kernel,
+        out_shape=[jax.ShapeDtypeStruct(value.shape, F32) for value in placed],
+        grid_spec=pltpu.PrefetchScalarGridSpec(
+            num_scalar_prefetch=1,
+            grid=(width // tile,),
+            in_specs=[rows_in, rows_in, pl.BlockSpec((half, tile), lambda i, side: (0, i))] + [ANY] * 3,
+            out_specs=[
+                rows_out,
+                rows_out,
+                pl.BlockSpec((1, half, tile), lambda i, side: (1 - side[0], 0, i)),
+            ],
+        ),
+        input_output_aliases={4: 0, 5: 1, 6: 2},
+        compiler_params=pltpu.CompilerParams(vmem_limit_bytes=ROOM),
+        name="place_other",
+        cost_estimate=cost(5),
+    )(side, *arrived, *placed)
+
+
+def project_kernel(t_ref, w_ref, side_ref, flag_ref, cos_ref, sin_ref, ga_ref, gq_ref, gk_ref, h_ref, q_ref, kv_ref, qp_ref, kp_ref):
+    rows = t_ref[...].astype(F32)
+    inverse = lax.rsqrt(jnp.mean(rows * rows, axis=1, keepdims=True) + EPSILON)
+    hidden = (rows * inverse * ga_ref[...]).astype(BF)
+    h_ref[...] = hidden
+    qkv = matmul(hidden, w_ref[...])
+    own = qkv[:, 2 * HEAD_WIDTH :]
+    other = matmul(hidden, side_ref[...])
+    first = flag_ref[0:1, :] > 0.5
+    cosine, sine_tab = cos_ref[...], sin_ref[...]
+
+    def turned(value, gain):
+        root = lax.rsqrt(jnp.mean(value * value, axis=1, keepdims=True) + EPSILON)
+        value = value * root * gain
+        return (value * cosine + pltpu.roll(value, HEAD_WIDTH // 2, 1) * sine_tab).astype(BF)
+
+    for head in range(2):
+        span = slice(head * HEAD_WIDTH, (head + 1) * HEAD_WIDTH)
+        q_ref[:, span] = turned(qkv[:, span], gq_ref[...])
+    qp_ref[...] = qkv[:, : 2 * HEAD_WIDTH]
+    keys = jnp.where(first, own, other)
+    kp_ref[...] = keys
+    kv_ref[:, :HEAD_WIDTH] = turned(keys, gk_ref[...])
+    kv_ref[:, HEAD_WIDTH:] = jnp.where(first, other, own).astype(BF)
+
+
+def project(tokens, weights, side, first, cosine, sine_tab, gain, gain_query, gain_key):
+    rows, width = tokens.shape
+    tile = 256
+    sds = jax.ShapeDtypeStruct
+
+    def by_rows(columns):
+        return pl.BlockSpec((tile, columns), lambda i: (i, 0))
+
+    def whole(value):
+        return pl.BlockSpec(value.shape, lambda i: (0, 0))
+
+    return pl.pallas_call(
+        project_kernel,
+        grid=(rows // tile,),
+        out_shape=(
+            sds((rows, width), BF),
+            sds((rows, 256), BF),
+            sds((rows, 256), BF),
+            sds((rows, 256), F32),
+            sds((rows, 128), F32),
+        ),
+        in_specs=[
+            by_rows(width),
+            whole(weights),
+            whole(side),
+            whole(first),
+            by_rows(128),
+            by_rows(128),
+            whole(gain),
+            whole(gain_query),
+            whole(gain_key),
+        ],
+        out_specs=[by_rows(width), by_rows(256), by_rows(256), by_rows(256), by_rows(128)],
+        compiler_params=pltpu.CompilerParams(vmem_limit_bytes=ROOM),
+        name="project",
+        cost_estimate=cost(8),
+    )(tokens, weights, side, first, cosine, sine_tab, gain, gain_query, gain_key)
+
+
+def project_back_kernel(dq_ref, ds_ref, qp_ref, kp_ref, cos_ref, sin_ref, h_ref, w_ref, side_ref, gq_ref, gk_ref, flag_ref, part_ref, late_ref, side_w, total, gains):
+    step = pl.program_id(0)
+    cosine, sine_tab = cos_ref[...], sin_ref[...]
+    key, first, own = flag_ref[0:1, :], flag_ref[1:2, :], flag_ref[2:3, :]
+    heads = 2 * HEAD_WIDTH
+
+    @pl.when(step == 0)
+    def _():
+        gains[...] = jnp.zeros_like(gains)
+        total[...] = jnp.zeros_like(total)
+        side_w[...] = jnp.where(
+            own > 0.5, w_ref[:, heads:].astype(F32), side_ref[...].astype(F32)
+        ).astype(BF)
+
+    def back(gradient, value, gain):
+        gradient = gradient * cosine - pltpu.roll(gradient, HEAD_WIDTH // 2, 1) * sine_tab
+        root = lax.rsqrt(jnp.mean(value * value, axis=1, keepdims=True) + EPSILON)
+        weighted = gradient * gain
+        mean_term = jnp.mean(weighted * value, axis=1, keepdims=True)
+        terms = jnp.sum(gradient * value * root, axis=0, keepdims=True)
+        return root * weighted - value * (root * root * root) * mean_term, terms
+
+    columns = []
+    for head in range(2):
+        span = slice(head * HEAD_WIDTH, (head + 1) * HEAD_WIDTH)
+        value, terms = back(dq_ref[:, span], qp_ref[:, span], gq_ref[...])
+        columns.append(value.astype(BF))
+        gains[0:1, :] += terms
+    d_side = ds_ref[...]
+    value, terms = back(d_side, kp_ref[...], gk_ref[...])
+    mine = jnp.where(first == (step // 2).astype(F32), 1.0, 0.0)
+    columns.append((jnp.where(key > 0.5, value, d_side) * mine).astype(BF))
+    gains[1:2, :] += terms * key * mine
+    d_all = jnp.concatenate(columns, axis=1)
+    part_ref[...] = (
+        times_transposed(d_all[:, :heads], w_ref[:, :heads])
+        + times_transposed(d_all[:, heads:], side_w[...])
+    ).astype(BF)
+    total[...] += transposed_times(h_ref[...], d_all)
+
+    @pl.when(step == pl.num_programs(0) - 1)
+    def _():
+        pieces, depth = late_ref.shape[0], h_ref.shape[1] // late_ref.shape[0]
+        for at in range(3):
+            value = total[:, at * HEAD_WIDTH : (at + 1) * HEAD_WIDTH].astype(BF)
+            late_ref[:, at * depth : (at + 1) * depth, :] = value.reshape(pieces, depth, HEAD_WIDTH)
+        late_ref[:, 3 * depth :, :] = jnp.broadcast_to(
+            gains[...].astype(BF)[None], (pieces,) + gains.shape
+        )
+
+
+def project_back(d_queries, d_side, q_pre, k_pre, cosine, sine_tab, hidden, weights, side, gain_query, gain_key, flags):
+    rows = d_queries.shape[0]
+    width = hidden.shape[1]
+    tile = 256
+    tiles = rows // tile
+    owners = 64
+    sds = jax.ShapeDtypeStruct
+    late = (owners, 3 * width // owners + 16, 128)
+
+    def by_rows(columns):
+        return pl.BlockSpec((tile, columns), lambda i: (i, 0))
+
+    def whole(value):
+        return pl.BlockSpec(value.shape, lambda i: (0, 0))
+
+    half_rows = pl.BlockSpec((tile, 128), lambda i: (i % (tiles // 2), 0))
+    return pl.pallas_call(
+        project_back_kernel,
+        grid=(tiles,),
+        out_shape=(sds((rows, width), BF), sds(late, BF)),
+        in_specs=[
+            by_rows(256),
+            half_rows,
+            by_rows(256),
+            by_rows(128),
+            by_rows(128),
+            by_rows(128),
+            by_rows(width),
+            whole(weights),
+            whole(side),
+            whole(gain_query),
+            whole(gain_key),
+            whole(flags),
+        ],
+        out_specs=[by_rows(width), pl.BlockSpec(late, lambda i: (0, 0, 0))],
+        scratch_shapes=[
+            pltpu.VMEM((width, 128), BF),
+            pltpu.VMEM((width, 384), F32),
+            pltpu.VMEM((16, 128), F32),
+        ],
+        compiler_params=pltpu.CompilerParams(vmem_limit_bytes=ROOM),
+        name="project_back",
+        cost_estimate=cost(12),
+    )(
+        d_queries, d_side, q_pre, k_pre, cosine, sine_tab, hidden, weights, side, gain_query, gain_key, flags
+    )
 
 
 def after(value, earlier):
@@ -902,29 +1314,30 @@
     row_tokens = 8 * rows
     row_blocks = row_tokens // BLK
 
-    def of_mine(weight):
-        return to_low(lax.dynamic_index_in_dim(weight, wsh, 0, keepdims=False))
-
-    def of_other(weight):
-        return to_low(lax.dynamic_index_in_dim(weight, 1 - wsh, 0, keepdims=False))
-
     def swap(value):
         return lax.ppermute(value, "wsh", [(0, 1), (1, 0)])
 
     depth = w_query.shape[0]
     q_part = to_low(w_query).reshape(depth, 8, 256).transpose(1, 0, 2)
-    k_part = jnp.repeat(to_low(key_weight).reshape(depth, 2, 128).transpose(1, 0, 2), 4, axis=0)
-    v_part = jnp.repeat(to_low(value_weight).reshape(depth, 2, 128).transpose(1, 0, 2), 4, axis=0)
-    w_pack = jnp.concatenate([q_part, k_part, v_part], axis=2)
+    sides = [
+        to_low(value[:, head * 128 : head * 128 + 128])
+        for head in (0, 0, 1, 1)
+        for value in (key_weight, value_weight)
+    ]
+    w_pack = jnp.concatenate([q_part, jnp.stack(sides)], axis=2)
     small = jnp.concatenate(
         [lanes_to(gain_attn[None, :]), lanes_to(gain_ffn[None, :]), jnp.zeros((6, 128), F32)], axis=0
     )
-    w_all, row_rows, small_all, chip_routes, chip_cot = gather_first(
-        w_pack, tokens, small, routes.T, cotangent
-    )
-    other_gate, small_all = after(of_other(w_gate), small_all)
-    gate_back = swap(other_gate)
-    w_qkv = w_all.reshape(width, 512)
+    w_all, row_rows, small_all, chip_routes, chip_cot, other_gate, other_up, other_down, w_side = gather_first(
+        w_pack, tokens, small, routes.T, cotangent, (w_gate, w_up, w_down)
+    )
+    w_main = w_all.reshape(width, 384)
+    w_side = w_side.reshape(width, 128)
+    is_key = lax.rem(lax.div(me, 2), 2) == 0
+
+    def flag(value):
+        return jnp.broadcast_to(value.astype(F32).reshape(1, 1), (8, 128))
+
     g_attn = to_low(small_all[:, 0, :depth].reshape(width)).astype(F32)
     g_ffn = to_low(small_all[:, 1, :depth].reshape(width)).astype(F32)
     g_query = rounded(gain_query)
@@ -991,32 +1404,26 @@
 
     q_pos, q_start = strips(positions), strips(starts)
 
-    stream = row_rows.reshape(row_tokens, width).astype(F32)
-    inverse_one = inverse_root(stream)
-    hidden_one = to_low(stream * inverse_one * g_attn)
-    qkv = matmul(hidden_one, w_qkv)
-    q_pre = qkv[:, :256].reshape(row_tokens, 2, HEAD_WIDTH)
-    k_pre = qkv[:, 256:384]
-    q_inverse = inverse_root(q_pre)
-    k_inverse = inverse_root(k_pre)
-    queries = to_low(rotate(q_pre * q_inverse * g_query, cosine[:, None], sine_tab[:, None]))
-    queries = queries.reshape(row_tokens, 256)
-    keys = to_low(rotate(k_pre * k_inverse * g_key, cosine, sine_tab))
-    kv = jnp.concatenate([keys, to_low(qkv[:, 384:])], axis=1)
-    (gate_back, late_all), kv = after((gate_back, late_all), kv)
+    row_rows = row_rows.reshape(row_tokens, width)
+    hidden_one, queries, kv, q_pre, k_pre = project(
+        row_rows, w_main, w_side, flag(core == 0), cosine, sine_tab, g_attn[None, :], g_query[None, :], g_key[None, :]
+    )
+    kv_all = gather_keys(kv, 1).reshape(block_count * BLK, 256)
+    late_all, kv_all = after(late_all, kv_all)
     wo_t = late_all[:, :256]
     wr = late_all[:, 256:]
-    kv_all = gather_keys(kv, 1).reshape(block_count * BLK, 256)
-    (cot_rows, other_up), kv_all = after((cot_rows, of_other(w_up)), kv_all)
-    up_back = swap(other_up)
+    (cot_rows, other_gate), kv_all = after((cot_rows, other_gate), kv_all)
+    gate_back = swap(other_gate)
     cot_there = exchange_behind(cot_rows.reshape(chips, slots, width)).reshape(chips * slots, width)
     heads, lse = attend(plan, queries, kv_all, q_pos, q_start)
 
     attn_parts = to_low(times_transposed(heads, wo_t)).reshape(8, rows, width)
-    (up_back, cot_there, other_down), attn_parts = after((up_back, cot_there, of_other(w_down)), attn_parts)
-    down_back = swap(other_down)
+    (gate_back, cot_there, other_up, other_down), attn_parts = after(
+        (gate_back, cot_there, other_up, other_down), attn_parts
+    )
+    up_back = swap(other_up)
     attn_total = reduce_row(attn_parts, 2, True)[0].reshape(2 * rows, width)
-    chip_stream = lax.dynamic_slice_in_dim(stream, (place - core) * rows, 2 * rows, 0)
+    chip_stream = lax.dynamic_slice_in_dim(row_rows, (place - core) * rows, 2 * rows, 0).astype(F32)
     chip_residual = chip_stream + attn_total
     chip_inverse_two = inverse_root(chip_residual)
     chip_hidden = to_low(chip_residual * chip_inverse_two * g_ffn)
@@ -1031,52 +1438,50 @@
         return lax.dynamic_slice_in_dim(value, core * rows, rows, 0)
 
     out_rows = matmul(pick_low, chip_hidden).astype(BF).reshape(chips, slots, width)
-    my_gates = my_quarter(gates)
-    slot_gates = jnp.sum(jnp.where(pick, my_gates[:, None, :], 0.0), axis=2)
-    gate_tile = jnp.pad(slot_gates[:, None, :], ((0, 0), (0, 7), (0, 128 - slots)))
+    expert_of = jnp.repeat(4 * chip_ids + quarter, slots)
+    of_expert = expert_of[:, None] == jnp.arange(experts, dtype=jnp.int32)[None, :]
+
+    def parted(value):
+        high = to_low(value)
+        return high, to_low(value - high.astype(F32))
+
+    slot_gates = [
+        jnp.sum(jnp.where(of_expert, matmul(pick_low, part), 0.0), axis=1, keepdims=True)
+        for part in parted(gates)
+    ]
+    gate_tile = to_low(
+        jnp.where(jnp.arange(128)[None, :] < 64, slot_gates[0], slot_gates[1])
+    ).reshape(chips, slots, 128)
+    (up_back, other_down), gate_tile = after((up_back, other_down), gate_tile)
+    down_back = swap(other_down)
     arrived, gate_there = exchange([out_rows, gate_tile], 3)
     arrived = arrived.reshape(chips * slots, width)
-    gate_col = gate_there[:, 0, :slots].reshape(chips * slots, 1)
-    d_pairs = to_low(gate_col * cot_there.astype(F32))
-    gate_w = (of_mine(w_gate), gate_back)
-    up_w = (of_mine(w_up), up_back)
-    down_w = (of_mine(w_down), down_back)
-    expert_out = 0.0
-    d_rows = 0.0
-    grads = []
-    for gate_half, up_half, down_half in zip(gate_w, up_w, down_w):
-        gate_pre = matmul(arrived, gate_half)
-        up_pre = matmul(arrived, up_half)
-        sigma = jax.nn.sigmoid(gate_pre)
-        activated = to_low(gate_pre * sigma * up_pre)
-        expert_out = expert_out + matmul(activated, down_half)
-        d_act = times_transposed(d_pairs, down_half)
-        grad_down = transposed_times(activated, d_pairs)
-        d_gate_pre = to_low(d_act * up_pre * sigma * (1.0 + gate_pre * (1.0 - sigma)))
-        d_up_pre = to_low(d_act * gate_pre * sigma)
-        grad_gate = transposed_times(arrived, d_gate_pre)
-        grad_up = transposed_times(arrived, d_up_pre)
-        d_rows = (
-            d_rows + times_transposed(d_gate_pre, gate_half) + times_transposed(d_up_pre, up_half)
-        )
-        grads.append((grad_gate, grad_up, grad_down))
-    d_gate_slots = jnp.sum(expert_out * cot_there.astype(F32), axis=1).reshape(chips, 1, slots)
-    d_gate_tile = jnp.pad(d_gate_slots, ((0, 0), (0, 7), (0, 128 - slots)))
+    side = wsh.reshape(1)
+    gate_there = gate_there.reshape(chips * slots, 128)
+    y_rows, d_rows, d_gate_slots, activated, d_gate_pre, d_up_pre, d_pairs = run_expert(
+        side, arrived, cot_there, gate_there, (w_gate, w_up, w_down), (gate_back, up_back, down_back)
+    )
+    *own_grads, other_gate, other_up, other_down = expert_grads(
+        side, arrived, d_pairs, activated, d_gate_pre, d_up_pre
+    )
+    gate_grad_back = swap(other_gate)
+    (other_up, other_down), d_gate_slots = after((other_up, other_down), d_gate_slots)
     d_back, d_gate_back = exchange(
-        [to_low(d_rows).reshape(chips, slots, width), d_gate_tile], 4
-    )
-    y_back = exchange_behind(to_low(gate_col * expert_out).reshape(chips, slots, width))
-    swapped_grads = [swap(to_low(back)) for back in grads[1]]
+        [d_rows.reshape(chips, slots, width), d_gate_slots.reshape(chips, slots, 128)], 4
+    )
+    (y_rows, gate_grad_back), d_back = after((y_rows, gate_grad_back), d_back)
+    y_back = exchange_behind(y_rows.reshape(chips, slots, width))
 
     def collect(back):
         return to_low(transposed_times(pick_low, back.reshape(chips * slots, width))).reshape(2, rows, width)
 
-    d_gate_slots = d_gate_back[:, 0, :slots]
-    d_gates_mine = jnp.sum(jnp.where(pick, d_gate_slots[:, :, None], 0.0), axis=1)
-    d_gates_part = jnp.where(
-        jnp.arange(4, dtype=jnp.int32)[None, :, None] == quarter[:, None, None], d_gates_mine[:, None, :], 0.0
-    ).reshape(experts, 2 * rows)
-    d_gates_part = d_gates_part.T.reshape(2, rows, experts)
+    d_gate_back = d_gate_back.reshape(chips * slots, 128)
+    d_gates_part = sum(
+        transposed_times(
+            pick_low, jnp.where(of_expert, d_gate_back[:, at : at + 1], jnp.zeros((), BF))
+        )
+        for at in (0, 64)
+    ).reshape(2, rows, experts)
     d_hidden_moe, d_gates = reduce_chip(collect(d_back), d_gates_part, 5)
     residual = my_rows(chip_residual)
 
@@ -1091,19 +1496,13 @@
     d_residual = cotangent.astype(F32) + d_res_norm
     gain_ffn_part = jnp.sum(ffn_gain_terms, axis=0)
 
+    other_up, d_residual = after(other_up, d_residual)
+    up_grad_back = swap(other_up)
     d_attn = gather_row(to_low(d_residual), 7).reshape(row_tokens, width)
+    (y_back, up_grad_back), d_attn_late = after((y_back, up_grad_back), d_attn)
+    other_down, up_grad_back = after(other_down, up_grad_back)
+    down_grad_back = swap(other_down)
     grad_out_t = transposed_times(d_attn, heads)
-    d_heads = to_low(matmul(d_attn, wo_t))
-    dots = jnp.sum(
-        d_heads.astype(F32).reshape(row_tokens, 2, HEAD_WIDTH)
-        * heads.astype(F32).reshape(row_tokens, 2, HEAD_WIDTH),
-        axis=-1,
-    )
-    dot_strips = (
-        jnp.take(dots.reshape(row_blocks, BLK, 2), order, axis=0)
-        .transpose(0, 2, 1)
-        .reshape(row_blocks // 2, 1, 4 * BLK)
-    )
     early = jnp.concatenate(
         [
             to_low(grad_out_t[:, :128]).reshape(64, depth, 128),
@@ -1116,44 +1515,34 @@
         axis=1,
     )
     early = lax.all_to_all(early, "ctx", split_axis=0, concat_axis=0, tiled=True)
-    y_back, d_heads = after(y_back, d_heads)
-    d_queries, d_kv = attend_back(plan, queries, d_heads, kv_all, q_pos, q_start, lse, dot_strips)
-    (early, swapped_grads), d_kv = after((early, swapped_grads), d_kv)
+    d_queries, d_kv = attend_back(plan, queries, heads, d_attn_late, wo_t, kv_all, q_pos, q_start, lse)
+    (early, down_grad_back), d_kv = after((early, down_grad_back), d_kv)
+    swapped_grads = (gate_grad_back, up_grad_back, down_grad_back)
     d_side = reduce_keys(d_kv, 8)
-    is_key = lax.rem(lax.div(me, 2), 2) == 0
-    half_rows = row_tokens // 2
-
-    def half_of(value):
-        return lax.dynamic_slice_in_dim(value, core * half_rows, half_rows, 0)
-
-    d_k_norm = rotate_back(d_side, half_of(cosine), half_of(sine_tab))
-    d_k_pre, key_gain_terms = norm_back(half_of(k_pre), half_of(k_inverse), g_key, d_k_norm)
-    key_gain_part = jnp.where(is_key, jnp.sum(key_gain_terms, axis=0), 0.0)
-    d_side_pre = to_low(jnp.where(is_key, d_k_pre, d_side))
-    d_q_norm = rotate_back(
-        d_queries.reshape(row_tokens, 2, HEAD_WIDTH), cosine[:, None], sine_tab[:, None]
-    )
-    d_q_pre, query_gain_terms = norm_back(q_pre, q_inverse, g_query, d_q_norm)
-    query_gain_part = jnp.sum(query_gain_terms, axis=(0, 1))
-    d_q_pre = to_low(d_q_pre.reshape(row_tokens, 256))
-    side_w = jnp.where(is_key, w_qkv[:, 256:384], w_qkv[:, 384:])
-    d_side_full = jnp.where(
-        (jnp.arange(row_tokens, dtype=jnp.int32) // half_rows == core)[:, None],
-        jnp.concatenate([d_side_pre, d_side_pre], axis=0),
-        jnp.zeros((), BF),
-    )
-    d_all = jnp.concatenate([d_q_pre, d_side_full], axis=1)
-    d_hidden_parts = to_low(
-        times_transposed(d_all, jnp.concatenate([w_qkv[:, :256], side_w], axis=1))
-    ).reshape(8, rows, width)
-    grad_in = to_low(transposed_times(hidden_one, d_all))
-    tail = jnp.broadcast_to(
-        jnp.pad(to_low(jnp.stack([query_gain_part, key_gain_part])), ((0, 14), (0, 0)))[None],
-        (64, 16, 128),
-    )
-    late = jnp.concatenate(
-        [grad_in[:, 128 * i : 128 * i + 128].reshape(64, depth, 128) for i in range(3)] + [tail], axis=1
-    )
+    flags = jnp.concatenate(
+        [
+            flag(is_key)[:1],
+            flag(core)[:1],
+            flag(is_key == (core == 0))[:1],
+            jnp.zeros((5, 128), F32),
+        ],
+        axis=0,
+    )
+    d_hidden_parts, late = project_back(
+        d_queries,
+        d_side,
+        q_pre,
+        k_pre,
+        cosine,
+        sine_tab,
+        hidden_one,
+        w_main,
+        w_side,
+        g_query[None, :],
+        g_key[None, :],
+        flags,
+    )
+    d_hidden_parts = d_hidden_parts.reshape(8, rows, width)
     late, d_hidden_parts = after(late, d_hidden_parts)
     late = lax.all_to_all(late, "ctx", split_axis=0, concat_axis=0, tiled=True)
     d_hidden_one, moe_total = reduce_row(d_hidden_parts, 9, False, collect(y_back))
@@ -1163,11 +1552,7 @@
     grad_tokens = d_residual + d_stream_norm
 
 
-    def paired(own, back):
-        back = back.astype(F32)
-        return jnp.where(wsh == 0, jnp.stack([own, back]), jnp.stack([back, own]))
-
-    grad_gate, grad_up, grad_down = [paired(own, back) for own, back in zip(grads[0], swapped_grads)]
+    grad_gate, grad_up, grad_down = place_other(side, swapped_grads, own_grads)
 
     def summed(value, terms):
         return jnp.sum(value.astype(F32).reshape((8,) + terms + value.shape[1:]), axis=0)

time: 827 us -> 680 us (0.82); the launches traced: 829 us -> 670 us
  matrix products: 127 us -> 29.4 us
  other arithmetic: 82.5 us -> 37.3 us
  Pallas kernels: 431 us -> 473 us
  waiting for transfers between devices: 69.3 us -> 40.9 us
  local copies, waits for them, and re-layouts: 56.2 us -> 30.3 us
    pallas_call x0 -> x5, Pallas kernels: none -> 68.7 us  [the longest x1 26 us: run_expert(): pl.pallas_call(expert_kernel, out_shape=(sds((count, width), BF), sds((co...]
    dot_general x9 -> x2, matrix products: 49.3 us -> 6.26 us  [times_transposed(): lax.dot_general(left, right, (((1,), (1,)), ((), ())), preferred_element_...]
    pallas_call x1, Pallas kernels: 59.4 us -> 25.9 us  [gather_row(): pl.pallas_call(body, out_shape=jax.ShapeDtypeStruct((8,) + block.shape, b...]
    dot_general x11 -> x5, matrix products: 42 us -> 8.77 us  [matmul(): return jnp.dot(left, right, preferred_element_type=jnp.float32)]
    dot_general x11 -> x6, matrix products: 35.1 us -> 14.2 us  [transposed_times(): lax.dot_general(left, right, (((0,), (0,)), ((), ())), preferred_element_...]
    pallas_call x2, Pallas kernels: 75.1 us -> 89.1 us  [reduce_row(): pl.pallas_call(body, out_shape=shapes, in_specs=[VMEM] * len(operands), o...]
    select_n x8 -> x0, other arithmetic: 10.7 us -> none  [the longest x3 9.45 us: paired(): return jnp.where(wsh == 0, jnp.stack([own, back]), jnp.stack([back, own]))]
    pallas_call x2, Pallas kernels: 99 us -> 89 us  [exchange(): pl.pallas_call(body, out_shape=[jax.ShapeDtypeStruct(a.shape, a.dtype) fo...]
  transfers between devices with their start and end apart: 11 -> 11, of which waited for: 6 -> 2; matrix products, arithmetic and copies ran while one was open for 19% -> 11% of each run, Pallas kernels for 14% -> 43%
where the time goes in v3:
time: 680 us; the launch traced here: 670 us
  Pallas kernels  473 us (70%)
  starting transfers between devices  51.6 us (8%)
  waiting for transfers between devices  40.9 us (6%)
  other arithmetic  37.3 us (5%)
  local copies, waits for them, and re-layouts  30.3 us (4%)
  matrix products  29.4 us (4%)
    pallas_call x2, Pallas kernels, reduce_row(): pl.pallas_call(body, out_shape=shapes, in_specs=[VMEM] * len(operands), o...  89.1 us
    pallas_call x2, Pallas kernels, exchange(): pl.pallas_call(body, out_shape=[jax.ShapeDtypeStruct(a.shape, a.dtype) fo...  89 us
    pallas_call x1, Pallas kernels, gather_first(): pl.pallas_call(body, out_shape=(sds((64,) + weights.shape[1:], weights.dt...  53.5 us
    ppermute x6, waiting for transfers between devices, swap(): return lax.ppermute(value, 'wsh', [(0, 1), (1, 0)])  40.9 us
    pallas_call x1, Pallas kernels, reduce_keys(): pl.pallas_call(body, out_shape=jax.ShapeDtypeStruct(block, F32), in_specs...  38.3 us
    pallas_call x1, Pallas kernels, attend_back(): pl.pallas_call(backward_kernel, out_shape=(sds(queries.shape, F32), sds(d...  34.9 us
    pallas_call x1, Pallas kernels, gather_keys(): pl.pallas_call(body, out_shape=jax.ShapeDtypeStruct((8,) + rows.shape, ro...  33 us
    pallas_call x1, Pallas kernels, run_expert(): pl.pallas_call(expert_kernel, out_shape=(sds((count, width), BF), sds((co...  26 us
  transfers between devices with their start and end apart: 11, of which 2 were waited for; matrix products, arithmetic and copies ran while one was open for 11% of the time, Pallas kernels for 43%

profile of v3, /device:TPU:0, one launch (start us, length us, event | category | flops | bytes accessed | tf_op | source)
XLA Modules:
  0.0 669.6 jit_solution(7367570184471396965)
XLA Ops:
  6.5 53.5 %gather_first.1 = (bf16[64,32,384]{2,1,0:T(8,128)(2,1)}, bf16[8,128,2048]{2,1,0:T(8,128)(2,1)}, f32[64,8,128]{2,1,0:T(8,128)}, s32[2,8,128]{2,1,0:T(8,128)}, bf1...) custom-call(bf16[8,32,384]{2,1,0:T(8,128)(2,1)} %pad_maximum_fusion., ...), custom_call_target="tpu_custom_call" | custom-call | bytes 72000000 | tf_op jit(solution)/shard_map/gather_first/pallas_call | solution.py:279
  60.1 1.3 tile.4
  61.4 5.9 all-to-all-start
  67.3 1.8 fusion.40
  71.4 1.9 fusion.29
  73.3 1.3 pad_maximum_fusion
  75.9 9.2 %project.1 = (bf16[1024,2048]{1,0:T(8,128)(2,1)}, bf16[1024,256]{1,0:T(8,128)(2,1)}, bf16[1024,256]{1,0:T(8,128)(2,1)}, f32[1024,256]{1,0:T(8,128)}, f32[1024,128]{1,0:T(8,128)}) custom-call(bf16[1024,2048]{1,0:T(8,128)(2,1)} %bitcast.183, bf16[2048,384]{1,0:T(8,128)(2,1)} %bitcast.185, bf16[2048,128]{1,0:T(8,128)(2,1)} %bitcast.193, ...), custom_call_target="tpu_custom_call" | custom-call | bytes 9600000 | tf_op jit(solution)/shard_map/project/pallas_call | solution.py:1151
  85.1 33.0 %gather_keys.1 = bf16[8,1024,256]{2,1,0:T(8,128)(2,1)} custom-call(bf16[1024,256]{1,0:T(8,128)(2,1)} %get-tuple-element.100.src), custom_call_target="tpu_custom_call" | custom-call | bytes 36000000 | tf_op jit(solution)/shard_map/gather_keys/pallas_call | solution.py:371
  118.3 2.6 convolution_convert_fusion.2
  120.9 1.2 copy-done.1
  122.1 9.3 %all-to-all-start.1 = ((bf16[32,24,2048]{2,1,0:T(8,128)(2,1)}), bf16[32,24,2048]{2,1,0:T(8,128)(2,1)S(1)}, u32[]{:S(2)}, u32[]{:S(2)}) async-start(bf16[32,24,2048]{2,1,0:T(8,128)(2,1)} %bitcast.27), calls=%async_computation.1 | async-start | bytes 6291456 | tf_op jit(solution)/shard_map/all_to_all | solution.py:710
  139.9 1.4 eq.115
  142.1 1.3 reduce_min.18
  143.4 1.2 compare_select_fusion.1
  145.1 1.8 scatter_custom_fusion.inverse
  147.6 1.2 maximum_minimum_fusion
  148.8 21.1 %attend.1 = (bf16[1024,256]{1,0:T(8,128)(2,1)}, f32[8,1,256]{2,1,0:T(1,128)}) custom-call(s32[16]{0:T(128)} %copy-done.20, s32[8]{0:T(128)} %get-tuple-element.191.low, s32[8]{0:T(128)} %get-tuple-element.189.inner_low, s32[8]{0:T(128)} %get-tuple-element.188.inner_high, s32[8]{0:T(128)} %get-tuple-element.190.high, s32[128]{0:T(128)} %scatter_custom_fusion.inverse, ...), custom_call_target="tpu_custom_call" | custom-call | bytes 20400000 | tf_op jit(solution)/shard_map/attend/pallas_call | solution.py:799
  169.9 4.3 convolution_convert_fusion
  174.3 1.7 copy-done
  175.9 41.2 %reduce_row.2 = f32[2,128,2048]{2,1,0:T(8,128)} custom-call(bf16[8,128,2048]{2,1,0:T(8,128)(2,1)} %bitcast.172), custom_call_target="tpu_custom_call" | custom-call | bytes 48000000 | tf_op jit(solution)/shard_map/reduce_row/pallas_call | solution.py:505
  217.1 2.2 multiply_reduce_fusion
  219.3 1.0 collective-permute-start.1
  220.6 1.9 fusion.69
  224.0 1.2 fusion.4
  225.3 1.6 select_convert_fusion.refs_1_
  226.9 29.5 %collective-permute-done.1.u_other = bf16[2048,384]{1,0:T(8,128)(2,1)} collective-permute-done((bf16[2048,384]{1,0:T(8,128)(2,1)}, bf16[2048,384]{1,0:T(8,128)(2,1)}, u32[]{:S(2)}, u32[]{:S(2)}) %collective-permute-start.1) | collective-permute-done | bytes 1572896 | tf_op jit(solution)/shard_map/ppermute | solution.py:1318
  256.4 1.3 collective-permute-start.2
  257.7 2.6 convolution_convert_fusion.1
  260.3 45.3 %exchange.2 = (bf16[32,24,2048]{2,1,0:T(8,128)(2,1)}, bf16[32,24,128]{2,1,0:T(8,128)(2,1)}) custom-call(bf16[32,24,2048]{2,1,0:T(8,128)(2,1)} %bitcast.173, bf16[32,24,128]{2,1,0:T(8,128)(2,1)} %select_convert_fusion.refs_1_), custom_call_target="tpu_custom_call" | custom-call | bytes 57600000 | tf_op jit(solution)/shard_map/exchange/pallas_call | solution.py:691
  305.7 1.1 copy-done.7
  306.8 26.0 %run_expert.1 = (bf16[768,2048]{1,0:T(8,128)(2,1)}, bf16[768,2048]{1,0:T(8,128)(2,1)}, bf16[768,128]{1,0:T(8,128)(2,1)}, bf16[768,768]{1,0:T(8,128)(2,1)}, bf16[...) custom-call(s32[1]{0:T(128)} %bitcast.33.side, bf16[768,2048]{1,0:T(8,128)(2,1)} %bitcast.176, ...), custom_call_target="tpu_custom_call" | custom-call | bytes 30000000 | tf_op jit(solution)/shard_map/run_expert/pallas_call | solution.py:987
  332.8 13.6 %expert_grads.1 = (f32[2,2048,384]{2,1,0:T(8,128)}, f32[2,2048,384]{2,1,0:T(8,128)}, f32[2,384,2048]{2,1,0:T(8,128)}, bf16[2048,384]{1,0:T(8,128)(2,1)}, bf16[20...) custom-call(s32[1]{0:T(128)} %bitcast.33.side, bf16[768,2048]{1,0:T(8,128)(2,1)} %bitcast.177, ...), custom_call_target="tpu_custom_call" | custom-call | bytes 14400000 | tf_op jit(solution)/shard_map/expert_grads/pallas_call | solution.py:1054
  346.4 1.1 collective-permute-start.3
  347.6 43.7 %exchange.3 = (bf16[32,24,2048]{2,1,0:T(8,128)(2,1)}, bf16[32,24,128]{2,1,0:T(8,128)(2,1)}) custom-call(bf16[32,24,2048]{2,1,0:T(8,128)(2,1)} %bitcast.191, bf16[32,24,128]{2,1,0:T(8,128)(2,1)} %bitcast.216), custom_call_target="tpu_custom_call" | custom-call | bytes 57600000 | tf_op jit(solution)/shard_map/exchange/pallas_call | solution.py:691
  391.3 1.3 slice_reduce_fusion
  392.9 1.0 convolution_add_fusion.1
  393.9 7.5 %all-to-all-start.2 = ((bf16[32,24,2048]{2,1,0:T(8,128)(2,1)}), bf16[32,24,2048]{2,1,0:T(8,128)(2,1)}, u32[]{:S(2)}, u32[]{:S(2)}) async-start(bf16[32,24,2048]{2,1,0:T(8,128)(2,1)} %bitcast.190), calls=%async_computation.2 | async-start | bytes 6291456 | tf_op jit(solution)/shard_map/all_to_all | solution.py:710
  401.4 3.9 fusion.1
  405.4 19.9 %reduce_chip.1 = (f32[128,2048]{1,0:T(8,128)}, f32[128,128]{1,0:T(8,128)}) custom-call(bf16[2,128,2048]{2,1,0:T(8,128)(2,1)} %bitcast.204, f32[2,128,128]{2,1,0:T(8,128)} %bitcast.217), custom_call_target="tpu_custom_call" | custom-call | bytes 20400000 | tf_op jit(solution)/shard_map/reduce_chip/pallas_call | solution.py:561
  425.3 1.0 multiply_reduce_fusion.4
  427.3 1.9 multiply_reduce_fusion.1
  430.8 25.9 %gather_row.1 = bf16[8,128,2048]{2,1,0:T(8,128)(2,1)} custom-call(bf16[128,2048]{1,0:T(8,128)(2,1)} %convert_element_type.228.src), custom_call_target="tpu_custom_call" | custom-call | bytes 31200000 | tf_op jit(solution)/shard_map/gather_row/pallas_call | solution.py:322
  456.8 1.4 convolution_convert_fusion.4
  458.1 3.6 convolution_convert_fusion.3
  461.9 1.4 fusion.3
  463.2 15.5 %all-to-all-start.3 = ((bf16[64,112,128]{2,1,0:T(8,128)(2,1)}), bf16[64,112,128]{2,1,0:T(8,128)(2,1)}, u32[]{:S(2)}, u32[]{:S(2)}) async-start(bf16[64,112,128]{2,1,0:T(8,128)(2,1)} %fusion.3), calls=%async_computation.3 | async-start | bytes 3670016 | tf_op jit(solution)/shard_map/all_to_all | solution.py:1517
  480.0 2.3 slice.110.wo_ref
  482.3 34.9 %attend_back.1 = (f32[1024,256]{1,0:T(8,128)}, bf16[2,8,2,512,128]{4,3,2,1,0:T(8,128)(2,1)}) custom-call(s32[16]{0:T(128)} %copy-done.20, s32[8]{0:T(128)} %get-tuple-element.191.low, s32[8]{0:T(128)} %get-tuple-element.189.inner_low, s32[8]{0:T(128)} %get-tuple-element.188.inner_high, s32[8]{0:T(128)} %get-tuple-element.190.high, ...), custom_call_target="tpu_custom_call" | custom-call | bytes 28800000 | tf_op jit(solution)/shard_map/attend_back/pallas_call | solution.py:893
  517.2 3.9 fusion.2
  521.1 11.3 %collective-permute-done.5.refs_2_ = bf16[384,2048]{1,0:T(8,128)(2,1)} collective-permute-done((bf16[384,2048]{1,0:T(8,128)(2,1)}, bf16[384,2048]{1,0:T(8,128)(2,1)}, u32[]{:S(2)}, u32[]{:S(2)}) %collective-permute-start.5) | collective-permute-done | bytes 1572896 | tf_op jit(solution)/shard_map/ppermute | solution.py:1318
  532.4 38.3 %reduce_keys.1.ds_ref = f32[512,128]{1,0:T(8,128)} custom-call(bf16[2,8,2,512,128]{4,3,2,1,0:T(8,128)(2,1)} %get-tuple-element.147.src), custom_call_target="tpu_custom_call" | custom-call | bytes 48000000 | tf_op jit(solution)/shard_map/reduce_keys/pallas_call | solution.py:633
  571.4 12.1 %project_back.1 = (bf16[1024,2048]{1,0:T(8,128)(2,1)}, bf16[64,112,128]{2,1,0:T(8,128)(2,1)}) custom-call(f32[1024,256]{1,0:T(8,128)} %get-tuple-element.142.dq_ref, f32[512,128]{1,0:T(8,128)} %reduce_keys.1.ds_ref, f32[1024,256]{1,0:T(8,128)} %get-tuple-element.148.qp_ref, f32[1024,128]{1,0:T(8,128)} %get-tuple-element.149.kp_ref, ...), custom_call_target="tpu_custom_call" | custom-call | bytes 14400000 | tf_op jit(solution)/shard_map/project_back/pallas_call | solution.py:1246
  583.4 9.5 %all-to-all-start.4 = ((bf16[64,112,128]{2,1,0:T(8,128)(2,1)}), bf16[64,112,128]{2,1,0:T(8,128)(2,1)}, u32[]{:S(2)}, u32[]{:S(2)}) async-start(bf16[64,112,128]{2,1,0:T(8,128)(2,1)} %get-tuple-element.157), calls=%async_computation.4 | async-start | bytes 3670016 | tf_op jit(solution)/shard_map/all_to_all | solution.py:1547
  592.9 1.3 slice.124
  594.4 1.8 convert_reduce_fusion.3
  597.3 47.9 %reduce_row.3 = (f32[128,2048]{1,0:T(8,128)}, f32[128,2048]{1,0:T(8,128)}) custom-call(bf16[8,128,2048]{2,1,0:T(8,128)(2,1)} %bitcast.187, bf16[2,128,2048]{2,1,0:T(8,128)(2,1)} %bitcast.201), custom_call_target="tpu_custom_call" | custom-call | bytes 48000000 | tf_op jit(solution)/shard_map/reduce_row/pallas_call | solution.py:505
  645.3 7.8 %place_other.1 = (f32[2,2048,384]{2,1,0:T(8,128)}, f32[2,2048,384]{2,1,0:T(8,128)}, f32[2,384,2048]{2,1,0:T(8,128)}) custom-call(s32[1]{0:T(128)} %bitcast.33.side, bf16[2048,384]{1,0:T(8,128)(2,1)} %collective-permute-done.3.refs_0_, bf16[2048,384]{1,0:T(8,128)(2,1)} %collective-permute-done.4.refs_1_, ...), custom_call_target="tpu_custom_call", output_to_operand_aliasing={{0}: (4, {}), {1}: (5, {}), {2}: (6, {})} | custom-call | bytes 6000000 | tf_op jit(solution)/shard_map/place_other/pallas_call | solution.py:1094
  653.1 1.6 convert_reduce_fusion.5
  655.0 1.1 dynamic-slice_add_fusion
  656.1 1.4 fusion.12
  657.5 1.3 slice.152
  659.5 1.2 slice.153
  662.4 1.0 convert_reduce_fusion.4
  663.4 4.9 psum.7
  (185 shorter events, 31.5 us)
Async XLA Ops:
  0.6 5.2 copy-start.24
  0.7 5.2 copy-start.25
  1.4 4.4 copy-start.15
  2.2 3.6 copy-start.13
  61.4 7.7 %copy-start.23 = (s32[128]{0:T(128)S(1)}, s32[128]{0:T(128)}, u32[]{:S(2)}) copy-start(s32[128]{0:T(128)} %param.25) | copy-start | bytes 1540
  61.4 7.9 %copy-start.27 = (s32[4]{0:T(128)S(1)}, s32[4]{0:T(128)}, u32[]{:S(2)}) copy-start(s32[4]{0:T(128)} %param.24) | copy-start | bytes 52
  61.4 8.1 %copy-start.17 = (s32[2,8,128]{2,1,0:T(8,128)S(1)}, s32[2,8,128]{2,1,0:T(8,128)}, u32[]{:S(2)}) copy-start(s32[2,8,128]{2,1,0:T(8,128)} %get-tuple-element.93) | copy-start | bytes 24580
  61.4 9.9 %copy-start.28 = (f32[128]{0:T(128)S(1)}, f32[128]{0:T(128)}, u32[]{:S(2)}) copy-start(f32[128]{0:T(128)} %param.33) | copy-start | bytes 1540
  61.4 9.9 %copy-start.29 = (f32[128]{0:T(128)S(1)}, f32[128]{0:T(128)}, u32[]{:S(2)}) copy-start(f32[128]{0:T(128)} %param.32) | copy-start | bytes 1540
  61.4 59.5 %all-to-all-start = ((bf16[64,32,384]{2,1,0:T(8,128)(2,1)}), bf16[64,32,384]{2,1,0:T(8,128)(2,1)S(1)}, u32[]{:S(2)}, u32[]{:S(2)}) async-start(bf16[64,32,384]{2,1,0:T(8,128)(2,1)} %bitcast.18), calls=%async_computation | async-start | bytes 3145728 | tf_op jit(solution)/shard_map/all_to_all | solution.py:1350
  85.1 33.1 %copy-start.8 = (bf16[2,128,2048]{2,1,0:T(8,128)(2,1)S(1)}, bf16[2,128,2048]{2,1,0:T(8,128)(2,1)}, u32[]{:S(2)}) copy-start(bf16[2,128,2048]{2,1,0:T(8,128)(2,1)} %get-tuple-element.94) | copy-start | bytes 3145732
  120.9 1.2 copy-start.1
  122.1 52.2 %all-to-all-start.1 = ((bf16[32,24,2048]{2,1,0:T(8,128)(2,1)}), bf16[32,24,2048]{2,1,0:T(8,128)(2,1)S(1)}, u32[]{:S(2)}, u32[]{:S(2)}) async-start(bf16[32,24,2048]{2,1,0:T(8,128)(2,1)} %bitcast.27), calls=%async_computation.1 | async-start | bytes 6291456 | tf_op jit(solution)/shard_map/all_to_all | solution.py:710
  131.8 4.2 copy-start.20
  135.1 39.1 %collective-permute-start = (bf16[2048,384]{1,0:T(8,128)(2,1)}, bf16[2048,384]{1,0:T(8,128)(2,1)}, u32[]{:S(2)}, u32[]{:S(2)}) collective-permute-start(bf16[2048,384]{1,0:T(8,128)(2,1)} %get-tuple-element.102), channel_id=1, source_target_pairs={{0,1},{1,0},{2,3},{3,2},{4,5},{5,4},{6,7},{7,6},{8,9},{9,8},{10,11... | collective-permute-start | bytes 4718600 | tf_op jit(solution)/shard_map/ppermute | solution.py:1318
  148.8 21.1 %copy-start.2 = (bf16[64,32,384]{2,1,0:T(8,128)(2,1)S(1)}, bf16[64,32,384]{2,1,0:T(8,128)(2,1)}, u32[]{:S(2)}) copy-start(bf16[64,32,384]{2,1,0:T(8,128)(2,1)} %copy-done.1) | copy-start | bytes 4718596
  174.3 1.7 copy-start
  219.3 3.2 copy-start.18
  219.3 37.1 %collective-permute-start.1 = (bf16[2048,384]{1,0:T(8,128)(2,1)}, bf16[2048,384]{1,0:T(8,128)(2,1)}, u32[]{:S(2)}, u32[]{:S(2)}) collective-permute-start(bf16[2048,384]{1,0:T(8,128)(2,1)} %get-tuple-element.111), channel_id=1, source_target_pairs={{0,1},{1,0},{2,3},{3,2},{4,5},{5,4},{6,7},{7,6},{8,9},{9,8},{10,11... | collective-permute-start | bytes 4718600 | tf_op jit(solution)/shard_map/ppermute | solution.py:1318
  220.3 3.2 copy-start.21
  220.6 39.8 %copy-start.3 = (bf16[256,2048]{1,0:T(8,128)(2,1)}, bf16[256,2048]{1,0:T(8,128)(2,1)S(1)}, u32[]{:S(2)}) copy-start(bf16[256,2048]{1,0:T(8,128)(2,1)S(1)} %multiply_convert_fusion) | copy-start | bytes 3145732
  222.9 0.7 copy-start.11
  256.4 49.2 %collective-permute-start.2 = (bf16[384,2048]{1,0:T(8,128)(2,1)}, bf16[384,2048]{1,0:T(8,128)(2,1)S(1)}, u32[]{:S(2)}, u32[]{:S(2)}) collective-permute-start(bf16[384,2048]{1,0:T(8,128)(2,1)} %get-tuple-element.119), channel_id=1, source_target_pairs={{0,1},{1,0},{2,3},{3,2},{4,5},{5,4},{6,7},{7,6},{8,9},{9,8},{10,11... | collective-permute-start | bytes 4718600 | tf_op jit(solution)/shard_map/ppermute | solution.py:1318
  305.7 1.1 copy-start.7
  332.8 14.7 %copy-start.19 = (f32[256]{0:T(256)S(1)}, f32[256]{0:T(256)}, u32[]{:S(2)}) copy-start(f32[256]{0:T(256)} %copy-done.18) | copy-start | bytes 3076
  346.4 46.2 %copy-start.22 = (s32[768]{0:T(1024)S(1)}, s32[768]{0:T(1024)}, u32[]{:S(2)}) copy-start(s32[768]{0:T(1024)} %eq.115) | copy-start | bytes 9220
  346.4 47.5 %collective-permute-start.3 = (bf16[2048,384]{1,0:T(8,128)(2,1)}, bf16[2048,384]{1,0:T(8,128)(2,1)}, u32[]{:S(2)}, u32[]{:S(2)}) collective-permute-start(bf16[2048,384]{1,0:T(8,128)(2,1)} %get-tuple-element.125), channel_id=1, source_target_pairs={{0,1},{1,0},{2,3},{3,2},{4,5},{5,4},{6,7},{7,6},{8,9},{9,8},{10,11... | collective-permute-start | bytes 4718600 | tf_op jit(solution)/shard_map/ppermute | solution.py:1318
  393.9 69.3 %all-to-all-start.2 = ((bf16[32,24,2048]{2,1,0:T(8,128)(2,1)}), bf16[32,24,2048]{2,1,0:T(8,128)(2,1)}, u32[]{:S(2)}, u32[]{:S(2)}) async-start(bf16[32,24,2048]{2,1,0:T(8,128)(2,1)} %bitcast.190), calls=%async_computation.2 | async-start | bytes 6291456 | tf_op jit(solution)/shard_map/all_to_all | solution.py:710
  401.4 23.9 %copy-start.12 = (f32[256,128]{1,0:T(8,128)S(1)}, f32[256,128]{1,0:T(8,128)}, u32[]{:S(2)}) copy-start(f32[256,128]{1,0:T(8,128)} %copy-done.11) | copy-start | bytes 393220
  425.3 3.9 copy-start.6
  429.6 49.2 %collective-permute-start.4 = (bf16[2048,384]{1,0:T(8,128)(2,1)}, bf16[2048,384]{1,0:T(8,128)(2,1)}, u32[]{:S(2)}, u32[]{:S(2)}) collective-permute-start(bf16[2048,384]{1,0:T(8,128)(2,1)} %get-tuple-element.138), channel_id=1, source_target_pairs={{0,1},{1,0},{2,3},{3,2},{4,5},{5,4},{6,7},{7,6},{8,9},{9,8},{10,11... | collective-permute-start | bytes 4718600 | tf_op jit(solution)/shard_map/ppermute | solution.py:1318
  463.2 15.7 %copy-start.26 = (f32[32]{0:T(128)S(1)}, f32[32]{0:T(128)}, u32[]{:S(2)}) copy-start(f32[32]{0:T(128)} %param.31) | copy-start | bytes 388
  463.2 57.9 %all-to-all-start.3 = ((bf16[64,112,128]{2,1,0:T(8,128)(2,1)}), bf16[64,112,128]{2,1,0:T(8,128)(2,1)}, u32[]{:S(2)}, u32[]{:S(2)}) async-start(bf16[64,112,128]{2,1,0:T(8,128)(2,1)} %fusion.3), calls=%async_computation.3 | async-start | bytes 3670016 | tf_op jit(solution)/shard_map/all_to_all | solution.py:1517
  478.8 53.7 %collective-permute-start.5 = (bf16[384,2048]{1,0:T(8,128)(2,1)}, bf16[384,2048]{1,0:T(8,128)(2,1)}, u32[]{:S(2)}, u32[]{:S(2)}) collective-permute-start(bf16[384,2048]{1,0:T(8,128)(2,1)} %get-tuple-element.145), channel_id=1, source_target_pairs={{0,1},{1,0},{2,3},{3,2},{4,5},{5,4},{6,7},{7,6},{8,9},{9,8},{10,11... | collective-permute-start | bytes 4718600 | tf_op jit(solution)/shard_map/ppermute | solution.py:1318
  583.4 74.1 %all-to-all-start.4 = ((bf16[64,112,128]{2,1,0:T(8,128)(2,1)}), bf16[64,112,128]{2,1,0:T(8,128)(2,1)}, u32[]{:S(2)}, u32[]{:S(2)}) async-start(bf16[64,112,128]{2,1,0:T(8,128)(2,1)} %get-tuple-element.157), calls=%async_computation.4 | async-start | bytes 3670016 | tf_op jit(solution)/shard_map/all_to_all | solution.py:1547
  645.2 9.4 %copy-start.4 = (bf16[128,2048]{1,0:T(8,128)(2,1)S(1)}, bf16[128,2048]{1,0:T(8,128)(2,1)}, u32[]{:S(2)}) copy-start(bf16[128,2048]{1,0:T(8,128)(2,1)} %t_in.1) | copy-start | bytes 1572868
  645.3 9.4 %copy-start.5 = (f32[128,2048]{1,0:T(8,128)S(1)}, f32[128,2048]{1,0:T(8,128)}, u32[]{:S(2)}) copy-start(f32[128,2048]{1,0:T(8,128)} %get-tuple-element.156) | copy-start | bytes 3145732
  653.1 1.9 copy-start.9
  658.8 1.9 copy-start.16
  658.8 2.7 copy-start.14
  659.5 9.9 %copy-start.10 = (f32[32,2048]{1,0:T(8,128)}, f32[32,2048]{1,0:T(8,128)S(1)}, u32[]{:S(2)}) copy-start(f32[32,2048]{1,0:T(8,128)S(1)} %reshape.505) | copy-start | bytes 786436

commit v4 on v3

--- a/solution.py
+++ b/solution.py
@@ -58,23 +58,6 @@
 
 def inverse_root(value_rows):
     return lax.rsqrt(jnp.mean(value_rows * value_rows, axis=-1, keepdims=True) + EPSILON)
-
-
-def rope_tables(positions):
-    half_dim = HEAD_WIDTH // 2
-    frequency = jnp.power(ROPE_BASE, -2.0 * jnp.arange(half_dim, dtype=jnp.float32) / HEAD_WIDTH)
-    angles = positions.astype(jnp.float32)[:, None] * frequency[None, :]
-    cosine, sine_tab = jnp.cos(angles), jnp.sin(angles)
-    return (
-        jnp.concatenate([cosine, cosine], axis=-1),
-        jnp.concatenate([-sine_tab, sine_tab], axis=-1),
-    )
-
-
-def seq_starts(positions, seq_lengths):
-    offsets = jnp.cumsum(seq_lengths) - seq_lengths
-    inside = offsets[None, :] <= positions[:, None]
-    return jnp.max(jnp.where(inside, offsets[None, :], 0), axis=1)
 
 
 def coords(c):
@@ -154,7 +137,7 @@
     return copies
 
 
-def row_gather_finish(out, me, wsh, copies, send, recv):
+def row_gather_onward(out, me, wsh, copies, send, recv):
     partner = shifted(me, 0, 0, 0, 1)
     half = out.shape[1] // 2
     onward = []
@@ -170,6 +153,12 @@
         forward = remote(block, block, send.at[5 + at], recv.at[5 + at], partner, wsh)
         forward.start()
         forwards.append(forward)
+    return onward, forwards
+
+
+def row_gather_end(out, me, wsh, copies, onward, forwards, send, recv):
+    partner = shifted(me, 0, 0, 0, 1)
+    half = out.shape[1] // 2
     far = lax.rem(shifted(me, 0, 0, 2, 0), 8)
     for at in (0, 1):
         onward[at].wait_recv()
@@ -212,66 +201,82 @@
     stores[-1].wait()
 
 
+COLUMN_STEPS = ((1, 0), (3, 0), (0, 1), (2, 0), (1, 1), (3, 1), (2, 1))
+ROW_STEPS = ((1, 0), (3, 0), (1, 1), (3, 1), (0, 1), (2, 0), (2, 1))
+
+
 def gather_first(weights, tokens, small, routes, cotangent, expert_weights):
     def body(w_in, t_in, s_in, r_in, c_in, *refs):
         sources, refs = refs[:3], refs[3:]
         w_out, t_out, s_out, r_out, c_out = refs[:5]
         lows, side_out, refs = refs[5:8], refs[8], refs[9:]
-        wide, row_s, row_r, pair, local, tall_f, flat_f, tall_b, flat_b, in_sems, out_sems = refs
+        wide, row_s, row_r, pair, local, col_s, col_r, tall_f, flat_f, tall_b, flat_b, in_sems, out_sems = refs
         me, wsh = lax.axis_index("ctx"), lax.axis_index("wsh")
         core = lax.rem(me, 2)
         place = lax.rem(me, 8)
-
-        def target(step):
-            return shifted(
-                me, lax.div(step, 16), lax.rem(lax.div(step, 8), 2), lax.rem(lax.div(step, 2), 4), lax.rem(step, 2)
-            )
-
-        barrier, amount = greet_many(64, lambda step: (target(step), wsh))
+        group = lax.div(me, 8)
+        partner = shifted(me, 0, 0, 0, 1)
+        row_peers = [shifted(me, 0, 0, dx, dk) for dx, dk in ROW_STEPS]
+        col_peers = [shifted(me, dz, dy, 0, 0) for dz, dy in COLUMN_STEPS]
+        barrier, amount = greet([(peer, wsh) for peer in row_peers + col_peers])
         locals_ = [
-            pltpu.make_async_copy(t_in, t_out.at[place], local.at[0]),
-            pltpu.make_async_copy(w_in.at[place], w_out.at[me], local.at[1]),
-            pltpu.make_async_copy(s_in, s_out.at[me], local.at[2]),
+            pltpu.make_async_copy(w_in.at[place], w_out.at[me], local.at[0]),
+            pltpu.make_async_copy(s_in, s_out.at[me], local.at[1]),
+            pltpu.make_async_copy(t_in, t_out.at[place], local.at[2]),
             pltpu.make_async_copy(r_in, r_out.at[core], local.at[3]),
             pltpu.make_async_copy(c_in, c_out.at[core], local.at[4]),
         ]
         for copy in locals_:
             copy.start()
         pl.semaphore_wait(barrier, amount)
+        for peer in row_peers:
+            remote(w_in.at[lax.rem(peer, 8)], w_out.at[me], wide.at[0], wide.at[1], peer, wsh).start()
+            remote(s_in, s_out.at[me], wide.at[2], wide.at[3], peer, wsh).start()
         row_copies = row_gather_start(t_in, t_out, me, wsh, row_s, row_r)
-
-        def send(step, carried):
-            turned = lax.rem(step * 13, 64)
-            ctx = target(turned)
-            remote(s_in, s_out.at[me], wide.at[0], wide.at[1], ctx, wsh).start()
-            remote(w_in.at[lax.rem(ctx, 8)], w_out.at[me], wide.at[2], wide.at[3], ctx, wsh).start()
-            return carried
-
-        lax.fori_loop(1, 64, send, 0)
-        partner = shifted(me, 0, 0, 0, 1)
         pair_copies = [
             remote(r_in, r_out.at[core], pair.at[0], pair.at[1], partner, wsh),
             remote(c_in, c_out.at[core], pair.at[2], pair.at[3], partner, wsh),
         ]
         for copy in pair_copies:
             copy.start()
+        locals_[0].wait()
+        locals_[1].wait()
+        for at, out in ((0, w_out), (2, s_out)):
+            rest = out.at[pl.ds(0, 7)]
+            done = remote(rest, rest, wide.at[at], wide.at[at + 1], partner, wsh)
+            done.wait_recv()
+            done.wait_send()
+        lanes = side_out.shape[2]
+        depth, columns = w_out.shape[1], w_out.shape[2]
+
+        def share(origin, at):
+            blocks = pl.ds(origin * 8, 8)
+            part = w_out.at[blocks, pl.ds(0, depth), pl.ds(columns - lanes, lanes)]
+            give = remote(part, side_out.at[blocks], col_s.at[2, at], col_r.at[2, at], partner, wsh)
+            give.start()
+            return give
+
+        mine = pl.ds(group * 8, 8)
+        col_copies = []
+        for at, peer in enumerate(col_peers):
+            for kind, out in enumerate((w_out, s_out)):
+                copy = remote(out.at[mine], out.at[mine], col_s.at[kind, at], col_r.at[kind, at], peer, wsh)
+                copy.start()
+                col_copies.append(copy)
+        shares = [share(group, 7)]
+        onward, forwards = row_gather_onward(t_out, me, wsh, row_copies, row_s, row_r)
         cast_steps((sources, (tall_f, flat_f), (tall_b, flat_b), in_sems, out_sems), lows, 1 - wsh)
-        row_gather_finish(t_out, me, wsh, row_copies, row_s, row_r)
-        for copy in pair_copies:
+        row_gather_end(t_out, me, wsh, row_copies, onward, forwards, row_s, row_r)
+        for at, (dz, dy) in enumerate(COLUMN_STEPS):
+            col_copies[2 * at].wait_recv()
+            col_copies[2 * at + 1].wait_recv()
+            shares.append(share(lax.div(shifted(me, 4 - dz, 2 - dy, 0, 0), 8), at))
+        for copy in pair_copies + shares:
             copy.wait()
-        for copy in locals_[:1] + locals_[2:]:
+        for copy in locals_[2:]:
             copy.wait()
-        for at, out in ((0, s_out), (2, w_out)):
-            rest = out.at[pl.ds(0, 63)]
-            done = remote(rest, rest, wide.at[at], wide.at[at + 1], partner, wsh)
-            done.wait_send()
-            done.wait_recv()
-        locals_[1].wait()
-        lanes = side_out.shape[2]
-        share = w_out.at[pl.ds(0, 64), pl.ds(0, w_out.shape[1]), pl.ds(w_out.shape[2] - lanes, lanes)]
-        give = remote(share, side_out, pair.at[4], pair.at[5], partner, wsh)
-        give.start()
-        give.wait()
+        for copy in col_copies:
+            copy.wait_send()
 
     sds = jax.ShapeDtypeStruct
     tall = (expert_weights[0].shape[1] // 4, expert_weights[0].shape[2])
@@ -293,8 +298,10 @@
             DMA((4,)),
             DMA((9,)),
             DMA((9,)),
-            DMA((6,)),
+            DMA((4,)),
             DMA((5,)),
+            DMA((3, 8)),
+            DMA((3, 8)),
             pltpu.VMEM((2,) + tall, F32),
             pltpu.VMEM((2,) + flat, F32),
             pltpu.VMEM((2,) + tall, BF),
@@ -304,7 +311,7 @@
         ],
         compiler_params=call_params(0),
         name="gather_first",
-        cost_estimate=cost(60),
+        cost_estimate=cost(40),
     )(weights, tokens, small, routes, cotangent, *expert_weights)
 
 
@@ -316,7 +323,8 @@
         mine.start()
         pl.semaphore_wait(barrier, amount)
         copies = row_gather_start(src, out, me, wsh, row_s, row_r)
-        row_gather_finish(out, me, wsh, copies, row_s, row_r)
+        onward, forwards = row_gather_onward(out, me, wsh, copies, row_s, row_r)
+        row_gather_end(out, me, wsh, copies, onward, forwards, row_s, row_r)
         mine.wait()
 
     return pl.pallas_call(
@@ -329,9 +337,6 @@
         name="gather_row",
         cost_estimate=cost(26),
     )(block)
-
-
-COLUMN_STEPS = ((1, 0), (3, 0), (0, 1), (2, 0), (1, 1), (3, 1), (2, 1))
 
 
 def gather_keys(rows, collective_id):
@@ -380,7 +385,92 @@
     )(rows)
 
 
-def reduce_row(parts, collective_id, both, extra=None):
+class Owned:
+    SCRATCH = 10
+
+    def __init__(self, src, out, scratch):
+        self.src, self.out = src, out
+        self.land_z, self.sum_z, self.land_y, self.reduced, *self.sems = scratch
+
+    @staticmethod
+    def scratch(value):
+        inner = value.shape[1:]
+        return [
+            pltpu.VMEM((3, 16) + inner, BF),
+            pltpu.VMEM((16,) + inner, BF),
+            pltpu.VMEM((8,) + inner, BF),
+            pltpu.VMEM((8,) + inner, BF),
+            DMA((3,)),
+            DMA((3,)),
+            DMA((1,)),
+            DMA((1,)),
+            DMA((7,)),
+            DMA((7,)),
+        ]
+
+    def along_z(self, me, wsh):
+        z, _, _, _ = coords(me)
+        self.copies_z = []
+        for at, dz in enumerate((1, 3, 2)):
+            blocks = pl.ds(lax.rem(z + dz, 4) * 16, 16)
+            copy = remote(
+                self.src.at[blocks],
+                self.land_z.at[at],
+                self.sems[0].at[at],
+                self.sems[1].at[at],
+                shifted(me, dz, 0, 0, 0),
+                wsh,
+            )
+            copy.start()
+            self.copies_z.append(copy)
+
+    def along_y(self, me, wsh):
+        z, y, _, _ = coords(me)
+        value = self.src[pl.ds(z * 16, 16)].astype(F32)
+        for at, copy in enumerate(self.copies_z):
+            copy.wait_recv()
+            value = value + self.land_z[at].astype(F32)
+        self.sum_z[...] = value.astype(BF)
+        self.copy_y = remote(
+            self.sum_z.at[pl.ds((1 - y) * 8, 8)],
+            self.land_y,
+            self.sems[2].at[0],
+            self.sems[3].at[0],
+            shifted(me, 0, 1, 0, 0),
+            wsh,
+        )
+        self.copy_y.start()
+
+    def along_row(self, me, wsh):
+        _, y, _, _ = coords(me)
+        self.copy_y.wait_recv()
+        value = self.sum_z[pl.ds(y * 8, 8)].astype(F32) + self.land_y[...].astype(F32)
+        self.reduced[...] = value.astype(BF)
+        place = lax.rem(me, 8)
+        self.copies_row = []
+        for at, (dx, dk) in enumerate(ROW_STEPS):
+            peer = shifted(me, 0, 0, dx, dk)
+            copy = remote(
+                self.reduced.at[lax.rem(peer, 8)],
+                self.out.at[place],
+                self.sems[4].at[at],
+                self.sems[5].at[at],
+                peer,
+                wsh,
+            )
+            copy.start()
+            self.copies_row.append(copy)
+        self.out[place] = self.reduced[place]
+
+    def finish(self):
+        for copy in self.copies_row:
+            copy.wait()
+        for copy in self.copies_z + [self.copy_y]:
+            copy.wait_send()
+
+
+def reduce_row(parts, collective_id, both, extra=None, swapped_whole=None, owned=()):
+    has_whole = swapped_whole is not None
     _, rows, width = parts.shape
     block = (rows, width)
     pieces = 4
@@ -391,8 +481,16 @@
         refs = list(refs)
         src = refs.pop(0)
         src2 = refs.pop(0) if has_extra else None
+        src3 = refs.pop(0) if has_whole else None
+        mine_in = [refs.pop(0) for _ in owned]
         out = refs.pop(0)
         out2 = refs.pop(0) if has_extra else None
+        out3 = refs.pop(0) if has_whole else None
+        mine_out = [refs.pop(0) for _ in owned]
+        blocks = []
+        for src4, out4 in reversed(list(zip(mine_in, mine_out))):
+            blocks.append(Owned(src4, out4, refs[-Owned.SCRATCH :]))
+            refs = refs[: -Owned.SCRATCH]
         arrived, summed, landed, swapped, total, send, recv, local = refs[:8]
         me, wsh = lax.axis_index("ctx"), lax.axis_index("wsh")
         other = 1 - wsh
@@ -400,8 +498,14 @@
         _, _, x, _ = coords(me)
         partner = shifted(me, 0, 0, 0, 1)
         peers = [shifted(me, 0, 0, dx, 0) for dx in (1, 2, 3)]
-        barrier, amount = greet([(peer, wsh) for peer in peers + [partner]] + [(me, other)])
+        row_peers = [shifted(me, 0, 0, dx, dk) for dx, dk in ROW_STEPS]
+        col_peers = [shifted(me, dz, dy, 0, 0) for dz, dy in COLUMN_STEPS]
+        greeted = row_peers + col_peers if owned else peers + [partner]
+        barrier, amount = greet([(peer, wsh) for peer in greeted] + [(me, other)])
         pl.semaphore_wait(barrier, amount)
+        if has_whole:
+            whole = remote(src3, out3, send.at[1, 9], recv.at[1, 9], me, other)
+            whole.start()
         spans = [pl.ds(piece * columns, columns) for piece in range(pieces)]
         everything = pl.ds(0, rows)
         first = []
@@ -418,6 +522,8 @@
                 )
                 copy.start()
                 first.append(copy)
+        for block4 in blocks:
+            block4.along_z(me, wsh)
         if has_extra:
             arrived2, swapped2 = refs[8:]
             give2 = remote(src2.at[1 - core], arrived2, send.at[0, 8], recv.at[0, 8], partner, wsh)
@@ -467,6 +573,10 @@
             )
             swap.start()
             swaps.append(swap)
+        for block4 in blocks:
+            block4.along_y(me, wsh)
+        for block4 in blocks:
+            block4.along_row(me, wsh)
         if has_extra:
             swap2.wait()
             out2[...] = swapped2[0].astype(F32) + swapped2[1].astype(F32)
@@ -485,6 +595,10 @@
             keep.wait()
         for copy in first + second:
             copy.wait_send()
+        for block4 in blocks:
+            block4.finish()
+        if has_whole:
+            whole.wait()
 
     shapes = [jax.ShapeDtypeStruct((2,) + block if both else block, F32)]
     scratch = [
@@ -502,11 +616,22 @@
         shapes.append(jax.ShapeDtypeStruct(block, F32))
         scratch += [pltpu.VMEM(block, BF), pltpu.VMEM((2,) + block, BF)]
         operands.append(extra)
+    spaces = [VMEM] * len(operands)
+    if has_whole:
+        shapes.append(jax.ShapeDtypeStruct(swapped_whole.shape, swapped_whole.dtype))
+        operands.append(swapped_whole)
+        spaces.append(ANY)
+    for value in owned:
+        block8 = (8,) + value.shape[1:]
+        shapes.append(jax.ShapeDtypeStruct(block8, BF))
+        operands.append(value)
+        spaces.append(VMEM)
+        scratch += Owned.scratch(value)
     return pl.pallas_call(
         body,
         out_shape=shapes,
-        in_specs=[VMEM] * len(operands),
-        out_specs=[VMEM] * len(operands),
+        in_specs=spaces,
+        out_specs=spaces,
         scratch_shapes=scratch,
         compiler_params=call_params(collective_id),
         name="reduce_row",
@@ -570,10 +695,11 @@
     )(*operands)
 
 
-def reduce_keys(parts, collective_id):
+def reduce_keys(parts, owned, collective_id):
     _, groups, _, rows, width = parts.shape
 
-    def body(src, out, arrived, mid, beside, summed, landed, send, recv):
+    def body(src, src4, out, out4, arrived, mid, beside, summed, landed, send, recv, *scratch4):
+        block4 = Owned(src4, out4, scratch4)
         me, wsh = lax.axis_index("ctx"), lax.axis_index("wsh")
         core = lax.rem(me, 2)
         _, _, x, _ = coords(me)
@@ -582,7 +708,8 @@
         neighbour = me + 2 - 4 * side
         steps = COLUMN_STEPS + ((0, 0),)
         peers = [shifted(me, dz, dy, 0, 0) for dz, dy in steps]
-        barrier, amount = greet([(peer, wsh) for peer in peers[:-1] + [partner, neighbour]])
+        row_peers = [shifted(me, 0, 0, dx, dk) for dx, dk in ROW_STEPS]
+        barrier, amount = greet([(peer, wsh) for peer in peers[:-1] + row_peers])
         pl.semaphore_wait(barrier, amount)
         first = []
         for at, peer in enumerate(peers):
@@ -598,6 +725,7 @@
                 )
                 copy.start()
                 first.append(copy)
+        block4.along_z(me, wsh)
         across = []
         for at, peer in enumerate(peers):
             group = lax.div(peer, 8)
@@ -623,18 +751,24 @@
                 copy = remote(summed.at[at], landed.at[at], send.at[3, at], recv.at[3, at], peer, wsh)
                 copy.start()
                 last.append(copy)
+        block4.along_y(me, wsh)
+        block4.along_row(me, wsh)
         for at, copy in enumerate(last):
             copy.wait_recv()
             out[...] += landed[at].astype(F32)
         for copy in first + across + last:
             copy.wait_send()
+        block4.finish()
 
     block = (rows, width)
     return pl.pallas_call(
         body,
-        out_shape=jax.ShapeDtypeStruct(block, F32),
-        in_specs=[VMEM],
-        out_specs=VMEM,
+        out_shape=(
+            jax.ShapeDtypeStruct(block, F32),
+            jax.ShapeDtypeStruct((8,) + owned.shape[1:], BF),
+        ),
+        in_specs=[VMEM, VMEM],
+        out_specs=[VMEM, VMEM],
         scratch_shapes=[
             pltpu.VMEM((2, groups) + block, BF),
             pltpu.VMEM((groups,) + block, BF),
@@ -643,11 +777,12 @@
             pltpu.VMEM((groups,) + block, BF),
             DMA((4, groups)),
             DMA((4, groups)),
-        ],
+        ]
+        + Owned.scratch(owned),
         compiler_params=call_params(collective_id),
         name="reduce_keys",
         cost_estimate=cost(40),
-    )(parts)
+    )(parts, owned)
 
 
 def exchange(arrays, collective_id):
@@ -712,9 +847,9 @@
     )
 
 
-def natural_order(inverse, kv_ref, keys, values, transposed):
+def natural_order(plan, kv_ref, keys, values, transposed):
     def one(block, carried):
-        rows = kv_ref[pl.ds(pl.multiple_of(inverse[block] * BLK, BLK), BLK), :]
+        rows = kv_ref[pl.ds(pl.multiple_of(plan[PLAN_INVERSE + block] * BLK, BLK), BLK), :]
         at = pl.ds(pl.multiple_of(block * BLK, BLK), BLK)
         keys[at, :] = rows[:, :HEAD_WIDTH]
         values[at, :] = rows[:, HEAD_WIDTH:]
@@ -746,10 +881,62 @@
         )
 
 
-def three_loops(step, low, inner_low, inner_high, high, chunk, state):
-    state = lax.fori_loop(low[step], inner_low[step], functools.partial(chunk, True), state)
-    state = lax.fori_loop(inner_low[step], inner_high[step], functools.partial(chunk, False), state)
-    return lax.fori_loop(inner_high[step], high[step], functools.partial(chunk, True), state)
+PLAN_BOUNDS, PLAN_INVERSE, PLAN_BLOCKS, PLAN_SIZE = 16, 64, 192, 256
+
+
+def start_of(lengths, position):
+    begin = lengths[0] * 0
+    start = position * 0
+    for at in range(lengths.shape[0]):
+        start = jnp.where(begin <= position, begin, start)
+        begin = begin + lengths[at]
+    return start
+
+
+def make_plan(block_order, lengths, base, plan):
+    def place(at, carried):
+        plan[PLAN_INVERSE + block_order[at]] = at
+        return carried
+
+    lax.fori_loop(0, block_order.shape[0], place, 0, unroll=8)
+
+    def rank(at, carried):
+        mine = block_order[base + at]
+        before = jnp.int32(0)
+        for other in range(16):
+            before = before + jnp.where(block_order[base + other] < mine, 1, 0)
+        plan[before] = at
+        plan[PLAN_BLOCKS + before] = mine
+        return carried
+
+    lax.fori_loop(0, 16, rank, 0)
+
+    def bound(step, carried):
+        one, two = plan[PLAN_BLOCKS + 2 * step], plan[PLAN_BLOCKS + 2 * step + 1]
+        low = lax.div(start_of(lengths, one * BLK), CHUNK)
+        high = lax.div(two * BLK, CHUNK) + 1
+        last = start_of(lengths, two * BLK + BLK - 1)
+        inner_low = jnp.minimum(jnp.maximum(lax.div(last + CHUNK - 1, CHUNK), low), high)
+        inner_high = jnp.minimum(jnp.maximum(lax.div(one * BLK + 1, CHUNK), inner_low), high)
+        for at, value in enumerate((low, inner_low, inner_high, high)):
+            plan[PLAN_BOUNDS + 4 * step + at] = value
+        return carried
+
+    lax.fori_loop(0, 8, bound, 0)
+
+
+def strips_of(plan, lengths, step):
+    lane = lax.broadcasted_iota(jnp.int32, (1, 4 * BLK), 1)
+    block = jnp.where(lane < 2 * BLK, plan[PLAN_BLOCKS + 2 * step], plan[PLAN_BLOCKS + 2 * step + 1])
+    position = block * BLK + lax.rem(lane, BLK)
+    return position, start_of(lengths, position)
+
+
+def three_loops(step, plan, chunk, state):
+    low, inner_low, inner_high, high = [plan[PLAN_BOUNDS + 4 * step + at] for at in range(4)]
+    state = lax.fori_loop(low, inner_low, functools.partial(chunk, True), state)
+    state = lax.fori_loop(inner_low, inner_high, functools.partial(chunk, False), state)
+    return lax.fori_loop(inner_high, high, functools.partial(chunk, True), state)
 
 
 def kept(scores, at, q_pos, q_start):
@@ -761,16 +948,17 @@
 TWO_SCALE = SCORE_SCALE / math.log(2.0)
 
 
-def forward_kernel(order, low, inner_low, inner_high, high, inverse, q_ref, kv_ref, pos_ref, start_ref, out_ref, lse_ref, keys, values, values_t, acc):
+def forward_kernel(block_order, lengths, group, q_ref, kv_ref, out_ref, lse_ref, plan, keys, values, values_t, acc):
     step = pl.program_id(0)
 
     @pl.when(step == 0)
     def _():
-        natural_order(inverse, kv_ref, keys, values, (values, values_t))
-
-    first, second = order[2 * step], order[2 * step + 1]
+        make_plan(block_order, lengths, group[0] * 16, plan)
+        natural_order(plan, kv_ref, keys, values, (values, values_t))
+
+    first, second = plan[2 * step], plan[2 * step + 1]
     q_t = stacked(q_ref, first, second).astype(F32).T.astype(BF)
-    q_pos, q_start = pos_ref[0], start_ref[0]
+    q_pos, q_start = strips_of(plan, lengths, step)
     width = 4 * BLK
     acc[...] = jnp.zeros_like(acc)
 
@@ -783,14 +971,12 @@
         acc[...] += matmul(values_t[:, pl.ds(at, CHUNK)], probs.astype(BF))
         return total + jnp.sum(probs, axis=0, keepdims=True)
 
-    total = three_loops(
-        step, low, inner_low, inner_high, high, chunk, jnp.zeros((1, width), F32)
-    )
+    total = three_loops(step, plan, chunk, jnp.zeros((1, width), F32))
     lse_ref[0] = jnp.log2(total)
     unstacked(out_ref, first, second, (acc[...] / total).T.astype(BF))
 
 
-def attend(plan, queries, kv, positions, starts):
+def attend(block_order, lengths, group, queries, kv):
     rows = queries.shape[0]
     steps = rows // (2 * BLK)
     everything = pl.BlockSpec(queries.shape, lambda i, *_: (0, 0))
@@ -798,12 +984,16 @@
     sds = jax.ShapeDtypeStruct
     return pl.pallas_call(
         forward_kernel,
-        out_shape=(sds(queries.shape, BF), sds((steps, 1, 4 * BLK), F32)),
+        out_shape=(
+            sds(queries.shape, BF),
+            sds((steps, 1, 4 * BLK), F32),
+            sds((PLAN_SIZE,), jnp.int32),
+        ),
         grid_spec=pltpu.PrefetchScalarGridSpec(
-            num_scalar_prefetch=6,
+            num_scalar_prefetch=3,
             grid=(steps,),
-            in_specs=[everything, pl.BlockSpec(kv.shape, lambda i, *_: (0, 0)), strip, strip],
-            out_specs=[everything, strip],
+            in_specs=[everything, pl.BlockSpec(kv.shape, lambda i, *_: (0, 0))],
+            out_specs=[everything, strip, pl.BlockSpec(memory_space=pltpu.SMEM)],
             scratch_shapes=[
                 pltpu.VMEM((kv.shape[0], HEAD_WIDTH), BF),
                 pltpu.VMEM((kv.shape[0], HEAD_WIDTH), BF),
@@ -814,19 +1004,19 @@
         compiler_params=pltpu.CompilerParams(vmem_limit_bytes=ROOM),
         name="attend",
         cost_estimate=cost(17),
-    )(*plan, queries, kv, positions, starts)
-
-
-def backward_kernel(order, low, inner_low, inner_high, high, inverse, q_ref, heads_ref, da_ref, wo_ref, kv_ref, pos_ref, start_ref, lse_ref, dq_ref, dkv_ref, keys, values, keys_t, d_keys, d_values, acc):
+    )(block_order, lengths, group, queries, kv)
+
+
+def backward_kernel(plan, lengths, q_ref, heads_ref, da_ref, wo_ref, kv_ref, lse_ref, dq_ref, dkv_ref, keys, values, keys_t, d_keys, d_values, acc):
     step = pl.program_id(0)
 
     @pl.when(step == 0)
     def _():
-        natural_order(inverse, kv_ref, keys, values, (keys, keys_t))
+        natural_order(plan, kv_ref, keys, values, (keys, keys_t))
         d_keys[...] = jnp.zeros_like(d_keys)
         d_values[...] = jnp.zeros_like(d_values)
 
-    first, second = order[2 * step], order[2 * step + 1]
+    first, second = plan[2 * step], plan[2 * step + 1]
     q = stacked(q_ref, first, second)
     d_rows = matmul(
         jnp.concatenate(
@@ -845,7 +1035,7 @@
     q_t = q.astype(F32).T.astype(BF)
     d_out_wide = d_out.astype(F32).T
     d_out_t = d_out_wide.astype(BF)
-    q_pos, q_start = pos_ref[0], start_ref[0]
+    q_pos, q_start = strips_of(plan, lengths, step)
     lse = lse_ref[0]
     dots = jnp.sum(d_out_wide * stacked(heads_ref, first, second).astype(F32).T, axis=0, keepdims=True)
     acc[...] = jnp.zeros_like(acc)
@@ -864,13 +1054,13 @@
         acc[...] += matmul(keys_t[:, here], d_scores)
         return carried
 
-    three_loops(step, low, inner_low, inner_high, high, chunk, 0)
+    three_loops(step, plan, chunk, 0)
     unstacked(dq_ref, first, second, (acc[...] * SCORE_SCALE).T)
 
     @pl.when(step == pl.num_programs(0) - 1)
     def _():
         def one(block, carried):
-            dealt = inverse[block]
+            dealt = plan[PLAN_INVERSE + block]
             group, inside = dealt // 16, dealt % 16
             half, rest = inside // 8, inside % 8
             at = pl.ds(pl.multiple_of(block * BLK, BLK), BLK)
@@ -882,7 +1072,7 @@
         lax.fori_loop(0, kv_ref.shape[0] // BLK, one, 0, unroll=4)
 
 
-def attend_back(plan, queries, heads, d_attn, wo_t, kv, positions, starts, lse):
+def attend_back(plan, lengths, queries, heads, d_attn, wo_t, kv, lse):
     rows = queries.shape[0]
     total = kv.shape[0]
     steps = rows // (2 * BLK)
@@ -894,16 +1084,14 @@
         backward_kernel,
         out_shape=(sds(queries.shape, F32), sds(dkv_shape, BF)),
         grid_spec=pltpu.PrefetchScalarGridSpec(
-            num_scalar_prefetch=6,
+            num_scalar_prefetch=2,
             grid=(steps,),
             in_specs=[
                 everything,
                 everything,
                 pl.BlockSpec(d_attn.shape, lambda i, *_: (0, 0)),
-                pl.BlockSpec(wo_t.shape, lambda i, *_: (0, 0)),
+                pl.BlockSpec((wo_t.shape[0], queries.shape[1]), lambda i, *_: (0, 0)),
                 pl.BlockSpec(kv.shape, lambda i, *_: (0, 0)),
-                strip,
-                strip,
                 strip,
             ],
             out_specs=[everything, pl.BlockSpec(dkv_shape, lambda i, *_: (0, 0, 0, 0, 0))],
@@ -919,10 +1107,10 @@
         compiler_params=pltpu.CompilerParams(vmem_limit_bytes=ROOM),
         name="attend_back",
         cost_estimate=cost(24),
-    )(*plan, queries, heads, d_attn, wo_t, kv, positions, starts, lse)
-
-
-def expert_kernel(side, x_ref, cot_ref, gate_ref, g_own, u_own, d_own, g_other, u_other, d_other, y_ref, dx_ref, dot_ref, a_ref, dg_ref, du_ref, dy_ref, gate_w, up_w, down_w, gate_f, up_f, down_f, sems):
+    )(plan, lengths, queries, heads, d_attn, wo_t, kv, lse)
+
+
+def expert_kernel(side, x_ref, cot_ref, gate_ref, g_own, u_own, d_own, g_other, u_other, u_rest, d_other, y_ref, dx_ref, a_ref, dg_ref, du_ref, dy_ref, gate_w, up_w, down_w, gate_f, up_f, down_f, sems):
     half = g_other.shape[1]
     own_copies, other_copies = [], []
     for at, (own, other, whole, stage, columns) in enumerate(
@@ -935,7 +1123,15 @@
         span = pl.ds(half, half)
         target = whole.at[pl.ds(0, whole.shape[0]), span] if columns else whole.at[span]
         own_copies.append(pltpu.make_async_copy(own.at[side[0]], stage, sems.at[at, 0]))
-        other_copies.append(pltpu.make_async_copy(other, target, sems.at[at, 1]))
+        if at == 1:
+            cut = u_other.shape[0]
+            parts = ((u_other, pl.ds(0, cut)), (u_rest, pl.ds(cut, u_rest.shape[0])))
+            for side_at, (part, place) in enumerate(parts):
+                other_copies.append(
+                    pltpu.make_async_copy(part, whole.at[place, span], sems.at[at, 1 + side_at])
+                )
+        else:
+            other_copies.append(pltpu.make_async_copy(other, target, sems.at[at, 1]))
 
     @pl.when(pl.program_id(0) == 0)
     def _():
@@ -963,8 +1159,8 @@
     y_ref[...] = (out * gates).astype(BF)
     dots = jnp.sum(out * cot, axis=1, keepdims=True)
     high = dots.astype(BF).astype(F32)
-    lane = lax.broadcasted_iota(jnp.int32, dot_ref.shape, 1)
-    dot_ref[...] = jnp.where(lane < 64, high, dots - high).astype(BF)
+    lane = lax.broadcasted_iota(jnp.int32, (dots.shape[0], 128), 1)
+    dx_ref[:, y_ref.shape[1] :] = jnp.where(lane < 64, high, dots - high).astype(BF)
     d_pairs = (cot * gates).astype(BF)
     dy_ref[...] = d_pairs
     d_act = times_transposed(d_pairs, down_w[...])
@@ -972,7 +1168,7 @@
     d_up = (d_act * silu).astype(BF)
     dg_ref[...] = d_gate
     du_ref[...] = d_up
-    dx_ref[...] = (times_transposed(d_gate, gate_w[...]) + times_transposed(d_up, up_w[...])).astype(BF)
+    dx_ref[:, : y_ref.shape[1]] = (times_transposed(d_gate, gate_w[...]) + times_transposed(d_up, up_w[...])).astype(BF)
 
 
 def run_expert(side, rows_in, cot, gates, own, other):
@@ -988,8 +1184,7 @@
         expert_kernel,
         out_shape=(
             sds((count, width), BF),
-            sds((count, width), BF),
-            sds((count, 128), BF),
+            sds((count, width + 128), BF),
             sds((count, 2 * half), BF),
             sds((count, 2 * half), BF),
             sds((count, 2 * half), BF),
@@ -998,11 +1193,10 @@
         grid_spec=pltpu.PrefetchScalarGridSpec(
             num_scalar_prefetch=1,
             grid=(count // tile,),
-            in_specs=[by_rows(width), by_rows(width), by_rows(128)] + [ANY] * 6,
+            in_specs=[by_rows(width), by_rows(width), by_rows(128)] + [ANY] * 7,
             out_specs=[
                 by_rows(width),
-                by_rows(width),
-                by_rows(128),
+                by_rows(width + 128),
                 by_rows(2 * half),
                 by_rows(2 * half),
                 by_rows(2 * half),
@@ -1015,7 +1209,7 @@
                 pltpu.VMEM((width, half), F32),
                 pltpu.VMEM((width, half), F32),
                 pltpu.VMEM((half, width), F32),
-                DMA((3, 2)),
+                DMA((3, 3)),
             ],
         ),
         compiler_params=pltpu.CompilerParams(vmem_limit_bytes=ROOM),
@@ -1111,7 +1305,20 @@
     )(side, *arrived, *placed)
 
 
-def project_kernel(t_ref, w_ref, side_ref, flag_ref, cos_ref, sin_ref, ga_ref, gq_ref, gk_ref, h_ref, q_ref, kv_ref, qp_ref, kp_ref):
+def project_kernel(block_order, lengths, group, t_ref, w_ref, side_ref, flag_ref, freq_ref, ga_ref, gq_ref, gk_ref, h_ref, q_ref, kv_ref, qp_ref, kp_ref, cos_ref, sin_ref):
+    tile = t_ref.shape[0]
+    row = lax.broadcasted_iota(jnp.int32, (tile, HEAD_WIDTH), 0)
+    lane = lax.broadcasted_iota(jnp.int32, (tile, HEAD_WIDTH), 1)
+    first_block = group[0] * 16 + pl.program_id(0) * (tile // BLK)
+    position = row * 0
+    for at in range(tile // BLK):
+        inside = block_order[first_block + at] * BLK + row - at * BLK
+        position = jnp.where(row >= at * BLK, inside, position)
+    angles = (position - start_of(lengths, position)).astype(F32) * freq_ref[...]
+    cosine = jnp.cos(angles)
+    sine_tab = jnp.where(lane < HEAD_WIDTH // 2, -1.0, 1.0) * jnp.sin(angles)
+    cos_ref[...] = cosine
+    sin_ref[...] = sine_tab
     rows = t_ref[...].astype(F32)
     inverse = lax.rsqrt(jnp.mean(rows * rows, axis=1, keepdims=True) + EPSILON)
     hidden = (rows * inverse * ga_ref[...]).astype(BF)
@@ -1120,7 +1327,6 @@
     own = qkv[:, 2 * HEAD_WIDTH :]
     other = matmul(hidden, side_ref[...])
     first = flag_ref[0:1, :] > 0.5
-    cosine, sine_tab = cos_ref[...], sin_ref[...]
 
     def turned(value, gain):
         root = lax.rsqrt(jnp.mean(value * value, axis=1, keepdims=True) + EPSILON)
@@ -1137,43 +1343,55 @@
     kv_ref[:, HEAD_WIDTH:] = jnp.where(first, other, own).astype(BF)
 
 
-def project(tokens, weights, side, first, cosine, sine_tab, gain, gain_query, gain_key):
+def project(block_order, lengths, group, tokens, weights, side, first, frequency, gain, gain_query, gain_key):
     rows, width = tokens.shape
     tile = 256
     sds = jax.ShapeDtypeStruct
 
     def by_rows(columns):
-        return pl.BlockSpec((tile, columns), lambda i: (i, 0))
+        return pl.BlockSpec((tile, columns), lambda i, *_: (i, 0))
 
     def whole(value):
-        return pl.BlockSpec(value.shape, lambda i: (0, 0))
+        return pl.BlockSpec(value.shape, lambda i, *_: (0, 0))
 
     return pl.pallas_call(
         project_kernel,
-        grid=(rows // tile,),
         out_shape=(
             sds((rows, width), BF),
             sds((rows, 256), BF),
             sds((rows, 256), BF),
             sds((rows, 256), F32),
             sds((rows, 128), F32),
+            sds((rows, 128), F32),
+            sds((rows, 128), F32),
         ),
-        in_specs=[
-            by_rows(width),
-            whole(weights),
-            whole(side),
-            whole(first),
-            by_rows(128),
-            by_rows(128),
-            whole(gain),
-            whole(gain_query),
-            whole(gain_key),
-        ],
-        out_specs=[by_rows(width), by_rows(256), by_rows(256), by_rows(256), by_rows(128)],
+        grid_spec=pltpu.PrefetchScalarGridSpec(
+            num_scalar_prefetch=3,
+            grid=(rows // tile,),
+            in_specs=[
+                by_rows(width),
+                whole(weights),
+                whole(side),
+                whole(first),
+                whole(frequency),
+                whole(gain),
+                whole(gain_query),
+                whole(gain_key),
+            ],
+            out_specs=[
+                by_rows(width),
+                by_rows(256),
+                by_rows(256),
+                by_rows(256),
+                by_rows(128),
+                by_rows(128),
+                by_rows(128),
+            ],
+        ),
         compiler_params=pltpu.CompilerParams(vmem_limit_bytes=ROOM),
         name="project",
         cost_estimate=cost(8),
-    )(tokens, weights, side, first, cosine, sine_tab, gain, gain_query, gain_key)
+    )(block_order, lengths, group, tokens, weights, side, first, frequency, gain, gain_query, gain_key)
 
 
 def project_back_kernel(dq_ref, ds_ref, qp_ref, kp_ref, cos_ref, sin_ref, h_ref, w_ref, side_ref, gq_ref, gk_ref, flag_ref, part_ref, late_ref, side_w, total, gains):
@@ -1312,7 +1530,6 @@
     place = lax.rem(me, 8)
     group = lax.div(me, 8)
     row_tokens = 8 * rows
-    row_blocks = row_tokens // BLK
 
     def swap(value):
         return lax.ppermute(value, "wsh", [(0, 1), (1, 0)])
@@ -1371,42 +1588,22 @@
     pick = my_ranks[:, None, :] == jnp.arange(slots, dtype=jnp.int32)[None, :, None]
     pick_low = pick.astype(BF).reshape(chips * slots, 2 * rows)
     cot_rows = matmul(pick_low, chip_cot.reshape(2 * rows, width)).astype(BF)
-    my_blocks = lax.dynamic_slice_in_dim(block_order, group * row_blocks, row_blocks, 0)
-    positions = (my_blocks[:, None] * BLK + jnp.arange(BLK, dtype=jnp.int32)[None, :]).reshape(row_tokens)
-    starts = seq_starts(positions, seq_lengths)
-    cosine, sine_tab = rope_tables(positions - starts)
-    inverse_order = (
-        jnp.zeros((block_count,), jnp.int32)
-        .at[block_order]
-        .set(jnp.arange(block_count, dtype=jnp.int32))
-    )
-    smaller = jnp.sum((my_blocks[None, :] < my_blocks[:, None]).astype(jnp.int32), axis=1)
-    order = jnp.sum(
-        jnp.where(
-            smaller[None, :] == jnp.arange(row_blocks, dtype=jnp.int32)[:, None],
-            jnp.arange(row_blocks, dtype=jnp.int32)[None, :],
-            0,
-        ),
-        axis=1,
-    )
-    block_starts = starts.reshape(row_blocks, BLK)
-    pair_blocks = jnp.take(my_blocks, order).reshape(-1, 2)
-    low = jnp.min(jnp.take(block_starts[:, 0], order).reshape(-1, 2), axis=1) // CHUNK
-    high = jnp.max(pair_blocks, axis=1) * BLK // CHUNK + 1
-    last_start = jnp.max(jnp.take(block_starts[:, BLK - 1], order).reshape(-1, 2), axis=1)
-    inner_low = jnp.clip((last_start + CHUNK - 1) // CHUNK, low, high)
-    inner_high = jnp.clip((jnp.min(pair_blocks, axis=1) * BLK + 1) // CHUNK, inner_low, high)
-    plan = (order, low, inner_low, inner_high, high, inverse_order)
-
-    def strips(per_token):
-        by_block = jnp.take(per_token.reshape(row_blocks, BLK), order, axis=0).reshape(-1, 2, 1, BLK)
-        return jnp.broadcast_to(by_block, (row_blocks // 2, 2, 2, BLK)).reshape(-1, 1, 4 * BLK)
-
-    q_pos, q_start = strips(positions), strips(starts)
-
+    half_dim = HEAD_WIDTH // 2
+    frequency = jnp.power(ROPE_BASE, -2.0 * jnp.arange(half_dim, dtype=jnp.float32) / HEAD_WIDTH)
+    frequency = jnp.concatenate([frequency, frequency])[None, :]
     row_rows = row_rows.reshape(row_tokens, width)
-    hidden_one, queries, kv, q_pre, k_pre = project(
-        row_rows, w_main, w_side, flag(core == 0), cosine, sine_tab, g_attn[None, :], g_query[None, :], g_key[None, :]
+    hidden_one, queries, kv, q_pre, k_pre, cosine, sine_tab = project(
+        block_order,
+        seq_lengths,
+        group.reshape(1),
+        row_rows,
+        w_main,
+        w_side,
+        flag(core == 0),
+        frequency,
+        g_attn[None, :],
+        g_query[None, :],
+        g_key[None, :],
     )
     kv_all = gather_keys(kv, 1).reshape(block_count * BLK, 256)
     late_all, kv_all = after(late_all, kv_all)
@@ -1415,14 +1612,15 @@
     (cot_rows, other_gate), kv_all = after((cot_rows, other_gate), kv_all)
     gate_back = swap(other_gate)
     cot_there = exchange_behind(cot_rows.reshape(chips, slots, width)).reshape(chips * slots, width)
-    heads, lse = attend(plan, queries, kv_all, q_pos, q_start)
+    heads, lse, plan = attend(block_order, seq_lengths, group.reshape(1), queries, kv_all)
 
     attn_parts = to_low(times_transposed(heads, wo_t)).reshape(8, rows, width)
     (gate_back, cot_there, other_up, other_down), attn_parts = after(
         (gate_back, cot_there, other_up, other_down), attn_parts
     )
-    up_back = swap(other_up)
-    attn_total = reduce_row(attn_parts, 2, True)[0].reshape(2 * rows, width)
+    up_cut = width * 5 // 8
+    attn_total, up_first = reduce_row(attn_parts, 2, True, swapped_whole=other_up[:up_cut])
+    attn_total = attn_total.reshape(2 * rows, width)
     chip_stream = lax.dynamic_slice_in_dim(row_rows, (place - core) * rows, 2 * rows, 0).astype(F32)
     chip_residual = chip_stream + attn_total
     chip_inverse_two = inverse_root(chip_residual)
@@ -1452,37 +1650,37 @@
     gate_tile = to_low(
         jnp.where(jnp.arange(128)[None, :] < 64, slot_gates[0], slot_gates[1])
     ).reshape(chips, slots, 128)
-    (up_back, other_down), gate_tile = after((up_back, other_down), gate_tile)
+    (other_down, other_up), gate_tile = after((other_down, other_up), gate_tile)
     down_back = swap(other_down)
+    up_back = (up_first, swap(other_up[up_cut:]))
     arrived, gate_there = exchange([out_rows, gate_tile], 3)
     arrived = arrived.reshape(chips * slots, width)
     side = wsh.reshape(1)
     gate_there = gate_there.reshape(chips * slots, 128)
-    y_rows, d_rows, d_gate_slots, activated, d_gate_pre, d_up_pre, d_pairs = run_expert(
-        side, arrived, cot_there, gate_there, (w_gate, w_up, w_down), (gate_back, up_back, down_back)
+    y_rows, d_rows, activated, d_gate_pre, d_up_pre, d_pairs = run_expert(
+        side, arrived, cot_there, gate_there, (w_gate, w_up, w_down), (gate_back, *up_back, down_back)
     )
     *own_grads, other_gate, other_up, other_down = expert_grads(
         side, arrived, d_pairs, activated, d_gate_pre, d_up_pre
     )
     gate_grad_back = swap(other_gate)
-    (other_up, other_down), d_gate_slots = after((other_up, other_down), d_gate_slots)
-    d_back, d_gate_back = exchange(
-        [d_rows.reshape(chips, slots, width), d_gate_slots.reshape(chips, slots, 128)], 4
-    )
-    (y_rows, gate_grad_back), d_back = after((y_rows, gate_grad_back), d_back)
+    d_back = exchange_behind(d_rows.reshape(chips, slots, width + 128))
+    y_rows, d_back = after(y_rows, d_back)
     y_back = exchange_behind(y_rows.reshape(chips, slots, width))
 
     def collect(back):
-        return to_low(transposed_times(pick_low, back.reshape(chips * slots, width))).reshape(2, rows, width)
-
-    d_gate_back = d_gate_back.reshape(chips * slots, 128)
+        return to_low(transposed_times(pick_low, back.reshape(chips * slots, -1)))
+
+    d_back = d_back.reshape(chips * slots, width + 128)
     d_gates_part = sum(
         transposed_times(
-            pick_low, jnp.where(of_expert, d_gate_back[:, at : at + 1], jnp.zeros((), BF))
+            pick_low, jnp.where(of_expert, d_back[:, at : at + 1], jnp.zeros((), BF))
         )
-        for at in (0, 64)
+        for at in (width, width + 64)
     ).reshape(2, rows, experts)
-    d_hidden_moe, d_gates = reduce_chip(collect(d_back), d_gates_part, 5)
+    d_part = collect(d_back)[:, :width].reshape(2, rows, width)
+    (gate_grad_back, other_up, other_down), d_part = after((gate_grad_back, other_up, other_down), d_part)
+    d_hidden_moe, d_gates = reduce_chip(d_part, d_gates_part, 5)
     residual = my_rows(chip_residual)
 
     own_gates = my_rows(gates)
@@ -1514,11 +1712,12 @@
         ],
         axis=1,
     )
-    early = lax.all_to_all(early, "ctx", split_axis=0, concat_axis=0, tiled=True)
-    d_queries, d_kv = attend_back(plan, queries, heads, d_attn_late, wo_t, kv_all, q_pos, q_start, lse)
-    (early, down_grad_back), d_kv = after((early, down_grad_back), d_kv)
+    d_queries, d_kv = attend_back(
+        plan, seq_lengths, queries, heads, d_attn_late, late_all, kv_all, lse
+    )
+    down_grad_back, d_kv = after(down_grad_back, d_kv)
     swapped_grads = (gate_grad_back, up_grad_back, down_grad_back)
-    d_side = reduce_keys(d_kv, 8)
+    d_side, early = reduce_keys(d_kv, early, 8)
     flags = jnp.concatenate(
         [
             flag(is_key)[:1],
@@ -1543,9 +1742,13 @@
         flags,
     )
     d_hidden_parts = d_hidden_parts.reshape(8, rows, width)
-    late, d_hidden_parts = after(late, d_hidden_parts)
-    late = lax.all_to_all(late, "ctx", split_axis=0, concat_axis=0, tiled=True)
-    d_hidden_one, moe_total = reduce_row(d_hidden_parts, 9, False, collect(y_back))
+    d_hidden_one, moe_total, late = reduce_row(
+        d_hidden_parts,
+        9,
+        False,
+        extra=collect(y_back).reshape(2, rows, width),
+        owned=(late,),
+    )
     out_stream = residual + moe_total
     own_stream = tokens.astype(F32)
     d_stream_norm, _ = norm_back(own_stream, inverse_root(own_stream), g_attn, d_hidden_one)
@@ -1554,21 +1757,17 @@
 
     grad_gate, grad_up, grad_down = place_other(side, swapped_grads, own_grads)
 
-    def summed(value, terms):
-        return jnp.sum(value.astype(F32).reshape((8,) + terms + value.shape[1:]), axis=0)
-
-    early_q = summed(early[:, : 2 * depth], (8,)).reshape(8, 2, depth, 128)
+    early, late = early.astype(F32), late.astype(F32)
+    early_q = early[:, : 2 * depth].reshape(8, 2, depth, 128)
     grad_out = early_q.transpose(0, 1, 3, 2).reshape(8 * 256, depth)
-    grad_router = jnp.sum(early[:, 2 * depth : 3 * depth].astype(F32), axis=0)
-    grad_gain_ffn = jnp.sum(early[:, 3 * depth, :depth].astype(F32), axis=0)
-    late_q = summed(late[:, : 2 * depth], (8,)).reshape(8, 2, depth, 128)
+    grad_router = jnp.sum(early[:, 2 * depth : 3 * depth], axis=0)
+    grad_gain_ffn = jnp.sum(early[:, 3 * depth, :depth], axis=0)
+    late_q = late[:, : 2 * depth].reshape(8, 2, depth, 128)
     grad_query = late_q.transpose(2, 0, 1, 3).reshape(depth, 8 * 256)
-    late_kv = jnp.sum(
-        late[:, 2 * depth : 3 * depth].astype(F32).reshape(8, 2, 2, 2, depth, 128), axis=(0, 3)
-    )
+    late_kv = jnp.sum(late[:, 2 * depth : 3 * depth].reshape(2, 2, 2, depth, 128), axis=2)
     grad_key = late_kv[:, 0].transpose(1, 0, 2).reshape(depth, 256)
     grad_value = late_kv[:, 1].transpose(1, 0, 2).reshape(depth, 256)
-    gain_parts = jnp.sum(late[:, 3 * depth : 3 * depth + 2].astype(F32), axis=0)
+    gain_parts = jnp.sum(late[:, 3 * depth : 3 * depth + 2], axis=0)
     gain_attn_part = (
         jnp.sum(rounded(w_query) * grad_query, axis=1)
         + jnp.sum(rounded(key_weight) * grad_key, axis=1)

time: 680 us -> 622 us (0.915)
  Pallas kernels: 473 us -> 440 us
  starting transfers between devices: 51.6 us -> 37.8 us
    pallas_call x2 -> x1, Pallas kernels: 89 us -> 46.8 us  [exchange(): pl.pallas_call(body, out_shape=[jax.ShapeDtypeStruct(a.shape, a.dtype) fo...]
    all_to_all x2 -> x3, waiting for transfers between devices: 0.01 us -> 36.2 us  [exchange_behind(): lax.all_to_all(value, ('ctx', 'wsh'), split_axis=0, concat_axis=0, tiled=...]
    ppermute x6, waiting for transfers between devices: 40.9 us -> 8.76 us  [swap(): return lax.ppermute(value, 'wsh', [(0, 1), (1, 0)])]
    pallas_call x4, Pallas kernels: 137 us -> 166 us  [the longest x2 95.3 us: reduce_row(): pl.pallas_call(body, out_shape=shapes, in_specs=spaces, out_specs=spaces,...]
    all_to_all x2 -> x0, starting transfers between devices: 25 us -> none  [the longest x1 15.5 us: local(): lax.all_to_all(early, 'ctx', split_axis=0, concat_axis=0, tiled=True)]
    pallas_call x1, Pallas kernels: 53.5 us -> 38.3 us  [gather_first(): pl.pallas_call(body, out_shape=(sds((64,) + weights.shape[1:], weights.dt...]
    all_to_all x2 -> x3, starting transfers between devices: 16.8 us -> 26.1 us  [exchange_behind(): lax.all_to_all(value, ('ctx', 'wsh'), split_axis=0, concat_axis=0, tiled=...]
  transfers between devices with their start and end apart: 11 -> 10, of which waited for: 2 -> 4; matrix products, arithmetic and copies ran while one was open for 11% -> 8% of each run, Pallas kernels for 43% -> 33%
where the time goes in v4:
time: 622 us; the launch traced here: 618 us
  Pallas kernels  440 us (71%)
  waiting for transfers between devices  45 us (7%)
  starting transfers between devices  37.8 us (6%)
  other arithmetic  34.5 us (6%)
  matrix products  29.4 us (5%)
  local copies, waits for them, and re-layouts  24.3 us (4%)
    pallas_call x2, Pallas kernels, reduce_row(): pl.pallas_call(body, out_shape=shapes, in_specs=spaces, out_specs=spaces,...  95.3 us
    pallas_call x1, Pallas kernels, reduce_keys(): pl.pallas_call(body, out_shape=(jax.ShapeDtypeStruct(block, F32), jax.Sha...  59.4 us
    pallas_call x1, Pallas kernels, exchange(): pl.pallas_call(body, out_shape=[jax.ShapeDtypeStruct(a.shape, a.dtype) fo...  46.8 us
    pallas_call x1, Pallas kernels, gather_first(): pl.pallas_call(body, out_shape=(sds((64,) + weights.shape[1:], weights.dt...  38.3 us
    all_to_all x3, waiting for transfers between devices, exchange_behind(): lax.all_to_all(value, ('ctx', 'wsh'), split_axis=0, concat_axis=0, tiled=...  36.2 us
    pallas_call x1, Pallas kernels, gather_keys(): pl.pallas_call(body, out_shape=jax.ShapeDtypeStruct((8,) + rows.shape, ro...  33.6 us
    pallas_call x1, Pallas kernels, attend_back(): pl.pallas_call(backward_kernel, out_shape=(sds(queries.shape, F32), sds(d...  32.3 us
    pallas_call x1, Pallas kernels, run_expert(): pl.pallas_call(expert_kernel, out_shape=(sds((count, width), BF), sds((co...  26.1 us
  transfers between devices with their start and end apart: 10, of which 4 were waited for; matrix products, arithmetic and copies ran while one was open for 8% of the time, Pallas kernels for 33%

profile of v4, /device:TPU:0, one launch (start us, length us, event | category | flops | bytes accessed | tf_op | source)
XLA Modules:
  0.0 618.0 jit_solution(16093297459184386830)
XLA Ops:
  2.3 1.0 convert_element_type.185
  4.0 1.0 convert_element_type.189
  5.8 1.3 fusion.46.s_in
  7.2 38.3 %gather_first.1 = (bf16[64,32,384]{2,1,0:T(8,128)(2,1)}, bf16[8,128,2048]{2,1,0:T(8,128)(2,1)}, f32[64,8,128]{2,1,0:T(8,128)}, s32[2,8,128]{2,1,0:T(8,128)}, bf1...) custom-call(bf16[8,32,384]{2,1,0:T(8,128)(2,1)} %pad_maximum_fusion., ...), custom_call_target="tpu_custom_call" | custom-call | bytes 48000000 | tf_op jit(solution)/shard_map/gather_first/pallas_call | solution.py:284
  45.5 1.3 tile.4
  46.9 8.0 %all-to-all-start = ((bf16[64,32,384]{2,1,0:T(8,128)(2,1)}), bf16[64,32,384]{2,1,0:T(8,128)(2,1)S(1)}, u32[]{:S(2)}, u32[]{:S(2)}) async-start(bf16[64,32,384]{2,1,0:T(8,128)(2,1)} %bitcast.18), calls=%async_computation | async-start | bytes 3145728 | tf_op jit(solution)/shard_map/all_to_all | solution.py:1567
  54.8 1.8 fusion.40
  60.2 11.2 %project.1 = (bf16[1024,2048]{1,0:T(8,128)(2,1)}, bf16[1024,256]{1,0:T(8,128)(2,1)}, bf16[1024,256]{1,0:T(8,128)(2,1)}, f32[1024,256]{1,0:T(8,128)}, f32[1024,12...) custom-call(s32[128]{0:T(128)} %block_order.3, s32[4]{0:T(128)} %lengths.5, s32[1]{0:T(128)} %bitcast.20.group, ...), custom_call_target="tpu_custom_call" | custom-call | bytes 9600000 | tf_op jit(solution)/shard_map/project/pallas_call | solution.py:1357
  71.3 33.6 %gather_keys.1 = bf16[8,1024,256]{2,1,0:T(8,128)(2,1)} custom-call(bf16[1024,256]{1,0:T(8,128)(2,1)} %get-tuple-element.100.src), custom_call_target="tpu_custom_call" | custom-call | bytes 36000000 | tf_op jit(solution)/shard_map/gather_keys/pallas_call | solution.py:376
  105.0 2.6 convolution_convert_fusion.2
  107.7 8.2 %all-to-all-start.1 = ((bf16[32,24,2048]{2,1,0:T(8,128)(2,1)}), bf16[32,24,2048]{2,1,0:T(8,128)(2,1)}, u32[]{:S(2)}, u32[]{:S(2)}) async-start(bf16[32,24,2048]{2,1,0:T(8,128)(2,1)} %bitcast.27), calls=%async_computation.1 | async-start | bytes 6291456 | tf_op jit(solution)/shard_map/all_to_all | solution.py:845
  117.0 0.9 bitcast_compare_fusion
  117.9 1.4 reshape.391
  120.0 1.4 eq.99
  121.9 19.0 %attend.1 = (bf16[1024,256]{1,0:T(8,128)(2,1)}, f32[8,1,256]{2,1,0:T(1,128)}, s32[256]{0:T(256)}) custom-call(s32[128]{0:T(128)} %block_order.3, s32[4]{0:T(128)} %lengths.5, s32[1]{0:T(128)} %bitcast.20.group, bf16[1024,256]{1,0:T(8,128)(2,1)} %get-tuple-element.106.q_ref, bf16[8192,256]{1,0:T(8,128)(2,1)} %bitcast.161), custom_call_target="tpu_custom_call" | custom-call | bytes 20400000 | tf_op jit(solution)/shard_map/attend/pallas_call | solution.py:985
  141.0 4.3 convolution_convert_fusion
  145.3 7.4 %collective-permute-done.g_other = bf16[2048,384]{1,0:T(8,128)(2,1)S(1)} collective-permute-done((bf16[2048,384]{1,0:T(8,128)(2,1)}, bf16[2048,384]{1,0:T(8,128)(2,1)S(1)}, u32[]{:S(2)}, u32[]{:S(2)}) %collective-permute-start) | collective-permute-done | bytes 1572896 | tf_op jit(solution)/shard_map/ppermute | solution.py:1535
  152.8 5.4 all-to-all-done.1
  158.2 2.2 slice.112.refs_1_
  160.5 42.4 %reduce_row.2 = (f32[2,128,2048]{2,1,0:T(8,128)}, bf16[1280,384]{1,0:T(8,128)(2,1)}) custom-call(bf16[8,128,2048]{2,1,0:T(8,128)(2,1)} %bitcast.163, bf16[1280,384]{1,0:T(8,128)(2,1)} %slice.112.refs_1_), custom_call_target="tpu_custom_call" | custom-call | bytes 48000000 | tf_op jit(solution)/shard_map/reduce_row/pallas_call | solution.py:630
  202.9 2.2 multiply_reduce_fusion
  205.4 1.9 fusion.63
  208.9 1.6 select_convert_fusion.refs_1_
  210.5 2.3 collective-permute-start.2
  212.8 1.1 slice.115
  214.2 2.7 convolution_convert_fusion.1
  216.9 46.8 %exchange.1 = (bf16[32,24,2048]{2,1,0:T(8,128)(2,1)}, bf16[32,24,128]{2,1,0:T(8,128)(2,1)}) custom-call(bf16[32,24,2048]{2,1,0:T(8,128)(2,1)} %bitcast.164, bf16[32,24,128]{2,1,0:T(8,128)(2,1)} %select_convert_fusion.refs_1_), custom_call_target="tpu_custom_call" | custom-call | bytes 57600000 | tf_op jit(solution)/shard_map/exchange/pallas_call | solution.py:826
  263.7 0.8 copy-done.11
  265.1 26.1 %run_expert.1 = (bf16[768,2048]{1,0:T(8,128)(2,1)}, bf16[768,2176]{1,0:T(8,128)(2,1)}, bf16[768,768]{1,0:T(8,128)(2,1)}, bf16[768,768]{1,0:T(8,128)(2,1)}, bf16[...) custom-call(s32[1]{0:T(128)} %bitcast.31.side, bf16[768,2048]{1,0:T(8,128)(2,1)} %bitcast.171, ...), custom_call_target="tpu_custom_call" | custom-call | bytes 30000000 | tf_op jit(solution)/shard_map/run_expert/pallas_call | solution.py:1183
  291.2 6.9 %all-to-all-start.2 = ((bf16[32,24,2176]{2,1,0:T(8,128)(2,1)}), bf16[32,24,2176]{2,1,0:T(8,128)(2,1)}, u32[]{:S(2)}, u32[]{:S(2)}) async-start(bf16[32,24,2176]{2,1,0:T(8,128)(2,1)} %bitcast.179), calls=%async_computation.2 | async-start | bytes 6684672 | tf_op jit(solution)/shard_map/all_to_all | solution.py:845
  298.2 13.6 %expert_grads.1 = (f32[2,2048,384]{2,1,0:T(8,128)}, f32[2,2048,384]{2,1,0:T(8,128)}, f32[2,384,2048]{2,1,0:T(8,128)}, bf16[2048,384]{1,0:T(8,128)(2,1)}, bf16[20...) custom-call(s32[1]{0:T(128)} %bitcast.31.side, bf16[768,2048]{1,0:T(8,128)(2,1)} %bitcast.172, ...), custom_call_target="tpu_custom_call" | custom-call | bytes 14400000 | tf_op jit(solution)/shard_map/expert_grads/pallas_call | solution.py:1248
  311.9 30.8 %all-to-all-done.2 = bf16[32,24,2176]{2,1,0:T(8,128)(2,1)} async-done(((bf16[32,24,2176]{2,1,0:T(8,128)(2,1)}), bf16[32,24,2176]{2,1,0:T(8,128)(2,1)}, u32[]{:S(2)}, u32[]{:S(2)}) %all-to-all-start.2) | async-done | bytes 3342368 | tf_op jit(solution)/shard_map/all_to_all | solution.py:845
  342.6 11.0 %all-to-all-start.3 = ((bf16[32,24,2048]{2,1,0:T(8,128)(2,1)}), bf16[32,24,2048]{2,1,0:T(8,128)(2,1)}, u32[]{:S(2)}, u32[]{:S(2)}) async-start(bf16[32,24,2048]{2,1,0:T(8,128)(2,1)} %bitcast.180), calls=%async_computation.3 | async-start | bytes 6291456 | tf_op jit(solution)/shard_map/all_to_all | solution.py:845
  353.6 1.3 slice_reduce_fusion
  355.3 3.1 convolution_bitcast_fusion
  358.4 1.0 convolution_add_fusion
  359.4 1.1 slice.199
  360.5 20.0 %reduce_chip.1 = (f32[128,2048]{1,0:T(8,128)}, f32[128,128]{1,0:T(8,128)}) custom-call(bf16[2,128,2048]{2,1,0:T(8,128)(2,1)} %bitcast.178, f32[2,128,128]{2,1,0:T(8,128)} %bitcast.202), custom_call_target="tpu_custom_call" | custom-call | bytes 20400000 | tf_op jit(solution)/shard_map/reduce_chip/pallas_call | solution.py:686
  380.5 1.0 multiply_reduce_fusion.4
  381.6 0.9 multiply_convert_fusion.1
  382.5 1.9 multiply_reduce_fusion.1
  385.7 1.0 convert_convert_fusion
  387.4 0.9 convert_element_type.209.src
  388.3 25.0 %gather_row.1 = bf16[8,128,2048]{2,1,0:T(8,128)(2,1)} custom-call(bf16[128,2048]{1,0:T(8,128)(2,1)} %convert_element_type.209.src), custom_call_target="tpu_custom_call" | custom-call | bytes 31200000 | tf_op jit(solution)/shard_map/gather_row/pallas_call | solution.py:330
  413.4 2.2 convolution_convert_fusion.4
  415.5 4.6 convolution_convert_fusion.3
  420.1 1.3 collective-permute-done.4.refs_1_
  421.9 1.3 fusion.62
  423.2 2.5 fusion.2.src4
  425.6 32.3 %attend_back.1 = (f32[1024,256]{1,0:T(8,128)}, bf16[2,8,2,512,128]{4,3,2,1,0:T(8,128)(2,1)}) custom-call(s32[256]{0:T(256)} %get-tuple-element.113.plan, s32[4]{0:T(128)} %lengths.5, bf16[1024,256]{1,0:T(8,128)(2,1)} %get-tuple-element.106.q_ref, bf16[1024,256]{1,0:T(8,128)(2,1)} %get-tuple-element.108.heads_ref, bf16[1024,2048]{1,0:T(8,128)(2,1)} %bitcast.166, ...), custom_call_target="tpu_custom_call" | custom-call | bytes 28800000 | tf_op jit(solution)/shard_map/attend_back/pallas_call | solution.py:1083
  457.9 3.9 fusion.1
  461.8 59.4 %reduce_keys.1 = (f32[512,128]{1,0:T(8,128)}, bf16[8,112,128]{2,1,0:T(8,128)(2,1)}) custom-call(bf16[2,8,2,512,128]{4,3,2,1,0:T(8,128)(2,1)} %get-tuple-element.147.src, bf16[64,112,128]{2,1,0:T(8,128)(2,1)} %fusion.2.src4), custom_call_target="tpu_custom_call" | custom-call | bytes 48000000 | tf_op jit(solution)/shard_map/reduce_keys/pallas_call | solution.py:764
  521.9 12.1 %project_back.1 = (bf16[1024,2048]{1,0:T(8,128)(2,1)}, bf16[64,112,128]{2,1,0:T(8,128)(2,1)}) custom-call(f32[1024,256]{1,0:T(8,128)} %get-tuple-element.142.dq_ref, f32[512,128]{1,0:T(8,128)} %get-tuple-element.148.ds_ref, f32[1024,256]{1,0:T(8,128)} %get-tuple-element.149.qp_ref, f32[1024,128]{1,0:T(8,128)} %get-tuple-element.150.kp_ref, ...), custom_call_target="tpu_custom_call" | custom-call | bytes 14400000 | tf_op jit(solution)/shard_map/project_back/pallas_call | solution.py:1464
  534.0 52.9 %reduce_row.3 = (f32[128,2048]{1,0:T(8,128)}, f32[128,2048]{1,0:T(8,128)}, bf16[8,112,128]{2,1,0:T(8,128)(2,1)}) custom-call(bf16[8,128,2048]{2,1,0:T(8,128)(2,1)} %bitcast.177, bf16[2,128,2048]{2,1,0:T(8,128)(2,1)} %bitcast.189, bf16[64,112,128]{2,1,0:T(8,128)(2,1)} %get-tuple-element.156.refs_2_), custom_call_target="tpu_custom_call" | custom-call | bytes 48000000 | tf_op jit(solution)/shard_map/reduce_row/pallas_call | solution.py:630
  586.9 1.0 slice.145
  587.9 1.0 convert_element_type.220
  589.5 0.9 copy.71
  590.4 1.9 reshape.382
  594.5 1.1 multiply_reduce_fusion.3
  596.3 4.9 psum.7
  603.5 2.3 dynamic-slice_add_fusion
  606.4 0.9 reshape.387
  607.3 2.8 fusion.11
  610.1 7.7 %place_other.1 = (f32[2,2048,384]{2,1,0:T(8,128)}, f32[2,2048,384]{2,1,0:T(8,128)}, f32[2,384,2048]{2,1,0:T(8,128)}) custom-call(s32[1]{0:T(128)} %bitcast.31.side, bf16[2048,384]{1,0:T(8,128)(2,1)} %collective-permute-done.3.refs_0_, bf16[2048,384]{1,0:T(8,128)(2,1)} %collective-permute-done.4.refs_1_, ...), custom_call_target="tpu_custom_call", output_to_operand_aliasing={{0}: (4, {}), {1}: (5, {}), {2}: (6, {})} | custom-call | bytes 6000000 | tf_op jit(solution)/shard_map/place_other/pallas_call | solution.py:1288
  (141 shorter events, 21.7 us)
Async XLA Ops:
  1.4 4.3 copy-start.14
  45.5 11.8 %copy-start.25 = (f32[128]{0:T(128)S(1)}, f32[128]{0:T(128)}, u32[]{:S(2)}) copy-start(f32[128]{0:T(128)} %param.29) | copy-start | bytes 1540
  45.5 11.8 %copy-start.26 = (f32[128]{0:T(128)S(1)}, f32[128]{0:T(128)}, u32[]{:S(2)}) copy-start(f32[128]{0:T(128)} %param.28) | copy-start | bytes 1540
  45.5 11.8 %copy-start.19 = (s32[2,8,128]{2,1,0:T(8,128)S(1)}, s32[2,8,128]{2,1,0:T(8,128)}, u32[]{:S(2)}) copy-start(s32[2,8,128]{2,1,0:T(8,128)} %get-tuple-element.93) | copy-start | bytes 24580
  46.9 60.8 %all-to-all-start = ((bf16[64,32,384]{2,1,0:T(8,128)(2,1)}), bf16[64,32,384]{2,1,0:T(8,128)(2,1)S(1)}, u32[]{:S(2)}, u32[]{:S(2)}) async-start(bf16[64,32,384]{2,1,0:T(8,128)(2,1)} %bitcast.18), calls=%async_computation | async-start | bytes 3145728 | tf_op jit(solution)/shard_map/all_to_all | solution.py:1567
  71.3 33.7 %copy-start.10 = (bf16[2,128,2048]{2,1,0:T(8,128)(2,1)S(1)}, bf16[2,128,2048]{2,1,0:T(8,128)(2,1)}, u32[]{:S(2)}) copy-start(bf16[2,128,2048]{2,1,0:T(8,128)(2,1)} %get-tuple-element.94) | copy-start | bytes 3145732
  107.7 33.3 %copy-start = (bf16[64,32,384]{2,1,0:T(8,128)(2,1)}, bf16[64,32,384]{2,1,0:T(8,128)(2,1)S(1)}, u32[]{:S(2)}) copy-start(bf16[64,32,384]{2,1,0:T(8,128)(2,1)S(1)} %all-to-all-done) | copy-start | bytes 4718596
  107.7 50.5 %all-to-all-start.1 = ((bf16[32,24,2048]{2,1,0:T(8,128)(2,1)}), bf16[32,24,2048]{2,1,0:T(8,128)(2,1)}, u32[]{:S(2)}, u32[]{:S(2)}) async-start(bf16[32,24,2048]{2,1,0:T(8,128)(2,1)} %bitcast.27), calls=%async_computation.1 | async-start | bytes 6291456 | tf_op jit(solution)/shard_map/all_to_all | solution.py:845
  115.9 36.9 %collective-permute-start = (bf16[2048,384]{1,0:T(8,128)(2,1)}, bf16[2048,384]{1,0:T(8,128)(2,1)S(1)}, u32[]{:S(2)}, u32[]{:S(2)}) collective-permute-start(bf16[2048,384]{1,0:T(8,128)(2,1)} %get-tuple-element.102), channel_id=1, source_target_pairs={{0,1},{1,0},{2,3},{3,2},{4,5},{5,4},{6,7},{7,6},{8,9},{9,8},{10,11... | collective-permute-start | bytes 4718600 | tf_op jit(solution)/shard_map/ppermute | solution.py:1535
  152.8 50.1 %copy-start.6 = (bf16[2048,384]{1,0:T(8,128)(2,1)}, bf16[2048,384]{1,0:T(8,128)(2,1)S(1)}, u32[]{:S(2)}) copy-start(bf16[2048,384]{1,0:T(8,128)(2,1)S(1)} %collective-permute-done.g_other) | copy-start | bytes 4718596
  202.9 2.3 copy-start.16
  205.1 2.6 copy-start.22
  205.1 2.9 copy-start.20
  205.4 11.5 %copy-start.1 = (bf16[256,2048]{1,0:T(8,128)(2,1)}, bf16[256,2048]{1,0:T(8,128)(2,1)S(1)}, u32[]{:S(2)}) copy-start(bf16[256,2048]{1,0:T(8,128)(2,1)S(1)} %multiply_convert_fusion) | copy-start | bytes 3145732
  207.7 0.7 copy-start.12
  210.5 53.2 %collective-permute-start.2 = (bf16[384,2048]{1,0:T(8,128)(2,1)}, bf16[384,2048]{1,0:T(8,128)(2,1)S(1)}, u32[]{:S(2)}, u32[]{:S(2)}) collective-permute-start(bf16[384,2048]{1,0:T(8,128)(2,1)} %get-tuple-element.122), channel_id=1, source_target_pairs={{0,1},{1,0},{2,3},{3,2},{4,5},{5,4},{6,7},{7,6},{8,9},{9,8},{10,11... | collective-permute-start | bytes 4718600 | tf_op jit(solution)/shard_map/ppermute | solution.py:1535
  213.9 49.8 %collective-permute-start.1 = (bf16[768,384]{1,0:T(8,128)(2,1)S(1)}, bf16[768,384]{1,0:T(8,128)(2,1)S(1)}, u32[]{:S(2)}, u32[]{:S(2)}) collective-permute-start(bf16[768,384]{1,0:T(8,128)(2,1)S(1)} %slice.115), channel_id=1, source_target_pairs={{0,1},{1,0},{2,3},{3,2},{4,5},{5,4},{6,7},{7,6},{8,9},{9,8},{10,11... | collective-permute-start | bytes 1769480 | tf_op jit(solution)/shard_map/ppermute | solution.py:1535
  263.7 0.8 copy-start.11
  263.7 1.3 copy-start.7
  291.2 6.9 %copy-start.21 = (f32[256]{0:T(256)S(1)}, f32[256]{0:T(256)}, u32[]{:S(2)}) copy-start(f32[256]{0:T(256)} %copy-done.20) | copy-start | bytes 3076
  291.2 51.4 %all-to-all-start.2 = ((bf16[32,24,2176]{2,1,0:T(8,128)(2,1)}), bf16[32,24,2176]{2,1,0:T(8,128)(2,1)}, u32[]{:S(2)}, u32[]{:S(2)}) async-start(bf16[32,24,2176]{2,1,0:T(8,128)(2,1)} %bitcast.179), calls=%async_computation.2 | async-start | bytes 6684672 | tf_op jit(solution)/shard_map/all_to_all | solution.py:845
  311.8 48.6 %collective-permute-start.3 = (bf16[2048,384]{1,0:T(8,128)(2,1)}, bf16[2048,384]{1,0:T(8,128)(2,1)}, u32[]{:S(2)}, u32[]{:S(2)}) collective-permute-start(bf16[2048,384]{1,0:T(8,128)(2,1)} %get-tuple-element.130), channel_id=1, source_target_pairs={{0,1},{1,0},{2,3},{3,2},{4,5},{5,4},{6,7},{7,6},{8,9},{9,8},{10,11... | collective-permute-start | bytes 4718600 | tf_op jit(solution)/shard_map/ppermute | solution.py:1535
  342.6 12.3 %copy-start.23 = (s32[768]{0:T(1024)S(1)}, s32[768]{0:T(1024)}, u32[]{:S(2)}) copy-start(s32[768]{0:T(1024)} %eq.99) | copy-start | bytes 9220
  342.6 78.8 %all-to-all-start.3 = ((bf16[32,24,2048]{2,1,0:T(8,128)(2,1)}), bf16[32,24,2048]{2,1,0:T(8,128)(2,1)}, u32[]{:S(2)}, u32[]{:S(2)}) async-start(bf16[32,24,2048]{2,1,0:T(8,128)(2,1)} %bitcast.180), calls=%async_computation.3 | async-start | bytes 6291456 | tf_op jit(solution)/shard_map/all_to_all | solution.py:845
  358.3 22.2 %copy-start.13 = (f32[256,128]{1,0:T(8,128)S(1)}, f32[256,128]{1,0:T(8,128)}, u32[]{:S(2)}) copy-start(f32[256,128]{1,0:T(8,128)} %copy-done.12) | copy-start | bytes 393220
  358.4 24.1 %copy-start.17 = (f32[2048]{0:T(1024)S(1)}, f32[2048]{0:T(1024)}, u32[]{:S(2)}) copy-start(f32[2048]{0:T(1024)} %reshape.391) | copy-start | bytes 24580
  359.4 25.1 %copy-start.5 = (bf16[128,2048]{1,0:T(8,128)(2,1)S(1)}, bf16[128,2048]{1,0:T(8,128)(2,1)}, u32[]{:S(2)}) copy-start(bf16[128,2048]{1,0:T(8,128)(2,1)} %c_in.1) | copy-start | bytes 1572868
  380.5 4.0 copy-start.4
  384.4 0.7 copy-start.24
  384.9 36.6 %collective-permute-start.4 = (bf16[2048,384]{1,0:T(8,128)(2,1)}, bf16[2048,384]{1,0:T(8,128)(2,1)}, u32[]{:S(2)}, u32[]{:S(2)}) collective-permute-start(bf16[2048,384]{1,0:T(8,128)(2,1)} %get-tuple-element.138), channel_id=1, source_target_pairs={{0,1},{1,0},{2,3},{3,2},{4,5},{5,4},{6,7},{7,6},{8,9},{9,8},{10,11... | collective-permute-start | bytes 4718600 | tf_op jit(solution)/shard_map/ppermute | solution.py:1535
  421.5 40.4 %collective-permute-start.5 = (bf16[384,2048]{1,0:T(8,128)(2,1)}, bf16[384,2048]{1,0:T(8,128)(2,1)S(1)}, u32[]{:S(2)}, u32[]{:S(2)}) collective-permute-start(bf16[384,2048]{1,0:T(8,128)(2,1)} %get-tuple-element.145), channel_id=1, source_target_pairs={{0,1},{1,0},{2,3},{3,2},{4,5},{5,4},{6,7},{7,6},{8,9},{9,8},{10,11... | collective-permute-start | bytes 4718600 | tf_op jit(solution)/shard_map/ppermute | solution.py:1535
  461.8 72.1 %copy-start.8 = (bf16[384,2048]{1,0:T(8,128)(2,1)}, bf16[384,2048]{1,0:T(8,128)(2,1)S(1)}, u32[]{:S(2)}) copy-start(bf16[384,2048]{1,0:T(8,128)(2,1)S(1)} %collective-permute-done.5.refs_2_) | copy-start | bytes 4718596
  534.0 59.1 %copy-start.15 = (bf16[32,256]{1,0:T(8,128)(2,1)S(1)}, bf16[32,256]{1,0:T(8,128)(2,1)}, u32[]{:S(2)}) copy-start(bf16[32,256]{1,0:T(8,128)(2,1)} %copy-done.14) | copy-start | bytes 49156
  586.9 15.4 %copy-start.9 = (bf16[8,112,128]{2,1,0:T(8,128)(2,1)S(1)}, bf16[8,112,128]{2,1,0:T(8,128)(2,1)}, u32[]{:S(2)}) copy-start(bf16[8,112,128]{2,1,0:T(8,128)(2,1)} %get-tuple-element.160) | copy-start | bytes 688132
  589.5 16.3 %copy-start.18 = (f32[2048]{0:T(1024)S(1)}, f32[2048]{0:T(1024)}, u32[]{:S(2)}) copy-start(f32[2048]{0:T(1024)} %reshape.392) | copy-start | bytes 24580
  601.3 4.6 copy-start.2
  601.3 4.6 copy-start.3

commit v5 on v4

--- a/solution.py
+++ b/solution.py
@@ -45,19 +45,6 @@
     return lax.dot_general(
         left, right, (((0,), (0,)), ((), ())), preferred_element_type=jnp.float32
     )
-
-
-def norm_back(value_rows, inverse_rms, gain_vec, gradient):
-    weighted = gradient * gain_vec
-    mean_term = jnp.mean(weighted * value_rows, axis=-1, keepdims=True)
-    d_values = (
-        inverse_rms * weighted - value_rows * (inverse_rms * inverse_rms * inverse_rms) * mean_term
-    )
-    return (d_values, gradient * value_rows * inverse_rms)
-
-
-def inverse_root(value_rows):
-    return lax.rsqrt(jnp.mean(value_rows * value_rows, axis=-1, keepdims=True) + EPSILON)
 
 
 def coords(c):
@@ -173,27 +160,26 @@
         forward.wait()
 
 
-def cast_steps(wide, narrow, side):
-    sources, staging, lows, in_sems, out_sems = wide
-    steps = []
-    for src, dst in zip(sources, narrow):
-        at = 0 if src.shape[1] > src.shape[2] else 1
-        rows = staging[at].shape[1]
-        for chunk in range(src.shape[1] // rows):
-            steps.append((src, dst, at, pl.ds(chunk * rows, rows)))
+def cast_steps(steps, staging, lows, in_sems, out_sems):
     loads, stores = [], []
-    for index, (src, dst, at, span) in enumerate(steps):
-        slot = index % 2
-        loads.append(pltpu.make_async_copy(src.at[side, span], staging[at].at[slot], in_sems.at[slot]))
-        stores.append(pltpu.make_async_copy(lows[at].at[slot], dst.at[span], out_sems.at[slot]))
+    for index, (src, begin, dst, to, count, at) in enumerate(steps):
+        slot, span = index % 2, pl.ds(0, count)
+        loads.append(
+            pltpu.make_async_copy(
+                src.at[pl.ds(begin, count)], staging[at].at[slot, span], in_sems.at[slot]
+            )
+        )
+        stores.append(
+            pltpu.make_async_copy(lows[at].at[slot, span], dst.at[pl.ds(to, count)], out_sems.at[slot])
+        )
     loads[0].start()
     loads[1].start()
-    for index, (_, _, at, _) in enumerate(steps):
-        slot = index % 2
+    for index, step in enumerate(steps):
+        slot, count, at = index % 2, step[-2], step[-1]
         loads[index].wait()
         if index >= 2:
             stores[index - 2].wait()
-        lows[at][slot] = staging[at][slot].astype(BF)
+        lows[at][slot, :count] = staging[at][slot, :count].astype(BF)
         stores[index].start()
         if index + 2 < len(steps):
             loads[index + 2].start()
@@ -201,16 +187,32 @@
     stores[-1].wait()
 
 
+def cut_steps(src, parts, rows, at):
+    steps, begin = [], 0
+    for part in parts:
+        for to in range(0, part.shape[0], rows):
+            count = min(rows, part.shape[0] - to)
+            steps.append((src, begin + to, part, to, count, at))
+        begin += part.shape[0]
+    return steps
+
+
 COLUMN_STEPS = ((1, 0), (3, 0), (0, 1), (2, 0), (1, 1), (3, 1), (2, 1))
 ROW_STEPS = ((1, 0), (3, 0), (1, 1), (3, 1), (0, 1), (2, 0), (2, 1))
 
 
-def gather_first(weights, tokens, small, routes, cotangent, expert_weights):
-    def body(w_in, t_in, s_in, r_in, c_in, *refs):
+UP_CUT = (1280, 768)
+DOWN_GRAD_CUT = (240, 144)
+
+
+def gather_first(weights, gains, tokens, routes, cotangent, expert_weights):
+    def body(q_in, k_in, v_in, ga_in, gf_in, t_in, r_in, c_in, *refs):
         sources, refs = refs[:3], refs[3:]
         w_out, t_out, s_out, r_out, c_out = refs[:5]
-        lows, side_out, refs = refs[5:8], refs[8], refs[9:]
-        wide, row_s, row_r, pair, local, col_s, col_r, tall_f, flat_f, tall_b, flat_b, in_sems, out_sems = refs
+        gate_out, up_out, up_rest, down_out, side_out = refs[5:10]
+        refs = refs[10:]
+        wide, row_s, row_r, pair, local, col_s, col_r, tall_f, flat_f, tall_b, flat_b, in_sems, out_sems = refs[:13]
+        w_in, s_in = refs[13:]
         me, wsh = lax.axis_index("ctx"), lax.axis_index("wsh")
         core = lax.rem(me, 2)
         place = lax.rem(me, 8)
@@ -219,6 +221,15 @@
         row_peers = [shifted(me, 0, 0, dx, dk) for dx, dk in ROW_STEPS]
         col_peers = [shifted(me, dz, dy, 0, 0) for dz, dy in COLUMN_STEPS]
         barrier, amount = greet([(peer, wsh) for peer in row_peers + col_peers])
+        heads = q_in.shape[1] // 8
+        for at in range(8):
+            w_in[at, :, :heads] = q_in[:, at * heads : (at + 1) * heads].astype(BF)
+            side = (k_in, v_in)[at % 2]
+            begin = at // 4 * HEAD_WIDTH
+            w_in[at, :, heads:] = side[:, begin : begin + HEAD_WIDTH].astype(BF)
+        s_in[...] = jnp.zeros_like(s_in)
+        s_in[0:1, : ga_in.shape[1]] = ga_in[...]
+        s_in[1:2, : gf_in.shape[1]] = gf_in[...]
         locals_ = [
             pltpu.make_async_copy(w_in.at[place], w_out.at[me], local.at[0]),
             pltpu.make_async_copy(s_in, s_out.at[me], local.at[1]),
@@ -265,7 +276,13 @@
                 col_copies.append(copy)
         shares = [share(group, 7)]
         onward, forwards = row_gather_onward(t_out, me, wsh, row_copies, row_s, row_r)
-        cast_steps((sources, (tall_f, flat_f), (tall_b, flat_b), in_sems, out_sems), lows, 1 - wsh)
+        gate_in, up_in, down_in = [source.at[1 - wsh] for source in sources]
+        buffers = ((tall_f, flat_f), (tall_b, flat_b), in_sems, out_sems)
+        tall_rows, flat_rows = tall_f.shape[1], flat_f.shape[1]
+        cast_steps(
+            cut_steps(gate_in, (gate_out,), tall_rows, 0) + cut_steps(up_in, (up_out, up_rest), tall_rows, 0) + cut_steps(down_in, (down_out,), flat_rows, 1),
+            *buffers,
+        )
         row_gather_end(t_out, me, wsh, row_copies, onward, forwards, row_s, row_r)
         for at, (dz, dy) in enumerate(COLUMN_STEPS):
             col_copies[2 * at].wait_recv()
@@ -279,21 +296,22 @@
             copy.wait_send()
 
     sds = jax.ShapeDtypeStruct
-    tall = (expert_weights[0].shape[1] // 4, expert_weights[0].shape[2])
-    flat = (expert_weights[2].shape[1] // 4, expert_weights[2].shape[2])
+    _, deep, half = expert_weights[0].shape
+    depth, packed = weights[0].shape[0], weights[0].shape[1] // 8 + HEAD_WIDTH
+    tall, flat = (deep // 4, half), (half // 4, deep)
     return pl.pallas_call(
         body,
         out_shape=(
-            sds((64,) + weights.shape[1:], weights.dtype),
+            sds((64, depth, packed), BF),
             sds((8,) + tokens.shape, tokens.dtype),
-            sds((64,) + small.shape, small.dtype),
+            sds((64, 8, 128), F32),
             sds((2,) + routes.shape, routes.dtype),
             sds((2,) + cotangent.shape, cotangent.dtype),
         )
-        + tuple(sds(value.shape[1:], BF) for value in expert_weights)
-        + (sds((64, weights.shape[1], 128), weights.dtype),),
-        in_specs=[ANY] * 8,
-        out_specs=[ANY] * 9,
+        + tuple(sds((count, half), BF) for count in (deep, *UP_CUT))
+        + (sds((half, deep), BF), sds((64, depth, 128), BF)),
+        in_specs=[VMEM] * 5 + [ANY] * 6,
+        out_specs=[ANY] * 10,
         scratch_shapes=[
             DMA((4,)),
             DMA((9,)),
@@ -308,35 +326,45 @@
             pltpu.VMEM((2,) + flat, BF),
             DMA((2,)),
             DMA((2,)),
+            pltpu.VMEM((8, depth, packed), BF),
+            pltpu.VMEM((8, 128), F32),
         ],
         compiler_params=call_params(0),
         name="gather_first",
         cost_estimate=cost(40),
-    )(weights, tokens, small, routes, cotangent, *expert_weights)
-
-
-def gather_row(block, collective_id):
-    def body(src, out, row_s, row_r, local):
+    )(*weights, *gains, tokens, routes, cotangent, *expert_weights)
+
+
+def gather_row(block, swapped, collective_id):
+    def body(src, src2, out, out2, row_s, row_r, pair, local):
         me, wsh = lax.axis_index("ctx"), lax.axis_index("wsh")
-        barrier, amount = greet([(shifted(me, 0, 0, dx, dk), wsh) for dx, dk in ((1, 0), (3, 0), (0, 1))])
+        barrier, amount = greet(
+            [(shifted(me, 0, 0, dx, dk), wsh) for dx, dk in ((1, 0), (3, 0), (0, 1))] + [(me, 1 - wsh)]
+        )
         mine = pltpu.make_async_copy(src, out.at[lax.rem(me, 8)], local)
         mine.start()
         pl.semaphore_wait(barrier, amount)
         copies = row_gather_start(src, out, me, wsh, row_s, row_r)
+        cross = remote(src2, out2, pair.at[0], pair.at[1], me, 1 - wsh)
+        cross.start()
         onward, forwards = row_gather_onward(out, me, wsh, copies, row_s, row_r)
         row_gather_end(out, me, wsh, copies, onward, forwards, row_s, row_r)
         mine.wait()
+        cross.wait()
 
     return pl.pallas_call(
         body,
-        out_shape=jax.ShapeDtypeStruct((8,) + block.shape, block.dtype),
-        in_specs=[ANY],
-        out_specs=ANY,
-        scratch_shapes=[DMA((9,)), DMA((9,)), DMA],
+        out_shape=(
+            jax.ShapeDtypeStruct((8,) + block.shape, block.dtype),
+            jax.ShapeDtypeStruct(swapped.shape, swapped.dtype),
+        ),
+        in_specs=[ANY, ANY],
+        out_specs=[ANY, ANY],
+        scratch_shapes=[DMA((9,)), DMA((9,)), DMA((2,)), DMA],
         compiler_params=call_params(collective_id),
         name="gather_row",
         cost_estimate=cost(26),
-    )(block)
+    )(block, swapped)
 
 
 def gather_keys(rows, collective_id):
@@ -471,7 +499,11 @@
 
 def reduce_row(parts, collective_id, both, extra=None, swapped_whole=None, owned=()):
     has_whole = swapped_whole is not None
-    _, rows, width = parts.shape
+    is_product = isinstance(parts, tuple)
+    if is_product:
+        rows, width = parts[0].shape[0] // 8, parts[1].shape[0]
+    else:
+        _, rows, width = parts.shape
     block = (rows, width)
     pieces = 4
     columns = width // pieces
@@ -479,8 +511,13 @@
 
     def body(*refs):
         refs = list(refs)
-        src = refs.pop(0)
-        src2 = refs.pop(0) if has_extra else None
+        if is_product:
+            heads_ref, out_w = refs.pop(0), refs.pop(0)
+            src = refs.pop(-1)
+        else:
+            src = refs.pop(0)
+        if has_extra:
+            pick_ref, back_ref = refs.pop(0), refs.pop(0)
         src3 = refs.pop(0) if has_whole else None
         mine_in = [refs.pop(0) for _ in owned]
         out = refs.pop(0)
@@ -504,12 +541,21 @@
         barrier, amount = greet([(peer, wsh) for peer in greeted] + [(me, other)])
         pl.semaphore_wait(barrier, amount)
         if has_whole:
-            whole = remote(src3, out3, send.at[1, 9], recv.at[1, 9], me, other)
+            whole = remote(
+                src3, out3, send.at[1, 9], recv.at[1, 9], me, other
+            )
             whole.start()
         spans = [pl.ds(piece * columns, columns) for piece in range(pieces)]
         everything = pl.ds(0, rows)
         first = []
         for piece, span in enumerate(spans):
+            if is_product:
+                columns_of = slice(piece * columns, (piece + 1) * columns)
+                src[:, :, columns_of] = (
+                    times_transposed(heads_ref[...], out_w[columns_of, : heads_ref.shape[1]])
+                    .astype(BF)
+                    .reshape(8, rows, columns)
+                )
             for at, dx in enumerate((2, 1, 3, 0)):
                 chip = lax.rem(x + dx, 4)
                 copy = remote(
@@ -525,7 +571,8 @@
         for block4 in blocks:
             block4.along_z(me, wsh)
         if has_extra:
-            arrived2, swapped2 = refs[8:]
+            arrived2, swapped2, src2 = refs[8:]
+            src2[...] = matmul(pick_ref[...], back_ref[...]).astype(BF).reshape(src2.shape)
             give2 = remote(src2.at[1 - core], arrived2, send.at[0, 8], recv.at[0, 8], partner, wsh)
             give2.start()
         second = []
@@ -573,8 +620,9 @@
             )
             swap.start()
             swaps.append(swap)
-        for block4 in blocks:
-            block4.along_y(me, wsh)
+            if piece == pieces - 2:
+                for block4 in blocks:
+                    block4.along_y(me, wsh)
         for block4 in blocks:
             block4.along_row(me, wsh)
         if has_extra:
@@ -611,94 +659,98 @@
         DMA((pieces, 10)),
         DMA,
     ]
-    operands = [parts]
+    operands = list(parts) if is_product else [parts]
+    out_spaces = [VMEM]
     if has_extra:
         shapes.append(jax.ShapeDtypeStruct(block, F32))
-        scratch += [pltpu.VMEM(block, BF), pltpu.VMEM((2,) + block, BF)]
-        operands.append(extra)
+        scratch += [pltpu.VMEM(block, BF), pltpu.VMEM((2,) + block, BF), pltpu.VMEM((2,) + block, BF)]
+        operands += list(extra)
+        out_spaces.append(VMEM)
     spaces = [VMEM] * len(operands)
     if has_whole:
         shapes.append(jax.ShapeDtypeStruct(swapped_whole.shape, swapped_whole.dtype))
         operands.append(swapped_whole)
         spaces.append(ANY)
+        out_spaces.append(ANY)
     for value in owned:
         block8 = (8,) + value.shape[1:]
         shapes.append(jax.ShapeDtypeStruct(block8, BF))
         operands.append(value)
         spaces.append(VMEM)
+        out_spaces.append(VMEM)
         scratch += Owned.scratch(value)
+    if is_product:
+        scratch.append(pltpu.VMEM((8,) + block, BF))
     return pl.pallas_call(
         body,
         out_shape=shapes,
         in_specs=spaces,
-        out_specs=spaces,
+        out_specs=out_spaces,
         scratch_shapes=scratch,
         compiler_params=call_params(collective_id),
         name="reduce_row",
-        cost_estimate=cost(40),
+        cost_estimate=cost(1),
     )(*operands)
 
 
-def reduce_chip(parts, extra, collective_id):
-    _, rows, width = parts.shape
-    extra_block = None if extra is None else extra.shape[1:]
-
-    def body(*refs):
-        if extra is None:
-            src, out, arrived, swapped, total, send, recv = refs
-        else:
-            src, src2, out, out2, arrived, swapped, total, arrived2, swapped2, send, recv = refs
+def reduce_chip(pick, back, of_expert, width, collective_id):
+    rows = pick.shape[0] // 2
+    lanes = of_expert.shape[1]
+
+    def body(pick_ref, back_ref, of_ref, out, out2, src, src2, arrived, swapped, arrived2, swapped2, send, recv):
         me, wsh = lax.axis_index("ctx"), lax.axis_index("wsh")
         other = 1 - wsh
         core = lax.rem(me, 2)
         partner = shifted(me, 0, 0, 0, 1)
         barrier, amount = greet([(partner, wsh), (me, other)])
+        src[...] = matmul(pick_ref[...], back_ref[:, :width]).astype(BF).reshape(src.shape)
+        parts = [back_ref[:, at : at + 1] * of_ref[...] for at in (width, width + 64)]
+        src2[...] = (matmul(pick_ref[...], parts[0]) + matmul(pick_ref[...], parts[1])).reshape(src2.shape)
         pl.semaphore_wait(barrier, amount)
         give = remote(src.at[1 - core], arrived, send.at[0], recv.at[0], partner, wsh)
         give.start()
-        if extra is not None:
-            give2 = remote(src2.at[1 - core], arrived2, send.at[2], recv.at[2], partner, wsh)
-            give2.start()
+        give2 = remote(src2.at[1 - core], arrived2, send.at[2], recv.at[2], partner, wsh)
+        give2.start()
         give.wait()
         swapped[0] = (src[core].astype(F32) + arrived[...].astype(F32)).astype(BF)
         swap = remote(swapped.at[0], swapped.at[1], send.at[1], recv.at[1], me, other)
         swap.start()
-        if extra is not None:
-            give2.wait()
-            swapped2[0] = src2[core] + arrived2[...]
-            swap2 = remote(swapped2.at[0], swapped2.at[1], send.at[3], recv.at[3], me, other)
-            swap2.start()
-            swap2.wait()
-            out2[...] = swapped2[0] + swapped2[1]
+        give2.wait()
+        swapped2[0] = src2[core] + arrived2[...]
+        swap2 = remote(swapped2.at[0], swapped2.at[1], send.at[3], recv.at[3], me, other)
+        swap2.start()
+        swap2.wait()
+        out2[...] = swapped2[0] + swapped2[1]
         swap.wait()
         out[...] = swapped[0].astype(F32) + swapped[1].astype(F32)
 
     sds = jax.ShapeDtypeStruct
-    block = (rows, width)
-    shapes = [sds(block, F32)]
-    scratch = [pltpu.VMEM(block, BF), pltpu.VMEM((2,) + block, BF), pltpu.VMEM(block, F32)]
-    operands = [parts]
-    if extra is not None:
-        shapes.append(sds(extra_block, F32))
-        scratch += [pltpu.VMEM(extra_block, F32), pltpu.VMEM((2,) + extra_block, F32)]
-        operands.append(extra)
-    scratch += [DMA((4,)), DMA((4,))]
+    block, block2 = (rows, width), (rows, lanes)
     return pl.pallas_call(
         body,
-        out_shape=shapes,
-        in_specs=[VMEM] * len(operands),
-        out_specs=[VMEM] * len(operands),
-        scratch_shapes=scratch,
+        out_shape=(sds(block, F32), sds(block2, F32)),
+        in_specs=[VMEM] * 3,
+        out_specs=[VMEM] * 2,
+        scratch_shapes=[
+            pltpu.VMEM((2,) + block, BF),
+            pltpu.VMEM((2,) + block2, F32),
+            pltpu.VMEM(block, BF),
+            pltpu.VMEM((2,) + block, BF),
+            pltpu.VMEM(block2, F32),
+            pltpu.VMEM((2,) + block2, F32),
+            DMA((4,)),
+            DMA((4,)),
+        ],
         compiler_params=call_params(collective_id),
         name="reduce_chip",
         cost_estimate=cost(17),
-    )(*operands)
-
-
-def reduce_keys(parts, owned, collective_id):
+    )(pick, back, of_expert)
+
+
+def reduce_keys(parts, owned, swapped, collective_id):
     _, groups, _, rows, width = parts.shape
 
-    def body(src, src4, out, out4, arrived, mid, beside, summed, landed, send, recv, *scratch4):
+    def body(src, src4, src5, out, out4, out5, arrived, mid, beside, summed, landed, send, recv, pair, *scratch4):
         block4 = Owned(src4, out4, scratch4)
         me, wsh = lax.axis_index("ctx"), lax.axis_index("wsh")
         core = lax.rem(me, 2)
@@ -709,7 +761,7 @@
         steps = COLUMN_STEPS + ((0, 0),)
         peers = [shifted(me, dz, dy, 0, 0) for dz, dy in steps]
         row_peers = [shifted(me, 0, 0, dx, dk) for dx, dk in ROW_STEPS]
-        barrier, amount = greet([(peer, wsh) for peer in peers[:-1] + row_peers])
+        barrier, amount = greet([(peer, wsh) for peer in peers[:-1] + row_peers] + [(me, 1 - wsh)])
         pl.semaphore_wait(barrier, amount)
         first = []
         for at, peer in enumerate(peers):
@@ -726,6 +778,8 @@
                 copy.start()
                 first.append(copy)
         block4.along_z(me, wsh)
+        cross = remote(src5, out5, pair.at[0], pair.at[1], me, 1 - wsh)
+        cross.start()
         across = []
         for at, peer in enumerate(peers):
             group = lax.div(peer, 8)
@@ -751,7 +805,8 @@
                 copy = remote(summed.at[at], landed.at[at], send.at[3, at], recv.at[3, at], peer, wsh)
                 copy.start()
                 last.append(copy)
-        block4.along_y(me, wsh)
+            if at == 5:
+                block4.along_y(me, wsh)
         block4.along_row(me, wsh)
         for at, copy in enumerate(last):
             copy.wait_recv()
@@ -759,6 +814,7 @@
         for copy in first + across + last:
             copy.wait_send()
         block4.finish()
+        cross.wait()
 
     block = (rows, width)
     return pl.pallas_call(
@@ -766,9 +822,10 @@
         out_shape=(
             jax.ShapeDtypeStruct(block, F32),
             jax.ShapeDtypeStruct((8,) + owned.shape[1:], BF),
+            jax.ShapeDtypeStruct(swapped.shape, swapped.dtype),
         ),
-        in_specs=[VMEM, VMEM],
-        out_specs=[VMEM, VMEM],
+        in_specs=[VMEM, VMEM, ANY],
+        out_specs=[VMEM, VMEM, ANY],
         scratch_shapes=[
             pltpu.VMEM((2, groups) + block, BF),
             pltpu.VMEM((groups,) + block, BF),
@@ -777,12 +834,13 @@
             pltpu.VMEM((groups,) + block, BF),
             DMA((4, groups)),
             DMA((4, groups)),
+            DMA((2,)),
         ]
         + Owned.scratch(owned),
         compiler_params=call_params(collective_id),
         name="reduce_keys",
         cost_estimate=cost(40),
-    )(parts, owned)
+    )(parts, owned, swapped)
 
 
 def exchange(arrays, collective_id):
@@ -1007,7 +1065,7 @@
     )(block_order, lengths, group, queries, kv)
 
 
-def backward_kernel(plan, lengths, q_ref, heads_ref, da_ref, wo_ref, kv_ref, lse_ref, dq_ref, dkv_ref, keys, values, keys_t, d_keys, d_values, acc):
+def backward_kernel(plan, lengths, q_ref, heads_ref, da_ref, wo_ref, kv_ref, lse_ref, part_ref, dq_ref, dkv_ref, early_ref, keys, values, keys_t, d_keys, d_values, acc):
     step = pl.program_id(0)
 
     @pl.when(step == 0)
@@ -1070,19 +1128,34 @@
             return carried
 
         lax.fori_loop(0, kv_ref.shape[0] // BLK, one, 0, unroll=4)
-
-
-def attend_back(plan, lengths, queries, heads, d_attn, wo_t, kv, lse):
+        owners = early_ref.shape[0]
+        depth = da_ref.shape[1] // owners
+        span = 256
+        for at in range(da_ref.shape[1] // span):
+            value = transposed_times(da_ref[:, at * span : (at + 1) * span], heads_ref[...])
+            some = slice(at * span // depth, (at + 1) * span // depth)
+            for head in range(2):
+                early_ref[some, head * depth : (head + 1) * depth, :] = (
+                    value[:, head * HEAD_WIDTH : (head + 1) * HEAD_WIDTH]
+                    .astype(BF)
+                    .reshape(span // depth, depth, HEAD_WIDTH)
+                )
+        early_ref[:, 2 * depth :, :] = part_ref[...]
+
+
+def attend_back(plan, lengths, queries, heads, d_attn, wo_t, kv, lse, part):
     rows = queries.shape[0]
     total = kv.shape[0]
     steps = rows // (2 * BLK)
     everything = pl.BlockSpec(queries.shape, lambda i, *_: (0, 0))
     strip = pl.BlockSpec((1, 1, 4 * BLK), lambda i, *_: (i, 0, 0))
     sds = jax.ShapeDtypeStruct
+    owners = part.shape[0]
+    early_shape = (owners, part.shape[1] + 2 * d_attn.shape[1] // owners, HEAD_WIDTH)
     dkv_shape = (2, total // rows, 2, rows // 2, HEAD_WIDTH)
     return pl.pallas_call(
         backward_kernel,
-        out_shape=(sds(queries.shape, F32), sds(dkv_shape, BF)),
+        out_shape=(sds(queries.shape, F32), sds(dkv_shape, BF), sds(early_shape, BF)),
         grid_spec=pltpu.PrefetchScalarGridSpec(
             num_scalar_prefetch=2,
             grid=(steps,),
@@ -1093,8 +1166,13 @@
                 pl.BlockSpec((wo_t.shape[0], queries.shape[1]), lambda i, *_: (0, 0)),
                 pl.BlockSpec(kv.shape, lambda i, *_: (0, 0)),
                 strip,
+                pl.BlockSpec(part.shape, lambda i, *_: (0, 0, 0)),
             ],
-            out_specs=[everything, pl.BlockSpec(dkv_shape, lambda i, *_: (0, 0, 0, 0, 0))],
+            out_specs=[
+                everything,
+                pl.BlockSpec(dkv_shape, lambda i, *_: (0, 0, 0, 0, 0)),
+                pl.BlockSpec(early_shape, lambda i, *_: (0, 0, 0)),
+            ],
             scratch_shapes=[
                 pltpu.VMEM((total, HEAD_WIDTH), BF),
                 pltpu.VMEM((total, HEAD_WIDTH), BF),
@@ -1107,31 +1185,29 @@
         compiler_params=pltpu.CompilerParams(vmem_limit_bytes=ROOM),
         name="attend_back",
         cost_estimate=cost(24),
-    )(plan, lengths, queries, heads, d_attn, wo_t, kv, lse)
+    )(plan, lengths, queries, heads, d_attn, wo_t, kv, lse, part)
 
 
 def expert_kernel(side, x_ref, cot_ref, gate_ref, g_own, u_own, d_own, g_other, u_other, u_rest, d_other, y_ref, dx_ref, a_ref, dg_ref, du_ref, dy_ref, gate_w, up_w, down_w, gate_f, up_f, down_f, sems):
-    half = g_other.shape[1]
+    half = gate_f.shape[1]
     own_copies, other_copies = [], []
-    for at, (own, other, whole, stage, columns) in enumerate(
+    for at, (own, others, whole, stage) in enumerate(
         (
-            (g_own, g_other, gate_w, gate_f, True),
-            (u_own, u_other, up_w, up_f, True),
-            (d_own, d_other, down_w, down_f, False),
+            (g_own, (g_other,), gate_w, gate_f),
+            (u_own, (u_other, u_rest), up_w, up_f),
+            (d_own, (d_other,), down_w, down_f),
         )
     ):
-        span = pl.ds(half, half)
-        target = whole.at[pl.ds(0, whole.shape[0]), span] if columns else whole.at[span]
         own_copies.append(pltpu.make_async_copy(own.at[side[0]], stage, sems.at[at, 0]))
-        if at == 1:
-            cut = u_other.shape[0]
-            parts = ((u_other, pl.ds(0, cut)), (u_rest, pl.ds(cut, u_rest.shape[0])))
-            for side_at, (part, place) in enumerate(parts):
-                other_copies.append(
-                    pltpu.make_async_copy(part, whole.at[place, span], sems.at[at, 1 + side_at])
-                )
-        else:
-            other_copies.append(pltpu.make_async_copy(other, target, sems.at[at, 1]))
+        begin = 0
+        for which, part in enumerate(others):
+            count = part.shape[0]
+            if at < 2:
+                target = whole.at[pl.ds(begin, count), pl.ds(half, half)]
+            else:
+                target = whole.at[pl.ds(half, half)]
+            other_copies.append(pltpu.make_async_copy(part, target, sems.at[at, 1 + which]))
+            begin += count
 
     @pl.when(pl.program_id(0) == 0)
     def _():
@@ -1173,7 +1249,7 @@
 
 def run_expert(side, rows_in, cot, gates, own, other):
     count, width = rows_in.shape
-    half = other[0].shape[1]
+    half = own[0].shape[2]
     tile = 256
     sds = jax.ShapeDtypeStruct
 
@@ -1218,21 +1294,36 @@
     )(side, rows_in, cot, gates, *own, *other)
 
 
-def expert_grads_kernel(side, x_ref, dy_ref, a_ref, dg_ref, du_ref, gate_ref, up_ref, down_ref, gate_out, up_out, down_out, a_t):
+def expert_grads_kernel(side, x_ref, dy_ref, a_ref, dg_ref, du_ref, gate_ref, up_ref, down_ref, gate_out, up_out, up_rest, down_out, down_rest, a_t):
     half = gate_ref.shape[-1]
-
-    @pl.when(pl.program_id(0) == 0)
+    step = pl.program_id(0)
+    turn_at = up_out.shape[0]
+
+    @pl.when(step == 0)
     def _():
         a_t[...] = a_ref[...].T
 
     x_t = x_ref[...].T
-    for grad_ref, own, other in ((dg_ref, gate_ref, gate_out), (du_ref, up_ref, up_out)):
-        value = matmul(x_t, grad_ref[...])
-        own[0] = value[:, :half]
-        other[...] = value[:, half:].astype(BF)
+    value = matmul(x_t, dg_ref[...])
+    gate_ref[0] = value[:, :half]
+    gate_out[...] = value[:, half:].astype(BF)
+    value = matmul(x_t, du_ref[...])
+    up_ref[0] = value[:, :half]
+    low = value[:, half:].astype(BF)
+
+    @pl.when(step < UP_CUT[0] // turn_at)
+    def _():
+        up_out[...] = low
+
+    @pl.when(step >= UP_CUT[0] // turn_at)
+    def _():
+        up_rest[...] = low
+
     value = matmul(a_t[...], dy_ref[...])
     down_ref[0] = value[:half]
-    down_out[...] = value[half:].astype(BF)
+    cut = half + down_out.shape[0]
+    down_out[...] = value[half:cut].astype(BF)
+    down_rest[...] = value[cut:].astype(BF)
 
 
 def expert_grads(side, rows_in, d_pairs, activated, d_gate, d_up):
@@ -1240,11 +1331,11 @@
     whole = activated.shape[1]
     half = whole // 2
     tile = 256
+    first = UP_CUT[0] // tile
     sds = jax.ShapeDtypeStruct
     columns = pl.BlockSpec((count, tile), lambda i, side: (0, i))
     full = pl.BlockSpec((count, whole), lambda i, side: (0, 0))
     own_rows = pl.BlockSpec((1, tile, half), lambda i, side: (side[0], i, 0))
-    other_rows = pl.BlockSpec((tile, half), lambda i, side: (i, 0))
     return pl.pallas_call(
         expert_grads_kernel,
         out_shape=(
@@ -1252,8 +1343,10 @@
             sds((2, width, half), F32),
             sds((2, half, width), F32),
             sds((width, half), BF),
-            sds((width, half), BF),
-            sds((half, width), BF),
+            sds((UP_CUT[0], half), BF),
+            sds((UP_CUT[1], half), BF),
+            sds((DOWN_GRAD_CUT[0], width), BF),
+            sds((DOWN_GRAD_CUT[1], width), BF),
         ),
         grid_spec=pltpu.PrefetchScalarGridSpec(
             num_scalar_prefetch=1,
@@ -1263,9 +1356,11 @@
                 own_rows,
                 own_rows,
                 pl.BlockSpec((1, half, tile), lambda i, side: (side[0], 0, i)),
-                other_rows,
-                other_rows,
-                pl.BlockSpec((half, tile), lambda i, side: (0, i)),
+                pl.BlockSpec((tile, half), lambda i, side: (i, 0)),
+                pl.BlockSpec((tile, half), lambda i, side: (jnp.minimum(i, first - 1), 0)),
+                pl.BlockSpec((tile, half), lambda i, side: (jnp.maximum(i - first, 0), 0)),
+                pl.BlockSpec((DOWN_GRAD_CUT[0], tile), lambda i, side: (0, i)),
+                pl.BlockSpec((DOWN_GRAD_CUT[1], tile), lambda i, side: (0, i)),
             ],
             scratch_shapes=[pltpu.VMEM((whole, count), BF)],
         ),
@@ -1275,34 +1370,325 @@
     )(side, rows_in, d_pairs, activated, d_gate, d_up)
 
 
-def place_kernel(side, *refs):
-    for at in range(3):
-        refs[6 + at][0] = refs[at][...].astype(F32)
-
-
-def place_other(side, arrived, placed):
-    tile = 256
-    width, half = arrived[0].shape
-    rows_in = pl.BlockSpec((tile, half), lambda i, side: (i, 0))
-    rows_out = pl.BlockSpec((1, tile, half), lambda i, side: (1 - side[0], i, 0))
+def route_kernel(where, routes_ref, cot_ref, pick_ref, turned_ref, of_ref, hits_ref, rows_ref):
+    slots, rows = pick_ref.shape[0], routes_ref.shape[2]
+    experts = of_ref.shape[1]
+    slot = lax.broadcasted_iota(jnp.int32, (slots, experts), 0)
+    lane = lax.broadcasted_iota(jnp.int32, (slots, experts), 1)
+    chip = lax.div(slot, 2 * CAP)
+    side = lax.rem(where[1] + lax.div(chip, 4) + where[2], 2)
+    of_expert = (lane == 4 * chip + 2 * where[0] + side).astype(F32).astype(BF)
+    of_ref[...] = of_expert
+    expert = lax.broadcasted_iota(jnp.int32, (experts, rows), 0)
+    before = (
+        lax.broadcasted_iota(jnp.int32, (rows, rows), 0) < lax.broadcasted_iota(jnp.int32, (rows, rows), 1)
+    ).astype(F32).astype(BF)
+    hits, ranks = [], []
+    for half in range(2):
+        hit = jnp.zeros((experts, rows), F32)
+        for choice in range(TOPK):
+            hit = hit + (routes_ref[half, choice : choice + 1, :] == expert).astype(F32)
+        rank = matmul(hit.astype(BF), before) + half * CAP
+        hits.append(hit)
+        ranks.append(jnp.where(hit > 0.5, rank, -1.0))
+    hits_ref[...] = jnp.concatenate(hits, axis=1).T
+    mine = matmul(of_expert, jnp.concatenate(ranks, axis=1).astype(BF))
+    wanted = lax.rem(lax.broadcasted_iota(jnp.int32, mine.shape, 0), 2 * CAP).astype(F32)
+    pick = (mine == wanted).astype(F32)
+    pick_low = pick.astype(BF)
+    pick_ref[...] = pick_low
+    turned_ref[...] = pick.T.astype(BF)
+    rows_ref[...] = matmul(pick_low, cot_ref[...]).astype(BF)
+
+
+def route(where, routes, cotangent, experts):
+    rows, width = cotangent.shape
+    slots = experts // 4 * 2 * CAP
+    sds = jax.ShapeDtypeStruct
     return pl.pallas_call(
-        place_kernel,
-        out_shape=[jax.ShapeDtypeStruct(value.shape, F32) for value in placed],
+        route_kernel,
+        out_shape=(
+            sds((slots, rows), BF),
+            sds((rows, slots), BF),
+            sds((slots, experts), BF),
+            sds((rows, experts), F32),
+            sds((slots, width), BF),
+        ),
+        in_specs=[pl.BlockSpec(memory_space=pltpu.SMEM), VMEM, VMEM],
+        out_specs=[VMEM] * 5,
+        compiler_params=pltpu.CompilerParams(vmem_limit_bytes=ROOM),
+        name="route",
+        cost_estimate=cost(5),
+    )(where, routes, cotangent)
+
+
+def middle_kernel(chip, t_ref, attn_ref, gain_ref, wr_ref, hits_ref, pick_ref, of_ref, res_ref, h_ref, inv_ref, gates_ref, rows_ref, tile_ref):
+    residual = t_ref[...].astype(F32) + attn_ref[...]
+    res_ref[...] = residual
+    inverse = lax.rsqrt(jnp.mean(residual * residual, axis=1, keepdims=True) + EPSILON)
+    inv_ref[...] = jnp.broadcast_to(inverse, inv_ref.shape)
+    hidden = (residual * inverse * gain_ref[...]).astype(BF)
+    h_ref[...] = hidden
+    pick = pick_ref[...]
+    rows_ref[...] = matmul(pick, hidden).astype(BF)
+    hit = hits_ref[...] > 0.5
+    logits = jnp.where(hit, matmul(hidden, wr_ref[...]), MASKED)
+    exps = jnp.where(hit, jnp.exp(logits - jnp.max(logits, axis=1, keepdims=True)), 0.0)
+    gates = exps / jnp.sum(exps, axis=1, keepdims=True)
+    gates_ref[...] = gates
+    high = gates.astype(BF)
+    chosen = [
+        jnp.sum(matmul(pick, part) * of_ref[...].astype(F32), axis=1, keepdims=True)
+        for part in (high, (gates - high.astype(F32)).astype(BF))
+    ]
+    lane = lax.broadcasted_iota(jnp.int32, tile_ref.shape, 1)
+    tile_ref[...] = jnp.where(lane < 64, chosen[0], chosen[1]).astype(BF)
+
+
+def middle(chip, row_rows, attn_total, gain, late_all, hits, pick, of_expert):
+    rows, width = attn_total.shape
+    slots, experts = of_expert.shape
+    sds = jax.ShapeDtypeStruct
+
+    def whole(value):
+        return pl.BlockSpec(value.shape, lambda i, chip: (0, 0))
+
+    def out(*shape):
+        return pl.BlockSpec(shape, lambda i, chip: (0, 0))
+
+    shapes = (
+        sds((rows, width), F32),
+        sds((rows, width), BF),
+        sds((rows, 128), F32),
+        sds((rows, experts), F32),
+        sds((slots, width), BF),
+        sds((slots, 128), BF),
+    )
+    return pl.pallas_call(
+        middle_kernel,
+        out_shape=shapes,
         grid_spec=pltpu.PrefetchScalarGridSpec(
             num_scalar_prefetch=1,
-            grid=(width // tile,),
-            in_specs=[rows_in, rows_in, pl.BlockSpec((half, tile), lambda i, side: (0, i))] + [ANY] * 3,
+            grid=(1,),
+            in_specs=[
+                pl.BlockSpec((rows, width), lambda i, chip: (chip[0], 0)),
+                whole(attn_total),
+                whole(gain),
+                pl.BlockSpec((width, experts), lambda i, chip: (0, 2)),
+                whole(hits),
+                whole(pick),
+                whole(of_expert),
+            ],
+            out_specs=[out(*value.shape) for value in shapes],
+        ),
+        compiler_params=pltpu.CompilerParams(vmem_limit_bytes=ROOM),
+        name="middle",
+        cost_estimate=cost(1),
+    )(chip, row_rows, attn_total, gain, late_all, hits, pick, of_expert)
+
+
+def turn_kernel(core, moe_ref, dg_ref, gates_ref, h_ref, res_ref, inv_ref, wr_ref, gain_ref, cot_ref, d_ref, low_ref, part_ref):
+    gates = gates_ref[...]
+    d_gates = dg_ref[...]
+    d_logits = (gates * (d_gates - jnp.sum(gates * d_gates, axis=1, keepdims=True))).astype(BF)
+    hidden = h_ref[...]
+    gradient = moe_ref[...] + times_transposed(d_logits, wr_ref[...])
+    residual, inverse = res_ref[...], inv_ref[:, 0:1]
+    weighted = gradient * gain_ref[...]
+    mean_term = jnp.mean(weighted * residual, axis=1, keepdims=True)
+    back = inverse * weighted - residual * (inverse * inverse * inverse) * mean_term
+    value = cot_ref[...].astype(F32) + back
+    d_ref[...] = value
+    low_ref[...] = value.astype(BF)
+    owners, rows, _ = part_ref.shape
+    depth = hidden.shape[1] // owners
+    grad_router = transposed_times(hidden, d_logits).astype(BF)
+    part_ref[:, :depth, :] = grad_router.reshape(owners, depth, grad_router.shape[1])
+    terms = jnp.sum(gradient * residual * inverse, axis=0, keepdims=True)
+    wide = jnp.broadcast_to(terms, (8, terms.shape[1]))
+    by_owner = jnp.concatenate(
+        [wide[:1, owner * depth : (owner + 1) * depth] for owner in range(owners)], axis=0
+    )
+    by_owner = jnp.concatenate([by_owner, jnp.zeros((owners, 128 - depth), F32)], axis=1)
+    part_ref[:, depth:, :] = jnp.broadcast_to(
+        by_owner[:, None, :], (owners, rows - depth, 128)
+    ).astype(BF)
+
+
+def turn(core, d_moe, d_gates, gates, hidden, residual, inverse, late_all, gain, cotangent):
+    rows, width = d_moe.shape
+    experts = gates.shape[1]
+    owners = 64
+    sds = jax.ShapeDtypeStruct
+
+    def mine(columns):
+        return pl.BlockSpec((rows, columns), lambda i, core: (core[0], 0))
+
+    def whole(*shape):
+        return pl.BlockSpec(shape, lambda i, core: (0,) * len(shape))
+
+    parts = (owners, width // owners + 16, 128)
+    return pl.pallas_call(
+        turn_kernel,
+        out_shape=(sds((rows, width), F32), sds((rows, width), BF), sds(parts, BF)),
+        grid_spec=pltpu.PrefetchScalarGridSpec(
+            num_scalar_prefetch=1,
+            grid=(1,),
+            in_specs=[
+                whole(rows, width),
+                whole(rows, experts),
+                mine(experts),
+                mine(width),
+                mine(width),
+                mine(128),
+                pl.BlockSpec((width, experts), lambda i, core: (0, 2)),
+                whole(1, width),
+                whole(rows, width),
+            ],
+            out_specs=[whole(rows, width), whole(rows, width), whole(*parts)],
+        ),
+        compiler_params=pltpu.CompilerParams(vmem_limit_bytes=ROOM),
+        name="turn",
+        cost_estimate=cost(6),
+    )(core, d_moe, d_gates, gates, hidden, residual, inverse, late_all, gain, cotangent)
+
+
+def last_kernel(side, g_in, u_in, u_rest, d_in, d_rest, *refs):
+    (t_ref, dh_ref, dr_ref, moe_ref, res_ref, ga_ref, late_ref, early_ref, wq_ref, wk_ref, wv_ref), refs = refs[3:14], refs[14:]
+    g_out, u_out, d_out, out_ref, gt_ref, gq_ref, gk_ref, gv_ref, go_ref, gr_ref, gains_ref, ffn_ref = refs[:12]
+    keys, router, gains, ffn, dots = refs[12:]
+    step = pl.program_id(0)
+    g_out[0] = g_in[...].astype(F32)
+    u_out[0] = jnp.where(step < UP_CUT[0] // u_in.shape[0], u_in[...], u_rest[...]).astype(F32)
+    d_out[0, : d_in.shape[0]] = d_in[...].astype(F32)
+    d_out[0, d_in.shape[0] :] = d_rest[...].astype(F32)
+    rows = t_ref[...].astype(F32)
+    out_ref[...] = res_ref[...] + moe_ref[...]
+    inverse = lax.rsqrt(jnp.mean(rows * rows, axis=1, keepdims=True) + EPSILON)
+    weighted = dh_ref[...] * ga_ref[...]
+    mean_term = jnp.mean(weighted * rows, axis=1, keepdims=True)
+    gt_ref[...] = dr_ref[...] + (
+        inverse * weighted - rows * (inverse * inverse * inverse) * mean_term
+    )
+
+    @pl.when(step == 0)
+    def _():
+        for ref in (keys, router, gains, ffn, dots):
+            ref[...] = jnp.zeros_like(ref)
+
+    depth = gq_ref.shape[0]
+    late, early = late_ref[0].astype(F32), early_ref[0].astype(F32)
+    query = jnp.concatenate([late[:depth], late[depth : 2 * depth]], axis=1)
+    gq_ref[...] = query
+    low_q = wq_ref[...].astype(BF).astype(F32)
+    dots[...] += jnp.sum(low_q * query, axis=1, keepdims=True)
+    keys[lax.div(step, 2)] += late[2 * depth : 3 * depth]
+    gains[...] += late[3 * depth :]
+    router[...] += early[2 * depth : 3 * depth]
+    ffn[...] += early[3 * depth : 3 * depth + 8]
+    go_ref[...] = jnp.concatenate([early[:depth], early[depth : 2 * depth]], axis=1)
+
+    @pl.when(step == pl.num_programs(0) - 1)
+    def _():
+        gk_ref[...] = jnp.concatenate([keys[0], keys[2]], axis=1)
+        gv_ref[...] = jnp.concatenate([keys[1], keys[3]], axis=1)
+        gr_ref[...] = router[...]
+        ffn_ref[...] = ffn[...]
+        total = (
+            dots[:, 0:1]
+            + jnp.sum(wk_ref[...].astype(BF).astype(F32) * gk_ref[...], axis=1, keepdims=True)
+            + jnp.sum(wv_ref[...].astype(BF).astype(F32) * gv_ref[...], axis=1, keepdims=True)
+        )
+        blank = jnp.zeros((128 - depth, 128), F32)
+        square = jnp.concatenate([jnp.broadcast_to(total, (depth, 128)), blank], axis=0).T
+        row = lax.broadcasted_iota(jnp.int32, gains_ref.shape, 0)
+        gains_ref[...] = jnp.where(row < 2, gains[:8], square[:8])
+
+
+def last(side, arrived, placed, tokens, d_hidden, d_residual, moe, residual, gain, late, early, weights):
+    width, half = arrived[0].shape
+    rows = tokens.shape[0]
+    steps = 8
+    tile, strip = width // steps, rows // steps
+    depth = weights[0].shape[0]
+    sds = jax.ShapeDtypeStruct
+
+    def whole(*shape):
+        return pl.BlockSpec(shape, lambda i, side: (0,) * len(shape))
+
+    first = UP_CUT[0] // tile
+    rows_out = pl.BlockSpec((1, tile, half), lambda i, side: (1 - side[0], i, 0))
+    columns_out = pl.BlockSpec((1, half, tile), lambda i, side: (1 - side[0], 0, i))
+    strips = pl.BlockSpec((strip, width), lambda i, side: (i, 0))
+    mine = pl.BlockSpec((strip, width), lambda i, side: (side[1] * steps + i, 0))
+    place = pl.BlockSpec((1,) + late.shape[1:], lambda i, side: (i, 0, 0))
+    query = pl.BlockSpec((depth, weights[0].shape[1] // steps), lambda i, side: (0, i))
+    narrow = (depth, weights[1].shape[1])
+    return pl.pallas_call(
+        last_kernel,
+        out_shape=[sds(value.shape, F32) for value in placed]
+        + [
+            sds((rows, width), F32),
+            sds((rows, width), F32),
+            sds(weights[0].shape, F32),
+            sds(narrow, F32),
+            sds(narrow, F32),
+            sds(weights[0].shape, F32),
+            sds((depth, 128), F32),
+            sds((8, 128), F32),
+            sds((8, 128), F32),
+        ],
+        grid_spec=pltpu.PrefetchScalarGridSpec(
+            num_scalar_prefetch=1,
+            grid=(steps,),
+            in_specs=[
+                pl.BlockSpec((tile, half), lambda i, side: (i, 0)),
+                pl.BlockSpec((tile, half), lambda i, side: (jnp.minimum(i, first - 1), 0)),
+                pl.BlockSpec((tile, half), lambda i, side: (jnp.maximum(i - first, 0), 0)),
+                pl.BlockSpec((DOWN_GRAD_CUT[0], tile), lambda i, side: (0, i)),
+                pl.BlockSpec((DOWN_GRAD_CUT[1], tile), lambda i, side: (0, i)),
+            ]
+            + [ANY] * 3
+            + [
+                strips,
+                strips,
+                strips,
+                strips,
+                mine,
+                whole(1, width),
+                place,
+                place,
+                query,
+                whole(*narrow),
+                whole(*narrow),
+            ],
             out_specs=[
                 rows_out,
                 rows_out,
-                pl.BlockSpec((1, half, tile), lambda i, side: (1 - side[0], 0, i)),
+                columns_out,
+                strips,
+                strips,
+                query,
+                whole(*narrow),
+                whole(*narrow),
+                query,
+                whole(depth, 128),
+                whole(8, 128),
+                whole(8, 128),
+            ],
+            scratch_shapes=[
+                pltpu.VMEM((4, depth, 128), F32),
+                pltpu.VMEM((depth, 128), F32),
+                pltpu.VMEM((16, 128), F32),
+                pltpu.VMEM((8, 128), F32),
+                pltpu.VMEM((depth, 128), F32),
             ],
         ),
-        input_output_aliases={4: 0, 5: 1, 6: 2},
+        input_output_aliases={6: 0, 7: 1, 8: 2},
         compiler_params=pltpu.CompilerParams(vmem_limit_bytes=ROOM),
-        name="place_other",
-        cost_estimate=cost(5),
-    )(side, *arrived, *placed)
+        name="last",
+        cost_estimate=cost(9),
+    )(side, *arrived, *placed, tokens, d_hidden, d_residual, moe, residual, gain, late, early, *weights)
 
 
 def project_kernel(block_order, lengths, group, t_ref, w_ref, side_ref, flag_ref, freq_ref, ga_ref, gq_ref, gk_ref, h_ref, q_ref, kv_ref, qp_ref, kp_ref, cos_ref, sin_ref):
@@ -1535,18 +1921,24 @@
         return lax.ppermute(value, "wsh", [(0, 1), (1, 0)])
 
     depth = w_query.shape[0]
-    q_part = to_low(w_query).reshape(depth, 8, 256).transpose(1, 0, 2)
-    sides = [
-        to_low(value[:, head * 128 : head * 128 + 128])
-        for head in (0, 0, 1, 1)
-        for value in (key_weight, value_weight)
-    ]
-    w_pack = jnp.concatenate([q_part, jnp.stack(sides)], axis=2)
-    small = jnp.concatenate(
-        [lanes_to(gain_attn[None, :]), lanes_to(gain_ffn[None, :]), jnp.zeros((6, 128), F32)], axis=0
-    )
-    w_all, row_rows, small_all, chip_routes, chip_cot, other_gate, other_up, other_down, w_side = gather_first(
-        w_pack, tokens, small, routes.T, cotangent, (w_gate, w_up, w_down)
+    (
+        w_all,
+        row_rows,
+        small_all,
+        chip_routes,
+        chip_cot,
+        other_gate,
+        up_first,
+        other_up,
+        other_down,
+        w_side,
+    ) = gather_first(
+        (w_query, key_weight, value_weight),
+        (gain_attn[None, :], gain_ffn[None, :]),
+        tokens,
+        routes.T,
+        cotangent,
+        (w_gate, w_up, w_down),
     )
     w_main = w_all.reshape(width, 384)
     w_side = w_side.reshape(width, 128)
@@ -1566,28 +1958,13 @@
     late_pack, small_all = after(late_pack, small_all)
     late_all = lax.all_to_all(late_pack, "ctx", split_axis=0, concat_axis=0, tiled=True).reshape(width, 384)
 
-    route_rows = chip_routes.transpose(0, 2, 1)
-    hits = jnp.any(
-        route_rows[:, :, :, None] == jnp.arange(experts, dtype=jnp.int32)[None, None, None, :], axis=2
-    )
-    before = jnp.tril(jnp.ones((rows, rows), BF), -1)
-    ranks = jnp.einsum("ts,hse->hte", before, hits.astype(BF), preferred_element_type=F32).astype(jnp.int32)
-    ranks = jnp.where(hits, ranks + jnp.array([0, CAP], jnp.int32)[:, None, None], -1)
-    hits = hits.reshape(2 * rows, experts)
     chips = experts // 4
-    chip_ids = jnp.arange(chips, dtype=jnp.int32)
-    quarter = core * 2 + (wsh + chip_ids // 4 + lax.div(me, 8)) % 2
-
-    def my_quarter(value):
-        by_chip = value.reshape(2 * rows, experts).T.reshape(chips, 4, 2 * rows)
-        two = lax.dynamic_slice_in_dim(by_chip, core * 2, 2, 1)
-        return jnp.where((quarter % 2 == 0)[:, None], two[:, 0], two[:, 1])
-
-    my_ranks = my_quarter(ranks)
     slots = 2 * CAP
-    pick = my_ranks[:, None, :] == jnp.arange(slots, dtype=jnp.int32)[None, :, None]
-    pick_low = pick.astype(BF).reshape(chips * slots, 2 * rows)
-    cot_rows = matmul(pick_low, chip_cot.reshape(2 * rows, width)).astype(BF)
+    y_half = lax.rem(lax.div(me, 8), 2)
+    pick_low, pick_turned, of_expert, hits, cot_rows = route(
+        jnp.stack([core, wsh, y_half]), chip_routes, chip_cot.reshape(2 * rows, width), experts
+    )
+
     half_dim = HEAD_WIDTH // 2
     frequency = jnp.power(ROPE_BASE, -2.0 * jnp.arange(half_dim, dtype=jnp.float32) / HEAD_WIDTH)
     frequency = jnp.concatenate([frequency, frequency])[None, :]
@@ -1607,52 +1984,31 @@
     )
     kv_all = gather_keys(kv, 1).reshape(block_count * BLK, 256)
     late_all, kv_all = after(late_all, kv_all)
-    wo_t = late_all[:, :256]
-    wr = late_all[:, 256:]
     (cot_rows, other_gate), kv_all = after((cot_rows, other_gate), kv_all)
     gate_back = swap(other_gate)
     cot_there = exchange_behind(cot_rows.reshape(chips, slots, width)).reshape(chips * slots, width)
     heads, lse, plan = attend(block_order, seq_lengths, group.reshape(1), queries, kv_all)
 
-    attn_parts = to_low(times_transposed(heads, wo_t)).reshape(8, rows, width)
-    (gate_back, cot_there, other_up, other_down), attn_parts = after(
-        (gate_back, cot_there, other_up, other_down), attn_parts
-    )
-    up_cut = width * 5 // 8
-    attn_total, up_first = reduce_row(attn_parts, 2, True, swapped_whole=other_up[:up_cut])
-    attn_total = attn_total.reshape(2 * rows, width)
-    chip_stream = lax.dynamic_slice_in_dim(row_rows, (place - core) * rows, 2 * rows, 0).astype(F32)
-    chip_residual = chip_stream + attn_total
-    chip_inverse_two = inverse_root(chip_residual)
-    chip_hidden = to_low(chip_residual * chip_inverse_two * g_ffn)
-    logits = matmul(chip_hidden, wr)
-    masked_logits = jnp.where(hits, logits, MASKED)
-    gate_exps = jnp.where(
-        hits, jnp.exp(masked_logits - jnp.max(masked_logits, axis=-1, keepdims=True)), 0.0
-    )
-    gates = gate_exps / jnp.sum(gate_exps, axis=-1, keepdims=True)
-
-    def my_rows(value):
-        return lax.dynamic_slice_in_dim(value, core * rows, rows, 0)
-
-    out_rows = matmul(pick_low, chip_hidden).astype(BF).reshape(chips, slots, width)
-    expert_of = jnp.repeat(4 * chip_ids + quarter, slots)
-    of_expert = expert_of[:, None] == jnp.arange(experts, dtype=jnp.int32)[None, :]
-
-    def parted(value):
-        high = to_low(value)
-        return high, to_low(value - high.astype(F32))
-
-    slot_gates = [
-        jnp.sum(jnp.where(of_expert, matmul(pick_low, part), 0.0), axis=1, keepdims=True)
-        for part in parted(gates)
-    ]
-    gate_tile = to_low(
-        jnp.where(jnp.arange(128)[None, :] < 64, slot_gates[0], slot_gates[1])
-    ).reshape(chips, slots, 128)
-    (other_down, other_up), gate_tile = after((other_down, other_up), gate_tile)
+    (other_up, other_down), heads = after((other_up, other_down), heads)
+    attn_total, up_first = reduce_row((heads, late_all), 2, True, swapped_whole=up_first)
+    residual, hidden_two, inverse_two, gates, out_rows, gate_tile = middle(
+        lax.div(place, 2).reshape(1),
+        row_rows,
+        attn_total.reshape(2 * rows, width),
+        g_ffn[None, :],
+        late_all,
+        hits,
+        pick_low,
+        of_expert,
+    )
+
+    out_rows = out_rows.reshape(chips, slots, width)
+    gate_tile = gate_tile.reshape(chips, slots, 128)
+    (gate_back, cot_there, other_down, other_up), gate_tile = after(
+        (gate_back, cot_there, other_down, other_up), gate_tile
+    )
     down_back = swap(other_down)
-    up_back = (up_first, swap(other_up[up_cut:]))
+    up_back = (up_first, swap(other_up))
     arrived, gate_there = exchange([out_rows, gate_tile], 3)
     arrived = arrived.reshape(chips * slots, width)
     side = wsh.reshape(1)
@@ -1660,64 +2016,41 @@
     y_rows, d_rows, activated, d_gate_pre, d_up_pre, d_pairs = run_expert(
         side, arrived, cot_there, gate_there, (w_gate, w_up, w_down), (gate_back, *up_back, down_back)
     )
-    *own_grads, other_gate, other_up, other_down = expert_grads(
+    *own_grads, other_gate, up_first, other_up, other_down, down_rest = expert_grads(
         side, arrived, d_pairs, activated, d_gate_pre, d_up_pre
     )
     gate_grad_back = swap(other_gate)
     d_back = exchange_behind(d_rows.reshape(chips, slots, width + 128))
-    y_rows, d_back = after(y_rows, d_back)
+    y_rows, _ = after(y_rows, (d_back, gate_grad_back))
     y_back = exchange_behind(y_rows.reshape(chips, slots, width))
 
-    def collect(back):
-        return to_low(transposed_times(pick_low, back.reshape(chips * slots, -1)))
-
     d_back = d_back.reshape(chips * slots, width + 128)
-    d_gates_part = sum(
-        transposed_times(
-            pick_low, jnp.where(of_expert, d_back[:, at : at + 1], jnp.zeros((), BF))
-        )
-        for at in (width, width + 64)
-    ).reshape(2, rows, experts)
-    d_part = collect(d_back)[:, :width].reshape(2, rows, width)
-    (gate_grad_back, other_up, other_down), d_part = after((gate_grad_back, other_up, other_down), d_part)
-    d_hidden_moe, d_gates = reduce_chip(d_part, d_gates_part, 5)
-    residual = my_rows(chip_residual)
-
-    own_gates = my_rows(gates)
-    hidden_two = my_rows(chip_hidden)
-    inverse_two = my_rows(chip_inverse_two)
-    d_chosen = own_gates * (d_gates - jnp.sum(own_gates * d_gates, axis=-1, keepdims=True))
-    d_logits = to_low(d_chosen)
-    grad_router = transposed_times(hidden_two, d_logits)
-    d_hidden_two = d_hidden_moe + times_transposed(d_logits, wr)
-    d_res_norm, ffn_gain_terms = norm_back(residual, inverse_two, g_ffn, d_hidden_two)
-    d_residual = cotangent.astype(F32) + d_res_norm
-    gain_ffn_part = jnp.sum(ffn_gain_terms, axis=0)
-
-    other_up, d_residual = after(other_up, d_residual)
+    (gate_grad_back, other_up, other_down), d_back = after((gate_grad_back, other_up, other_down), d_back)
+    d_hidden_moe, d_gates = reduce_chip(pick_turned, d_back, of_expert, width, 5)
+    d_residual, d_residual_low, part = turn(
+        core.reshape(1),
+        d_hidden_moe,
+        d_gates,
+        gates,
+        hidden_two,
+        residual,
+        inverse_two,
+        late_all,
+        g_ffn[None, :],
+        cotangent,
+    )
+
+    d_attn, up_first = gather_row(d_residual_low, up_first, 7)
+    d_attn = d_attn.reshape(row_tokens, width)
+    (y_back, other_up, other_down), d_attn_late = after((y_back, other_up, other_down), d_attn)
     up_grad_back = swap(other_up)
-    d_attn = gather_row(to_low(d_residual), 7).reshape(row_tokens, width)
-    (y_back, up_grad_back), d_attn_late = after((y_back, up_grad_back), d_attn)
-    other_down, up_grad_back = after(other_down, up_grad_back)
     down_grad_back = swap(other_down)
-    grad_out_t = transposed_times(d_attn, heads)
-    early = jnp.concatenate(
-        [
-            to_low(grad_out_t[:, :128]).reshape(64, depth, 128),
-            to_low(grad_out_t[:, 128:]).reshape(64, depth, 128),
-            to_low(grad_router).reshape(64, depth, 128),
-            jnp.pad(
-                to_low(gain_ffn_part).reshape(64, 1, depth), ((0, 0), (0, 15), (0, 128 - depth))
-            ),
-        ],
-        axis=1,
-    )
-    d_queries, d_kv = attend_back(
-        plan, seq_lengths, queries, heads, d_attn_late, late_all, kv_all, lse
-    )
-    down_grad_back, d_kv = after(down_grad_back, d_kv)
-    swapped_grads = (gate_grad_back, up_grad_back, down_grad_back)
-    d_side, early = reduce_keys(d_kv, early, 8)
+    d_queries, d_kv, early = attend_back(
+        plan, seq_lengths, queries, heads, d_attn_late, late_all, kv_all, lse, part
+    )
+    (up_grad_back, down_grad_back), d_kv = after((up_grad_back, down_grad_back), d_kv)
+    d_side, early, down_rest = reduce_keys(d_kv, early, down_rest, 8)
+    swapped_grads = (gate_grad_back, up_first, up_grad_back, down_grad_back, down_rest)
     flags = jnp.concatenate(
         [
             flag(is_key)[:1],
@@ -1746,45 +2079,48 @@
         d_hidden_parts,
         9,
         False,
-        extra=collect(y_back).reshape(2, rows, width),
+        extra=(pick_turned, y_back.reshape(chips * slots, width)),
         owned=(late,),
     )
-    out_stream = residual + moe_total
-    own_stream = tokens.astype(F32)
-    d_stream_norm, _ = norm_back(own_stream, inverse_root(own_stream), g_attn, d_hidden_one)
-    grad_tokens = d_residual + d_stream_norm
-
-
-    grad_gate, grad_up, grad_down = place_other(side, swapped_grads, own_grads)
-
-    early, late = early.astype(F32), late.astype(F32)
-    early_q = early[:, : 2 * depth].reshape(8, 2, depth, 128)
-    grad_out = early_q.transpose(0, 1, 3, 2).reshape(8 * 256, depth)
-    grad_router = jnp.sum(early[:, 2 * depth : 3 * depth], axis=0)
-    grad_gain_ffn = jnp.sum(early[:, 3 * depth, :depth], axis=0)
-    late_q = late[:, : 2 * depth].reshape(8, 2, depth, 128)
-    grad_query = late_q.transpose(2, 0, 1, 3).reshape(depth, 8 * 256)
-    late_kv = jnp.sum(late[:, 2 * depth : 3 * depth].reshape(2, 2, 2, depth, 128), axis=2)
-    grad_key = late_kv[:, 0].transpose(1, 0, 2).reshape(depth, 256)
-    grad_value = late_kv[:, 1].transpose(1, 0, 2).reshape(depth, 256)
-    gain_parts = jnp.sum(late[:, 3 * depth : 3 * depth + 2], axis=0)
-    gain_attn_part = (
-        jnp.sum(rounded(w_query) * grad_query, axis=1)
-        + jnp.sum(rounded(key_weight) * grad_key, axis=1)
-        + jnp.sum(rounded(value_weight) * grad_value, axis=1)
-    ) / rounded(gain_attn)
-    gain_parts = lax.psum(jnp.concatenate([gain_parts, lanes_to(gain_attn_part[None, :])], axis=0), "wsh")
+    (
+        grad_gate,
+        grad_up,
+        grad_down,
+        out_stream,
+        grad_tokens,
+        grad_query,
+        grad_key,
+        grad_value,
+        grad_out_t,
+        grad_router,
+        gain_parts,
+        grad_gain_ffn,
+    ) = last(
+        jnp.stack([wsh, core]),
+        swapped_grads,
+        own_grads,
+        tokens,
+        d_hidden_one,
+        d_residual,
+        moe_total,
+        residual,
+        g_attn[None, :],
+        late,
+        early,
+        (w_query, key_weight, value_weight),
+    )
+    gain_parts = lax.psum(gain_parts, "wsh")
     return (
         out_stream,
         grad_tokens,
         grad_query,
         grad_key,
         grad_value,
-        grad_out,
-        gain_parts[2, :depth],
+        grad_out_t.T,
+        gain_parts[2, :depth] / rounded(gain_attn),
         gain_parts[0],
         gain_parts[1],
-        grad_gain_ffn,
+        grad_gain_ffn[0, :depth],
         grad_router,
         grad_gate,
         grad_up,

time: 622 us -> 568 us (0.913)
  other arithmetic: 34.5 us -> 4.9 us
  matrix products: 29.4 us -> 0 us
  Pallas kernels: 440 us -> 465 us
  local copies, waits for them, and re-layouts: 24.3 us -> 9.87 us
  waiting for transfers between devices: 45 us -> 38.3 us
    pallas_call x6 -> x9, Pallas kernels: 186 us -> 223 us  [the longest x2 102 us: reduce_row(): pl.pallas_call(body, out_shape=shapes, in_specs=spaces, out_specs=out_spa...]
    all_to_all x3, waiting for transfers between devices: 36.2 us -> 0.01 us  [exchange_behind(): lax.all_to_all(value, ('ctx', 'wsh'), split_axis=0, concat_axis=0, tiled=...]
    ppermute x6, waiting for transfers between devices: 8.76 us -> 38.3 us  [swap(): return lax.ppermute(value, 'wsh', [(0, 1), (1, 0)])]
    dot_general x14 -> x0, matrix products: 29.4 us -> none  [the longest x6 15.1 us: transposed_times(): lax.dot_general(left, right, (((0,), (0,)), ((), ())), preferred_element_...]
    pallas_call x1, Pallas kernels: 59.4 us -> 46.4 us  [reduce_keys(): pl.pallas_call(body, out_shape=(jax.ShapeDtypeStruct(block, F32), jax.Sha...]
    reduce_sum x11 -> x0, other arithmetic: 8.09 us -> none  [the longest x2 2.51 us: inverse_root(): jnp.mean(value_rows * value_rows, axis=-1, keepdims=True) + EPSILON]
    slice x7 -> x0, local copies, waits for them, and re-layouts: 8.03 us -> none  [the longest x1 2.24 us: local(): other_up[:up_cut]]
  transfers between devices with their start and end apart: 10 -> 10, of which waited for: 4 -> 3; matrix products, arithmetic and copies ran while one was open for 8% -> 1% of each run, Pallas kernels for 33% -> 50%
where the time goes in v5:
time: 568 us; the launch traced here: 563 us
  Pallas kernels  465 us (82%)
  starting transfers between devices  38.4 us (7%)
  waiting for transfers between devices  38.3 us (7%)
  local copies, waits for them, and re-layouts  9.87 us (2%)
    pallas_call x2, Pallas kernels, reduce_row(): pl.pallas_call(body, out_shape=shapes, in_specs=spaces, out_specs=out_spa...  102 us
    pallas_call x1, Pallas kernels, reduce_keys(): pl.pallas_call(body, out_shape=(jax.ShapeDtypeStruct(block, F32), jax.Sha...  46.4 us
    pallas_call x1, Pallas kernels, exchange(): pl.pallas_call(body, out_shape=[jax.ShapeDtypeStruct(a.shape, a.dtype) fo...  46.1 us
    pallas_call x1, Pallas kernels, gather_first(): pl.pallas_call(body, out_shape=(sds((64, depth, packed), BF), sds((8,) +...  39.5 us
    ppermute x6, waiting for transfers between devices, swap(): return lax.ppermute(value, 'wsh', [(0, 1), (1, 0)])  38.3 us
    pallas_call x1, Pallas kernels, gather_keys(): pl.pallas_call(body, out_shape=jax.ShapeDtypeStruct((8,) + rows.shape, ro...  34.9 us
    pallas_call x1, Pallas kernels, gather_row(): pl.pallas_call(body, out_shape=(jax.ShapeDtypeStruct((8,) + block.shape,...  34.4 us
    pallas_call x1, Pallas kernels, attend_back(): pl.pallas_call(backward_kernel, out_shape=(sds(queries.shape, F32), sds(d...  32.3 us
  transfers between devices with their start and end apart: 10, of which 3 were waited for; matrix products, arithmetic and copies ran while one was open for 1% of the time, Pallas kernels for 50%

profile of v5, /device:TPU:0, one launch (start us, length us, event | category | flops | bytes accessed | tf_op | source)
XLA Modules:
  0.0 562.6 jit_solution(18205945677061997512)
XLA Ops:
  0.6 1.0 convert_element_type.81
  1.6 0.7 convert_element_type.82
  2.4 39.5 %gather_first.1 = (bf16[64,32,384]{2,1,0:T(8,128)(2,1)}, bf16[8,128,2048]{2,1,0:T(8,128)(2,1)}, f32[64,8,128]{2,1,0:T(8,128)}, s32[2,8,128]{2,1,0:T(8,128)}, bf1...) custom-call(f32[32,2048]{1,0:T(8,128)} %refs_11_.1, ...), custom_call_target="tpu_custom_call" | custom-call | bytes 48000000 | tf_op jit(solution)/shard_map/gather_first/pallas_call | solution.py:302
  41.9 0.0 copy-start.7
  42.0 0.0 copy-start.12
  42.0 0.0 copy-start.13
  42.0 1.3 tile.4
  43.3 7.7 %all-to-all-start = ((bf16[64,32,384]{2,1,0:T(8,128)(2,1)}), bf16[64,32,384]{2,1,0:T(8,128)(2,1)S(1)}, u32[]{:S(2)}, u32[]{:S(2)}) async-start(bf16[64,32,384]{2,1,0:T(8,128)(2,1)} %bitcast.17), calls=%async_computation | async-start | bytes 3145728 | tf_op jit(solution)/shard_map/all_to_all | solution.py:1959
  51.0 0.2 fusion
  51.3 0.7 reshape.164.ga_ref.refs_8_
  51.9 0.6 maximum_bitcast_fusion.freq_ref
  52.5 0.6 bitcast_convert_fusion
  53.1 0.6 broadcast_in_dim.22.flag_ref
  53.7 11.1 %project.1 = (bf16[1024,2048]{1,0:T(8,128)(2,1)}, bf16[1024,256]{1,0:T(8,128)(2,1)}, bf16[1024,256]{1,0:T(8,128)(2,1)}, f32[1024,256]{1,0:T(8,128)}, f32[1024,12...) custom-call(s32[128]{0:T(128)} %block_order.3, s32[4]{0:T(128)} %lengths.5, s32[1]{0:T(128)} %bitcast.7.group, ...), custom_call_target="tpu_custom_call" | custom-call | bytes 9600000 | tf_op jit(solution)/shard_map/project/pallas_call | solution.py:1743
  64.9 34.9 %gather_keys.1 = bf16[8,1024,256]{2,1,0:T(8,128)(2,1)} custom-call(bf16[1024,256]{1,0:T(8,128)(2,1)} %get-tuple-element.131.src), custom_call_target="tpu_custom_call" | custom-call | bytes 36000000 | tf_op jit(solution)/shard_map/gather_keys/pallas_call | solution.py:404
  99.8 0.6 pad_add_fusion.1.where
  100.4 4.6 route.1
  105.0 0.0 all-to-all-done
  105.0 1.1 copy-done
  106.1 6.9 %all-to-all-start.1 = ((bf16[32,24,2048]{2,1,0:T(8,128)(2,1)}), bf16[32,24,2048]{2,1,0:T(8,128)(2,1)}, u32[]{:S(2)}, u32[]{:S(2)}) async-start(bf16[32,24,2048]{2,1,0:T(8,128)(2,1)} %bitcast.69), calls=%async_computation.1 | async-start | bytes 6291456 | tf_op jit(solution)/shard_map/all_to_all | solution.py:903
  113.0 0.7 collective-permute-start
  113.7 0.7 reshape.167.gain_ref
  114.4 17.7 %attend.1 = (bf16[1024,256]{1,0:T(8,128)(2,1)}, f32[8,1,256]{2,1,0:T(1,128)}, s32[256]{0:T(256)}) custom-call(s32[128]{0:T(128)} %block_order.3, s32[4]{0:T(128)} %lengths.5, s32[1]{0:T(128)} %bitcast.7.group, bf16[1024,256]{1,0:T(8,128)(2,1)} %get-tuple-element.125.q_ref, bf16[8192,256]{1,0:T(8,128)(2,1)} %bitcast.57), custom_call_target="tpu_custom_call" | custom-call | bytes 20400000 | tf_op jit(solution)/shard_map/attend/pallas_call | solution.py:1043
  132.1 54.8 %reduce_row.2 = (f32[2,128,2048]{2,1,0:T(8,128)}, bf16[1280,384]{1,0:T(8,128)(2,1)}) custom-call(bf16[1024,256]{1,0:T(8,128)(2,1)} %get-tuple-element.135.refs_0_.heads_ref, bf16[2048,384]{1,0:T(8,128)(2,1)} %bitcast.53, bf16[1280,384]{1,0:T(8,128)(2,1)} %get-tuple-element.137.refs_2_), custom_call_target="tpu_custom_call" | custom-call | bytes 1200000 | tf_op jit(solution)/shard_map/reduce_row/pallas_call | solution.py:684
  187.0 5.9 %middle.1 = (f32[256,2048]{1,0:T(8,128)}, bf16[256,2048]{1,0:T(8,128)(2,1)}, f32[256,128]{1,0:T(8,128)}, f32[256,128]{1,0:T(8,128)}, bf16[768,2048]{1,0:T(8,128)(2,1)}, /*index=5*/bf16[768,128]{1,0:T(8,128)(2,1)}) custom-call(s32[1]{0:T(128)} %bitcast.2.chip, bf16[1024,2048]{1,0:T(8,128)(2,1)} %bitcast.60, f32[256,2048]{1,0:T(8,128)} %bitcast.72, ...), custom_call_target="tpu_custom_call" | custom-call | bytes 1200000 | tf_op jit(solution)/shard_map/middle/pallas_call | solution.py:1467
  192.9 0.0 collective-permute-done.g_other
  192.9 0.0 all-to-all-done.1
  192.9 0.0 copy-done.9
  192.9 0.4 collective-permute-start.2
  193.3 1.9 collective-permute-start.1
  195.2 46.1 %exchange.1 = (bf16[32,24,2048]{2,1,0:T(8,128)(2,1)}, bf16[32,24,128]{2,1,0:T(8,128)(2,1)}) custom-call(bf16[32,24,2048]{2,1,0:T(8,128)(2,1)} %bitcast.71, bf16[32,24,128]{2,1,0:T(8,128)(2,1)} %bitcast.79), custom_call_target="tpu_custom_call" | custom-call | bytes 57600000 | tf_op jit(solution)/shard_map/exchange/pallas_call | solution.py:884
  241.3 1.0 collective-permute-done.1.u_rest
  242.3 0.0 collective-permute-done.2.d_other
  242.3 0.8 copy-done.6
  243.1 0.5 copy-done.3
  243.6 26.1 %run_expert.1 = (bf16[768,2048]{1,0:T(8,128)(2,1)}, bf16[768,2176]{1,0:T(8,128)(2,1)}, bf16[768,768]{1,0:T(8,128)(2,1)}, bf16[768,768]{1,0:T(8,128)(2,1)}, bf16[...) custom-call(s32[1]{0:T(128)} %bitcast.side, bf16[768,2048]{1,0:T(8,128)(2,1)} %bitcast.62, ...), custom_call_target="tpu_custom_call" | custom-call | bytes 30000000 | tf_op jit(solution)/shard_map/run_expert/pallas_call | solution.py:1259
  269.7 9.2 %all-to-all-start.2 = ((bf16[32,24,2176]{2,1,0:T(8,128)(2,1)}), bf16[32,24,2176]{2,1,0:T(8,128)(2,1)S(1)}, u32[]{:S(2)}, u32[]{:S(2)}) async-start(bf16[32,24,2176]{2,1,0:T(8,128)(2,1)} %bitcast.68), calls=%async_computation.2 | async-start | bytes 6684672 | tf_op jit(solution)/shard_map/all_to_all | solution.py:903
  278.9 14.6 %expert_grads.1 = (f32[2,2048,384]{2,1,0:T(8,128)}, f32[2,2048,384]{2,1,0:T(8,128)}, f32[2,384,2048]{2,1,0:T(8,128)}, bf16[2048,384]{1,0:T(8,128)(2,1)}, bf16[12...) custom-call(s32[1]{0:T(128)} %bitcast.side, ...), custom_call_target="tpu_custom_call" | custom-call | bytes 14400000 | tf_op jit(solution)/shard_map/expert_grads/pallas_call | solution.py:1339
  293.4 0.1 collective-permute-start.3
  293.5 35.9 %collective-permute-done.3.g_in = bf16[2048,384]{1,0:T(8,128)(2,1)} collective-permute-done((bf16[2048,384]{1,0:T(8,128)(2,1)}, bf16[2048,384]{1,0:T(8,128)(2,1)}, u32[]{:S(2)}, u32[]{:S(2)}) %collective-permute-start.3) | collective-permute-done | bytes 1572896 | tf_op jit(solution)/shard_map/ppermute | solution.py:1921
  329.4 0.0 all-to-all-done.2
  329.4 1.7 copy-done.1
  331.1 9.3 %all-to-all-start.3 = ((bf16[32,24,2048]{2,1,0:T(8,128)(2,1)}), bf16[32,24,2048]{2,1,0:T(8,128)(2,1)}, u32[]{:S(2)}, u32[]{:S(2)}) async-start(bf16[32,24,2048]{2,1,0:T(8,128)(2,1)} %bitcast.70), calls=%async_computation.3 | async-start | bytes 6291456 | tf_op jit(solution)/shard_map/all_to_all | solution.py:903
  340.4 20.8 %reduce_chip.1 = (f32[128,2048]{1,0:T(8,128)}, f32[128,128]{1,0:T(8,128)}) custom-call(bf16[256,768]{1,0:T(8,128)(2,1)} %get-tuple-element.165.pick_ref.refs_1_, bf16[768,2176]{1,0:T(8,128)(2,1)} %bitcast.61, bf16[768,128]{1,0:T(8,128)(2,1)} %get-tuple-element.141.of_ref), custom_call_target="tpu_custom_call" | custom-call | bytes 20400000 | tf_op jit(solution)/shard_map/reduce_chip/pallas_call | solution.py:729
  361.3 0.0 copy-start.8
  361.3 4.5 turn.1
  365.7 34.4 %gather_row.1 = (bf16[8,128,2048]{2,1,0:T(8,128)(2,1)}, bf16[1280,384]{1,0:T(8,128)(2,1)}) custom-call(bf16[128,2048]{1,0:T(8,128)(2,1)} %get-tuple-element.173.src, bf16[1280,384]{1,0:T(8,128)(2,1)} %get-tuple-element.174.src2), custom_call_target="tpu_custom_call" | custom-call | bytes 31200000 | tf_op jit(solution)/shard_map/gather_row/pallas_call | solution.py:355
  400.2 0.0 all-to-all-done.3
  400.2 0.1 collective-permute-start.5
  400.3 2.2 collective-permute-start.4
  402.5 0.6 pad_add_fusion.side
  403.1 0.1 maximum_maximum_fusion
  403.2 32.3 %attend_back.1 = (f32[1024,256]{1,0:T(8,128)}, bf16[2,8,2,512,128]{4,3,2,1,0:T(8,128)(2,1)}, bf16[64,112,128]{2,1,0:T(8,128)(2,1)}) custom-call(s32[256]{0:T(256)} %get-tuple-element.183.plan, s32[4]{0:T(128)} %lengths.5, bf16[1024,256]{1,0:T(8,128)(2,1)} %get-tuple-element.125.q_ref, bf16[1024,256]{1,0:T(8,128)(2,1)} %get-tuple-element.135.refs_0_.heads_ref, ...), custom_call_target="tpu_custom_call" | custom-call | bytes 28800000 | tf_op jit(solution)/shard_map/attend_back/pallas_call | solution.py:1156
  435.5 1.4 collective-permute-done.4.u_rest
  436.9 0.0 collective-permute-done.5.d_in
  436.9 46.4 %reduce_keys.1 = (f32[512,128]{1,0:T(8,128)}, bf16[8,112,128]{2,1,0:T(8,128)(2,1)}, bf16[144,2048]{1,0:T(8,128)(2,1)}) custom-call(bf16[2,8,2,512,128]{4,3,2,1,0:T(8,128)(2,1)} %get-tuple-element.190.src, bf16[64,112,128]{2,1,0:T(8,128)(2,1)} %get-tuple-element.191.src4, bf16[144,2048]{1,0:T(8,128)(2,1)} %get-tuple-element.192.src5), custom_call_target="tpu_custom_call" | custom-call | bytes 48000000 | tf_op jit(solution)/shard_map/reduce_keys/pallas_call | solution.py:820
  483.3 0.7 broadcast.30.flag_ref
  484.0 12.3 %project_back.1 = (bf16[1024,2048]{1,0:T(8,128)(2,1)}, bf16[64,112,128]{2,1,0:T(8,128)(2,1)}) custom-call(f32[1024,256]{1,0:T(8,128)} %get-tuple-element.197.dq_ref, f32[512,128]{1,0:T(8,128)} %get-tuple-element.198.ds_ref, f32[1024,256]{1,0:T(8,128)} %get-tuple-element.199.qp_ref, f32[1024,128]{1,0:T(8,128)} %get-tuple-element.200.kp_ref, ...), custom_call_target="tpu_custom_call" | custom-call | bytes 14400000 | tf_op jit(solution)/shard_map/project_back/pallas_call | solution.py:1850
  496.3 46.9 %reduce_row.3 = (f32[128,2048]{1,0:T(8,128)}, f32[128,2048]{1,0:T(8,128)}, bf16[8,112,128]{2,1,0:T(8,128)(2,1)}) custom-call(bf16[8,128,2048]{2,1,0:T(8,128)(2,1)} %bitcast.66, bf16[256,768]{1,0:T(8,128)(2,1)} %get-tuple-element.165.pick_ref.refs_1_, bf16[768,2048]{1,0:T(8,128)(2,1)} %bitcast.34.refs_2_, bf16[64,112,128]{2,1,0:T(8,128)(2,1)} %get-tuple-element.206.refs_3_), custom_call_target="tpu_custom_call" | custom-call | bytes 1200000 | tf_op jit(solution)/shard_map/reduce_row/pallas_call | solution.py:684
  543.2 11.9 %last.1 = (f32[2,2048,384]{2,1,0:T(8,128)}, f32[2,2048,384]{2,1,0:T(8,128)}, f32[2,384,2048]{2,1,0:T(8,128)}, f32[128,2048]{1,0:T(8,128)}, f32[128,2048]{1,0:T(8...) custom-call(s32[2]{0:T(128)} %pad_add_fusion.side, ...), custom_call_target="tpu_custom_call", output_to_operand_aliasing={{0}: (6, {}), {1}: (7, {}), {2}: (8, {})} | custom-call | bytes 10800000 | tf_op jit(solution)/shard_map/last/pallas_call | solution.py:1627
  555.1 4.9 psum.7
  560.1 0.5 slice_bitcast_fusion.1
  560.6 0.5 bitcast_divide_fusion
  561.1 1.2 slice_bitcast_fusion
  (29 shorter events, 0.2 us)
Async XLA Ops:
  41.9 9.0 %copy-start.7 = (f32[64,8,128]{2,1,0:T(8,128)S(1)}, f32[64,8,128]{2,1,0:T(8,128)}, u32[]{:S(2)}) copy-start(f32[64,8,128]{2,1,0:T(8,128)} %get-tuple-element.124) | copy-start | bytes 786436
  42.0 10.0 %copy-start.12 = (f32[128]{0:T(128)S(1)}, f32[128]{0:T(128)}, u32[]{:S(2)}) copy-start(f32[128]{0:T(128)} %param.27) | copy-start | bytes 1540
  42.0 9.9 %copy-start.13 = (f32[128]{0:T(128)S(1)}, f32[128]{0:T(128)}, u32[]{:S(2)}) copy-start(f32[128]{0:T(128)} %param.28) | copy-start | bytes 1540
  43.3 61.6 %all-to-all-start = ((bf16[64,32,384]{2,1,0:T(8,128)(2,1)}), bf16[64,32,384]{2,1,0:T(8,128)(2,1)S(1)}, u32[]{:S(2)}, u32[]{:S(2)}) async-start(bf16[64,32,384]{2,1,0:T(8,128)(2,1)} %bitcast.17), calls=%async_computation | async-start | bytes 3145728 | tf_op jit(solution)/shard_map/all_to_all | solution.py:1959
  105.0 1.1 copy-start
  106.1 86.8 %all-to-all-start.1 = ((bf16[32,24,2048]{2,1,0:T(8,128)(2,1)}), bf16[32,24,2048]{2,1,0:T(8,128)(2,1)}, u32[]{:S(2)}, u32[]{:S(2)}) async-start(bf16[32,24,2048]{2,1,0:T(8,128)(2,1)} %bitcast.69), calls=%async_computation.1 | async-start | bytes 6291456 | tf_op jit(solution)/shard_map/all_to_all | solution.py:903
  113.0 79.9 %collective-permute-start = (bf16[2048,384]{1,0:T(8,128)(2,1)}, bf16[2048,384]{1,0:T(8,128)(2,1)S(1)}, u32[]{:S(2)}, u32[]{:S(2)}) collective-permute-start(bf16[2048,384]{1,0:T(8,128)(2,1)} %get-tuple-element.143), channel_id=1, source_target_pairs={{0,1},{1,0},{2,3},{3,2},{4,5},{5,4},{6,7},{7,6},{8,9},{9,8},{10,11... | collective-permute-start | bytes 4718600 | tf_op jit(solution)/shard_map/ppermute | solution.py:1921
  187.0 5.9 %copy-start.9 = (bf16[384,2048]{1,0:T(8,128)(2,1)S(1)}, bf16[384,2048]{1,0:T(8,128)(2,1)}, u32[]{:S(2)}) copy-start(bf16[384,2048]{1,0:T(8,128)(2,1)} %get-tuple-element.155) | copy-start | bytes 4718596
  192.9 49.4 %copy-start.2 = (bf16[2048,384]{1,0:T(8,128)(2,1)}, bf16[2048,384]{1,0:T(8,128)(2,1)S(1)}, u32[]{:S(2)}) copy-start(bf16[2048,384]{1,0:T(8,128)(2,1)S(1)} %collective-permute-done.g_other) | copy-start | bytes 4718596
  192.9 49.4 %collective-permute-start.2 = (bf16[384,2048]{1,0:T(8,128)(2,1)S(1)}, bf16[384,2048]{1,0:T(8,128)(2,1)S(1)}, u32[]{:S(2)}, u32[]{:S(2)}) collective-permute-start(bf16[384,2048]{1,0:T(8,128)(2,1)S(1)} %copy-done.9), channel_id=1, source_target_pairs={{0,1},{1,0},{2,3},{3,2},{4,5},{5,4},{6,7},{7,6},{8,9},{9,8},{10,11... | collective-permute-start | bytes 4718600 | tf_op jit(solution)/shard_map/ppermute | solution.py:1921
  193.3 49.0 %collective-permute-start.1 = (bf16[768,384]{1,0:T(8,128)(2,1)}, bf16[768,384]{1,0:T(8,128)(2,1)S(1)}, u32[]{:S(2)}, u32[]{:S(2)}) collective-permute-start(bf16[768,384]{1,0:T(8,128)(2,1)} %get-tuple-element.154), channel_id=1, source_target_pairs={{0,1},{1,0},{2,3},{3,2},{4,5},{5,4},{6,7},{7,6},{8,9},{9,8},{10,11... | collective-permute-start | bytes 1769480 | tf_op jit(solution)/shard_map/ppermute | solution.py:1921
  242.3 0.8 copy-start.6
  242.3 1.3 copy-start.3
  269.7 59.7 %all-to-all-start.2 = ((bf16[32,24,2176]{2,1,0:T(8,128)(2,1)}), bf16[32,24,2176]{2,1,0:T(8,128)(2,1)S(1)}, u32[]{:S(2)}, u32[]{:S(2)}) async-start(bf16[32,24,2176]{2,1,0:T(8,128)(2,1)} %bitcast.68), calls=%async_computation.2 | async-start | bytes 6684672 | tf_op jit(solution)/shard_map/all_to_all | solution.py:903
  293.4 36.0 %collective-permute-start.3 = (bf16[2048,384]{1,0:T(8,128)(2,1)}, bf16[2048,384]{1,0:T(8,128)(2,1)}, u32[]{:S(2)}, u32[]{:S(2)}) collective-permute-start(bf16[2048,384]{1,0:T(8,128)(2,1)} %get-tuple-element.160), channel_id=1, source_target_pairs={{0,1},{1,0},{2,3},{3,2},{4,5},{5,4},{6,7},{7,6},{8,9},{9,8},{10,11... | collective-permute-start | bytes 4718600 | tf_op jit(solution)/shard_map/ppermute | solution.py:1921
  329.4 1.7 copy-start.1
  331.1 69.1 %all-to-all-start.3 = ((bf16[32,24,2048]{2,1,0:T(8,128)(2,1)}), bf16[32,24,2048]{2,1,0:T(8,128)(2,1)}, u32[]{:S(2)}, u32[]{:S(2)}) async-start(bf16[32,24,2048]{2,1,0:T(8,128)(2,1)} %bitcast.70), calls=%async_computation.3 | async-start | bytes 6291456 | tf_op jit(solution)/shard_map/all_to_all | solution.py:903
  361.2 38.9 %copy-start.10 = (bf16[240,2048]{1,0:T(8,128)(2,1)S(1)}, bf16[240,2048]{1,0:T(8,128)(2,1)}, u32[]{:S(2)}) copy-start(bf16[240,2048]{1,0:T(8,128)(2,1)} %get-tuple-element.182) | copy-start | bytes 2949124
  361.3 39.0 %copy-start.11 = (bf16[768,384]{1,0:T(8,128)(2,1)S(1)}, bf16[768,384]{1,0:T(8,128)(2,1)}, u32[]{:S(2)}) copy-start(bf16[768,384]{1,0:T(8,128)(2,1)} %get-tuple-element.181) | copy-start | bytes 1769476
  361.3 41.2 %copy-start.8 = (f32[32]{0:T(128)S(1)}, f32[32]{0:T(128)}, u32[]{:S(2)}) copy-start(f32[32]{0:T(128)} %param.26) | copy-start | bytes 388
  400.2 36.8 %collective-permute-start.5 = (bf16[240,2048]{1,0:T(8,128)(2,1)S(1)}, bf16[240,2048]{1,0:T(8,128)(2,1)S(1)}, u32[]{:S(2)}, u32[]{:S(2)}) collective-permute-start(bf16[240,2048]{1,0:T(8,128)(2,1)S(1)} %copy-done.10), channel_id=1, source_target_pairs={{0,1},{1,0},{2,3},{3,2},{4,5},{5,4},{6,7},{7,6},{8,9},{9,8},{10,11... | collective-permute-start | bytes 2949128 | tf_op jit(solution)/shard_map/ppermute | solution.py:1921
  400.3 36.6 %collective-permute-start.4 = (bf16[768,384]{1,0:T(8,128)(2,1)S(1)}, bf16[768,384]{1,0:T(8,128)(2,1)S(1)}, u32[]{:S(2)}, u32[]{:S(2)}) collective-permute-start(bf16[768,384]{1,0:T(8,128)(2,1)S(1)} %copy-done.11), channel_id=1, source_target_pairs={{0,1},{1,0},{2,3},{3,2},{4,5},{5,4},{6,7},{7,6},{8,9},{9,8},{10,11... | collective-permute-start | bytes 1769480 | tf_op jit(solution)/shard_map/ppermute | solution.py:1921
  436.9 46.4 %copy-start.5 = (bf16[768,384]{1,0:T(8,128)(2,1)}, bf16[768,384]{1,0:T(8,128)(2,1)S(1)}, u32[]{:S(2)}) copy-start(bf16[768,384]{1,0:T(8,128)(2,1)S(1)} %collective-permute-done.4.u_rest) | copy-start | bytes 1769476
  436.9 46.4 %copy-start.4 = (bf16[240,2048]{1,0:T(8,128)(2,1)}, bf16[240,2048]{1,0:T(8,128)(2,1)S(1)}, u32[]{:S(2)}) copy-start(bf16[240,2048]{1,0:T(8,128)(2,1)S(1)} %collective-permute-done.5.d_in) | copy-start | bytes 2949124

commit v6 on v5

--- a/solution.py
+++ b/solution.py
@@ -376,25 +376,39 @@
         core = lax.rem(me, 2)
         group = lax.div(me, 8)
         partner = shifted(me, 0, 0, 0, 1)
-        peers = [shifted(me, dz, dy, 0, 0) for dz, dy in COLUMN_STEPS]
-        barrier, amount = greet([(peer, wsh) for peer in peers + [partner]])
+        across = shifted(me, 0, 1, 0, 0)
+        steps = (1, 3, 2)
+        peers = [shifted(me, dz, 0, 0, 0) for dz in steps]
+        barrier, amount = greet([(peer, wsh) for peer in peers + [across, partner]])
         mine = pltpu.make_async_copy(src, out.at[group], local)
         mine.start()
         pl.semaphore_wait(barrier, amount)
         my_half = pl.ds(pl.multiple_of(core * half, half), half)
         copies = []
-        for at, peer in enumerate(peers):
+        for at, peer in enumerate([across] + peers):
             copy = remote(src.at[my_half], out.at[group, my_half], send.at[at], recv.at[at], peer, wsh)
             copy.start()
             copies.append(copy)
         forwards = []
-        for at, (dz, dy) in enumerate(COLUMN_STEPS):
-            copies[at].wait_recv()
-            origin = lax.div(shifted(me, 4 - dz, 2 - dy, 0, 0), 8)
+
+        def hand_on(origin, at):
             part = out.at[origin, my_half]
             forward = remote(part, part, send.at[7 + at], recv.at[7 + at], partner, wsh)
             forward.start()
             forwards.append(forward)
+
+        copies[0].wait_recv()
+        beside = lax.div(across, 8)
+        for at, peer in enumerate(peers):
+            part = out.at[beside, my_half]
+            copy = remote(part, part, send.at[4 + at], recv.at[4 + at], peer, wsh)
+            copy.start()
+            copies.append(copy)
+        hand_on(beside, 0)
+        for dy in range(2):
+            for at, dz in enumerate(steps):
+                copies[1 + 3 * dy + at].wait_recv()
+                hand_on(lax.div(shifted(me, 4 - dz, dy, 0, 0), 8), 1 + 3 * dy + at)
         for copy in copies:
             copy.wait_send()
         for forward in forwards:
@@ -865,7 +879,7 @@
         pl.semaphore_wait(barrier, count)
 
         def one(step, carried):
-            ctx, side = target(lax.rem(step * 13, 32))
+            ctx, side = target(lax.rem(step * 27, 32))
             for at in range(amount):
                 remote(
                     ins[at].at[lax.div(ctx, 2)], outs[at].at[chip], send.at[at], recv.at[at], ctx, side
@@ -1200,31 +1214,46 @@
     ):
         own_copies.append(pltpu.make_async_copy(own.at[side[0]], stage, sems.at[at, 0]))
         begin = 0
+        other_copies.append([])
         for which, part in enumerate(others):
             count = part.shape[0]
             if at < 2:
                 target = whole.at[pl.ds(begin, count), pl.ds(half, half)]
             else:
                 target = whole.at[pl.ds(half, half)]
-            other_copies.append(pltpu.make_async_copy(part, target, sems.at[at, 1 + which]))
+            other_copies[at].append(pltpu.make_async_copy(part, target, sems.at[at, 1 + which]))
             begin += count
 
     @pl.when(pl.program_id(0) == 0)
     def _():
-        for copy in own_copies + other_copies:
-            copy.start()
-        own_copies[0].wait()
+        for which in range(3):
+            own_copies[which].start()
+            for copy in other_copies[which]:
+                copy.start()
+
+    def ready(which, fill):
+        @pl.when(pl.program_id(0) == 0)
+        def _():
+            own_copies[which].wait()
+            fill()
+            for copy in other_copies[which]:
+                copy.wait()
+
+    def fill_gate():
         gate_w[:, :half] = gate_f[...].astype(BF)
-        own_copies[1].wait()
+
+    def fill_up():
         up_w[:, :half] = up_f[...].astype(BF)
-        own_copies[2].wait()
+
+    def fill_down():
         down_w[:half, :] = down_f[...].astype(BF)
-        for copy in other_copies:
-            copy.wait()
 
     x = x_ref[...]
+    ready(0, fill_gate)
     gate_pre = matmul(x, gate_w[...])
+    ready(1, fill_up)
     up_pre = matmul(x, up_w[...])
+    ready(2, fill_down)
     sigma = 1.0 / (1.0 + jnp.exp(-gate_pre))
     silu = gate_pre * sigma
     activated = (silu * up_pre).astype(BF)
@@ -1294,8 +1323,42 @@
     )(side, rows_in, cot, gates, *own, *other)
 
 
-def expert_grads_kernel(side, x_ref, dy_ref, a_ref, dg_ref, du_ref, gate_ref, up_ref, down_ref, gate_out, up_out, up_rest, down_out, down_rest, a_t):
+def gate_grads_kernel(side, x_ref, dg_ref, gate_ref, gate_out):
     half = gate_ref.shape[-1]
+    value = matmul(x_ref[...].T, dg_ref[...])
+    gate_ref[0] = value[:, :half]
+    gate_out[...] = value[:, half:].astype(BF)
+
+
+def gate_grads(side, rows_in, d_gate):
+    count, width = rows_in.shape
+    whole = d_gate.shape[1]
+    half = whole // 2
+    tile = 1024
+    sds = jax.ShapeDtypeStruct
+    return pl.pallas_call(
+        gate_grads_kernel,
+        out_shape=(sds((2, width, half), F32), sds((width, half), BF)),
+        grid_spec=pltpu.PrefetchScalarGridSpec(
+            num_scalar_prefetch=1,
+            grid=(width // tile,),
+            in_specs=[
+                pl.BlockSpec((count, tile), lambda i, side: (0, i)),
+                pl.BlockSpec((count, whole), lambda i, side: (0, 0)),
+            ],
+            out_specs=[
+                pl.BlockSpec((1, tile, half), lambda i, side: (side[0], i, 0)),
+                pl.BlockSpec((tile, half), lambda i, side: (i, 0)),
+            ],
+        ),
+        compiler_params=pltpu.CompilerParams(vmem_limit_bytes=ROOM),
+        name="gate_grads",
+        cost_estimate=cost(5),
+    )(side, rows_in, d_gate)
+
+
+def expert_grads_kernel(side, x_ref, dy_ref, a_ref, du_ref, up_ref, down_ref, up_out, up_rest, down_out, down_rest, a_t):
+    half = up_ref.shape[-1]
     step = pl.program_id(0)
     turn_at = up_out.shape[0]
 
@@ -1303,11 +1366,7 @@
     def _():
         a_t[...] = a_ref[...].T
 
-    x_t = x_ref[...].T
-    value = matmul(x_t, dg_ref[...])
-    gate_ref[0] = value[:, :half]
-    gate_out[...] = value[:, half:].astype(BF)
-    value = matmul(x_t, du_ref[...])
+    value = matmul(x_ref[...].T, du_ref[...])
     up_ref[0] = value[:, :half]
     low = value[:, half:].astype(BF)
 
@@ -1326,7 +1385,7 @@
     down_rest[...] = value[cut:].astype(BF)
 
 
-def expert_grads(side, rows_in, d_pairs, activated, d_gate, d_up):
+def expert_grads(side, rows_in, d_pairs, activated, d_up):
     count, width = rows_in.shape
     whole = activated.shape[1]
     half = whole // 2
@@ -1335,14 +1394,11 @@
     sds = jax.ShapeDtypeStruct
     columns = pl.BlockSpec((count, tile), lambda i, side: (0, i))
     full = pl.BlockSpec((count, whole), lambda i, side: (0, 0))
-    own_rows = pl.BlockSpec((1, tile, half), lambda i, side: (side[0], i, 0))
     return pl.pallas_call(
         expert_grads_kernel,
         out_shape=(
             sds((2, width, half), F32),
-            sds((2, width, half), F32),
             sds((2, half, width), F32),
-            sds((width, half), BF),
             sds((UP_CUT[0], half), BF),
             sds((UP_CUT[1], half), BF),
             sds((DOWN_GRAD_CUT[0], width), BF),
@@ -1351,12 +1407,10 @@
         grid_spec=pltpu.PrefetchScalarGridSpec(
             num_scalar_prefetch=1,
             grid=(width // tile,),
-            in_specs=[columns, columns, full, full, full],
+            in_specs=[columns, columns, full, full],
             out_specs=[
-                own_rows,
-                own_rows,
+                pl.BlockSpec((1, tile, half), lambda i, side: (side[0], i, 0)),
                 pl.BlockSpec((1, half, tile), lambda i, side: (side[0], 0, i)),
-                pl.BlockSpec((tile, half), lambda i, side: (i, 0)),
                 pl.BlockSpec((tile, half), lambda i, side: (jnp.minimum(i, first - 1), 0)),
                 pl.BlockSpec((tile, half), lambda i, side: (jnp.maximum(i - first, 0), 0)),
                 pl.BlockSpec((DOWN_GRAD_CUT[0], tile), lambda i, side: (0, i)),
@@ -1366,8 +1420,8 @@
         ),
         compiler_params=pltpu.CompilerParams(vmem_limit_bytes=ROOM),
         name="expert_grads",
-        cost_estimate=cost(12),
-    )(side, rows_in, d_pairs, activated, d_gate, d_up)
+        cost_estimate=cost(10),
+    )(side, rows_in, d_pairs, activated, d_up)
 
 
 def route_kernel(where, routes_ref, cot_ref, pick_ref, turned_ref, of_ref, hits_ref, rows_ref):
@@ -2016,16 +2070,18 @@
     y_rows, d_rows, activated, d_gate_pre, d_up_pre, d_pairs = run_expert(
         side, arrived, cot_there, gate_there, (w_gate, w_up, w_down), (gate_back, *up_back, down_back)
     )
-    *own_grads, other_gate, up_first, other_up, other_down, down_rest = expert_grads(
-        side, arrived, d_pairs, activated, d_gate_pre, d_up_pre
-    )
+    own_gate, other_gate = gate_grads(side, arrived, d_gate_pre)
+    activated, other_gate = after(activated, other_gate)
+    own_up, own_down, up_first, other_up, other_down, down_rest = expert_grads(
+        side, arrived, d_pairs, activated, d_up_pre
+    )
+    own_grads = (own_gate, own_up, own_down)
     gate_grad_back = swap(other_gate)
     d_back = exchange_behind(d_rows.reshape(chips, slots, width + 128))
-    y_rows, _ = after(y_rows, (d_back, gate_grad_back))
-    y_back = exchange_behind(y_rows.reshape(chips, slots, width))
-
     d_back = d_back.reshape(chips * slots, width + 128)
-    (gate_grad_back, other_up, other_down), d_back = after((gate_grad_back, other_up, other_down), d_back)
+    (gate_grad_back, other_up, other_down, down_rest), d_back = after(
+        (gate_grad_back, other_up, other_down, down_rest), d_back
+    )
     d_hidden_moe, d_gates = reduce_chip(pick_turned, d_back, of_expert, width, 5)
     d_residual, d_residual_low, part = turn(
         core.reshape(1),
@@ -2042,13 +2098,14 @@
 
     d_attn, up_first = gather_row(d_residual_low, up_first, 7)
     d_attn = d_attn.reshape(row_tokens, width)
-    (y_back, other_up, other_down), d_attn_late = after((y_back, other_up, other_down), d_attn)
+    (y_rows, other_up, other_down), d_attn_late = after((y_rows, other_up, other_down), d_attn)
+    y_back = exchange_behind(y_rows.reshape(chips, slots, width))
     up_grad_back = swap(other_up)
     down_grad_back = swap(other_down)
     d_queries, d_kv, early = attend_back(
         plan, seq_lengths, queries, heads, d_attn_late, late_all, kv_all, lse, part
     )
-    (up_grad_back, down_grad_back), d_kv = after((up_grad_back, down_grad_back), d_kv)
+    (y_back, up_grad_back, down_grad_back), d_kv = after((y_back, up_grad_back, down_grad_back), d_kv)
     d_side, early, down_rest = reduce_keys(d_kv, early, down_rest, 8)
     swapped_grads = (gate_grad_back, up_first, up_grad_back, down_grad_back, down_rest)
     flags = jnp.concatenate(

time: 568 us -> 563 us (level)
    all_to_all x3, waiting for transfers between devices: 0.01 us -> 9.3 us  [exchange_behind(): lax.all_to_all(value, ('ctx', 'wsh'), split_axis=0, concat_axis=0, tiled=...]
    ppermute x6, waiting for transfers between devices: 38.3 us -> 29.7 us  [swap(): return lax.ppermute(value, 'wsh', [(0, 1), (1, 0)])]
    pallas_call x1, Pallas kernels: 34.4 us -> 28 us  [gather_row(): pl.pallas_call(body, out_shape=(jax.ShapeDtypeStruct((8,) + block.shape,...]
    pallas_call x1, Pallas kernels: 32.3 us -> 26.1 us  [attend_back(): pl.pallas_call(backward_kernel, out_shape=(sds(queries.shape, F32), sds(d...]
    pallas_call x0 -> x1, Pallas kernels: none -> 6.2 us  [gate_grads(): pl.pallas_call(gate_grads_kernel, out_shape=(sds((2, width, half), F32),...]
  transfers between devices with their start and end apart: 10 -> 10, of which waited for: 3 -> 5; matrix products, arithmetic and copies ran while one was open for 1% -> 1% of each run, Pallas kernels for 50% -> 40%
where the time goes in v6:
time: 563 us; the launch traced here: 554 us
  Pallas kernels  460 us (82%)
  waiting for transfers between devices  39 us (7%)
  starting transfers between devices  33.2 us (6%)
  local copies, waits for them, and re-layouts  9.96 us (2%)
    pallas_call x2, Pallas kernels, reduce_row(): pl.pallas_call(body, out_shape=shapes, in_specs=spaces, out_specs=out_spa...  106 us
    pallas_call x1, Pallas kernels, reduce_keys(): pl.pallas_call(body, out_shape=(jax.ShapeDtypeStruct(block, F32), jax.Sha...  48.8 us
    pallas_call x1, Pallas kernels, exchange(): pl.pallas_call(body, out_shape=[jax.ShapeDtypeStruct(a.shape, a.dtype) fo...  46.3 us
    pallas_call x1, Pallas kernels, gather_first(): pl.pallas_call(body, out_shape=(sds((64, depth, packed), BF), sds((8,) +...  39.5 us
    pallas_call x1, Pallas kernels, gather_keys(): pl.pallas_call(body, out_shape=jax.ShapeDtypeStruct((8,) + rows.shape, ro...  34.7 us
    ppermute x6, waiting for transfers between devices, swap(): return lax.ppermute(value, 'wsh', [(0, 1), (1, 0)])  29.7 us
    pallas_call x1, Pallas kernels, gather_row(): pl.pallas_call(body, out_shape=(jax.ShapeDtypeStruct((8,) + block.shape,...  28 us
    pallas_call x1, Pallas kernels, run_expert(): pl.pallas_call(expert_kernel, out_shape=(sds((count, width), BF), sds((co...  26.6 us
  transfers between devices with their start and end apart: 10, of which 5 were waited for; matrix products, arithmetic and copies ran while one was open for 1% of the time, Pallas kernels for 40%

profile of v6, /device:TPU:0, one launch (start us, length us, event | category | flops | bytes accessed | tf_op | source)
XLA Modules:
  0.0 553.6 jit_solution(6406276557103051174)
XLA Ops:
  0.6 1.0 convert_element_type.81
  1.6 0.7 convert_element_type.82
  2.4 39.5 %gather_first.1 = (bf16[64,32,384]{2,1,0:T(8,128)(2,1)}, bf16[8,128,2048]{2,1,0:T(8,128)(2,1)}, f32[64,8,128]{2,1,0:T(8,128)}, s32[2,8,128]{2,1,0:T(8,128)}, bf1...) custom-call(f32[32,2048]{1,0:T(8,128)} %refs_11_.1, ...), custom_call_target="tpu_custom_call" | custom-call | bytes 48000000 | tf_op jit(solution)/shard_map/gather_first/pallas_call | solution.py:302
  42.0 0.0 copy-start.6
  42.0 0.0 copy-start.9
  42.0 0.0 copy-start.10
  42.0 1.3 tile.4
  43.3 7.7 %all-to-all-start = ((bf16[64,32,384]{2,1,0:T(8,128)(2,1)}), bf16[64,32,384]{2,1,0:T(8,128)(2,1)S(1)}, u32[]{:S(2)}, u32[]{:S(2)}) async-start(bf16[64,32,384]{2,1,0:T(8,128)(2,1)} %bitcast.17), calls=%async_computation | async-start | bytes 3145728 | tf_op jit(solution)/shard_map/all_to_all | solution.py:2013
  51.0 0.2 fusion
  51.3 0.7 reshape.164.ga_ref.refs_8_
  52.0 0.6 maximum_bitcast_fusion.freq_ref
  52.5 0.6 bitcast_convert_fusion
  53.1 0.6 broadcast_in_dim.22.flag_ref
  53.7 11.2 %project.1 = (bf16[1024,2048]{1,0:T(8,128)(2,1)}, bf16[1024,256]{1,0:T(8,128)(2,1)}, bf16[1024,256]{1,0:T(8,128)(2,1)}, f32[1024,256]{1,0:T(8,128)}, f32[1024,12...) custom-call(s32[128]{0:T(128)} %block_order.3, s32[4]{0:T(128)} %lengths.5, s32[1]{0:T(128)} %bitcast.7.group, ...), custom_call_target="tpu_custom_call" | custom-call | bytes 9600000 | tf_op jit(solution)/shard_map/project/pallas_call | solution.py:1797
  64.9 34.7 %gather_keys.1 = bf16[8,1024,256]{2,1,0:T(8,128)(2,1)} custom-call(bf16[1024,256]{1,0:T(8,128)(2,1)} %get-tuple-element.134.src), custom_call_target="tpu_custom_call" | custom-call | bytes 36000000 | tf_op jit(solution)/shard_map/gather_keys/pallas_call | solution.py:418
  99.6 0.6 pad_add_fusion.1.where
  100.1 4.6 route.1
  104.7 0.0 all-to-all-done
  104.7 1.2 copy-done
  105.9 4.8 all-to-all-start.1
  110.8 0.9 collective-permute-start
  111.7 0.7 reshape.167.gain_ref
  112.4 13.3 %attend.1 = (bf16[1024,256]{1,0:T(8,128)(2,1)}, f32[8,1,256]{2,1,0:T(1,128)}, s32[256]{0:T(256)}) custom-call(s32[128]{0:T(128)} %block_order.3, s32[4]{0:T(128)} %lengths.5, s32[1]{0:T(128)} %bitcast.7.group, bf16[1024,256]{1,0:T(8,128)(2,1)} %get-tuple-element.128.q_ref, bf16[8192,256]{1,0:T(8,128)(2,1)} %bitcast.57), custom_call_target="tpu_custom_call" | custom-call | bytes 20400000 | tf_op jit(solution)/shard_map/attend/pallas_call | solution.py:1057
  125.7 59.0 %reduce_row.2 = (f32[2,128,2048]{2,1,0:T(8,128)}, bf16[1280,384]{1,0:T(8,128)(2,1)}) custom-call(bf16[1024,256]{1,0:T(8,128)(2,1)} %get-tuple-element.138.refs_0_.heads_ref, bf16[2048,384]{1,0:T(8,128)(2,1)} %bitcast.53, bf16[1280,384]{1,0:T(8,128)(2,1)} %get-tuple-element.140.refs_2_), custom_call_target="tpu_custom_call" | custom-call | bytes 1200000 | tf_op jit(solution)/shard_map/reduce_row/pallas_call | solution.py:698
  184.7 5.9 %middle.1 = (f32[256,2048]{1,0:T(8,128)}, bf16[256,2048]{1,0:T(8,128)(2,1)}, f32[256,128]{1,0:T(8,128)}, f32[256,128]{1,0:T(8,128)}, bf16[768,2048]{1,0:T(8,128)(2,1)}, /*index=5*/bf16[768,128]{1,0:T(8,128)(2,1)}) custom-call(s32[1]{0:T(128)} %bitcast.2.chip, bf16[1024,2048]{1,0:T(8,128)(2,1)} %bitcast.63, f32[256,2048]{1,0:T(8,128)} %bitcast.74, ...), custom_call_target="tpu_custom_call" | custom-call | bytes 1200000 | tf_op jit(solution)/shard_map/middle/pallas_call | solution.py:1521
  190.6 0.0 collective-permute-done.g_other
  190.6 0.0 all-to-all-done.1
  190.6 0.8 collective-permute-start.2
  191.3 1.5 collective-permute-start.1
  192.9 46.3 %exchange.1 = (bf16[32,24,2048]{2,1,0:T(8,128)(2,1)}, bf16[32,24,128]{2,1,0:T(8,128)(2,1)}) custom-call(bf16[32,24,2048]{2,1,0:T(8,128)(2,1)} %bitcast.73, bf16[32,24,128]{2,1,0:T(8,128)(2,1)} %bitcast.81), custom_call_target="tpu_custom_call" | custom-call | bytes 57600000 | tf_op jit(solution)/shard_map/exchange/pallas_call | solution.py:898
  239.3 0.7 collective-permute-done.1.u_rest
  240.0 0.0 collective-permute-done.2.d_other
  240.0 0.8 copy-done.5
  240.8 0.5 copy-done.4
  241.3 26.6 %run_expert.1 = (bf16[768,2048]{1,0:T(8,128)(2,1)}, bf16[768,2176]{1,0:T(8,128)(2,1)}, bf16[768,768]{1,0:T(8,128)(2,1)}, bf16[768,768]{1,0:T(8,128)(2,1)}, bf16[...) custom-call(s32[1]{0:T(128)} %bitcast.side, bf16[768,2048]{1,0:T(8,128)(2,1)} %bitcast.59, ...), custom_call_target="tpu_custom_call" | custom-call | bytes 30000000 | tf_op jit(solution)/shard_map/run_expert/pallas_call | solution.py:1288
  267.9 9.2 %all-to-all-start.2 = ((bf16[32,24,2176]{2,1,0:T(8,128)(2,1)}), bf16[32,24,2176]{2,1,0:T(8,128)(2,1)S(1)}, u32[]{:S(2)}, u32[]{:S(2)}) async-start(bf16[32,24,2176]{2,1,0:T(8,128)(2,1)} %bitcast.70), calls=%async_computation.2 | async-start | bytes 6684672 | tf_op jit(solution)/shard_map/all_to_all | solution.py:917
  277.1 6.2 %gate_grads.1 = (f32[2,2048,384]{2,1,0:T(8,128)}, bf16[2048,384]{1,0:T(8,128)(2,1)}) custom-call(s32[1]{0:T(128)} %bitcast.side, bf16[768,2048]{1,0:T(8,128)(2,1)} %bitcast.60, bf16[768,768]{1,0:T(8,128)(2,1)} %get-tuple-element.160.dg_ref), custom_call_target="tpu_custom_call" | custom-call | bytes 6000000 | tf_op jit(solution)/shard_map/gate_grads/pallas_call | solution.py:1339
  283.3 0.0 collective-permute-start.3
  283.4 13.6 %expert_grads.1 = (f32[2,2048,384]{2,1,0:T(8,128)}, f32[2,384,2048]{2,1,0:T(8,128)}, bf16[1280,384]{1,0:T(8,128)(2,1)}, bf16[768,384]{1,0:T(8,128)(2,1)}, bf16[2...) custom-call(s32[1]{0:T(128)} %bitcast.side, bf16[768,2048]{1,0:T(8,128)(2,1)} %bitcast.61, ...), custom_call_target="tpu_custom_call" | custom-call | bytes 12000000 | tf_op jit(solution)/shard_map/expert_grads/pallas_call | solution.py:1397
  297.0 22.2 %collective-permute-done.3.g_in = bf16[2048,384]{1,0:T(8,128)(2,1)} collective-permute-done((bf16[2048,384]{1,0:T(8,128)(2,1)}, bf16[2048,384]{1,0:T(8,128)(2,1)}, u32[]{:S(2)}, u32[]{:S(2)}) %collective-permute-start.3) | collective-permute-done | bytes 1572896 | tf_op jit(solution)/shard_map/ppermute | solution.py:1975
  319.2 2.5 all-to-all-done.2
  321.7 1.7 copy-done.1
  323.4 20.8 %reduce_chip.1 = (f32[128,2048]{1,0:T(8,128)}, f32[128,128]{1,0:T(8,128)}) custom-call(bf16[256,768]{1,0:T(8,128)(2,1)} %get-tuple-element.171.pick_ref.refs_1_, bf16[768,2176]{1,0:T(8,128)(2,1)} %bitcast.64, bf16[768,128]{1,0:T(8,128)(2,1)} %get-tuple-element.144.of_ref), custom_call_target="tpu_custom_call" | custom-call | bytes 20400000 | tf_op jit(solution)/shard_map/reduce_chip/pallas_call | solution.py:743
  344.2 4.4 turn.1
  348.6 28.0 %gather_row.1 = (bf16[8,128,2048]{2,1,0:T(8,128)(2,1)}, bf16[1280,384]{1,0:T(8,128)(2,1)}) custom-call(bf16[128,2048]{1,0:T(8,128)(2,1)} %get-tuple-element.179.src, bf16[1280,384]{1,0:T(8,128)(2,1)} %get-tuple-element.180.src2), custom_call_target="tpu_custom_call" | custom-call | bytes 31200000 | tf_op jit(solution)/shard_map/gather_row/pallas_call | solution.py:355
  376.7 0.0 copy-start.7
  376.7 6.2 %all-to-all-start.3 = ((bf16[32,24,2048]{2,1,0:T(8,128)(2,1)}), bf16[32,24,2048]{2,1,0:T(8,128)(2,1)S(1)}, u32[]{:S(2)}, u32[]{:S(2)}) async-start(bf16[32,24,2048]{2,1,0:T(8,128)(2,1)} %bitcast.71), calls=%async_computation.3 | async-start | bytes 6291456 | tf_op jit(solution)/shard_map/all_to_all | solution.py:917
  382.8 0.5 collective-permute-start.5
  383.4 1.6 collective-permute-start.4
  385.0 0.6 pad_add_fusion.side
  385.5 0.1 maximum_maximum_fusion
  385.6 26.1 %attend_back.1 = (f32[1024,256]{1,0:T(8,128)}, bf16[2,8,2,512,128]{4,3,2,1,0:T(8,128)(2,1)}, bf16[64,112,128]{2,1,0:T(8,128)(2,1)}) custom-call(s32[256]{0:T(256)} %get-tuple-element.189.plan, s32[4]{0:T(128)} %lengths.5, bf16[1024,256]{1,0:T(8,128)(2,1)} %get-tuple-element.128.q_ref, bf16[1024,256]{1,0:T(8,128)(2,1)} %get-tuple-element.138.refs_0_.heads_ref, ...), custom_call_target="tpu_custom_call" | custom-call | bytes 28800000 | tf_op jit(solution)/shard_map/attend_back/pallas_call | solution.py:1170
  411.7 6.8 %collective-permute-done.4.u_rest = bf16[768,384]{1,0:T(8,128)(2,1)} collective-permute-done((bf16[768,384]{1,0:T(8,128)(2,1)}, bf16[768,384]{1,0:T(8,128)(2,1)}, u32[]{:S(2)}, u32[]{:S(2)}) %collective-permute-start.4) | collective-permute-done | bytes 589856 | tf_op jit(solution)/shard_map/ppermute | solution.py:1975
  418.5 0.0 collective-permute-done.5.d_in
  418.5 6.8 %all-to-all-done.3 = bf16[32,24,2048]{2,1,0:T(8,128)(2,1)S(1)} async-done(((bf16[32,24,2048]{2,1,0:T(8,128)(2,1)}), bf16[32,24,2048]{2,1,0:T(8,128)(2,1)S(1)}, u32[]{:S(2)}, u32[]{:S(2)}) %all-to-all-start.3) | async-done | bytes 3145760 | tf_op jit(solution)/shard_map/all_to_all | solution.py:917
  425.3 48.8 %reduce_keys.1 = (f32[512,128]{1,0:T(8,128)}, bf16[8,112,128]{2,1,0:T(8,128)(2,1)}, bf16[144,2048]{1,0:T(8,128)(2,1)}) custom-call(bf16[2,8,2,512,128]{4,3,2,1,0:T(8,128)(2,1)} %get-tuple-element.196.src, bf16[64,112,128]{2,1,0:T(8,128)(2,1)} %get-tuple-element.197.src4, bf16[144,2048]{1,0:T(8,128)(2,1)} %get-tuple-element.198.src5), custom_call_target="tpu_custom_call" | custom-call | bytes 48000000 | tf_op jit(solution)/shard_map/reduce_keys/pallas_call | solution.py:834
  474.0 0.7 broadcast.30.flag_ref
  474.7 12.3 %project_back.1 = (bf16[1024,2048]{1,0:T(8,128)(2,1)}, bf16[64,112,128]{2,1,0:T(8,128)(2,1)}) custom-call(f32[1024,256]{1,0:T(8,128)} %get-tuple-element.203.dq_ref, f32[512,128]{1,0:T(8,128)} %get-tuple-element.204.ds_ref, f32[1024,256]{1,0:T(8,128)} %get-tuple-element.205.qp_ref, f32[1024,128]{1,0:T(8,128)} %get-tuple-element.206.kp_ref, ...), custom_call_target="tpu_custom_call" | custom-call | bytes 14400000 | tf_op jit(solution)/shard_map/project_back/pallas_call | solution.py:1904
  487.0 47.0 %reduce_row.3 = (f32[128,2048]{1,0:T(8,128)}, f32[128,2048]{1,0:T(8,128)}, bf16[8,112,128]{2,1,0:T(8,128)(2,1)}) custom-call(bf16[8,128,2048]{2,1,0:T(8,128)(2,1)} %bitcast.68, bf16[256,768]{1,0:T(8,128)(2,1)} %get-tuple-element.171.pick_ref.refs_1_, bf16[768,2048]{1,0:T(8,128)(2,1)} %bitcast.65, bf16[64,112,128]{2,1,0:T(8,128)(2,1)} %get-tuple-element.212.refs_3_), custom_call_target="tpu_custom_call" | custom-call | bytes 1200000 | tf_op jit(solution)/shard_map/reduce_row/pallas_call | solution.py:698
  534.0 11.9 %last.1 = (f32[2,2048,384]{2,1,0:T(8,128)}, f32[2,2048,384]{2,1,0:T(8,128)}, f32[2,384,2048]{2,1,0:T(8,128)}, f32[128,2048]{1,0:T(8,128)}, f32[128,2048]{1,0:T(8...) custom-call(s32[2]{0:T(128)} %pad_add_fusion.side, ...), custom_call_target="tpu_custom_call", output_to_operand_aliasing={{0}: (6, {}), {1}: (7, {}), {2}: (8, {})} | custom-call | bytes 10800000 | tf_op jit(solution)/shard_map/last/pallas_call | solution.py:1681
  545.9 4.9 psum.7
  550.9 0.5 slice_bitcast_fusion.1
  551.4 0.5 bitcast_divide_fusion
  551.9 1.2 slice_bitcast_fusion
  (24 shorter events, 0.2 us)
Async XLA Ops:
  42.0 9.0 %copy-start.6 = (f32[64,8,128]{2,1,0:T(8,128)S(1)}, f32[64,8,128]{2,1,0:T(8,128)}, u32[]{:S(2)}) copy-start(f32[64,8,128]{2,1,0:T(8,128)} %get-tuple-element.127) | copy-start | bytes 786436
  42.0 10.0 %copy-start.9 = (f32[128]{0:T(128)S(1)}, f32[128]{0:T(128)}, u32[]{:S(2)}) copy-start(f32[128]{0:T(128)} %param.27) | copy-start | bytes 1540
  42.0 10.0 %copy-start.10 = (f32[128]{0:T(128)S(1)}, f32[128]{0:T(128)}, u32[]{:S(2)}) copy-start(f32[128]{0:T(128)} %param.28) | copy-start | bytes 1540
  43.3 61.4 %all-to-all-start = ((bf16[64,32,384]{2,1,0:T(8,128)(2,1)}), bf16[64,32,384]{2,1,0:T(8,128)(2,1)S(1)}, u32[]{:S(2)}, u32[]{:S(2)}) async-start(bf16[64,32,384]{2,1,0:T(8,128)(2,1)} %bitcast.17), calls=%async_computation | async-start | bytes 3145728 | tf_op jit(solution)/shard_map/all_to_all | solution.py:2013
  104.7 1.2 copy-start
  105.9 84.6 %all-to-all-start.1 = ((bf16[32,24,2048]{2,1,0:T(8,128)(2,1)}), bf16[32,24,2048]{2,1,0:T(8,128)(2,1)}, u32[]{:S(2)}, u32[]{:S(2)}) async-start(bf16[32,24,2048]{2,1,0:T(8,128)(2,1)} %bitcast.72), calls=%async_computation.1 | async-start | bytes 6291456 | tf_op jit(solution)/shard_map/all_to_all | solution.py:917
  110.8 79.8 %collective-permute-start = (bf16[2048,384]{1,0:T(8,128)(2,1)}, bf16[2048,384]{1,0:T(8,128)(2,1)S(1)}, u32[]{:S(2)}, u32[]{:S(2)}) collective-permute-start(bf16[2048,384]{1,0:T(8,128)(2,1)} %get-tuple-element.146), channel_id=1, source_target_pairs={{0,1},{1,0},{2,3},{3,2},{4,5},{5,4},{6,7},{7,6},{8,9},{9,8},{10,11... | collective-permute-start | bytes 4718600 | tf_op jit(solution)/shard_map/ppermute | solution.py:1975
  184.7 5.9 %copy-start.8 = (bf16[384,2048]{1,0:T(8,128)(2,1)S(1)}, bf16[384,2048]{1,0:T(8,128)(2,1)}, u32[]{:S(2)}) copy-start(bf16[384,2048]{1,0:T(8,128)(2,1)} %get-tuple-element.158) | copy-start | bytes 4718596
  190.6 49.4 %copy-start.3 = (bf16[2048,384]{1,0:T(8,128)(2,1)}, bf16[2048,384]{1,0:T(8,128)(2,1)S(1)}, u32[]{:S(2)}) copy-start(bf16[2048,384]{1,0:T(8,128)(2,1)S(1)} %collective-permute-done.g_other) | copy-start | bytes 4718596
  190.6 49.4 %collective-permute-start.2 = (bf16[384,2048]{1,0:T(8,128)(2,1)S(1)}, bf16[384,2048]{1,0:T(8,128)(2,1)S(1)}, u32[]{:S(2)}, u32[]{:S(2)}) collective-permute-start(bf16[384,2048]{1,0:T(8,128)(2,1)S(1)} %copy-done.8), channel_id=1, source_target_pairs={{0,1},{1,0},{2,3},{3,2},{4,5},{5,4},{6,7},{7,6},{8,9},{9,8},{10,11... | collective-permute-start | bytes 4718600 | tf_op jit(solution)/shard_map/ppermute | solution.py:1975
  191.3 48.6 %collective-permute-start.1 = (bf16[768,384]{1,0:T(8,128)(2,1)}, bf16[768,384]{1,0:T(8,128)(2,1)S(1)}, u32[]{:S(2)}, u32[]{:S(2)}) collective-permute-start(bf16[768,384]{1,0:T(8,128)(2,1)} %get-tuple-element.157), channel_id=1, source_target_pairs={{0,1},{1,0},{2,3},{3,2},{4,5},{5,4},{6,7},{7,6},{8,9},{9,8},{10,11... | collective-permute-start | bytes 1769480 | tf_op jit(solution)/shard_map/ppermute | solution.py:1975
  240.0 0.8 copy-start.5
  240.0 1.3 copy-start.4
  267.9 53.8 %all-to-all-start.2 = ((bf16[32,24,2176]{2,1,0:T(8,128)(2,1)}), bf16[32,24,2176]{2,1,0:T(8,128)(2,1)S(1)}, u32[]{:S(2)}, u32[]{:S(2)}) async-start(bf16[32,24,2176]{2,1,0:T(8,128)(2,1)} %bitcast.70), calls=%async_computation.2 | async-start | bytes 6684672 | tf_op jit(solution)/shard_map/all_to_all | solution.py:917
  283.3 35.9 %collective-permute-start.3 = (bf16[2048,384]{1,0:T(8,128)(2,1)}, bf16[2048,384]{1,0:T(8,128)(2,1)}, u32[]{:S(2)}, u32[]{:S(2)}) collective-permute-start(bf16[2048,384]{1,0:T(8,128)(2,1)} %get-tuple-element.162), channel_id=1, source_target_pairs={{0,1},{1,0},{2,3},{3,2},{4,5},{5,4},{6,7},{7,6},{8,9},{9,8},{10,11... | collective-permute-start | bytes 4718600 | tf_op jit(solution)/shard_map/ppermute | solution.py:1975
  321.7 1.7 copy-start.1
  376.7 8.3 %copy-start.7 = (f32[32]{0:T(128)S(1)}, f32[32]{0:T(128)}, u32[]{:S(2)}) copy-start(f32[32]{0:T(128)} %param.26) | copy-start | bytes 388
  376.7 48.6 %all-to-all-start.3 = ((bf16[32,24,2048]{2,1,0:T(8,128)(2,1)}), bf16[32,24,2048]{2,1,0:T(8,128)(2,1)S(1)}, u32[]{:S(2)}, u32[]{:S(2)}) async-start(bf16[32,24,2048]{2,1,0:T(8,128)(2,1)} %bitcast.71), calls=%async_computation.3 | async-start | bytes 6291456 | tf_op jit(solution)/shard_map/all_to_all | solution.py:917
  382.8 35.6 %collective-permute-start.5 = (bf16[240,2048]{1,0:T(8,128)(2,1)}, bf16[240,2048]{1,0:T(8,128)(2,1)}, u32[]{:S(2)}, u32[]{:S(2)}) collective-permute-start(bf16[240,2048]{1,0:T(8,128)(2,1)} %get-tuple-element.188), channel_id=1, source_target_pairs={{0,1},{1,0},{2,3},{3,2},{4,5},{5,4},{6,7},{7,6},{8,9},{9,8},{10,11... | collective-permute-start | bytes 2949128 | tf_op jit(solution)/shard_map/ppermute | solution.py:1975
  383.4 35.1 %collective-permute-start.4 = (bf16[768,384]{1,0:T(8,128)(2,1)}, bf16[768,384]{1,0:T(8,128)(2,1)}, u32[]{:S(2)}, u32[]{:S(2)}) collective-permute-start(bf16[768,384]{1,0:T(8,128)(2,1)} %get-tuple-element.187), channel_id=1, source_target_pairs={{0,1},{1,0},{2,3},{3,2},{4,5},{5,4},{6,7},{7,6},{8,9},{9,8},{10,11... | collective-permute-start | bytes 1769480 | tf_op jit(solution)/shard_map/ppermute | solution.py:1975
  425.3 48.8 %copy-start.2 = (bf16[32,24,2048]{2,1,0:T(8,128)(2,1)}, bf16[32,24,2048]{2,1,0:T(8,128)(2,1)S(1)}, u32[]{:S(2)}) copy-start(bf16[32,24,2048]{2,1,0:T(8,128)(2,1)S(1)} %all-to-all-done.3) | copy-start | bytes 9437188

commit v7 on v6

--- a/solution.py
+++ b/solution.py
@@ -205,14 +205,14 @@
 DOWN_GRAD_CUT = (240, 144)
 
 
-def gather_first(weights, gains, tokens, routes, cotangent, expert_weights):
-    def body(q_in, k_in, v_in, ga_in, gf_in, t_in, r_in, c_in, *refs):
+def gather_first(weights, out_weight, router, gains, tokens, routes, cotangent, expert_weights):
+    def body(q_in, k_in, v_in, o_in, ro_in, ga_in, gf_in, t_in, r_in, c_in, *refs):
         sources, refs = refs[:3], refs[3:]
         w_out, t_out, s_out, r_out, c_out = refs[:5]
-        gate_out, up_out, up_rest, down_out, side_out = refs[5:10]
-        refs = refs[10:]
+        gate_out, up_out, up_rest, down_out, side_out, late_out = refs[5:11]
+        refs = refs[11:]
         wide, row_s, row_r, pair, local, col_s, col_r, tall_f, flat_f, tall_b, flat_b, in_sems, out_sems = refs[:13]
-        w_in, s_in = refs[13:]
+        w_in, s_in, late_in, late_sem = refs[13:]
         me, wsh = lax.axis_index("ctx"), lax.axis_index("wsh")
         core = lax.rem(me, 2)
         place = lax.rem(me, 8)
@@ -227,6 +227,8 @@
             side = (k_in, v_in)[at % 2]
             begin = at // 4 * HEAD_WIDTH
             w_in[at, :, heads:] = side[:, begin : begin + HEAD_WIDTH].astype(BF)
+            late_in[at, :, :heads] = o_in[:, at * heads : (at + 1) * heads].astype(BF)
+            late_in[at, :, heads:] = ro_in[...].astype(BF)
         s_in[...] = jnp.zeros_like(s_in)
         s_in[0:1, : ga_in.shape[1]] = ga_in[...]
         s_in[1:2, : gf_in.shape[1]] = gf_in[...]
@@ -239,6 +241,9 @@
         ]
         for copy in locals_:
             copy.start()
+        late_copies = [
+            pltpu.make_async_copy(late_in, late_out.at[pl.ds(at * 8, 8)], late_sem.at[at]) for at in range(8)
+        ]
         pl.semaphore_wait(barrier, amount)
         for peer in row_peers:
             remote(w_in.at[lax.rem(peer, 8)], w_out.at[me], wide.at[0], wide.at[1], peer, wsh).start()
@@ -276,6 +281,8 @@
                 col_copies.append(copy)
         shares = [share(group, 7)]
         onward, forwards = row_gather_onward(t_out, me, wsh, row_copies, row_s, row_r)
+        for copy in late_copies:
+            copy.start()
         gate_in, up_in, down_in = [source.at[1 - wsh] for source in sources]
         buffers = ((tall_f, flat_f), (tall_b, flat_b), in_sems, out_sems)
         tall_rows, flat_rows = tall_f.shape[1], flat_f.shape[1]
@@ -288,7 +295,7 @@
             col_copies[2 * at].wait_recv()
             col_copies[2 * at + 1].wait_recv()
             shares.append(share(lax.div(shifted(me, 4 - dz, 2 - dy, 0, 0), 8), at))
-        for copy in pair_copies + shares:
+        for copy in pair_copies + shares + late_copies:
             copy.wait()
         for copy in locals_[2:]:
             copy.wait()
@@ -309,9 +316,13 @@
             sds((2,) + cotangent.shape, cotangent.dtype),
         )
         + tuple(sds((count, half), BF) for count in (deep, *UP_CUT))
-        + (sds((half, deep), BF), sds((64, depth, 128), BF)),
-        in_specs=[VMEM] * 5 + [ANY] * 6,
-        out_specs=[ANY] * 10,
+        + (
+            sds((half, deep), BF),
+            sds((64, depth, 128), BF),
+            sds((64, depth, out_weight.shape[1] // 8 + router.shape[1]), BF),
+        ),
+        in_specs=[VMEM] * 7 + [ANY] * 6,
+        out_specs=[ANY] * 11,
         scratch_shapes=[
             DMA((4,)),
             DMA((9,)),
@@ -328,11 +339,13 @@
             DMA((2,)),
             pltpu.VMEM((8, depth, packed), BF),
             pltpu.VMEM((8, 128), F32),
+            pltpu.VMEM((8, depth, out_weight.shape[1] // 8 + router.shape[1]), BF),
+            DMA((8,)),
         ],
         compiler_params=call_params(0),
         name="gather_first",
         cost_estimate=cost(40),
-    )(*weights, *gains, tokens, routes, cotangent, *expert_weights)
+    )(*weights, out_weight, router, *gains, tokens, routes, cotangent, *expert_weights)
 
 
 def gather_row(block, swapped, collective_id):
@@ -367,11 +380,13 @@
     )(block, swapped)
 
 
-def gather_keys(rows, collective_id):
+def gather_keys(rows, routes, cotangent, experts, collective_id):
+    chip_rows, deep = cotangent.shape
+    slots = experts // 4 * 2 * CAP
     count = rows.shape[0]
     half = count // 2
 
-    def body(src, out, send, recv, local):
+    def body(src, routes_ref, cot_ref, out, pick_ref, turned_ref, of_ref, hits_ref, rows_out, send, recv, local, rows_ref, rows_sem):
         me, wsh = lax.axis_index("ctx"), lax.axis_index("wsh")
         core = lax.rem(me, 2)
         group = lax.div(me, 8)
@@ -405,6 +420,9 @@
             copy.start()
             copies.append(copy)
         hand_on(beside, 0)
+        route_rows((core, wsh, lax.rem(group, 2)), routes_ref, cot_ref, pick_ref, turned_ref, of_ref, hits_ref, rows_ref)
+        rows_copy = pltpu.make_async_copy(rows_ref, rows_out, rows_sem)
+        rows_copy.start()
         for dy in range(2):
             for at, dz in enumerate(steps):
                 copies[1 + 3 * dy + at].wait_recv()
@@ -414,17 +432,44 @@
         for forward in forwards:
             forward.wait()
         mine.wait()
-
+        rows_copy.wait()
+
+    sds = jax.ShapeDtypeStruct
     return pl.pallas_call(
         body,
-        out_shape=jax.ShapeDtypeStruct((8,) + rows.shape, rows.dtype),
-        in_specs=[ANY],
-        out_specs=ANY,
-        scratch_shapes=[DMA((14,)), DMA((14,)), DMA],
+        out_shape=(
+            sds((8,) + rows.shape, rows.dtype),
+            sds((slots, chip_rows), BF),
+            sds((chip_rows, slots), BF),
+            sds((slots, experts), BF),
+            sds((chip_rows, experts), F32),
+            sds((slots, deep), BF),
+        ),
+        in_specs=[ANY, VMEM, VMEM],
+        out_specs=[ANY, VMEM, VMEM, VMEM, VMEM, ANY],
+        scratch_shapes=[DMA((14,)), DMA((14,)), DMA, pltpu.VMEM((slots, deep), BF), DMA],
         compiler_params=call_params(collective_id),
         name="gather_keys",
         cost_estimate=cost(30),
-    )(rows)
+    )(rows, routes, cotangent)
+
+
+class Staged:
+    def __init__(self, sources, buffers, sems):
+        self.copies = [
+            pltpu.make_async_copy(src, buffer, sems.at[at])
+            for at, (src, buffer) in enumerate(zip(sources, buffers))
+        ]
+        for copy in self.copies:
+            copy.start()
+
+    def ready(self, *which):
+        for at in which:
+            self.copies[at].wait()
+
+    @staticmethod
+    def scratch(values):
+        return [pltpu.VMEM(value.shape, value.dtype) for value in values] + [DMA((len(values),))]
 
 
 class Owned:
@@ -525,15 +570,21 @@
 
     def body(*refs):
         refs = list(refs)
+        stage_sems = refs.pop(-1)
+        buffers = [refs.pop(-1) for _ in staged_values][::-1]
+        sources = [refs.pop(0) for _ in staged_values[: len(staged_values) - len(owned)]]
+        held = list(buffers)
         if is_product:
-            heads_ref, out_w = refs.pop(0), refs.pop(0)
+            heads_ref, out_w = held.pop(0), held.pop(0)
             src = refs.pop(-1)
         else:
-            src = refs.pop(0)
+            src = held.pop(0)
         if has_extra:
-            pick_ref, back_ref = refs.pop(0), refs.pop(0)
+            pick_ref, back_ref = held.pop(0), held.pop(0)
         src3 = refs.pop(0) if has_whole else None
-        mine_in = [refs.pop(0) for _ in owned]
+        sources += [refs.pop(0) for _ in owned]
+        mine_in = held
+        staged = Staged(sources, buffers, stage_sems)
         out = refs.pop(0)
         out2 = refs.pop(0) if has_extra else None
         out3 = refs.pop(0) if has_whole else None
@@ -554,6 +605,7 @@
         greeted = row_peers + col_peers if owned else peers + [partner]
         barrier, amount = greet([(peer, wsh) for peer in greeted] + [(me, other)])
         pl.semaphore_wait(barrier, amount)
+        staged.ready(*range(2 if is_product else 1))
         if has_whole:
             whole = remote(
                 src3, out3, send.at[1, 9], recv.at[1, 9], me, other
@@ -582,9 +634,11 @@
                 )
                 copy.start()
                 first.append(copy)
+        staged.ready(*range(len(staged_values) - len(owned), len(staged_values)))
         for block4 in blocks:
             block4.along_z(me, wsh)
         if has_extra:
+            staged.ready(1, 2)
             arrived2, swapped2, src2 = refs[8:]
             src2[...] = matmul(pick_ref[...], back_ref[...]).astype(BF).reshape(src2.shape)
             give2 = remote(src2.at[1 - core], arrived2, send.at[0, 8], recv.at[0, 8], partner, wsh)
@@ -680,7 +734,8 @@
         scratch += [pltpu.VMEM(block, BF), pltpu.VMEM((2,) + block, BF), pltpu.VMEM((2,) + block, BF)]
         operands += list(extra)
         out_spaces.append(VMEM)
-    spaces = [VMEM] * len(operands)
+    spaces = [ANY] * len(operands)
+    staged_values = list(operands) + list(owned)
     if has_whole:
         shapes.append(jax.ShapeDtypeStruct(swapped_whole.shape, swapped_whole.dtype))
         operands.append(swapped_whole)
@@ -690,11 +745,12 @@
         block8 = (8,) + value.shape[1:]
         shapes.append(jax.ShapeDtypeStruct(block8, BF))
         operands.append(value)
-        spaces.append(VMEM)
+        spaces.append(ANY)
         out_spaces.append(VMEM)
         scratch += Owned.scratch(value)
     if is_product:
         scratch.append(pltpu.VMEM((8,) + block, BF))
+    scratch += Staged.scratch(staged_values)
     return pl.pallas_call(
         body,
         out_shape=shapes,
@@ -711,12 +767,14 @@
     rows = pick.shape[0] // 2
     lanes = of_expert.shape[1]
 
-    def body(pick_ref, back_ref, of_ref, out, out2, src, src2, arrived, swapped, arrived2, swapped2, send, recv):
+    def body(pick_in, back_in, of_in, out, out2, src, src2, arrived, swapped, arrived2, swapped2, send, recv, pick_ref, back_ref, of_ref, sems):
+        staged = Staged((pick_in, back_in, of_in), (pick_ref, back_ref, of_ref), sems)
         me, wsh = lax.axis_index("ctx"), lax.axis_index("wsh")
         other = 1 - wsh
         core = lax.rem(me, 2)
         partner = shifted(me, 0, 0, 0, 1)
         barrier, amount = greet([(partner, wsh), (me, other)])
+        staged.ready(0, 1, 2)
         src[...] = matmul(pick_ref[...], back_ref[:, :width]).astype(BF).reshape(src.shape)
         parts = [back_ref[:, at : at + 1] * of_ref[...] for at in (width, width + 64)]
         src2[...] = (matmul(pick_ref[...], parts[0]) + matmul(pick_ref[...], parts[1])).reshape(src2.shape)
@@ -743,7 +801,7 @@
     return pl.pallas_call(
         body,
         out_shape=(sds(block, F32), sds(block2, F32)),
-        in_specs=[VMEM] * 3,
+        in_specs=[ANY] * 3,
         out_specs=[VMEM] * 2,
         scratch_shapes=[
             pltpu.VMEM((2,) + block, BF),
@@ -754,7 +812,8 @@
             pltpu.VMEM((2,) + block2, F32),
             DMA((4,)),
             DMA((4,)),
-        ],
+        ]
+        + Staged.scratch((pick, back, of_expert)),
         compiler_params=call_params(collective_id),
         name="reduce_chip",
         cost_estimate=cost(17),
@@ -764,8 +823,10 @@
 def reduce_keys(parts, owned, swapped, collective_id):
     _, groups, _, rows, width = parts.shape
 
-    def body(src, src4, src5, out, out4, out5, arrived, mid, beside, summed, landed, send, recv, pair, *scratch4):
-        block4 = Owned(src4, out4, scratch4)
+    def body(src_in, src4_in, src5, out, out4, out5, arrived, mid, beside, summed, landed, send, recv, pair, *scratch4):
+        src, src4, sems = scratch4[-3:]
+        staged = Staged((src_in, src4_in), (src, src4), sems)
+        block4 = Owned(src4, out4, scratch4[:-3])
         me, wsh = lax.axis_index("ctx"), lax.axis_index("wsh")
         core = lax.rem(me, 2)
         _, _, x, _ = coords(me)
@@ -777,6 +838,7 @@
         row_peers = [shifted(me, 0, 0, dx, dk) for dx, dk in ROW_STEPS]
         barrier, amount = greet([(peer, wsh) for peer in peers[:-1] + row_peers] + [(me, 1 - wsh)])
         pl.semaphore_wait(barrier, amount)
+        staged.ready(0, 1)
         first = []
         for at, peer in enumerate(peers):
             group = lax.div(peer, 8)
@@ -838,7 +900,7 @@
             jax.ShapeDtypeStruct((8,) + owned.shape[1:], BF),
             jax.ShapeDtypeStruct(swapped.shape, swapped.dtype),
         ),
-        in_specs=[VMEM, VMEM, ANY],
+        in_specs=[ANY, ANY, ANY],
         out_specs=[VMEM, VMEM, ANY],
         scratch_shapes=[
             pltpu.VMEM((2, groups) + block, BF),
@@ -850,7 +912,8 @@
             DMA((4, groups)),
             DMA((2,)),
         ]
-        + Owned.scratch(owned),
+        + Owned.scratch(owned)
+        + Staged.scratch((parts, owned)),
         compiler_params=call_params(collective_id),
         name="reduce_keys",
         cost_estimate=cost(40),
@@ -1079,14 +1142,18 @@
     )(block_order, lengths, group, queries, kv)
 
 
-def backward_kernel(plan, lengths, q_ref, heads_ref, da_ref, wo_ref, kv_ref, lse_ref, part_ref, dq_ref, dkv_ref, early_ref, keys, values, keys_t, d_keys, d_values, acc):
+def backward_kernel(plan, lengths, q_ref, heads_ref, da_in, wo_ref, kv_ref, lse_ref, part_ref, dq_ref, dkv_out, early_ref, keys, values, keys_t, d_keys, d_values, acc, da_ref, dkv_ref, sems):
     step = pl.program_id(0)
+    load = pltpu.make_async_copy(da_in, da_ref, sems.at[0])
+    store = pltpu.make_async_copy(dkv_ref, dkv_out, sems.at[1])
 
     @pl.when(step == 0)
     def _():
+        load.start()
         natural_order(plan, kv_ref, keys, values, (keys, keys_t))
         d_keys[...] = jnp.zeros_like(d_keys)
         d_values[...] = jnp.zeros_like(d_values)
+        load.wait()
 
     first, second = plan[2 * step], plan[2 * step + 1]
     q = stacked(q_ref, first, second)
@@ -1142,6 +1209,7 @@
             return carried
 
         lax.fori_loop(0, kv_ref.shape[0] // BLK, one, 0, unroll=4)
+        store.start()
         owners = early_ref.shape[0]
         depth = da_ref.shape[1] // owners
         span = 256
@@ -1155,6 +1223,7 @@
                     .reshape(span // depth, depth, HEAD_WIDTH)
                 )
         early_ref[:, 2 * depth :, :] = part_ref[...]
+        store.wait()
 
 
 def attend_back(plan, lengths, queries, heads, d_attn, wo_t, kv, lse, part):
@@ -1176,7 +1245,7 @@
             in_specs=[
                 everything,
                 everything,
-                pl.BlockSpec(d_attn.shape, lambda i, *_: (0, 0)),
+                ANY,
                 pl.BlockSpec((wo_t.shape[0], queries.shape[1]), lambda i, *_: (0, 0)),
                 pl.BlockSpec(kv.shape, lambda i, *_: (0, 0)),
                 strip,
@@ -1184,7 +1253,7 @@
             ],
             out_specs=[
                 everything,
-                pl.BlockSpec(dkv_shape, lambda i, *_: (0, 0, 0, 0, 0)),
+                ANY,
                 pl.BlockSpec(early_shape, lambda i, *_: (0, 0, 0)),
             ],
             scratch_shapes=[
@@ -1194,6 +1263,9 @@
                 pltpu.VMEM((total, HEAD_WIDTH), F32),
                 pltpu.VMEM((total, HEAD_WIDTH), F32),
                 pltpu.VMEM((HEAD_WIDTH, 4 * BLK), F32),
+                pltpu.VMEM(d_attn.shape, BF),
+                pltpu.VMEM(dkv_shape, BF),
+                DMA((2,)),
             ],
         ),
         compiler_params=pltpu.CompilerParams(vmem_limit_bytes=ROOM),
@@ -1424,7 +1496,7 @@
     )(side, rows_in, d_pairs, activated, d_up)
 
 
-def route_kernel(where, routes_ref, cot_ref, pick_ref, turned_ref, of_ref, hits_ref, rows_ref):
+def route_rows(where, routes_ref, cot_ref, pick_ref, turned_ref, of_ref, hits_ref, rows_ref):
     slots, rows = pick_ref.shape[0], routes_ref.shape[2]
     experts = of_ref.shape[1]
     slot = lax.broadcasted_iota(jnp.int32, (slots, experts), 0)
@@ -1455,27 +1527,6 @@
     rows_ref[...] = matmul(pick_low, cot_ref[...]).astype(BF)
 
 
-def route(where, routes, cotangent, experts):
-    rows, width = cotangent.shape
-    slots = experts // 4 * 2 * CAP
-    sds = jax.ShapeDtypeStruct
-    return pl.pallas_call(
-        route_kernel,
-        out_shape=(
-            sds((slots, rows), BF),
-            sds((rows, slots), BF),
-            sds((slots, experts), BF),
-            sds((rows, experts), F32),
-            sds((slots, width), BF),
-        ),
-        in_specs=[pl.BlockSpec(memory_space=pltpu.SMEM), VMEM, VMEM],
-        out_specs=[VMEM] * 5,
-        compiler_params=pltpu.CompilerParams(vmem_limit_bytes=ROOM),
-        name="route",
-        cost_estimate=cost(5),
-    )(where, routes, cotangent)
-
-
 def middle_kernel(chip, t_ref, attn_ref, gain_ref, wr_ref, hits_ref, pick_ref, of_ref, res_ref, h_ref, inv_ref, gates_ref, rows_ref, tile_ref):
     residual = t_ref[...].astype(F32) + attn_ref[...]
     res_ref[...] = residual
@@ -1614,8 +1665,7 @@
     step = pl.program_id(0)
     g_out[0] = g_in[...].astype(F32)
     u_out[0] = jnp.where(step < UP_CUT[0] // u_in.shape[0], u_in[...], u_rest[...]).astype(F32)
-    d_out[0, : d_in.shape[0]] = d_in[...].astype(F32)
-    d_out[0, d_in.shape[0] :] = d_rest[...].astype(F32)
+    d_out[0] = jnp.where(step < DOWN_GRAD_CUT[0] // d_in.shape[0], d_in[...], d_rest[...]).astype(F32)
     rows = t_ref[...].astype(F32)
     out_ref[...] = res_ref[...] + moe_ref[...]
     inverse = lax.rsqrt(jnp.mean(rows * rows, axis=1, keepdims=True) + EPSILON)
@@ -1672,7 +1722,9 @@
 
     first = UP_CUT[0] // tile
     rows_out = pl.BlockSpec((1, tile, half), lambda i, side: (1 - side[0], i, 0))
-    columns_out = pl.BlockSpec((1, half, tile), lambda i, side: (1 - side[0], 0, i))
+    short = half // steps
+    short_first = DOWN_GRAD_CUT[0] // short
+    short_out = pl.BlockSpec((1, short, width), lambda i, side: (1 - side[0], i, 0))
     strips = pl.BlockSpec((strip, width), lambda i, side: (i, 0))
     mine = pl.BlockSpec((strip, width), lambda i, side: (side[1] * steps + i, 0))
     place = pl.BlockSpec((1,) + late.shape[1:], lambda i, side: (i, 0, 0))
@@ -1699,8 +1751,8 @@
                 pl.BlockSpec((tile, half), lambda i, side: (i, 0)),
                 pl.BlockSpec((tile, half), lambda i, side: (jnp.minimum(i, first - 1), 0)),
                 pl.BlockSpec((tile, half), lambda i, side: (jnp.maximum(i - first, 0), 0)),
-                pl.BlockSpec((DOWN_GRAD_CUT[0], tile), lambda i, side: (0, i)),
-                pl.BlockSpec((DOWN_GRAD_CUT[1], tile), lambda i, side: (0, i)),
+                pl.BlockSpec((short, width), lambda i, side: (jnp.minimum(i, short_first - 1), 0)),
+                pl.BlockSpec((short, width), lambda i, side: (jnp.maximum(i - short_first, 0), 0)),
             ]
             + [ANY] * 3
             + [
@@ -1719,7 +1771,7 @@
             out_specs=[
                 rows_out,
                 rows_out,
-                columns_out,
+                short_out,
                 strips,
                 strips,
                 query,
@@ -1986,8 +2038,11 @@
         other_up,
         other_down,
         w_side,
+        late_pack,
     ) = gather_first(
         (w_query, key_weight, value_weight),
+        w_out.T,
+        w_router,
         (gain_attn[None, :], gain_ffn[None, :]),
         tokens,
         routes.T,
@@ -2006,18 +2061,10 @@
     g_query = rounded(gain_query)
     g_key = rounded(gain_key)
 
-    o_part = to_low(w_out).T.reshape(depth, 8, 256).transpose(1, 0, 2)
-    r_part = jnp.broadcast_to(to_low(w_router)[None], (8, depth, experts))
-    late_pack = jnp.tile(jnp.concatenate([o_part, r_part], axis=2), (8, 1, 1))
-    late_pack, small_all = after(late_pack, small_all)
     late_all = lax.all_to_all(late_pack, "ctx", split_axis=0, concat_axis=0, tiled=True).reshape(width, 384)
 
     chips = experts // 4
     slots = 2 * CAP
-    y_half = lax.rem(lax.div(me, 8), 2)
-    pick_low, pick_turned, of_expert, hits, cot_rows = route(
-        jnp.stack([core, wsh, y_half]), chip_routes, chip_cot.reshape(2 * rows, width), experts
-    )
 
     half_dim = HEAD_WIDTH // 2
     frequency = jnp.power(ROPE_BASE, -2.0 * jnp.arange(half_dim, dtype=jnp.float32) / HEAD_WIDTH)
@@ -2036,7 +2083,10 @@
         g_query[None, :],
         g_key[None, :],
     )
-    kv_all = gather_keys(kv, 1).reshape(block_count * BLK, 256)
+    kv_all, pick_low, pick_turned, of_expert, hits, cot_rows = gather_keys(
+        kv, chip_routes, chip_cot.reshape(2 * rows, width), experts, 1
+    )
+    kv_all = kv_all.reshape(block_count * BLK, 256)
     late_all, kv_all = after(late_all, kv_all)
     (cot_rows, other_gate), kv_all = after((cot_rows, other_gate), kv_all)
     gate_back = swap(other_gate)

time: 563 us -> 548 us (0.973)
  Pallas kernels: 460 us -> 450 us
    pallas_call x2 -> x1, Pallas kernels: 39.2 us -> 36 us  [gather_keys(): pl.pallas_call(body, out_shape=(sds((8,) + rows.shape, rows.dtype), sds((...]
where the time goes in v7:
time: 548 us; the launch traced here: 542 us
  Pallas kernels  450 us (82%)
  waiting for transfers between devices  42.1 us (8%)
  starting transfers between devices  32.7 us (6%)
  local copies, waits for them, and re-layouts  8.31 us (2%)
    pallas_call x2, Pallas kernels, reduce_row(): pl.pallas_call(body, out_shape=shapes, in_specs=spaces, out_specs=out_spa...  105 us
    pallas_call x1, Pallas kernels, exchange(): pl.pallas_call(body, out_shape=[jax.ShapeDtypeStruct(a.shape, a.dtype) fo...  46.5 us
    pallas_call x1, Pallas kernels, reduce_keys(): pl.pallas_call(body, out_shape=(jax.ShapeDtypeStruct(block, F32), jax.Sha...  46 us
    pallas_call x1, Pallas kernels, gather_first(): pl.pallas_call(body, out_shape=(sds((64, depth, packed), BF), sds((8,) +...  40.2 us
    pallas_call x1, Pallas kernels, gather_keys(): pl.pallas_call(body, out_shape=(sds((8,) + rows.shape, rows.dtype), sds((...  36 us
    ppermute x6, waiting for transfers between devices, swap(): return lax.ppermute(value, 'wsh', [(0, 1), (1, 0)])  33.1 us
    pallas_call x1, Pallas kernels, gather_row(): pl.pallas_call(body, out_shape=(jax.ShapeDtypeStruct((8,) + block.shape,...  29.3 us
    pallas_call x1, Pallas kernels, run_expert(): pl.pallas_call(expert_kernel, out_shape=(sds((count, width), BF), sds((co...  26.7 us
  transfers between devices with their start and end apart: 10, of which 5 were waited for; matrix products, arithmetic and copies ran while one was open for 1% of the time, Pallas kernels for 40%

profile of v7, /device:TPU:0, one launch (start us, length us, event | category | flops | bytes accessed | tf_op | source)
XLA Modules:
  0.0 541.6 jit_solution(12101577683068420191)
XLA Ops:
  0.6 40.2 %gather_first.1 = (bf16[64,32,384]{2,1,0:T(8,128)(2,1)}, bf16[8,128,2048]{2,1,0:T(8,128)(2,1)}, f32[64,8,128]{2,1,0:T(8,128)}, s32[2,8,128]{2,1,0:T(8,128)}, bf1...) custom-call(f32[32,2048]{1,0:T(8,128)} %refs_11_.1, ...), custom_call_target="tpu_custom_call" | custom-call | bytes 48000000 | tf_op jit(solution)/shard_map/gather_first/pallas_call | solution.py:309
  40.9 0.0 copy-start.5
  40.9 0.0 copy-start.8
  40.9 0.0 copy-start.9
  40.9 7.2 %all-to-all-start = ((bf16[64,32,384]{2,1,0:T(8,128)(2,1)}), bf16[64,32,384]{2,1,0:T(8,128)(2,1)S(1)}, u32[]{:S(2)}, u32[]{:S(2)}) async-start(bf16[64,32,384]{2,1,0:T(8,128)(2,1)} %get-tuple-element.135), calls=%async_computation | async-start | bytes 3145728 | tf_op jit(solution)/shard_map/all_to_all | solution.py:2064
  48.2 0.0 copy-done.5
  48.2 0.2 fusion
  48.4 0.7 reshape.155.ga_ref.refs_8_
  49.1 0.0 copy-done.8
  49.1 0.0 copy-done.9
  49.1 0.6 maximum_bitcast_fusion.freq_ref
  49.7 0.6 bitcast_convert_fusion
  50.3 0.6 broadcast_in_dim.20.flag_ref
  50.9 11.2 %project.1 = (bf16[1024,2048]{1,0:T(8,128)(2,1)}, bf16[1024,256]{1,0:T(8,128)(2,1)}, bf16[1024,256]{1,0:T(8,128)(2,1)}, f32[1024,256]{1,0:T(8,128)}, f32[1024,12...) custom-call(s32[128]{0:T(128)} %block_order.3, s32[4]{0:T(128)} %lengths.5, s32[1]{0:T(128)} %bitcast.8.group, ...), custom_call_target="tpu_custom_call" | custom-call | bytes 9600000 | tf_op jit(solution)/shard_map/project/pallas_call | solution.py:1849
  62.0 36.0 %gather_keys.1 = (bf16[8,1024,256]{2,1,0:T(8,128)(2,1)}, bf16[768,256]{1,0:T(8,128)(2,1)}, bf16[256,768]{1,0:T(8,128)(2,1)}, bf16[768,128]{1,0:T(8,128)(2,1)}, f...) custom-call(bf16[1024,256]{1,0:T(8,128)(2,1)} %get-tuple-element.130.src, s32[2,8,128]{2,1,0:T(8,128)} %get-tuple-element.131.routes_ref, ...), custom_call_target="tpu_custom_call" | custom-call | bytes 36000000 | tf_op jit(solution)/shard_map/gather_keys/pallas_call | solution.py:438
  98.0 0.0 all-to-all-done
  98.0 0.0 copy-start
  98.0 0.0 copy-start.7
  98.0 1.1 copy-done
  99.2 4.9 all-to-all-start.1
  104.1 0.8 collective-permute-start
  105.0 0.7 reshape.158.gain_ref
  105.6 12.2 %attend.1 = (bf16[1024,256]{1,0:T(8,128)(2,1)}, f32[8,1,256]{2,1,0:T(1,128)}, s32[256]{0:T(256)}) custom-call(s32[128]{0:T(128)} %block_order.3, s32[4]{0:T(128)} %lengths.5, s32[1]{0:T(128)} %bitcast.8.group, bf16[1024,256]{1,0:T(8,128)(2,1)} %get-tuple-element.129.q_ref, bf16[8192,256]{1,0:T(8,128)(2,1)} %bitcast.56), custom_call_target="tpu_custom_call" | custom-call | bytes 20400000 | tf_op jit(solution)/shard_map/attend/pallas_call | solution.py:1120
  117.8 59.9 %reduce_row.2 = (f32[2,128,2048]{2,1,0:T(8,128)}, bf16[1280,384]{1,0:T(8,128)(2,1)}) custom-call(bf16[1024,256]{1,0:T(8,128)(2,1)} %get-tuple-element.140.refs_0_.heads_ref, bf16[2048,384]{1,0:T(8,128)(2,1)} %bitcast.47, bf16[1280,384]{1,0:T(8,128)(2,1)} %get-tuple-element.142.refs_2_), custom_call_target="tpu_custom_call" | custom-call | bytes 1200000 | tf_op jit(solution)/shard_map/reduce_row/pallas_call | solution.py:754
  177.8 5.8 %middle.1 = (f32[256,2048]{1,0:T(8,128)}, bf16[256,2048]{1,0:T(8,128)(2,1)}, f32[256,128]{1,0:T(8,128)}, f32[256,128]{1,0:T(8,128)}, bf16[768,2048]{1,0:T(8,128)(2,1)}, /*index=5*/bf16[768,128]{1,0:T(8,128)(2,1)}) custom-call(s32[1]{0:T(128)} %bitcast.2.chip, bf16[1024,2048]{1,0:T(8,128)(2,1)} %bitcast.55, f32[256,2048]{1,0:T(8,128)} %bitcast.68, ...), custom_call_target="tpu_custom_call" | custom-call | bytes 1200000 | tf_op jit(solution)/shard_map/middle/pallas_call | solution.py:1572
  183.5 0.0 collective-permute-done.g_other
  183.5 0.0 all-to-all-done.1
  183.5 0.8 collective-permute-start.2
  184.3 1.5 collective-permute-start.1
  185.8 46.5 %exchange.1 = (bf16[32,24,2048]{2,1,0:T(8,128)(2,1)}, bf16[32,24,128]{2,1,0:T(8,128)(2,1)}) custom-call(bf16[32,24,2048]{2,1,0:T(8,128)(2,1)} %bitcast.67, bf16[32,24,128]{2,1,0:T(8,128)(2,1)} %bitcast.74), custom_call_target="tpu_custom_call" | custom-call | bytes 57600000 | tf_op jit(solution)/shard_map/exchange/pallas_call | solution.py:961
  232.3 0.9 collective-permute-done.1.u_rest
  233.2 0.0 collective-permute-done.2.d_other
  233.2 0.0 copy-done.3
  233.3 1.1 copy-done.4
  234.4 26.7 %run_expert.1 = (bf16[768,2048]{1,0:T(8,128)(2,1)}, bf16[768,2176]{1,0:T(8,128)(2,1)}, bf16[768,768]{1,0:T(8,128)(2,1)}, bf16[768,768]{1,0:T(8,128)(2,1)}, bf16[...) custom-call(s32[1]{0:T(128)} %bitcast.side, bf16[768,2048]{1,0:T(8,128)(2,1)} %bitcast.51, ...), custom_call_target="tpu_custom_call" | custom-call | bytes 30000000 | tf_op jit(solution)/shard_map/run_expert/pallas_call | solution.py:1360
  261.0 9.2 %all-to-all-start.2 = ((bf16[32,24,2176]{2,1,0:T(8,128)(2,1)}), bf16[32,24,2176]{2,1,0:T(8,128)(2,1)S(1)}, u32[]{:S(2)}, u32[]{:S(2)}) async-start(bf16[32,24,2176]{2,1,0:T(8,128)(2,1)} %bitcast.64), calls=%async_computation.2 | async-start | bytes 6684672 | tf_op jit(solution)/shard_map/all_to_all | solution.py:980
  270.2 6.2 %gate_grads.1 = (f32[2,2048,384]{2,1,0:T(8,128)}, bf16[2048,384]{1,0:T(8,128)(2,1)}) custom-call(s32[1]{0:T(128)} %bitcast.side, bf16[768,2048]{1,0:T(8,128)(2,1)} %bitcast.52, bf16[768,768]{1,0:T(8,128)(2,1)} %get-tuple-element.162.dg_ref), custom_call_target="tpu_custom_call" | custom-call | bytes 6000000 | tf_op jit(solution)/shard_map/gate_grads/pallas_call | solution.py:1411
  276.4 0.0 collective-permute-start.3
  276.4 13.6 %expert_grads.1 = (f32[2,2048,384]{2,1,0:T(8,128)}, f32[2,384,2048]{2,1,0:T(8,128)}, bf16[1280,384]{1,0:T(8,128)(2,1)}, bf16[768,384]{1,0:T(8,128)(2,1)}, bf16[2...) custom-call(s32[1]{0:T(128)} %bitcast.side, bf16[768,2048]{1,0:T(8,128)(2,1)} %bitcast.53, ...), custom_call_target="tpu_custom_call" | custom-call | bytes 12000000 | tf_op jit(solution)/shard_map/expert_grads/pallas_call | solution.py:1469
  290.0 22.3 %collective-permute-done.3.g_in = bf16[2048,384]{1,0:T(8,128)(2,1)} collective-permute-done((bf16[2048,384]{1,0:T(8,128)(2,1)}, bf16[2048,384]{1,0:T(8,128)(2,1)}, u32[]{:S(2)}, u32[]{:S(2)}) %collective-permute-start.3) | collective-permute-done | bytes 1572896 | tf_op jit(solution)/shard_map/ppermute | solution.py:2027
  312.3 2.5 all-to-all-done.2
  314.8 1.7 copy-done.1
  316.5 19.5 %reduce_chip.1 = (f32[128,2048]{1,0:T(8,128)}, f32[128,128]{1,0:T(8,128)}) custom-call(bf16[256,768]{1,0:T(8,128)(2,1)} %get-tuple-element.173.pick_in.refs_1_, bf16[768,2176]{1,0:T(8,128)(2,1)} %bitcast.58, bf16[768,128]{1,0:T(8,128)(2,1)} %get-tuple-element.146.of_ref.of_in), custom_call_target="tpu_custom_call" | custom-call | bytes 20400000 | tf_op jit(solution)/shard_map/reduce_chip/pallas_call | solution.py:801
  336.0 4.4 turn.1
  340.4 29.3 %gather_row.1 = (bf16[8,128,2048]{2,1,0:T(8,128)(2,1)}, bf16[1280,384]{1,0:T(8,128)(2,1)}) custom-call(bf16[128,2048]{1,0:T(8,128)(2,1)} %get-tuple-element.181.src, bf16[1280,384]{1,0:T(8,128)(2,1)} %get-tuple-element.182.src2), custom_call_target="tpu_custom_call" | custom-call | bytes 31200000 | tf_op jit(solution)/shard_map/gather_row/pallas_call | solution.py:368
  369.7 0.0 copy-start.6
  369.8 6.1 %all-to-all-start.3 = ((bf16[32,24,2048]{2,1,0:T(8,128)(2,1)}), bf16[32,24,2048]{2,1,0:T(8,128)(2,1)S(1)}, u32[]{:S(2)}, u32[]{:S(2)}) async-start(bf16[32,24,2048]{2,1,0:T(8,128)(2,1)} %bitcast.65), calls=%async_computation.3 | async-start | bytes 6291456 | tf_op jit(solution)/shard_map/all_to_all | solution.py:980
  375.9 0.3 collective-permute-start.5
  376.2 1.8 collective-permute-start.4
  378.0 0.6 pad_add_fusion.side
  378.6 0.1 maximum_maximum_fusion
  378.7 22.7 %attend_back.1 = (f32[1024,256]{1,0:T(8,128)}, bf16[2,8,2,512,128]{4,3,2,1,0:T(8,128)(2,1)}, bf16[64,112,128]{2,1,0:T(8,128)(2,1)}) custom-call(s32[256]{0:T(256)} %get-tuple-element.191.plan, s32[4]{0:T(128)} %lengths.5, bf16[1024,256]{1,0:T(8,128)(2,1)} %get-tuple-element.129.q_ref, bf16[1024,256]{1,0:T(8,128)(2,1)} %get-tuple-element.140.refs_0_.heads_ref, ...), custom_call_target="tpu_custom_call" | custom-call | bytes 28800000 | tf_op jit(solution)/shard_map/attend_back/pallas_call | solution.py:1239
  401.4 9.9 %collective-permute-done.4.u_rest = bf16[768,384]{1,0:T(8,128)(2,1)} collective-permute-done((bf16[768,384]{1,0:T(8,128)(2,1)}, bf16[768,384]{1,0:T(8,128)(2,1)}, u32[]{:S(2)}, u32[]{:S(2)}) %collective-permute-start.4) | collective-permute-done | bytes 589856 | tf_op jit(solution)/shard_map/ppermute | solution.py:2027
  411.3 0.0 collective-permute-done.5.d_in
  411.3 6.5 %all-to-all-done.3 = bf16[32,24,2048]{2,1,0:T(8,128)(2,1)S(1)} async-done(((bf16[32,24,2048]{2,1,0:T(8,128)(2,1)}), bf16[32,24,2048]{2,1,0:T(8,128)(2,1)S(1)}, u32[]{:S(2)}, u32[]{:S(2)}) %all-to-all-start.3) | async-done | bytes 3145760 | tf_op jit(solution)/shard_map/all_to_all | solution.py:980
  417.8 46.0 %reduce_keys.1 = (f32[512,128]{1,0:T(8,128)}, bf16[8,112,128]{2,1,0:T(8,128)(2,1)}, bf16[144,2048]{1,0:T(8,128)(2,1)}) custom-call(bf16[2,8,2,512,128]{4,3,2,1,0:T(8,128)(2,1)} %get-tuple-element.198.src_in, bf16[64,112,128]{2,1,0:T(8,128)(2,1)} %get-tuple-element.199.src4_in, bf16[144,2048]{1,0:T(8,128)(2,1)} %get-tuple-element.200.src5), custom_call_target="tpu_custom_call" | custom-call | bytes 48000000 | tf_op jit(solution)/shard_map/reduce_keys/pallas_call | solution.py:896
  463.8 0.7 broadcast.25.flag_ref
  464.4 12.3 %project_back.1 = (bf16[1024,2048]{1,0:T(8,128)(2,1)}, bf16[64,112,128]{2,1,0:T(8,128)(2,1)}) custom-call(f32[1024,256]{1,0:T(8,128)} %get-tuple-element.205.dq_ref, f32[512,128]{1,0:T(8,128)} %get-tuple-element.206.ds_ref, f32[1024,256]{1,0:T(8,128)} %get-tuple-element.207.qp_ref, f32[1024,128]{1,0:T(8,128)} %get-tuple-element.208.kp_ref, ...), custom_call_target="tpu_custom_call" | custom-call | bytes 14400000 | tf_op jit(solution)/shard_map/project_back/pallas_call | solution.py:1956
  476.8 45.1 %reduce_row.3 = (f32[128,2048]{1,0:T(8,128)}, f32[128,2048]{1,0:T(8,128)}, bf16[8,112,128]{2,1,0:T(8,128)(2,1)}) custom-call(bf16[8,128,2048]{2,1,0:T(8,128)(2,1)} %bitcast.62, bf16[256,768]{1,0:T(8,128)(2,1)} %get-tuple-element.173.pick_in.refs_1_, bf16[768,2048]{1,0:T(8,128)(2,1)} %bitcast.59, bf16[64,112,128]{2,1,0:T(8,128)(2,1)} %get-tuple-element.214.refs_3_), custom_call_target="tpu_custom_call" | custom-call | bytes 1200000 | tf_op jit(solution)/shard_map/reduce_row/pallas_call | solution.py:754
  521.9 12.1 %last.1 = (f32[2,2048,384]{2,1,0:T(8,128)}, f32[2,2048,384]{2,1,0:T(8,128)}, f32[2,384,2048]{2,1,0:T(8,128)}, f32[128,2048]{1,0:T(8,128)}, f32[128,2048]{1,0:T(8...) custom-call(s32[2]{0:T(128)} %pad_add_fusion.side, ...), custom_call_target="tpu_custom_call", output_to_operand_aliasing={{0}: (6, {}), {1}: (7, {}), {2}: (8, {})} | custom-call | bytes 10800000 | tf_op jit(solution)/shard_map/last/pallas_call | solution.py:1733
  533.9 4.9 psum.7
  538.9 0.5 slice_bitcast_fusion.1
  539.4 0.5 bitcast_divide_fusion
  539.9 1.2 slice_bitcast_fusion
  (13 shorter events, 0.1 us)
Async XLA Ops:
  40.9 7.3 %copy-start.5 = (f32[64,8,128]{2,1,0:T(8,128)S(1)}, f32[64,8,128]{2,1,0:T(8,128)}, u32[]{:S(2)}) copy-start(f32[64,8,128]{2,1,0:T(8,128)} %get-tuple-element.128) | copy-start | bytes 786436
  40.9 8.2 %copy-start.8 = (f32[128]{0:T(128)S(1)}, f32[128]{0:T(128)}, u32[]{:S(2)}) copy-start(f32[128]{0:T(128)} %param.27) | copy-start | bytes 1540
  40.9 8.2 %copy-start.9 = (f32[128]{0:T(128)S(1)}, f32[128]{0:T(128)}, u32[]{:S(2)}) copy-start(f32[128]{0:T(128)} %param.28) | copy-start | bytes 1540
  40.9 57.1 %all-to-all-start = ((bf16[64,32,384]{2,1,0:T(8,128)(2,1)}), bf16[64,32,384]{2,1,0:T(8,128)(2,1)S(1)}, u32[]{:S(2)}, u32[]{:S(2)}) async-start(bf16[64,32,384]{2,1,0:T(8,128)(2,1)} %get-tuple-element.135), calls=%async_computation | async-start | bytes 3145728 | tf_op jit(solution)/shard_map/all_to_all | solution.py:2064
  98.0 1.2 copy-start
  98.0 6.1 %copy-start.7 = (bf16[2048,384]{1,0:T(8,128)(2,1)S(1)}, bf16[2048,384]{1,0:T(8,128)(2,1)}, u32[]{:S(2)}) copy-start(bf16[2048,384]{1,0:T(8,128)(2,1)} %get-tuple-element.148) | copy-start | bytes 4718596
  99.2 84.3 %all-to-all-start.1 = ((bf16[32,24,2048]{2,1,0:T(8,128)(2,1)}), bf16[32,24,2048]{2,1,0:T(8,128)(2,1)}, u32[]{:S(2)}, u32[]{:S(2)}) async-start(bf16[32,24,2048]{2,1,0:T(8,128)(2,1)} %bitcast.66), calls=%async_computation.1 | async-start | bytes 6291456 | tf_op jit(solution)/shard_map/all_to_all | solution.py:980
  104.1 79.4 %collective-permute-start = (bf16[2048,384]{1,0:T(8,128)(2,1)S(1)}, bf16[2048,384]{1,0:T(8,128)(2,1)S(1)}, u32[]{:S(2)}, u32[]{:S(2)}) collective-permute-start(bf16[2048,384]{1,0:T(8,128)(2,1)S(1)} %copy-done.7), channel_id=1, source_target_pairs={{0,1},{1,0},{2,3},{3,2},{4,5},{5,4},{6,7},{7,6},{8,9},{9,8},{10,11... | collective-permute-start | bytes 4718600 | tf_op jit(solution)/shard_map/ppermute | solution.py:2027
  183.5 49.7 %copy-start.3 = (bf16[2048,384]{1,0:T(8,128)(2,1)}, bf16[2048,384]{1,0:T(8,128)(2,1)S(1)}, u32[]{:S(2)}) copy-start(bf16[2048,384]{1,0:T(8,128)(2,1)S(1)} %collective-permute-done.g_other) | copy-start | bytes 4718596
  183.5 49.7 %collective-permute-start.2 = (bf16[384,2048]{1,0:T(8,128)(2,1)}, bf16[384,2048]{1,0:T(8,128)(2,1)S(1)}, u32[]{:S(2)}, u32[]{:S(2)}) collective-permute-start(bf16[384,2048]{1,0:T(8,128)(2,1)} %get-tuple-element.160), channel_id=1, source_target_pairs={{0,1},{1,0},{2,3},{3,2},{4,5},{5,4},{6,7},{7,6},{8,9},{9,8},{10,11... | collective-permute-start | bytes 4718600 | tf_op jit(solution)/shard_map/ppermute | solution.py:2027
  184.3 48.9 %collective-permute-start.1 = (bf16[768,384]{1,0:T(8,128)(2,1)}, bf16[768,384]{1,0:T(8,128)(2,1)}, u32[]{:S(2)}, u32[]{:S(2)}) collective-permute-start(bf16[768,384]{1,0:T(8,128)(2,1)} %get-tuple-element.159), channel_id=1, source_target_pairs={{0,1},{1,0},{2,3},{3,2},{4,5},{5,4},{6,7},{7,6},{8,9},{9,8},{10,11... | collective-permute-start | bytes 1769480 | tf_op jit(solution)/shard_map/ppermute | solution.py:2027
  233.2 1.1 copy-start.4
  261.0 53.8 %all-to-all-start.2 = ((bf16[32,24,2176]{2,1,0:T(8,128)(2,1)}), bf16[32,24,2176]{2,1,0:T(8,128)(2,1)S(1)}, u32[]{:S(2)}, u32[]{:S(2)}) async-start(bf16[32,24,2176]{2,1,0:T(8,128)(2,1)} %bitcast.64), calls=%async_computation.2 | async-start | bytes 6684672 | tf_op jit(solution)/shard_map/all_to_all | solution.py:980
  276.4 35.9 %collective-permute-start.3 = (bf16[2048,384]{1,0:T(8,128)(2,1)}, bf16[2048,384]{1,0:T(8,128)(2,1)}, u32[]{:S(2)}, u32[]{:S(2)}) collective-permute-start(bf16[2048,384]{1,0:T(8,128)(2,1)} %get-tuple-element.164), channel_id=1, source_target_pairs={{0,1},{1,0},{2,3},{3,2},{4,5},{5,4},{6,7},{7,6},{8,9},{9,8},{10,11... | collective-permute-start | bytes 4718600 | tf_op jit(solution)/shard_map/ppermute | solution.py:2027
  314.8 1.7 copy-start.1
  369.7 8.3 %copy-start.6 = (f32[32]{0:T(128)S(1)}, f32[32]{0:T(128)}, u32[]{:S(2)}) copy-start(f32[32]{0:T(128)} %param.26) | copy-start | bytes 388
  369.8 48.0 %all-to-all-start.3 = ((bf16[32,24,2048]{2,1,0:T(8,128)(2,1)}), bf16[32,24,2048]{2,1,0:T(8,128)(2,1)S(1)}, u32[]{:S(2)}, u32[]{:S(2)}) async-start(bf16[32,24,2048]{2,1,0:T(8,128)(2,1)} %bitcast.65), calls=%async_computation.3 | async-start | bytes 6291456 | tf_op jit(solution)/shard_map/all_to_all | solution.py:980
  375.9 35.4 %collective-permute-start.5 = (bf16[240,2048]{1,0:T(8,128)(2,1)}, bf16[240,2048]{1,0:T(8,128)(2,1)}, u32[]{:S(2)}, u32[]{:S(2)}) collective-permute-start(bf16[240,2048]{1,0:T(8,128)(2,1)} %get-tuple-element.190), channel_id=1, source_target_pairs={{0,1},{1,0},{2,3},{3,2},{4,5},{5,4},{6,7},{7,6},{8,9},{9,8},{10,11... | collective-permute-start | bytes 2949128 | tf_op jit(solution)/shard_map/ppermute | solution.py:2027
  376.2 35.0 %collective-permute-start.4 = (bf16[768,384]{1,0:T(8,128)(2,1)}, bf16[768,384]{1,0:T(8,128)(2,1)}, u32[]{:S(2)}, u32[]{:S(2)}) collective-permute-start(bf16[768,384]{1,0:T(8,128)(2,1)} %get-tuple-element.189), channel_id=1, source_target_pairs={{0,1},{1,0},{2,3},{3,2},{4,5},{5,4},{6,7},{7,6},{8,9},{9,8},{10,11... | collective-permute-start | bytes 1769480 | tf_op jit(solution)/shard_map/ppermute | solution.py:2027
  417.8 46.0 %copy-start.2 = (bf16[32,24,2048]{2,1,0:T(8,128)(2,1)}, bf16[32,24,2048]{2,1,0:T(8,128)(2,1)S(1)}, u32[]{:S(2)}) copy-start(bf16[32,24,2048]{2,1,0:T(8,128)(2,1)S(1)} %all-to-all-done.3) | copy-start | bytes 9437188

commit v8 on v7

--- a/solution.py
+++ b/solution.py
@@ -202,6 +202,7 @@
 
 
 UP_CUT = (1280, 768)
+UP_GRAD_CUT = (768, 1280)
 DOWN_GRAD_CUT = (240, 144)
 
 
@@ -556,8 +557,9 @@
             copy.wait_send()
 
 
-def reduce_row(parts, collective_id, both, extra=None, swapped_whole=None, owned=()):
+def reduce_row(parts, collective_id, closing=None, extra=None, swapped_whole=None, owned=()):
     has_whole = swapped_whole is not None
+    both = closing is not None
     is_product = isinstance(parts, tuple)
     if is_product:
         rows, width = parts[0].shape[0] // 8, parts[1].shape[0]
@@ -572,10 +574,12 @@
         refs = list(refs)
         stage_sems = refs.pop(-1)
         buffers = [refs.pop(-1) for _ in staged_values][::-1]
-        sources = [refs.pop(0) for _ in staged_values[: len(staged_values) - len(owned)]]
+        sources = [refs.pop(0) for _ in range(len(staged_values) - len(owned) - (len(closing) if both else 0))]
         held = list(buffers)
         if is_product:
             heads_ref, out_w = held.pop(0), held.pop(0)
+            if both:
+                attn = refs.pop(-1)
             src = refs.pop(-1)
         else:
             src = held.pop(0)
@@ -583,9 +587,15 @@
             pick_ref, back_ref = held.pop(0), held.pop(0)
         src3 = refs.pop(0) if has_whole else None
         sources += [refs.pop(0) for _ in owned]
-        mine_in = held
+        if both:
+            own_chip = lax.div(lax.rem(lax.axis_index("ctx"), 8), 2)
+            rows_in, *others_in = [refs.pop(0) for _ in closing]
+            sources += [rows_in.at[pl.ds(pl.multiple_of(own_chip * 2 * rows, 2 * rows), 2 * rows)]] + others_in
+            mine_in, closing_in = held[: len(owned)], held[len(owned) :]
+        else:
+            mine_in = held
         staged = Staged(sources, buffers, stage_sems)
-        out = refs.pop(0)
+        out = [refs.pop(0) for _ in range(6)] if both else refs.pop(0)
         out2 = refs.pop(0) if has_extra else None
         out3 = refs.pop(0) if has_whole else None
         mine_out = [refs.pop(0) for _ in owned]
@@ -634,7 +644,8 @@
                 )
                 copy.start()
                 first.append(copy)
-        staged.ready(*range(len(staged_values) - len(owned), len(staged_values)))
+        if owned:
+            staged.ready(*range(len(staged_values) - len(owned), len(staged_values)))
         for block4 in blocks:
             block4.along_z(me, wsh)
         if has_extra:
@@ -703,12 +714,17 @@
             else:
                 out[:, span] = swapped[0, :, span].astype(F32) + swapped[1, :, span].astype(F32)
         if both:
-            keep = pltpu.make_async_copy(total, out.at[core], local)
+            mine = pl.ds(pl.multiple_of(core * rows, rows), rows)
+            keep = pltpu.make_async_copy(total, attn.at[mine], local)
             keep.start()
-            give = remote(total, out.at[core], send.at[0, 9], recv.at[0, 9], partner, wsh)
+            give = remote(total, attn.at[mine], send.at[0, 9], recv.at[0, 9], partner, wsh)
             give.start()
+            staged.ready(*range(len(staged_values) - len(closing), len(staged_values)))
             give.wait()
             keep.wait()
+            tokens_ref, gain_ref, hits_ref, pick_ref, of_ref = closing_in
+            router_ref = out_w.at[pl.ds(0, width), pl.ds(heads_ref.shape[1], of_ref.shape[1])]
+            middle_rows(tokens_ref, attn, gain_ref, router_ref, hits_ref, pick_ref, of_ref, *out)
         for copy in first + second:
             copy.wait_send()
         for block4 in blocks:
@@ -716,7 +732,21 @@
         if has_whole:
             whole.wait()
 
-    shapes = [jax.ShapeDtypeStruct((2,) + block if both else block, F32)]
+    if both:
+        slots, experts = closing[4].shape
+        shapes = [
+            jax.ShapeDtypeStruct(shape, dtype)
+            for shape, dtype in (
+                ((2 * rows, width), F32),
+                ((2 * rows, width), BF),
+                ((2 * rows, 128), F32),
+                ((2 * rows, experts), F32),
+                ((slots, width), BF),
+                ((slots, 128), BF),
+            )
+        ]
+    else:
+        shapes = [jax.ShapeDtypeStruct(block, F32)]
     scratch = [
         pltpu.VMEM((4,) + block, BF),
         pltpu.VMEM((3,) + block, BF),
@@ -728,7 +758,7 @@
         DMA,
     ]
     operands = list(parts) if is_product else [parts]
-    out_spaces = [VMEM]
+    out_spaces = [VMEM] * len(shapes)
     if has_extra:
         shapes.append(jax.ShapeDtypeStruct(block, F32))
         scratch += [pltpu.VMEM(block, BF), pltpu.VMEM((2,) + block, BF), pltpu.VMEM((2,) + block, BF)]
@@ -750,6 +780,11 @@
         scratch += Owned.scratch(value)
     if is_product:
         scratch.append(pltpu.VMEM((8,) + block, BF))
+    if both:
+        scratch.append(pltpu.VMEM((2 * rows, width), F32))
+        operands += list(closing)
+        spaces += [ANY] * len(closing)
+        staged_values += [jax.ShapeDtypeStruct((2 * rows, width), BF)] + list(closing[1:])
     scratch += Staged.scratch(staged_values)
     return pl.pallas_call(
         body,
@@ -763,16 +798,29 @@
     )(*operands)
 
 
-def reduce_chip(pick, back, of_expert, width, collective_id):
-    rows = pick.shape[0] // 2
+def reduce_chip(pick, back, of_expert, gates, hidden, residual, inverse, late_all, gain, cotangent, collective_id):
+    rows, width = cotangent.shape
     lanes = of_expert.shape[1]
-
-    def body(pick_in, back_in, of_in, out, out2, src, src2, arrived, swapped, arrived2, swapped2, send, recv, pick_ref, back_ref, of_ref, sems):
-        staged = Staged((pick_in, back_in, of_in), (pick_ref, back_ref, of_ref), sems)
+    owners = 64
+
+    def body(*refs):
+        ins, outs, refs = refs[:10], refs[10:13], refs[13:]
+        src, src2, arrived, swapped, arrived2, swapped2, send, recv = refs[:8]
+        buffers, sems, moe, d_gates = refs[8:18], refs[18], refs[19], refs[20]
         me, wsh = lax.axis_index("ctx"), lax.axis_index("wsh")
         other = 1 - wsh
         core = lax.rem(me, 2)
         partner = shifted(me, 0, 0, 0, 1)
+        mine = pl.ds(pl.multiple_of(core * rows, rows), rows)
+        pick_in, back_in, of_in, gates_in, hidden_in, residual_in, inverse_in, late_in, gain_in, cot_in = ins
+        staged = Staged(
+            (pick_in, back_in, of_in)
+            + tuple(ref.at[mine] for ref in (gates_in, hidden_in, residual_in, inverse_in))
+            + (late_in.at[pl.ds(0, width), pl.ds(2 * HEAD_WIDTH, lanes)], gain_in, cot_in),
+            buffers,
+            sems,
+        )
+        pick_ref, back_ref, of_ref = buffers[:3]
         barrier, amount = greet([(partner, wsh), (me, other)])
         staged.ready(0, 1, 2)
         src[...] = matmul(pick_ref[...], back_ref[:, :width]).astype(BF).reshape(src.shape)
@@ -791,18 +839,32 @@
         swapped2[0] = src2[core] + arrived2[...]
         swap2 = remote(swapped2.at[0], swapped2.at[1], send.at[3], recv.at[3], me, other)
         swap2.start()
+        staged.ready(*range(3, 10))
         swap2.wait()
-        out2[...] = swapped2[0] + swapped2[1]
+        d_gates[...] = swapped2[0] + swapped2[1]
         swap.wait()
-        out[...] = swapped[0].astype(F32) + swapped[1].astype(F32)
+        moe[...] = swapped[0].astype(F32) + swapped[1].astype(F32)
+        turn_rows(moe, d_gates, *buffers[3:], *outs)
 
     sds = jax.ShapeDtypeStruct
     block, block2 = (rows, width), (rows, lanes)
+    staged_values = (
+        pick,
+        back,
+        of_expert,
+        sds((rows, gates.shape[1]), F32),
+        sds(block, BF),
+        sds(block, F32),
+        sds((rows, inverse.shape[1]), F32),
+        sds((width, lanes), BF),
+        gain,
+        cotangent,
+    )
     return pl.pallas_call(
         body,
-        out_shape=(sds(block, F32), sds(block2, F32)),
-        in_specs=[ANY] * 3,
-        out_specs=[VMEM] * 2,
+        out_shape=(sds(block, F32), sds(block, BF), sds((owners, width // owners + 16, 128), BF)),
+        in_specs=[ANY] * 10,
+        out_specs=[VMEM] * 3,
         scratch_shapes=[
             pltpu.VMEM((2,) + block, BF),
             pltpu.VMEM((2,) + block2, F32),
@@ -813,11 +875,12 @@
             DMA((4,)),
             DMA((4,)),
         ]
-        + Staged.scratch((pick, back, of_expert)),
+        + Staged.scratch(staged_values)
+        + [pltpu.VMEM(block, F32), pltpu.VMEM(block2, F32)],
         compiler_params=call_params(collective_id),
         name="reduce_chip",
         cost_estimate=cost(17),
-    )(pick, back, of_expert)
+    )(pick, back, of_expert, gates, hidden, residual, inverse, late_all, gain, cotangent)
 
 
 def reduce_keys(parts, owned, swapped, collective_id):
@@ -1442,11 +1505,11 @@
     up_ref[0] = value[:, :half]
     low = value[:, half:].astype(BF)
 
-    @pl.when(step < UP_CUT[0] // turn_at)
+    @pl.when(step < UP_GRAD_CUT[0] // turn_at)
     def _():
         up_out[...] = low
 
-    @pl.when(step >= UP_CUT[0] // turn_at)
+    @pl.when(step >= UP_GRAD_CUT[0] // turn_at)
     def _():
         up_rest[...] = low
 
@@ -1462,7 +1525,7 @@
     whole = activated.shape[1]
     half = whole // 2
     tile = 256
-    first = UP_CUT[0] // tile
+    first = UP_GRAD_CUT[0] // tile
     sds = jax.ShapeDtypeStruct
     columns = pl.BlockSpec((count, tile), lambda i, side: (0, i))
     full = pl.BlockSpec((count, whole), lambda i, side: (0, 0))
@@ -1471,8 +1534,8 @@
         out_shape=(
             sds((2, width, half), F32),
             sds((2, half, width), F32),
-            sds((UP_CUT[0], half), BF),
-            sds((UP_CUT[1], half), BF),
+            sds((UP_GRAD_CUT[0], half), BF),
+            sds((UP_GRAD_CUT[1], half), BF),
             sds((DOWN_GRAD_CUT[0], width), BF),
             sds((DOWN_GRAD_CUT[1], width), BF),
         ),
@@ -1527,7 +1590,7 @@
     rows_ref[...] = matmul(pick_low, cot_ref[...]).astype(BF)
 
 
-def middle_kernel(chip, t_ref, attn_ref, gain_ref, wr_ref, hits_ref, pick_ref, of_ref, res_ref, h_ref, inv_ref, gates_ref, rows_ref, tile_ref):
+def middle_rows(t_ref, attn_ref, gain_ref, wr_ref, hits_ref, pick_ref, of_ref, res_ref, h_ref, inv_ref, gates_ref, rows_ref, tile_ref):
     residual = t_ref[...].astype(F32) + attn_ref[...]
     res_ref[...] = residual
     inverse = lax.rsqrt(jnp.mean(residual * residual, axis=1, keepdims=True) + EPSILON)
@@ -1550,49 +1613,7 @@
     tile_ref[...] = jnp.where(lane < 64, chosen[0], chosen[1]).astype(BF)
 
 
-def middle(chip, row_rows, attn_total, gain, late_all, hits, pick, of_expert):
-    rows, width = attn_total.shape
-    slots, experts = of_expert.shape
-    sds = jax.ShapeDtypeStruct
-
-    def whole(value):
-        return pl.BlockSpec(value.shape, lambda i, chip: (0, 0))
-
-    def out(*shape):
-        return pl.BlockSpec(shape, lambda i, chip: (0, 0))
-
-    shapes = (
-        sds((rows, width), F32),
-        sds((rows, width), BF),
-        sds((rows, 128), F32),
-        sds((rows, experts), F32),
-        sds((slots, width), BF),
-        sds((slots, 128), BF),
-    )
-    return pl.pallas_call(
-        middle_kernel,
-        out_shape=shapes,
-        grid_spec=pltpu.PrefetchScalarGridSpec(
-            num_scalar_prefetch=1,
-            grid=(1,),
-            in_specs=[
-                pl.BlockSpec((rows, width), lambda i, chip: (chip[0], 0)),
-                whole(attn_total),
-                whole(gain),
-                pl.BlockSpec((width, experts), lambda i, chip: (0, 2)),
-                whole(hits),
-                whole(pick),
-                whole(of_expert),
-            ],
-            out_specs=[out(*value.shape) for value in shapes],
-        ),
-        compiler_params=pltpu.CompilerParams(vmem_limit_bytes=ROOM),
-        name="middle",
-        cost_estimate=cost(1),
-    )(chip, row_rows, attn_total, gain, late_all, hits, pick, of_expert)
-
-
-def turn_kernel(core, moe_ref, dg_ref, gates_ref, h_ref, res_ref, inv_ref, wr_ref, gain_ref, cot_ref, d_ref, low_ref, part_ref):
+def turn_rows(moe_ref, dg_ref, gates_ref, h_ref, res_ref, inv_ref, wr_ref, gain_ref, cot_ref, d_ref, low_ref, part_ref):
     gates = gates_ref[...]
     d_gates = dg_ref[...]
     d_logits = (gates * (d_gates - jnp.sum(gates * d_gates, axis=1, keepdims=True))).astype(BF)
@@ -1620,51 +1641,13 @@
     ).astype(BF)
 
 
-def turn(core, d_moe, d_gates, gates, hidden, residual, inverse, late_all, gain, cotangent):
-    rows, width = d_moe.shape
-    experts = gates.shape[1]
-    owners = 64
-    sds = jax.ShapeDtypeStruct
-
-    def mine(columns):
-        return pl.BlockSpec((rows, columns), lambda i, core: (core[0], 0))
-
-    def whole(*shape):
-        return pl.BlockSpec(shape, lambda i, core: (0,) * len(shape))
-
-    parts = (owners, width // owners + 16, 128)
-    return pl.pallas_call(
-        turn_kernel,
-        out_shape=(sds((rows, width), F32), sds((rows, width), BF), sds(parts, BF)),
-        grid_spec=pltpu.PrefetchScalarGridSpec(
-            num_scalar_prefetch=1,
-            grid=(1,),
-            in_specs=[
-                whole(rows, width),
-                whole(rows, experts),
-                mine(experts),
-                mine(width),
-                mine(width),
-                mine(128),
-                pl.BlockSpec((width, experts), lambda i, core: (0, 2)),
-                whole(1, width),
-                whole(rows, width),
-            ],
-            out_specs=[whole(rows, width), whole(rows, width), whole(*parts)],
-        ),
-        compiler_params=pltpu.CompilerParams(vmem_limit_bytes=ROOM),
-        name="turn",
-        cost_estimate=cost(6),
-    )(core, d_moe, d_gates, gates, hidden, residual, inverse, late_all, gain, cotangent)
-
-
 def last_kernel(side, g_in, u_in, u_rest, d_in, d_rest, *refs):
     (t_ref, dh_ref, dr_ref, moe_ref, res_ref, ga_ref, late_ref, early_ref, wq_ref, wk_ref, wv_ref), refs = refs[3:14], refs[14:]
     g_out, u_out, d_out, out_ref, gt_ref, gq_ref, gk_ref, gv_ref, go_ref, gr_ref, gains_ref, ffn_ref = refs[:12]
     keys, router, gains, ffn, dots = refs[12:]
     step = pl.program_id(0)
     g_out[0] = g_in[...].astype(F32)
-    u_out[0] = jnp.where(step < UP_CUT[0] // u_in.shape[0], u_in[...], u_rest[...]).astype(F32)
+    u_out[0] = jnp.where(step < UP_GRAD_CUT[0] // u_in.shape[0], u_in[...], u_rest[...]).astype(F32)
     d_out[0] = jnp.where(step < DOWN_GRAD_CUT[0] // d_in.shape[0], d_in[...], d_rest[...]).astype(F32)
     rows = t_ref[...].astype(F32)
     out_ref[...] = res_ref[...] + moe_ref[...]
@@ -1720,7 +1703,7 @@
     def whole(*shape):
         return pl.BlockSpec(shape, lambda i, side: (0,) * len(shape))
 
-    first = UP_CUT[0] // tile
+    first = UP_GRAD_CUT[0] // tile
     rows_out = pl.BlockSpec((1, tile, half), lambda i, side: (1 - side[0], i, 0))
     short = half // steps
     short_first = DOWN_GRAD_CUT[0] // short
@@ -2094,16 +2077,11 @@
     heads, lse, plan = attend(block_order, seq_lengths, group.reshape(1), queries, kv_all)
 
     (other_up, other_down), heads = after((other_up, other_down), heads)
-    attn_total, up_first = reduce_row((heads, late_all), 2, True, swapped_whole=up_first)
-    residual, hidden_two, inverse_two, gates, out_rows, gate_tile = middle(
-        lax.div(place, 2).reshape(1),
-        row_rows,
-        attn_total.reshape(2 * rows, width),
-        g_ffn[None, :],
-        late_all,
-        hits,
-        pick_low,
-        of_expert,
+    residual, hidden_two, inverse_two, gates, out_rows, gate_tile, up_first = reduce_row(
+        (heads, late_all),
+        2,
+        closing=(row_rows, g_ffn[None, :], hits, pick_low, of_expert),
+        swapped_whole=up_first,
     )
 
     out_rows = out_rows.reshape(chips, slots, width)
@@ -2132,11 +2110,10 @@
     (gate_grad_back, other_up, other_down, down_rest), d_back = after(
         (gate_grad_back, other_up, other_down, down_rest), d_back
     )
-    d_hidden_moe, d_gates = reduce_chip(pick_turned, d_back, of_expert, width, 5)
-    d_residual, d_residual_low, part = turn(
-        core.reshape(1),
-        d_hidden_moe,
-        d_gates,
+    d_residual, d_residual_low, part = reduce_chip(
+        pick_turned,
+        d_back,
+        of_expert,
         gates,
         hidden_two,
         residual,
@@ -2144,6 +2121,7 @@
         late_all,
         g_ffn[None, :],
         cotangent,
+        5,
     )
 
     d_attn, up_first = gather_row(d_residual_low, up_first, 7)
@@ -2185,7 +2163,6 @@
     d_hidden_one, moe_total, late = reduce_row(
         d_hidden_parts,
         9,
-        False,
         extra=(pick_turned, y_back.reshape(chips * slots, width)),
         owned=(late,),
     )

time: 548 us -> 542 us (0.989)
  waiting for transfers between devices: 42.1 us -> 32.4 us
    pallas_call x1, Pallas kernels: 22.7 us -> 35.7 us  [attend_back(): pl.pallas_call(backward_kernel, out_shape=(sds(queries.shape, F32), sds(d...]
    pallas_call x1, Pallas kernels: 12.2 us -> 21.2 us  [attend(): pl.pallas_call(forward_kernel, out_shape=(sds(queries.shape, BF), sds((st...]
    pallas_call x3 -> x1, Pallas kernels: 29.7 us -> 20.8 us  [reduce_chip(): pl.pallas_call(body, out_shape=(sds(block, F32), sds(block, BF), sds((own...]
    pallas_call x2, Pallas kernels: 105 us -> 96.4 us  [reduce_row(): pl.pallas_call(body, out_shape=shapes, in_specs=spaces, out_specs=out_spa...]
    all_to_all x3, waiting for transfers between devices: 8.99 us -> 2.47 us  [exchange_behind(): lax.all_to_all(value, ('ctx', 'wsh'), split_axis=0, concat_axis=0, tiled=...]
  transfers between devices with their start and end apart: 10 -> 10, of which waited for: 5 -> 4; matrix products, arithmetic and copies ran while one was open for 1% -> 1% of each run, Pallas kernels for 40% -> 42%
where the time goes in v8:
time: 542 us; the launch traced here: 535 us
  Pallas kernels  452 us (83%)
  starting transfers between devices  33.5 us (6%)
  waiting for transfers between devices  32.4 us (6%)
  local copies, waits for them, and re-layouts  8.33 us (2%)
    pallas_call x2, Pallas kernels, reduce_row(): pl.pallas_call(body, out_shape=shapes, in_specs=spaces, out_specs=out_spa...  96.4 us
    pallas_call x1, Pallas kernels, exchange(): pl.pallas_call(body, out_shape=[jax.ShapeDtypeStruct(a.shape, a.dtype) fo...  46.4 us
    pallas_call x1, Pallas kernels, reduce_keys(): pl.pallas_call(body, out_shape=(jax.ShapeDtypeStruct(block, F32), jax.Sha...  45.3 us
    pallas_call x1, Pallas kernels, gather_first(): pl.pallas_call(body, out_shape=(sds((64, depth, packed), BF), sds((8,) +...  40.2 us
    pallas_call x1, Pallas kernels, gather_keys(): pl.pallas_call(body, out_shape=(sds((8,) + rows.shape, rows.dtype), sds((...  36.1 us
    pallas_call x1, Pallas kernels, attend_back(): pl.pallas_call(backward_kernel, out_shape=(sds(queries.shape, F32), sds(d...  35.7 us
    ppermute x6, waiting for transfers between devices, swap(): return lax.ppermute(value, 'wsh', [(0, 1), (1, 0)])  29.9 us
    pallas_call x1, Pallas kernels, gather_row(): pl.pallas_call(body, out_shape=(jax.ShapeDtypeStruct((8,) + block.shape,...  27.4 us
  transfers between devices with their start and end apart: 10, of which 4 were waited for; matrix products, arithmetic and copies ran while one was open for 1% of the time, Pallas kernels for 42%

profile of v8, /device:TPU:0, one launch (start us, length us, event | category | flops | bytes accessed | tf_op | source)
XLA Modules:
  0.0 535.0 jit_solution(8290100705611885197)
XLA Ops:
  0.6 40.2 %gather_first.1 = (bf16[64,32,384]{2,1,0:T(8,128)(2,1)}, bf16[8,128,2048]{2,1,0:T(8,128)(2,1)}, f32[64,8,128]{2,1,0:T(8,128)}, s32[2,8,128]{2,1,0:T(8,128)}, bf1...) custom-call(f32[32,2048]{1,0:T(8,128)} %refs_11_.1, ...), custom_call_target="tpu_custom_call" | custom-call | bytes 48000000 | tf_op jit(solution)/shard_map/gather_first/pallas_call | solution.py:310
  40.9 0.0 copy-start.5
  40.9 0.0 copy-start.8
  40.9 0.0 copy-start.9
  40.9 7.3 %all-to-all-start = ((bf16[64,32,384]{2,1,0:T(8,128)(2,1)}), bf16[64,32,384]{2,1,0:T(8,128)(2,1)S(1)}, u32[]{:S(2)}, u32[]{:S(2)}) async-start(bf16[64,32,384]{2,1,0:T(8,128)(2,1)} %get-tuple-element.132), calls=%async_computation | async-start | bytes 3145728 | tf_op jit(solution)/shard_map/all_to_all | solution.py:2047
  48.2 0.0 copy-done.5
  48.2 0.2 fusion
  48.4 0.7 reshape.146.ga_ref.refs_8_
  49.1 0.0 copy-done.8
  49.1 0.0 copy-done.9
  49.1 0.6 maximum_bitcast_fusion.freq_ref
  49.7 0.5 bitcast_convert_fusion
  50.2 0.6 broadcast_in_dim.20.flag_ref
  50.8 11.2 %project.1 = (bf16[1024,2048]{1,0:T(8,128)(2,1)}, bf16[1024,256]{1,0:T(8,128)(2,1)}, bf16[1024,256]{1,0:T(8,128)(2,1)}, f32[1024,256]{1,0:T(8,128)}, f32[1024,12...) custom-call(s32[128]{0:T(128)} %block_order.3, s32[4]{0:T(128)} %lengths.5, s32[1]{0:T(128)} %bitcast.6.group, ...), custom_call_target="tpu_custom_call" | custom-call | bytes 9600000 | tf_op jit(solution)/shard_map/project/pallas_call | solution.py:1832
  62.0 36.1 %gather_keys.1 = (bf16[8,1024,256]{2,1,0:T(8,128)(2,1)}, bf16[768,256]{1,0:T(8,128)(2,1)}, bf16[256,768]{1,0:T(8,128)(2,1)}, bf16[768,128]{1,0:T(8,128)(2,1)}, f...) custom-call(bf16[1024,256]{1,0:T(8,128)(2,1)} %get-tuple-element.127.src, s32[2,8,128]{2,1,0:T(8,128)} %get-tuple-element.128.routes_ref, ...), custom_call_target="tpu_custom_call" | custom-call | bytes 36000000 | tf_op jit(solution)/shard_map/gather_keys/pallas_call | solution.py:439
  98.1 0.0 all-to-all-done
  98.1 0.0 copy-start
  98.1 0.0 copy-start.7
  98.1 1.1 copy-done
  99.2 4.9 all-to-all-start.1
  104.2 0.0 copy-done.7
  104.2 0.9 collective-permute-start
  105.0 0.7 reshape.149.refs_4_.refs_8_
  105.7 21.2 %attend.1 = (bf16[1024,256]{1,0:T(8,128)(2,1)}, f32[8,1,256]{2,1,0:T(1,128)}, s32[256]{0:T(256)}) custom-call(s32[128]{0:T(128)} %block_order.3, s32[4]{0:T(128)} %lengths.5, s32[1]{0:T(128)} %bitcast.6.group, bf16[1024,256]{1,0:T(8,128)(2,1)} %get-tuple-element.126.q_ref, bf16[8192,256]{1,0:T(8,128)(2,1)} %bitcast.53), custom_call_target="tpu_custom_call" | custom-call | bytes 20400000 | tf_op jit(solution)/shard_map/attend/pallas_call | solution.py:1183
  126.9 54.9 %reduce_row.2 = (f32[256,2048]{1,0:T(8,128)}, bf16[256,2048]{1,0:T(8,128)(2,1)}, f32[256,128]{1,0:T(8,128)}, f32[256,128]{1,0:T(8,128)}, bf16[768,2048]{1,0:T(8,...) custom-call(bf16[1024,256]{1,0:T(8,128)(2,1)} %get-tuple-element.137.refs_0_.heads_ref, ...), custom_call_target="tpu_custom_call" | custom-call | bytes 1200000 | tf_op jit(solution)/shard_map/reduce_row/pallas_call | solution.py:789
  181.8 0.0 collective-permute-done.g_other
  181.8 0.0 copy-start.3
  181.8 0.0 all-to-all-done.1
  181.8 0.8 collective-permute-start.2
  182.6 1.5 collective-permute-start.1
  184.1 46.4 %exchange.1 = (bf16[32,24,2048]{2,1,0:T(8,128)(2,1)}, bf16[32,24,128]{2,1,0:T(8,128)(2,1)}) custom-call(bf16[32,24,2048]{2,1,0:T(8,128)(2,1)} %bitcast.64, bf16[32,24,128]{2,1,0:T(8,128)(2,1)} %bitcast.70), custom_call_target="tpu_custom_call" | custom-call | bytes 57600000 | tf_op jit(solution)/shard_map/exchange/pallas_call | solution.py:1024
  230.6 1.0 collective-permute-done.1.u_rest
  231.5 0.0 collective-permute-done.2.d_other
  231.5 1.1 copy-done.4
  232.7 26.7 %run_expert.1 = (bf16[768,2048]{1,0:T(8,128)(2,1)}, bf16[768,2176]{1,0:T(8,128)(2,1)}, bf16[768,768]{1,0:T(8,128)(2,1)}, bf16[768,768]{1,0:T(8,128)(2,1)}, bf16[...) custom-call(s32[1]{0:T(128)} %bitcast.side, bf16[768,2048]{1,0:T(8,128)(2,1)} %bitcast.45, ...), custom_call_target="tpu_custom_call" | custom-call | bytes 30000000 | tf_op jit(solution)/shard_map/run_expert/pallas_call | solution.py:1423
  259.3 9.2 %all-to-all-start.2 = ((bf16[32,24,2176]{2,1,0:T(8,128)(2,1)}), bf16[32,24,2176]{2,1,0:T(8,128)(2,1)S(1)}, u32[]{:S(2)}, u32[]{:S(2)}) async-start(bf16[32,24,2176]{2,1,0:T(8,128)(2,1)} %bitcast.61), calls=%async_computation.2 | async-start | bytes 6684672 | tf_op jit(solution)/shard_map/all_to_all | solution.py:1043
  268.5 6.2 %gate_grads.1 = (f32[2,2048,384]{2,1,0:T(8,128)}, bf16[2048,384]{1,0:T(8,128)(2,1)}) custom-call(s32[1]{0:T(128)} %bitcast.side, bf16[768,2048]{1,0:T(8,128)(2,1)} %bitcast.46, bf16[768,768]{1,0:T(8,128)(2,1)} %get-tuple-element.158.dg_ref), custom_call_target="tpu_custom_call" | custom-call | bytes 6000000 | tf_op jit(solution)/shard_map/gate_grads/pallas_call | solution.py:1474
  274.8 0.0 collective-permute-start.3
  274.8 13.6 %expert_grads.1 = (f32[2,2048,384]{2,1,0:T(8,128)}, f32[2,384,2048]{2,1,0:T(8,128)}, bf16[768,384]{1,0:T(8,128)(2,1)}, bf16[1280,384]{1,0:T(8,128)(2,1)}, bf16[2...) custom-call(s32[1]{0:T(128)} %bitcast.side, bf16[768,2048]{1,0:T(8,128)(2,1)} %bitcast.47, ...), custom_call_target="tpu_custom_call" | custom-call | bytes 12000000 | tf_op jit(solution)/shard_map/expert_grads/pallas_call | solution.py:1532
  288.4 22.3 %collective-permute-done.3.g_in = bf16[2048,384]{1,0:T(8,128)(2,1)} collective-permute-done((bf16[2048,384]{1,0:T(8,128)(2,1)}, bf16[2048,384]{1,0:T(8,128)(2,1)}, u32[]{:S(2)}, u32[]{:S(2)}) %collective-permute-start.3) | collective-permute-done | bytes 1572896 | tf_op jit(solution)/shard_map/ppermute | solution.py:2010
  310.6 2.5 all-to-all-done.2
  313.1 1.7 copy-done.1
  314.8 20.8 %reduce_chip.1 = (f32[128,2048]{1,0:T(8,128)}, bf16[128,2048]{1,0:T(8,128)(2,1)}, bf16[64,48,128]{2,1,0:T(8,128)(2,1)}) custom-call(bf16[256,768]{1,0:T(8,128)(2,1)} %get-tuple-element.169.refs_0_.refs_1_, bf16[768,2176]{1,0:T(8,128)(2,1)} %bitcast.55, bf16[768,128]{1,0:T(8,128)(2,1)} %get-tuple-element.142.refs_7_.refs_2_, ...), custom_call_target="tpu_custom_call" | custom-call | bytes 20400000 | tf_op jit(solution)/shard_map/reduce_chip/pallas_call | solution.py:863
  335.6 27.4 %gather_row.1 = (bf16[8,128,2048]{2,1,0:T(8,128)(2,1)}, bf16[768,384]{1,0:T(8,128)(2,1)}) custom-call(bf16[128,2048]{1,0:T(8,128)(2,1)} %get-tuple-element.175.src, bf16[768,384]{1,0:T(8,128)(2,1)} %get-tuple-element.176.src2), custom_call_target="tpu_custom_call" | custom-call | bytes 31200000 | tf_op jit(solution)/shard_map/gather_row/pallas_call | solution.py:369
  363.1 0.0 copy-start.6
  363.1 6.9 %all-to-all-start.3 = ((bf16[32,24,2048]{2,1,0:T(8,128)(2,1)}), bf16[32,24,2048]{2,1,0:T(8,128)(2,1)S(1)}, u32[]{:S(2)}, u32[]{:S(2)}) async-start(bf16[32,24,2048]{2,1,0:T(8,128)(2,1)} %bitcast.62), calls=%async_computation.3 | async-start | bytes 6291456 | tf_op jit(solution)/shard_map/all_to_all | solution.py:1043
  370.0 1.6 collective-permute-start.4
  371.6 0.5 collective-permute-start.5
  372.1 0.0 copy-done.6
  372.1 0.6 pad_add_fusion.side
  372.7 0.1 maximum_maximum_fusion
  372.8 35.7 %attend_back.1 = (f32[1024,256]{1,0:T(8,128)}, bf16[2,8,2,512,128]{4,3,2,1,0:T(8,128)(2,1)}, bf16[64,112,128]{2,1,0:T(8,128)(2,1)}) custom-call(s32[256]{0:T(256)} %get-tuple-element.185.plan, s32[4]{0:T(128)} %lengths.5, bf16[1024,256]{1,0:T(8,128)(2,1)} %get-tuple-element.126.q_ref, bf16[1024,256]{1,0:T(8,128)(2,1)} %get-tuple-element.137.refs_0_.heads_ref, ...), custom_call_target="tpu_custom_call" | custom-call | bytes 28800000 | tf_op jit(solution)/shard_map/attend_back/pallas_call | solution.py:1302
  408.5 0.0 collective-permute-done.4.u_rest
  408.5 6.7 %collective-permute-done.5.d_in = bf16[240,2048]{1,0:T(8,128)(2,1)} collective-permute-done((bf16[240,2048]{1,0:T(8,128)(2,1)}, bf16[240,2048]{1,0:T(8,128)(2,1)}, u32[]{:S(2)}, u32[]{:S(2)}) %collective-permute-start.5) | collective-permute-done | bytes 983072 | tf_op jit(solution)/shard_map/ppermute | solution.py:2010
  415.2 0.0 all-to-all-done.3
  415.2 45.3 %reduce_keys.1 = (f32[512,128]{1,0:T(8,128)}, bf16[8,112,128]{2,1,0:T(8,128)(2,1)}, bf16[144,2048]{1,0:T(8,128)(2,1)}) custom-call(bf16[2,8,2,512,128]{4,3,2,1,0:T(8,128)(2,1)} %get-tuple-element.192.src_in, bf16[64,112,128]{2,1,0:T(8,128)(2,1)} %get-tuple-element.193.src4_in, bf16[144,2048]{1,0:T(8,128)(2,1)} %get-tuple-element.194.src5), custom_call_target="tpu_custom_call" | custom-call | bytes 48000000 | tf_op jit(solution)/shard_map/reduce_keys/pallas_call | solution.py:959
  460.5 0.7 broadcast.24.flag_ref
  461.2 12.3 %project_back.1 = (bf16[1024,2048]{1,0:T(8,128)(2,1)}, bf16[64,112,128]{2,1,0:T(8,128)(2,1)}) custom-call(f32[1024,256]{1,0:T(8,128)} %get-tuple-element.199.dq_ref, f32[512,128]{1,0:T(8,128)} %get-tuple-element.200.ds_ref, f32[1024,256]{1,0:T(8,128)} %get-tuple-element.201.qp_ref, f32[1024,128]{1,0:T(8,128)} %get-tuple-element.202.kp_ref, ...), custom_call_target="tpu_custom_call" | custom-call | bytes 14400000 | tf_op jit(solution)/shard_map/project_back/pallas_call | solution.py:1939
  473.5 41.5 %reduce_row.3 = (f32[128,2048]{1,0:T(8,128)}, f32[128,2048]{1,0:T(8,128)}, bf16[8,112,128]{2,1,0:T(8,128)(2,1)}) custom-call(bf16[8,128,2048]{2,1,0:T(8,128)(2,1)} %bitcast.59, bf16[256,768]{1,0:T(8,128)(2,1)} %get-tuple-element.169.refs_0_.refs_1_, bf16[768,2048]{1,0:T(8,128)(2,1)} %bitcast.56, bf16[64,112,128]{2,1,0:T(8,128)(2,1)} %get-tuple-element.208.refs_3_), custom_call_target="tpu_custom_call" | custom-call | bytes 1200000 | tf_op jit(solution)/shard_map/reduce_row/pallas_call | solution.py:789
  515.0 12.3 %last.1 = (f32[2,2048,384]{2,1,0:T(8,128)}, f32[2,2048,384]{2,1,0:T(8,128)}, f32[2,384,2048]{2,1,0:T(8,128)}, f32[128,2048]{1,0:T(8,128)}, f32[128,2048]{1,0:T(8...) custom-call(s32[2]{0:T(128)} %pad_add_fusion.side, ...), custom_call_target="tpu_custom_call", output_to_operand_aliasing={{0}: (6, {}), {1}: (7, {}), {2}: (8, {})} | custom-call | bytes 10800000 | tf_op jit(solution)/shard_map/last/pallas_call | solution.py:1716
  527.4 4.9 psum.7
  532.3 0.5 slice_bitcast_fusion.1
  532.8 0.5 bitcast_divide_fusion
  533.4 1.2 slice_bitcast_fusion
  (11 shorter events, 0.0 us)
Async XLA Ops:
  40.9 7.3 %copy-start.5 = (f32[64,8,128]{2,1,0:T(8,128)S(1)}, f32[64,8,128]{2,1,0:T(8,128)}, u32[]{:S(2)}) copy-start(f32[64,8,128]{2,1,0:T(8,128)} %get-tuple-element.125) | copy-start | bytes 786436
  40.9 8.2 %copy-start.8 = (f32[128]{0:T(128)S(1)}, f32[128]{0:T(128)}, u32[]{:S(2)}) copy-start(f32[128]{0:T(128)} %param.27) | copy-start | bytes 1540
  40.9 8.2 %copy-start.9 = (f32[128]{0:T(128)S(1)}, f32[128]{0:T(128)}, u32[]{:S(2)}) copy-start(f32[128]{0:T(128)} %param.28) | copy-start | bytes 1540
  40.9 57.2 %all-to-all-start = ((bf16[64,32,384]{2,1,0:T(8,128)(2,1)}), bf16[64,32,384]{2,1,0:T(8,128)(2,1)S(1)}, u32[]{:S(2)}, u32[]{:S(2)}) async-start(bf16[64,32,384]{2,1,0:T(8,128)(2,1)} %get-tuple-element.132), calls=%async_computation | async-start | bytes 3145728 | tf_op jit(solution)/shard_map/all_to_all | solution.py:2047
  98.1 1.1 copy-start
  98.1 6.1 %copy-start.7 = (bf16[2048,384]{1,0:T(8,128)(2,1)S(1)}, bf16[2048,384]{1,0:T(8,128)(2,1)}, u32[]{:S(2)}) copy-start(bf16[2048,384]{1,0:T(8,128)(2,1)} %get-tuple-element.144) | copy-start | bytes 4718596
  99.2 82.6 %all-to-all-start.1 = ((bf16[32,24,2048]{2,1,0:T(8,128)(2,1)}), bf16[32,24,2048]{2,1,0:T(8,128)(2,1)}, u32[]{:S(2)}, u32[]{:S(2)}) async-start(bf16[32,24,2048]{2,1,0:T(8,128)(2,1)} %bitcast.63), calls=%async_computation.1 | async-start | bytes 6291456 | tf_op jit(solution)/shard_map/all_to_all | solution.py:1043
  104.2 77.6 %collective-permute-start = (bf16[2048,384]{1,0:T(8,128)(2,1)S(1)}, bf16[2048,384]{1,0:T(8,128)(2,1)S(1)}, u32[]{:S(2)}, u32[]{:S(2)}) collective-permute-start(bf16[2048,384]{1,0:T(8,128)(2,1)S(1)} %copy-done.7), channel_id=1, source_target_pairs={{0,1},{1,0},{2,3},{3,2},{4,5},{5,4},{6,7},{7,6},{8,9},{9,8},{10,11... | collective-permute-start | bytes 4718600 | tf_op jit(solution)/shard_map/ppermute | solution.py:2010
  181.8 49.7 %copy-start.3 = (bf16[2048,384]{1,0:T(8,128)(2,1)}, bf16[2048,384]{1,0:T(8,128)(2,1)S(1)}, u32[]{:S(2)}) copy-start(bf16[2048,384]{1,0:T(8,128)(2,1)S(1)} %collective-permute-done.g_other) | copy-start | bytes 4718596
  181.8 49.7 %collective-permute-start.2 = (bf16[384,2048]{1,0:T(8,128)(2,1)}, bf16[384,2048]{1,0:T(8,128)(2,1)S(1)}, u32[]{:S(2)}, u32[]{:S(2)}) collective-permute-start(bf16[384,2048]{1,0:T(8,128)(2,1)} %get-tuple-element.156), channel_id=1, source_target_pairs={{0,1},{1,0},{2,3},{3,2},{4,5},{5,4},{6,7},{7,6},{8,9},{9,8},{10,11... | collective-permute-start | bytes 4718600 | tf_op jit(solution)/shard_map/ppermute | solution.py:2010
  182.6 48.9 %collective-permute-start.1 = (bf16[768,384]{1,0:T(8,128)(2,1)}, bf16[768,384]{1,0:T(8,128)(2,1)}, u32[]{:S(2)}, u32[]{:S(2)}) collective-permute-start(bf16[768,384]{1,0:T(8,128)(2,1)} %get-tuple-element.155), channel_id=1, source_target_pairs={{0,1},{1,0},{2,3},{3,2},{4,5},{5,4},{6,7},{7,6},{8,9},{9,8},{10,11... | collective-permute-start | bytes 1769480 | tf_op jit(solution)/shard_map/ppermute | solution.py:2010
  231.5 1.1 copy-start.4
  259.3 53.8 %all-to-all-start.2 = ((bf16[32,24,2176]{2,1,0:T(8,128)(2,1)}), bf16[32,24,2176]{2,1,0:T(8,128)(2,1)S(1)}, u32[]{:S(2)}, u32[]{:S(2)}) async-start(bf16[32,24,2176]{2,1,0:T(8,128)(2,1)} %bitcast.61), calls=%async_computation.2 | async-start | bytes 6684672 | tf_op jit(solution)/shard_map/all_to_all | solution.py:1043
  274.8 35.9 %collective-permute-start.3 = (bf16[2048,384]{1,0:T(8,128)(2,1)}, bf16[2048,384]{1,0:T(8,128)(2,1)}, u32[]{:S(2)}, u32[]{:S(2)}) collective-permute-start(bf16[2048,384]{1,0:T(8,128)(2,1)} %get-tuple-element.160), channel_id=1, source_target_pairs={{0,1},{1,0},{2,3},{3,2},{4,5},{5,4},{6,7},{7,6},{8,9},{9,8},{10,11... | collective-permute-start | bytes 4718600 | tf_op jit(solution)/shard_map/ppermute | solution.py:2010
  313.1 1.7 copy-start.1
  363.1 9.0 %copy-start.6 = (f32[32]{0:T(128)S(1)}, f32[32]{0:T(128)}, u32[]{:S(2)}) copy-start(f32[32]{0:T(128)} %param.26) | copy-start | bytes 388
  363.1 52.1 %all-to-all-start.3 = ((bf16[32,24,2048]{2,1,0:T(8,128)(2,1)}), bf16[32,24,2048]{2,1,0:T(8,128)(2,1)S(1)}, u32[]{:S(2)}, u32[]{:S(2)}) async-start(bf16[32,24,2048]{2,1,0:T(8,128)(2,1)} %bitcast.62), calls=%async_computation.3 | async-start | bytes 6291456 | tf_op jit(solution)/shard_map/all_to_all | solution.py:1043
  370.0 38.5 %collective-permute-start.4 = (bf16[1280,384]{1,0:T(8,128)(2,1)}, bf16[1280,384]{1,0:T(8,128)(2,1)}, u32[]{:S(2)}, u32[]{:S(2)}) collective-permute-start(bf16[1280,384]{1,0:T(8,128)(2,1)} %get-tuple-element.183), channel_id=1, source_target_pairs={{0,1},{1,0},{2,3},{3,2},{4,5},{5,4},{6,7},{7,6},{8,9},{9,8},{10,11... | collective-permute-start | bytes 2949128 | tf_op jit(solution)/shard_map/ppermute | solution.py:2010
  371.6 43.6 %collective-permute-start.5 = (bf16[240,2048]{1,0:T(8,128)(2,1)}, bf16[240,2048]{1,0:T(8,128)(2,1)}, u32[]{:S(2)}, u32[]{:S(2)}) collective-permute-start(bf16[240,2048]{1,0:T(8,128)(2,1)} %get-tuple-element.184), channel_id=1, source_target_pairs={{0,1},{1,0},{2,3},{3,2},{4,5},{5,4},{6,7},{7,6},{8,9},{9,8},{10,11... | collective-permute-start | bytes 2949128 | tf_op jit(solution)/shard_map/ppermute | solution.py:2010
  415.2 45.3 %copy-start.2 = (bf16[32,24,2048]{2,1,0:T(8,128)(2,1)}, bf16[32,24,2048]{2,1,0:T(8,128)(2,1)S(1)}, u32[]{:S(2)}) copy-start(bf16[32,24,2048]{2,1,0:T(8,128)(2,1)S(1)} %all-to-all-done.3) | copy-start | bytes 9437188
